TPU v7x, 256 devices: a whole 4x4x8 slice. The times are simulated.
256 devices in a mesh: dp: 32 (over z, y_hi, core), mp: 8 (over y_lo, x).
Axes of the slice: x: 4, y: 4 (y_hi: 2, y_lo: 2; y = y_hi * 2 + y_lo), z: 8, core: 2. Of those that a mesh axis runs over, the one named last changes fastest.
Arguments:
- audio: bfloat16 [64, 4096, 512], P('dp', 'mp'), may hold values from -6 to 6
- lengths: int32 [64], replicated, may hold values from 1 to 2048, as said below
- moved_slots: int32 [16, 1], replicated, may hold values from 0 to 1, as said below
- conv_weight: bfloat16 [1024, 512], replicated, may hold values from -0.1875 to 0.1875
- channel_params: float32 [512, 5], replicated, may hold values from 0.5 to 1.5
- proj_weight: bfloat16 [512, 120], replicated, may hold values from -0.25 to 0.25
- pos_weight: bfloat16 [128, 120, 120], replicated, may hold values from -0.046875 to 0.046875
- cotangent: bfloat16 [64, 2048, 120], P('dp', 'mp'), may hold values from -6 to 6
Outputs:
- hidden: bfloat16 [64, 2048, 120], P('dp', 'mp')
- grad_features: bfloat16 [64, 4096, 512], P('dp', 'mp')
- grad_pos: float32 [128, 120, 120], P('dp')
- grad_conv: float32 [1024, 512], P('dp')
- grad_proj: float32 [512, 120], P('dp')
- grad_channels: float32 [512, 5], P('dp')
Inputs may be any that keep to these rules, and one draw needn't show every extreme that they name: `lengths`: some utterance has all 2048 frames in every draw. `moved_slots`: each row holds one slot number, 0 or 1.
All inputs are finite; a program needn't handle non-finite values.
Results may differ from a plain program's by a relative error of at most 0.025.
Values may be sent and summed in bfloat16 or wider, within the bound.
No kernel may reach another device: no remote copies, remote signals or barrier semaphores. Data moves between devices by JAX's collectives and lax.ppermute only.
A program may use at most 128 MiB of HBM per device.

v0:
```python
import jax
import jax.numpy as jnp
from jax import lax
from jax.sharding import PartitionSpec as P

epsilon = 1e-05
root_half = 0.7071067811865476
density = 0.3989422804014327


def extended(block, sides, width):
    for axis, dim in sides:
        count = lax.axis_size(axis)
        forward = [(i, i + 1) for i in range(count - 1)]
        backward = [(target, source) for source, target in forward]
        low = lax.ppermute(
            lax.slice_in_dim(block, block.shape[dim] - width, None, axis=dim), axis, forward
        )
        high = lax.ppermute(lax.slice_in_dim(block, 0, width, axis=dim), axis, backward)
        block = jnp.concatenate([low, block, high], axis=dim)
    return block


def shortened(value):
    return jax.tree.map(lambda a: a.astype(jnp.bfloat16) if a.dtype == jnp.float32 else a, value)


def partner(block, axis, bit):
    count = lax.axis_size(axis)
    route = []
    for low in range(count):
        high = low | 1 << bit
        if high != low and high < count:
            route += [(low, high), (high, low)]
    return lax.ppermute(block, axis, route)


def gelu_exact(values):
    return 0.5 * values * (1.0 + lax.erf(values * root_half))


def gelu_slope(values):
    return (
        0.5 * (1.0 + lax.erf(values * root_half))
        + values * jnp.exp(-0.5 * values * values) * density
    )


def layer_norm(values, gain_row, shift_row):
    centre = jnp.mean(values, axis=-1, keepdims=True)
    offset = values - centre
    inverse = lax.rsqrt(jnp.mean(offset * offset, axis=-1, keepdims=True) + epsilon)
    normed = offset * inverse
    return (normed, inverse, normed * gain_row + shift_row)


def norm_backward(grad_out, normed, inverse, gain_row):
    scaled = grad_out * gain_row
    first_mean = jnp.mean(scaled, axis=-1, keepdims=True)
    second = jnp.mean(scaled * normed, axis=-1, keepdims=True)
    return inverse * (scaled - first_mean - normed * second)


def encode_forward(audio_rows, frame_mask, conv_weight, channel_params, proj_weight):
    paired = audio_rows.reshape(audio_rows.shape[0] // 2, 2 * audio_rows.shape[1])
    conv_out = (
        jnp.dot(paired, conv_weight, preferred_element_type=jnp.float32) + channel_params[:, 0]
    )
    normed_one, inverse_one, affine = layer_norm(
        conv_out, channel_params[:, 1], channel_params[:, 2]
    )
    encoded = gelu_exact(affine).astype(jnp.bfloat16)
    normed_two, inverse_two, projected_in = layer_norm(
        encoded.astype(jnp.float32), channel_params[:, 3], channel_params[:, 4]
    )
    projected_in = projected_in.astype(jnp.bfloat16)
    projected = jnp.dot(projected_in, proj_weight, preferred_element_type=jnp.float32)
    features = (projected * frame_mask[:, None]).astype(jnp.bfloat16)
    return (features, (normed_one, inverse_one, affine, normed_two, inverse_two, projected_in))


def blank_forward(audio_rows, frame_mask, conv_weight, channel_params, proj_weight):
    rows = frame_mask.shape[0]
    channels = conv_weight.shape[1]
    wide = jnp.zeros((rows, channels), jnp.float32)
    narrow = jnp.zeros((rows, 1), jnp.float32)
    features = jnp.zeros((rows, proj_weight.shape[1]), jnp.bfloat16)
    return (features, (wide, narrow, wide, wide, narrow, jnp.zeros((rows, channels), jnp.bfloat16)))


def encode_backward(audio_rows, stored, feature_grad, conv_weight, channel_params, proj_weight):
    normed_one, inverse_one, affine, normed_two, inverse_two, projected_in = stored
    paired = audio_rows.reshape(audio_rows.shape[0] // 2, 2 * audio_rows.shape[1])
    proj_grad = lax.dot_general(
        projected_in, feature_grad, (((0,), (0,)), ((), ())), preferred_element_type=jnp.float32
    )
    normed_grad = lax.dot_general(
        feature_grad, proj_weight, (((1,), (1,)), ((), ())), preferred_element_type=jnp.float32
    )
    encoded_grad = norm_backward(normed_grad, normed_two, inverse_two, channel_params[:, 3])
    affine_grad = encoded_grad * gelu_slope(affine)
    conv_grad = norm_backward(affine_grad, normed_one, inverse_one, channel_params[:, 1])
    conv_operand = conv_grad.astype(jnp.bfloat16)
    weight_grad = lax.dot_general(
        paired, conv_operand, (((0,), (0,)), ((), ())), preferred_element_type=jnp.float32
    )
    audio_grad = lax.dot_general(
        conv_operand, conv_weight, (((1,), (1,)), ((), ())), preferred_element_type=jnp.float32
    )
    audio_grad = audio_grad.astype(jnp.bfloat16).reshape(audio_rows.shape)
    vector_grad = jnp.stack(
        [
            jnp.sum(conv_grad, axis=0),
            jnp.sum(affine_grad * normed_one, axis=0),
            jnp.sum(affine_grad, axis=0),
            jnp.sum(normed_grad * normed_two, axis=0),
            jnp.sum(normed_grad, axis=0),
        ],
        axis=1,
    )
    return (weight_grad, proj_grad, vector_grad, audio_grad)


def mix_forward(padded, features, frame_mask, pos_weight):
    mixed_pre = lax.conv_general_dilated(
        padded[None],
        pos_weight,
        (1,),
        "VALID",
        dimension_numbers=("NWC", "WIO", "NWC"),
        preferred_element_type=jnp.float32,
    )[0]
    hidden = ((features.astype(jnp.float32) + gelu_exact(mixed_pre)) * frame_mask[:, None]).astype(
        jnp.bfloat16
    )
    return (mixed_pre, hidden)


def blank_mixing(padded, features, frame_mask, pos_weight):
    return (jnp.zeros(features.shape, jnp.float32), jnp.zeros(features.shape, jnp.bfloat16))


def mix_backward(padded, slope_pad, slope_rows, back_rows, frame_mask, flipped):
    kernel_grad = lax.conv_general_dilated(
        padded[:, :, None],
        slope_rows[:, None, :],
        (1,),
        "VALID",
        dimension_numbers=("WNC", "WIO", "WNC"),
        preferred_element_type=jnp.float32,
    )
    spread = lax.conv_general_dilated(
        slope_pad[None],
        flipped,
        (1,),
        "VALID",
        dimension_numbers=("NWC", "WIO", "NWC"),
        preferred_element_type=jnp.float32,
    )[0]
    feature_grad = ((back_rows.astype(jnp.float32) + spread) * frame_mask[:, None]).astype(
        jnp.bfloat16
    )
    return (kernel_grad, feature_grad)


def slot_backward(
    audio_rows,
    stored,
    padded,
    slope_pad,
    slope_rows,
    back_rows,
    frame_mask,
    conv_weight,
    channel_params,
    proj_weight,
    flipped,
):
    kernel_grad, feature_grad = mix_backward(
        padded, slope_pad, slope_rows, back_rows, frame_mask, flipped
    )
    weight_grad, proj_grad, vector_grad, audio_grad = encode_backward(
        audio_rows, stored, feature_grad, conv_weight, channel_params, proj_weight
    )
    return (kernel_grad, weight_grad, proj_grad, vector_grad, audio_grad)


def blank_backward(
    audio_rows,
    stored,
    padded,
    slope_pad,
    slope_rows,
    back_rows,
    frame_mask,
    conv_weight,
    channel_params,
    proj_weight,
    flipped,
):
    return (
        jnp.zeros(flipped.shape, jnp.float32),
        jnp.zeros(conv_weight.shape, jnp.float32),
        jnp.zeros(proj_weight.shape, jnp.float32),
        jnp.zeros(channel_params.shape, jnp.float32),
        jnp.zeros(audio_rows.shape, jnp.bfloat16),
    )


def skip_unless(living, function, blank, operands):
    return lax.cond(living, function, blank, *operands)


def per_device(
    audio, lengths, moved_slots, conv_weight, channel_params, proj_weight, pos_weight, cotangent
):
    slot_count = audio.shape[0]
    frames_dev = cotangent.shape[1]
    group_width = cotangent.shape[2]
    data_size = lax.axis_size("dp")
    model_size = lax.axis_size("mp")
    half_axis = data_size // 2
    swap_bit = half_axis.bit_length() - 1
    data_index = lax.axis_index("dp")
    model_index = lax.axis_index("mp")
    chosen = lax.dynamic_index_in_dim(moved_slots, data_index % half_axis, 0, keepdims=False)
    positions = jnp.arange(slot_count, dtype=jnp.int32)
    matches = chosen[None, :] == positions[:, None]
    is_moved = jnp.any(matches, axis=1)
    pick_index = jnp.sum(
        matches.astype(jnp.int32) * jnp.arange(chosen.shape[0], dtype=jnp.int32)[None, :], axis=1
    )
    own_lengths = lax.dynamic_slice_in_dim(lengths, data_index * slot_count, slot_count)

    def place(rows, received):
        return jnp.where(is_moved[:, None, None], jnp.take(received, pick_index, axis=0), rows)

    frame_ids = model_index * frames_dev + jnp.arange(frames_dev, dtype=jnp.int32)
    frame_masks = (frame_ids[None, :] < own_lengths[:, None]).astype(jnp.float32)
    living_all = model_index * frames_dev < own_lengths

    def forward_slot(members):
        audio_rows, frame_mask, living = members
        return skip_unless(
            living,
            encode_forward,
            blank_forward,
            (audio_rows, frame_mask, conv_weight, channel_params, proj_weight),
        )

    features, stored = lax.map(forward_slot, (audio, frame_masks, living_all))
    reach = pos_weight.shape[0] // 2
    padded = extended(features, (("mp", 1),), reach)[:, :-1]

    def mixing_slot(members):
        padded_rows, feature_rows, frame_mask, living = members
        return skip_unless(
            living, mix_forward, blank_mixing, (padded_rows, feature_rows, frame_mask, pos_weight)
        )

    mixed_pre, states = lax.map(mixing_slot, (padded, features, frame_masks, living_all))
    back_hidden, back_rows = partner(
        (shortened(jnp.take(states, chosen, axis=0)), jnp.take(cotangent, chosen, axis=0)),
        "dp",
        swap_bit,
    )
    hidden = place(states, back_hidden)
    back = place(cotangent, back_rows)
    slopes = (back.astype(jnp.float32) * gelu_slope(mixed_pre) * frame_masks[:, :, None]).astype(
        jnp.bfloat16
    )
    slope_pads = extended(slopes, (("mp", 1),), reach)[:, 1:]
    flipped = jnp.flip(pos_weight, 0).transpose(0, 2, 1)

    def backward_slot(totals, members):
        (
            audio_rows,
            stored_rows,
            padded_rows,
            slope_pad,
            slope_rows,
            back_slot,
            frame_mask,
            living,
        ) = members
        kernel_grad, weight_grad, proj_grad, vector_grad, audio_grad = skip_unless(
            living,
            slot_backward,
            blank_backward,
            (
                audio_rows,
                stored_rows,
                padded_rows,
                slope_pad,
                slope_rows,
                back_slot,
                frame_mask,
                conv_weight,
                channel_params,
                proj_weight,
                flipped,
            ),
        )
        totals = (
            totals[0] + kernel_grad,
            totals[1] + weight_grad,
            totals[2] + proj_grad,
            totals[3] + vector_grad,
        )
        return (totals, audio_grad)

    initial = (
        jnp.zeros(pos_weight.shape, jnp.float32),
        jnp.zeros(conv_weight.shape, jnp.float32),
        jnp.zeros(proj_weight.shape, jnp.float32),
        jnp.zeros(channel_params.shape, jnp.float32),
    )
    totals, audio_grads = lax.scan(
        backward_slot,
        initial,
        (audio, stored, padded, slope_pads, slopes, back, frame_masks, living_all),
    )
    grad_scale = (slot_count * data_size * frames_dev * model_size) ** (-0.5)
    scaled = (
        totals[0].reshape(-1, group_width) * grad_scale,
        totals[1] * grad_scale,
        totals[2] * grad_scale,
        totals[3] * grad_scale,
    )
    shares = (
        lax.psum_scatter(
            scaled[0].astype(jnp.bfloat16), "dp", scatter_dimension=0, tiled=True
        ).astype(jnp.float32),
        lax.psum_scatter(
            scaled[1].astype(jnp.bfloat16), "dp", scatter_dimension=0, tiled=True
        ).astype(jnp.float32),
        lax.psum_scatter(
            scaled[2].astype(jnp.bfloat16), "dp", scatter_dimension=0, tiled=True
        ).astype(jnp.float32),
        lax.psum_scatter(
            scaled[3].astype(jnp.bfloat16), "dp", scatter_dimension=0, tiled=True
        ).astype(jnp.float32),
    )
    joined = (
        lax.psum(shares[0].astype(jnp.bfloat16), "mp").astype(jnp.float32),
        lax.psum(shares[1].astype(jnp.bfloat16), "mp").astype(jnp.float32),
        lax.psum(shares[2].astype(jnp.bfloat16), "mp").astype(jnp.float32),
        lax.psum(shares[3].astype(jnp.bfloat16), "mp").astype(jnp.float32),
    )
    grad_pos = joined[0].reshape(-1, group_width, group_width)
    return (hidden, audio_grads, grad_pos, joined[1], joined[2], joined[3])


def solution(mesh):
    return jax.shard_map(
        per_device,
        mesh=mesh,
        in_specs=(P("dp", "mp", None), P(), P(), P(), P(), P(), P(), P("dp", "mp", None)),
        out_specs=(
            P("dp", "mp", None),
            P("dp", "mp", None),
            P("dp", None, None),
            P("dp", None),
            P("dp", None),
            P("dp", None),
        ),
        check_vma=False,
    )
```

profile of v0, /device:TPU:2, one launch (start us, length us, event | category | flops | bytes accessed | tf_op | source)
XLA Modules:
  0.0 748.5 jit_solution(3544253481749167537)
XLA Ops:
  7.3 1.0 copy.98
  9.1 17.6 %while.56 = (s32[]{:T(128)}, bf16[2,256,120]{1,2,0:T(8,128)(2,1)S(1)}, f32[2,256,512]{2,1,0:T(8,128)S(1)}, f32[2,256,1]{1,2,0:T(1,128)S(1)}, f32[2,256,512]{2,1,...) while((s32[]{:T(128)}, ...), condition=%wide.region_7.8_spmd.clone, body=%wide.region_0.7_spmd.clone.sunk | while | flops 304150016 | bytes 12170540 | solution.py:251
  10.4 8.4 %conditional.9 = (bf16[1,256,120]{1,2,0:T(8,128)(2,1)S(1)}, f32[1,256,512]{2,1,0:T(8,128)S(1)}, f32[1,256,1]{1,2,0:T(1,128)}, f32[1,256,512]{2,1,0:T(8,128)S(1)}...) conditional(s32[]{:T(128)} %bitcast.112, () %tuple.182, ...), branch_computations={%region_1.1_spmd, %region_2.6_spmd} | conditional | flops 304148992 | bytes 8369216 | solution.py:211
  10.4 0.9 fusion.59
  11.4 1.1 constant_dynamic-slice_fusion.1
  12.6 1.8 fusion.60
  15.2 1.0 convert_reduce_fusion
  17.0 1.0 fusion.7
  18.0 0.9 fusion.16
  19.7 1.1 constant_dynamic-update-slice_fusion.21
  22.8 1.3 conditional.9
  24.9 1.1 constant_dynamic-update-slice_fusion.21
  26.8 11.3 %collective-permute-start.1 = (bf16[2,64,120]{1,2,0:T(8,128)(2,1)S(1)}, bf16[2,64,120]{1,2,0:T(8,128)(2,1)S(1)}, u32[]{:S(2)}, u32[]{:S(2)}) collective-permute-start(bf16[2,64,120]{1,2,0:T(8,128)(2,1)S(1)} %get-tuple-element.1140), channel_id=1, source_target_pairs={{1,0},{2,1},{3,2},{4,3},{5,4},{6,5},{7,6},{9,8},{10,9},{11,10},{12... | collective-permute-start | bytes 92168 | tf_op jit(solution)/shard_map/ppermute | solution.py:19
  38.1 1.9 collective-permute-start
  42.6 7.0 collective-permute-start.3
  50.5 6.4 copy.100
  56.9 6.7 copy.108
  64.0 11.8 %while.57 = (s32[]{:T(128)}, f32[2,256,120]{1,2,0:T(8,128)S(1)}, bf16[2,256,120]{1,2,0:T(8,128)(2,1)S(1)}, pred[2]{0:T(512)(128)(4,1)S(1)}, bf16[2,383,120]{2,0,...) while((s32[]{:T(128)}, f32[2,256,120]{1,2,0:T(8,128)S(1)}, ...), condition=%wide.region_11.12_spmd.clone, body=%wide.region_8.11_spmd.clone.sunk | while | flops 943965184 | bytes 5106404 | solution.py:261
  65.4 8.5 %conditional.10 = (f32[1,256,120]{2,0,1:T(1,128)S(1)}, bf16[1,256,120]{2,0,1:T(2,128)(2,1)S(1)}) conditional(s32[]{:T(128)} %bitcast.113, () %tuple.185, (bf16[2,383,120]{2,0,1:T(2,128)(2,1)S(1)}, s32[]{:T(128)}, bf16[128,120,120]{2,1,0:T(8,128)(2,1)}, bf16[2,256,120]{2,0,1:T(2,128)(2,1)S(1)}, f32[2,256]{1,0:T(2,128)S(1)}) %tuple.186), branch_computations={%region_9.9_spmd, %region_10.10_spmd} | conditional | flops 943964160 | bytes 4365876 | solution.py:211
  65.4 8.5 %multiply_convert_fusion.1 = (bf16[1,256,120]{2,0,1:T(2,128)(2,1)S(1)}, f32[1,256,120]{2,0,1:T(1,128)S(1)}) fusion(bf16[2,256,120]{2,0,1:T(2,128)(2,1)S(1)} %get-tuple-element.490, s32[]{:T(128)} %get-tuple-element.488, f32[256]{0:T(256)S(1)} %bitcast.141, bf16[128,120,120]{2,1,0:T(8,128)(2,1)} %get-tuple-element.489, ...), kind=kOutput, calls=%fused_computation.30 | convolution fusion | flops 943964160 | bytes 4363808 | tf_op jit(solution)/shard_map/while/body/eval_jaxpr/cond/branch_1_fun/conv_general_dilated | solution.py:125
  75.9 0.8 fusion.55
  76.7 0.9 fusion.62
  77.7 10.8 %collective-permute-start.5 = (bf16[2,64,120]{1,2,0:T(8,128)(2,1)S(1)}, bf16[2,64,120]{1,2,0:T(8,128)(2,1)S(1)}, u32[]{:S(2)}, u32[]{:S(2)}) collective-permute-start(bf16[2,64,120]{1,2,0:T(8,128)(2,1)S(1)} %get-tuple-element.1138), channel_id=1, source_target_pairs={{1,0},{2,1},{3,2},{4,3},{5,4},{6,5},{7,6},{9,8},{10,9},{11,10},{12... | collective-permute-start | bytes 92168 | tf_op jit(solution)/shard_map/ppermute | solution.py:19
  88.5 1.9 collective-permute-start.4
  90.4 4.3 reverse_bitcast_fusion
  94.7 0.8 copy.109
  95.5 1.1 pad_maximum_fusion
  96.6 0.9 copy.110
  97.4 69.6 %while.58 = (s32[]{:T(128)}, f32[128,120,120]{2,1,0:T(8,128)}, f32[1024,512]{1,0:T(8,128)}, f32[512,120]{0,1:T(8,128)}, f32[512,5]{0,1:T(8,128)}, /*index=5*/bf1...) while((s32[]{:T(128)}, f32[128,120,120]{2,1,0:T(8,128)}, ...), condition=%wide.region_24.27_spmd.clone, body=%wide.region_12.26_spmd.clone.sunk | while | flops 2497117696 | bytes 107997728 | solution.py:318
  99.4 27.9 %conditional.11 = (f32[128,120,120]{2,1,0:T(8,128)}, f32[1024,512]{1,0:T(8,128)}, f32[512,120]{0,1:T(8,128)}, f32[512,5]{0,1:T(8,128)}, bf16[1,512,512]{2,1,0:T(8,128)(2,1)}) conditional(s32[]{:T(128)} %bitcast.114, () %tuple.188, (bf16[2,383,120]{1,2,0:T(8,128)(2,1)S(1)}, s32[]{:T(128)}, bf16[2,256,120]{1,2,0:T(8,128)(2,1)}, ...), branch_computations={%region_13.15_spmd, %region_14.25_spmd} | conditional | flops 2492253696 | bytes 49074540 | solution.py:211
  99.6 0.8 dynamic-slice_bitcast_fusion.1
  100.6 9.9 %fusion.64 = f32[128,120,120]{2,1,0:T(8,128)} fusion(bf16[383,120,1]{1,2,0:T(2,128)(2,1)S(1)} %copy.94, bf16[256,1,120]{2,1,0:T(2,128)(2,1)S(1)} %copy.95), kind=kOutput, calls=%fused_computation.134 | convolution fusion | flops 943718400 | bytes 7526160 | tf_op jit(solution)/shard_map/while/body/eval_jaxpr/cond/branch_1_fun/conv_general_dilated | solution.py:144
  110.8 0.8 fusion.61
  111.7 8.5 %multiply_convert_fusion.2 = (bf16[1,256,120]{2,0,1:T(2,128)(2,1)S(1)}, f32[1,256,120]{2,0,1:T(1,128)S(1)}) fusion(f32[256]{0:T(256)S(1)} %bitcast.135, bf16[128,120,120]{2,1,0:T(8,128)(2,1)} %get-tuple-element.511, bf16[2,383,120]{2,0,1:T(2,128)(2,1)S(1)} %copy-done.25, s32[]{:T(128)} %get-tuple-element.504, bf16[2,256,120]{2,0,1:T(2,128)(2,1)S(1)} %copy-done.28), kind=kOutput, calls=%fused_computation.65 | convolution fusion | flops 943841280 | bytes 4363808 | tf_op jit(solution)/shard_map/while/body/eval_jaxpr/cond/branch_1_fun/conv_general_dilated | solution.py:152
  121.5 1.8 fusion.42
  123.4 1.8 fusion.37
  126.3 1.0 broadcast_in_dim.143
  127.3 7.2 select_add_fusion.8
  134.6 2.4 select_add_fusion.9
  137.0 1.3 select_add_fusion.10
  138.4 0.8 select_add_fusion.11
  139.2 1.1 constant_dynamic-update-slice_fusion.25
  140.3 0.9 copy-done.39
  143.3 7.4 conditional.11
  143.3 3.6 broadcast.281
  146.9 1.6 broadcast.282
  149.8 0.8 broadcast_in_dim.140
  150.7 9.5 %select_add_fusion.8 = f32[128,120,120]{2,1,0:T(8,128)} fusion(f32[128,120,120]{2,1,0:T(8,128)} %get-tuple-element.1465, f32[128,120,120]{2,1,0:T(8,128)} %get-tuple-element.1603, pred[]{:T(512)S(6)} %compare.5), kind=kLoop, calls=%fused_computation.96.clone.1 | loop fusion | flops 3686400 | bytes 22118400 | tf_op jit(solution)/shard_map/while/body/eval_jaxpr/add | solution.py:305
  160.2 2.4 select_add_fusion.9
  162.6 1.3 select_add_fusion.10
  164.8 1.1 constant_dynamic-update-slice_fusion.25
  165.9 0.9 copy-done.39
  167.1 6.0 multiply_convert_fusion.5
  173.8 0.8 copy.115
  175.5 1.3 multiply_convert_fusion.6
  176.9 22.1 %collective-permute-start.2 = (bf16[1,256,120]{1,2,0:T(8,128)(2,1)S(1)}, bf16[1,256,120]{1,2,0:T(8,128)(2,1)S(1)}, u32[]{:S(2)}, u32[]{:S(2)}) collective-permute-start(bf16[1,256,120]{1,2,0:T(8,128)(2,1)S(1)} %dynamic-slice_select_fusion.1), channel_id=1, source_target_pairs={{0,128},{128,0},{8,136},{136,8},{16,144},{144,16},{24,152},{152,24... | collective-permute-start | bytes 184328 | tf_op jit(solution)/shard_map/ppermute | solution.py:35
  199.0 124.1 %reduce-scatter.9.cloned.1.call-done = bf16[480,120]{1,0:T(8,128)(2,1)} async-done(((bf16[15360,120]{1,0:T(8,128)(2,1)}), bf16[480,120]{1,0:T(8,128)(2,1)}) %reduce-scatter.9.cloned.1.call-update) | async-done | bytes 115216 | tf_op jit(solution)/shard_map/reduce_scatter | solution.py:331
  323.9 110.2 %reduce-scatter.15.cloned.1.call-done = bf16[16,5]{1,0:T(8,128)(2,1)} async-done(((bf16[512,5]{1,0:T(8,128)(2,1)}), bf16[16,5]{1,0:T(8,128)(2,1)}) %reduce-scatter.15.cloned.1.call-update) | async-done | bytes 176
  434.8 111.3 %reduce-scatter.13.cloned.1.call-done = bf16[16,120]{1,0:T(8,128)(2,1)} async-done(((bf16[512,120]{1,0:T(8,128)(2,1)}), bf16[16,120]{1,0:T(8,128)(2,1)}) %reduce-scatter.13.cloned.1.call-update) | async-done | bytes 3856
  546.1 0.8 copy.114
  546.9 116.5 %reduce-scatter.11.cloned.1.call-done = bf16[32,512]{1,0:T(8,128)(2,1)} async-done(((bf16[1024,512]{1,0:T(8,128)(2,1)}), bf16[32,512]{1,0:T(8,128)(2,1)}) %reduce-scatter.11.cloned.1.call-update) | async-done | bytes 32784 | tf_op jit(solution)/shard_map/reduce_scatter | solution.py:334
  663.4 30.0 %all-reduce = (bf16[16,120]{0,1:T(8,128)(2,1)S(1)}, bf16[32,512]{1,0:T(8,128)(2,1)S(1)}, bf16[16,5]{0,1:T(8,128)(2,1)S(1)}) all-reduce(bf16[16,120]{0,1:T(8,128)(2,1)S(1)} %copy.114, bf16[32,512]{1,0:T(8,128)(2,1)} %reduce-scatter.11.cloned.1.call-done, bf16[16,5]{0,1:T(8,128)(2,1)S(1)} %copy.116), channel_id=1, replica_groups=mesh['dp'=32,'mp'=8] {'mp'}, use_global_device_ids=true, to_apply=%region_30.33 | all-reduce | flops 18384 | bytes 73536 | tf_op jit(solution)/shard_map/psum | solution.py:347
  695.2 45.1 %all-reduce.3.cloned.1.call-done = bf16[4,120,120]{2,1,0:T(8,128)(2,1)} async-done(((bf16[4,120,120]{2,1,0:T(8,128)(2,1)}), bf16[4,120,120]{2,1,0:T(8,128)(2,1)}) %all-reduce.3.cloned.1.call-update) | async-done | bytes 115216 | tf_op jit(solution)/shard_map/psum | solution.py:345
  740.3 1.6 reshape.226
  (225 shorter events, 25.1 us)
Async XLA Ops:
  7.2 32.9 %copy-start = (s32[16,1]{0,1:T(1,128)S(1)}, s32[16,1]{0,1:T(1,128)}, u32[]{:S(2)}) copy-start(s32[16,1]{0,1:T(1,128)} %param.26) | copy-start | bytes 196
  7.2 315.9 %reduce-scatter.9.cloned.1.call-start = ((), (), s32[]{:S(2)}) async-start(), calls=%async_computation.4 | async-start | bytes 4055040 | tf_op jit(solution)/shard_map/reduce_scatter | solution.py:331
  9.1 33.5 %copy-start.22 = (bf16[2,256,120]{1,2,0:T(8,128)(2,1)S(1)}, bf16[2,256,120]{1,2,0:T(8,128)(2,1)}, u32[]{:S(2)}) copy-start(bf16[2,256,120]{1,2,0:T(8,128)(2,1)} %param.31) | copy-start | bytes 368644
  26.7 30.2 %copy-start.6 = (f32[2,256,512]{2,1,0:T(8,128)}, f32[2,256,512]{2,1,0:T(8,128)S(1)}, u32[]{:S(2)}) copy-start(f32[2,256,512]{2,1,0:T(8,128)S(1)} %get-tuple-element.1595) | copy-start | bytes 3145732
  26.7 30.2 %copy-start.13 = (bf16[512,120]{1,0:T(8,128)(2,1)}, bf16[512,120]{1,0:T(8,128)(2,1)S(1)}, u32[]{:S(2)}) copy-start(bf16[512,120]{1,0:T(8,128)(2,1)S(1)} %get-tuple-element.1663) | copy-start | bytes 368644
  26.7 30.2 %copy-start.30 = (f32[2,256,1]{1,2,0:T(1,128)}, f32[2,256,1]{1,2,0:T(1,128)S(1)}, u32[]{:S(2)}) copy-start(f32[2,256,1]{1,2,0:T(1,128)S(1)} %get-tuple-element.1586) | copy-start | bytes 6148
  26.7 30.2 %copy-start.32 = (f32[2,256,1]{1,2,0:T(1,128)}, f32[2,256,1]{1,2,0:T(1,128)S(1)}, u32[]{:S(2)}) copy-start(f32[2,256,1]{1,2,0:T(1,128)S(1)} %get-tuple-element.1587) | copy-start | bytes 6148
  26.8 36.9 %collective-permute-start.1 = (bf16[2,64,120]{1,2,0:T(8,128)(2,1)S(1)}, bf16[2,64,120]{1,2,0:T(8,128)(2,1)S(1)}, u32[]{:S(2)}, u32[]{:S(2)}) collective-permute-start(bf16[2,64,120]{1,2,0:T(8,128)(2,1)S(1)} %get-tuple-element.1140), channel_id=1, source_target_pairs={{1,0},{2,1},{3,2},{4,3},{5,4},{6,5},{7,6},{9,8},{10,9},{11,10},{12... | collective-permute-start | bytes 92168 | tf_op jit(solution)/shard_map/ppermute | solution.py:19
  38.1 25.6 %collective-permute-start = (bf16[2,64,120]{1,2,0:T(8,128)(2,1)S(1)}, bf16[2,64,120]{1,2,0:T(8,128)(2,1)S(1)}, u32[]{:S(2)}, u32[]{:S(2)}) collective-permute-start(bf16[2,64,120]{1,2,0:T(8,128)(2,1)S(1)} %get-tuple-element.1139), channel_id=1, source_target_pairs={{0,1},{1,2},{2,3},{3,4},{4,5},{5,6},{6,7},{8,9},{9,10},{10,11},{11... | collective-permute-start | bytes 92168 | tf_op jit(solution)/shard_map/ppermute | solution.py:16
  42.6 33.3 %collective-permute-start.3 = (bf16[1,256,120]{1,2,0:T(8,128)(2,1)S(1)}, bf16[1,256,120]{1,2,0:T(8,128)(2,1)S(1)}, u32[]{:S(2)}, u32[]{:S(2)}) collective-permute-start(bf16[1,256,120]{1,2,0:T(8,128)(2,1)S(1)} %dynamic-slice_select_fusion), channel_id=1, source_target_pairs={{0,128},{128,0},{8,136},{136,8},{16,144},{144,16},{24,152},{152,24... | collective-permute-start | bytes 184328 | tf_op jit(solution)/shard_map/ppermute | solution.py:35
  50.4 25.5 %copy-start.34 = (pred[2]{0:T(512)(128)(4,1)}, pred[2]{0:T(512)(128)(4,1)S(1)}, u32[]{:S(2)}) copy-start(pred[2]{0:T(512)(128)(4,1)S(1)} %iota_compare_fusion) | copy-start | bytes 10
  75.9 18.8 %copy-start.17 = (bf16[2,256,120]{1,2,0:T(8,128)(2,1)}, bf16[2,256,120]{1,2,0:T(8,128)(2,1)S(1)}, u32[]{:S(2)}) copy-start(bf16[2,256,120]{1,2,0:T(8,128)(2,1)S(1)} %get-tuple-element.570) | copy-start | bytes 368644
  77.7 17.8 %collective-permute-start.5 = (bf16[2,64,120]{1,2,0:T(8,128)(2,1)S(1)}, bf16[2,64,120]{1,2,0:T(8,128)(2,1)S(1)}, u32[]{:S(2)}, u32[]{:S(2)}) collective-permute-start(bf16[2,64,120]{1,2,0:T(8,128)(2,1)S(1)} %get-tuple-element.1138), channel_id=1, source_target_pairs={{1,0},{2,1},{3,2},{4,3},{5,4},{6,5},{7,6},{9,8},{10,9},{11,10},{12... | collective-permute-start | bytes 92168 | tf_op jit(solution)/shard_map/ppermute | solution.py:19
  88.5 7.0 collective-permute-start.4
  97.4 2.0 copy-start.15
  97.4 2.0 copy-start.23
  97.4 2.0 copy-start.26
  97.4 2.0 copy-start.36
  100.6 9.9 %copy-start.5 = (bf16[2,512,512]{2,1,0:T(8,128)(2,1)S(1)}, bf16[2,512,512]{2,1,0:T(8,128)(2,1)}, u32[]{:S(2)}) copy-start(bf16[2,512,512]{2,1,0:T(8,128)(2,1)} %get-tuple-element.506) | copy-start | bytes 3145732 | tf_op jit(solution)/shard_map/while/body/eval_jaxpr/cond
  100.6 10.9 %copy-start.29 = (f32[2,256]{1,0:T(2,128)S(1)}, f32[2,256]{1,0:T(2,128)}, u32[]{:S(2)}) copy-start(f32[2,256]{1,0:T(2,128)} %get-tuple-element.512) | copy-start | bytes 6148 | tf_op jit(solution)/shard_map/while/body/eval_jaxpr/cond
  100.6 11.0 %copy-start.25 = (bf16[2,383,120]{2,0,1:T(2,128)(2,1)S(1)}, bf16[2,383,120]{2,0,1:T(2,128)(2,1)}, u32[]{:S(2)}) copy-start(bf16[2,383,120]{2,0,1:T(2,128)(2,1)} %get-tuple-element.510) | copy-start | bytes 551524 | tf_op jit(solution)/shard_map/while/body/eval_jaxpr/cond
  100.6 11.0 %copy-start.28 = (bf16[2,256,120]{2,0,1:T(2,128)(2,1)S(1)}, bf16[2,256,120]{2,0,1:T(2,128)(2,1)}, u32[]{:S(2)}) copy-start(bf16[2,256,120]{2,0,1:T(2,128)(2,1)} %get-tuple-element.509) | copy-start | bytes 368644 | tf_op jit(solution)/shard_map/while/body/eval_jaxpr/cond
  111.6 8.6 %copy-start.8 = (f32[2,256,512]{2,1,0:T(8,128)S(1)}, f32[2,256,512]{2,1,0:T(8,128)}, u32[]{:S(2)}) copy-start(f32[2,256,512]{2,1,0:T(8,128)} %get-tuple-element.515) | copy-start | bytes 3145732 | tf_op jit(solution)/shard_map/while/body/eval_jaxpr/cond
  111.6 8.6 %copy-start.14 = (bf16[512,120]{1,0:T(8,128)(2,1)S(1)}, bf16[512,120]{1,0:T(8,128)(2,1)}, u32[]{:S(2)}) copy-start(bf16[512,120]{1,0:T(8,128)(2,1)} %get-tuple-element.513) | copy-start | bytes 368644 | tf_op jit(solution)/shard_map/while/body/eval_jaxpr/cond
  111.6 9.0 %copy-start.31 = (f32[2,256,1]{1,2,0:T(1,128)S(1)}, f32[2,256,1]{1,2,0:T(1,128)}, u32[]{:S(2)}) copy-start(f32[2,256,1]{1,2,0:T(1,128)} %get-tuple-element.507) | copy-start | bytes 6148 | tf_op jit(solution)/shard_map/while/body/eval_jaxpr/cond
  111.6 9.0 %copy-start.33 = (f32[2,256,1]{1,2,0:T(1,128)S(1)}, f32[2,256,1]{1,2,0:T(1,128)}, u32[]{:S(2)}) copy-start(f32[2,256,1]{1,2,0:T(1,128)} %get-tuple-element.508) | copy-start | bytes 6148 | tf_op jit(solution)/shard_map/while/body/eval_jaxpr/cond
  111.6 9.0 %copy-start.7 = (f32[2,256,512]{2,1,0:T(8,128)S(1)}, f32[2,256,512]{2,1,0:T(8,128)}, u32[]{:S(2)}) copy-start(f32[2,256,512]{2,1,0:T(8,128)} %get-tuple-element.517) | copy-start | bytes 3145732 | tf_op jit(solution)/shard_map/while/body/eval_jaxpr/cond
  111.7 9.0 %copy-start.12 = (f32[2,256,512]{2,1,0:T(8,128)S(1)}, f32[2,256,512]{2,1,0:T(8,128)}, u32[]{:S(2)}) copy-start(f32[2,256,512]{2,1,0:T(8,128)} %get-tuple-element.516) | copy-start | bytes 3145732 | tf_op jit(solution)/shard_map/while/body/eval_jaxpr/cond
  120.6 5.2 copy-start.1
  127.3 7.2 copy-start.2
  134.5 2.5 copy-start.9
  134.5 3.8 copy-start.19
  134.5 4.6 copy-start.38
  134.6 6.7 copy-start.16
  134.6 6.7 copy-start.24
  134.6 6.7 copy-start.27
  134.6 6.7 copy-start.37
  137.0 3.3 copy-start.3
  138.4 1.9 copy-start.10
  139.2 1.1 copy-start.20
  141.3 2.0 copy-start.15
  141.3 2.0 copy-start.23
  141.3 2.0 copy-start.26
  141.3 2.0 copy-start.36
  150.7 9.5 %copy-start.2 = (f32[1024,512]{1,0:T(8,128)S(1)}, f32[1024,512]{1,0:T(8,128)}, u32[]{:S(2)}) copy-start(f32[1024,512]{1,0:T(8,128)} %get-tuple-element.1604) | copy-start | bytes 6291460 | tf_op jit(solution)/shard_map/while
  160.1 2.5 copy-start.9
  160.1 3.8 copy-start.19
  160.1 4.6 copy-start.38
  160.1 6.7 copy-start.16
  160.1 6.7 copy-start.24
  160.2 6.7 copy-start.27
  160.2 6.7 copy-start.37
  162.6 3.3 copy-start.3
  164.0 1.9 copy-start.10
  164.7 1.1 copy-start.20
  173.0 1.6 copy-start.11
  173.1 2.5 copy-start.4
  173.1 3.8 copy-start.18
  173.1 150.1 %copy-start.35 = (pred[2]{0:T(512)(128)(4,1)S(1)}, pred[2]{0:T(512)(128)(4,1)}, u32[]{:S(2)}) copy-start(pred[2]{0:T(512)(128)(4,1)} %copy-done.34) | copy-start | bytes 10
  173.1 261.0 %reduce-scatter.15.cloned.1.call-start = ((), (), s32[]{:S(2)}) async-start(), calls=%async_computation.8 | async-start | bytes 135168
  174.6 371.5 %reduce-scatter.13.cloned.1.call-start = ((), (), s32[]{:S(2)}) async-start(), calls=%async_computation.7 | async-start | bytes 135168
  175.5 487.9 %reduce-scatter.11.cloned.1.call-start = ((), (), s32[]{:S(2)}) async-start(), calls=%async_computation.6 | async-start | bytes 1081344 | tf_op jit(solution)/shard_map/reduce_scatter | solution.py:334
  176.8 563.5 %all-reduce.3.cloned.1.call-start = ((), (), s32[]{:S(2)}) async-start(), calls=%async_computation.5 | async-start | bytes 245760 | tf_op jit(solution)/shard_map/psum | solution.py:345
  176.9 146.2 %collective-permute-start.2 = (bf16[1,256,120]{1,2,0:T(8,128)(2,1)S(1)}, bf16[1,256,120]{1,2,0:T(8,128)(2,1)S(1)}, u32[]{:S(2)}, u32[]{:S(2)}) collective-permute-start(bf16[1,256,120]{1,2,0:T(8,128)(2,1)S(1)} %dynamic-slice_select_fusion.1), channel_id=1, source_target_pairs={{0,128},{128,0},{8,136},{136,8},{16,144},{144,16},{24,152},{152,24... | collective-permute-start | bytes 184328 | tf_op jit(solution)/shard_map/ppermute | solution.py:35
  (3 other events, 2.7 us)
Sparse Core Ops, SparseCore 0:
  173.2 149.8 reduce-scatter.8
  327.0 107.0 reduce-scatter.14
  439.0 107.0 reduce-scatter.12
  550.0 113.2 reduce-scatter.10
  666.0 74.2 all-reduce.2
where the time goes:
time: 752 us; the launch traced here: 748 us
  waiting for transfers between devices  507 us (67%)
  starting transfers between devices  55.2 us (7%)
  local copies, waits for them, and re-layouts  54.9 us (7%)
  other arithmetic  45.9 us (6%)
  matrix products  34.2 us (5%)
  blocking collectives  30 us (4%)
  between operations  16.1 us (2%)
    unnamed x7, waiting for transfers between devices  222 us
    reduce_scatter x1, waiting for transfers between devices, per_device(): lax.psum_scatter(scaled[0].astype(jnp.bfloat16), 'dp', scatter_dimension=...  124 us
    reduce_scatter x1, waiting for transfers between devices, per_device(): lax.psum_scatter(scaled[1].astype(jnp.bfloat16), 'dp', scatter_dimension=...  116 us
    psum x1, waiting for transfers between devices, per_device(): lax.psum(shares[0].astype(jnp.bfloat16), 'mp').astype(jnp.float32)  45.1 us
    psum x1, blocking collectives, per_device(): lax.psum(shares[2].astype(jnp.bfloat16), 'mp').astype(jnp.float32)  30 us
    ppermute x2, starting transfers between devices, partner(): return lax.ppermute(block, axis, route)  29.1 us
    ppermute x2, starting transfers between devices, extended(): lax.ppermute(lax.slice_in_dim(block, 0, width, axis=dim), axis, backward)  22.1 us
    unnamed x38, local copies, waits for them, and re-layouts  20.6 us
  transfers between devices with their start and end apart: 11, of which 5 were waited for; matrix products, arithmetic and copies ran while one was open for 5% of the time, Pallas kernels for 0%

commit v1 on v0

v1 whole, which is shorter than its diff:
```python
import functools

import jax
import jax.numpy as jnp
from jax import lax
from jax.experimental import pallas as pl
from jax.experimental.pallas import tpu as pltpu
from jax.sharding import PartitionSpec as P

epsilon = 1e-05
root_half = 0.7071067811865476
density = 0.3989422804014327

SLOTS = 2
T = 256
C = 512
GC = 120
LANES = 128
K = 128
REACH = 64
EXT = T + 2 * REACH
NEAR = 16
GROUPS = 2
PER_GROUP = 4
SPAN = T + NEAR * (PER_GROUP - 1)
CHUNK = 32
VMEM_LIMIT = 56 * 1024 * 1024

f32 = jnp.float32
bf16 = jnp.bfloat16

VMEM = pl.BlockSpec(memory_space=pltpu.VMEM)
SMEM = pl.BlockSpec(memory_space=pltpu.SMEM)


def params(**more):
    return pltpu.CompilerParams(vmem_limit_bytes=VMEM_LIMIT, **more)


def cost(flops, moved, trans=0):
    return pl.CostEstimate(flops=flops, bytes_accessed=moved, transcendentals=trans)


def phi(values):
    return 0.5 * (1.0 + lax.erf(values * root_half))


def bell(values):
    return jnp.exp(-0.5 * values * values) * density


def row_mask(info_ref, slot, first, rows):
    ids = info_ref[0] + first + lax.broadcasted_iota(jnp.int32, (rows, 1), 0)
    return ids < info_ref[2 + slot]


def alive(info_ref, slot):
    return info_ref[0] < info_ref[2 + slot]


def nt(a, b):
    return lax.dot_general(a, b, (((1,), (1,)), ((), ())), preferred_element_type=f32)


def tn(a, b):
    return lax.dot_general(a, b, (((0,), (0,)), ((), ())), preferred_element_type=f32)


def nn(a, b):
    return jnp.dot(a, b, preferred_element_type=f32)


def arrange_body(pos_ref, fwd_ref, bwd_ref):
    fwd_ref[...] = jnp.zeros_like(fwd_ref)
    bwd_ref[...] = jnp.zeros_like(bwd_ref)
    for q in range(K // NEAR):
        for r in range(NEAR):
            fwd_ref[r * LANES : r * LANES + GC, q * LANES : q * LANES + GC] = pos_ref[q * NEAR + r]
            bwd_ref[q * LANES : q * LANES + GC, r * LANES : r * LANES + GC] = pos_ref[
                K - 1 - q * NEAR - r
            ]


def arrange(pos_weight):
    deep, wide = NEAR * LANES, K // NEAR * LANES
    return pl.pallas_call(
        arrange_body,
        out_shape=(
            jax.ShapeDtypeStruct((deep, wide), bf16),
            jax.ShapeDtypeStruct((wide, deep), bf16),
        ),
        in_specs=[VMEM],
        out_specs=(VMEM, VMEM),
        compiler_params=params(),
        cost_estimate=cost(0, 12 << 20),
        name="arrange",
    )(pos_weight)


def encode_body(
    info_ref,
    audio_ref,
    conv_ref,
    chan_ref,
    proj_ref,
    feat_ref,
    tail_ref,
    head_ref,
    pair_ref,
    q_ref,
    slope_ref,
    m_ref,
    inv_ref,
    wide,
    proj,
    mid,
):
    slot = pl.program_id(0)

    @pl.when(slot == 0)
    def _():
        proj[...] = jnp.zeros_like(proj)
        proj[:, :GC] = proj_ref[...]

    living = alive(info_ref, slot)

    @pl.when(living)
    def _():
        for c in range(C // LANES):
            wide[c] = audio_ref[0, :, c * LANES : (c + 1) * LANES].astype(f32)
            for tap in range(2):
                at = tap * C + c * LANES
                pair_ref[0, :, at : at + LANES] = wide[c, pl.ds(tap, T, stride=2), :].astype(bf16)
        mid[...] = nn(pair_ref[0], conv_ref[...])
        bias, gain, shift = chan_ref[0:1, :], chan_ref[1:2, :], chan_ref[2:3, :]
        gain_two, shift_two = chan_ref[3:4, :], chan_ref[4:5, :]
        for at in range(0, T, CHUNK):
            rows = slice(at, at + CHUNK)
            conv = mid[rows, :] + bias
            offset = conv - jnp.mean(conv, axis=-1, keepdims=True)
            inverse = lax.rsqrt(jnp.mean(offset * offset, axis=-1, keepdims=True) + epsilon)
            q = offset * inverse
            pre = q * gain + shift
            below = phi(pre)
            encoded = (pre * below).astype(bf16).astype(f32)
            slope_ref[0, rows, :] = below + pre * bell(pre)
            q_ref[0, rows, :] = q
            offset = encoded - jnp.mean(encoded, axis=-1, keepdims=True)
            inverse_two = lax.rsqrt(jnp.mean(offset * offset, axis=-1, keepdims=True) + epsilon)
            m = offset * inverse_two
            m_ref[0, rows, :] = m
            inv_ref[0, rows, :] = jnp.concatenate(
                [
                    jnp.broadcast_to(inverse, (CHUNK, LANES)),
                    jnp.broadcast_to(inverse_two, (CHUNK, LANES)),
                ],
                axis=1,
            )
            normed = (m * gain_two + shift_two).astype(bf16)
            projected = nn(normed, proj[...])
            mask = row_mask(info_ref, slot, at, CHUNK)
            feat_ref[0, rows, :] = jnp.where(mask, projected, 0.0).astype(bf16)

    @pl.when(jnp.logical_not(living))
    def _():
        feat_ref[...] = jnp.zeros_like(feat_ref)

    tail_ref[0] = feat_ref[0, T - REACH :, :]
    head_ref[0] = feat_ref[0, :REACH, :]


def by_slot(*dims):
    return pl.BlockSpec((1,) + dims, lambda s: (s,) + (0,) * len(dims))


def whole(*dims):
    return pl.BlockSpec(dims, lambda s: (0,) * len(dims))


def encode(info, audio, conv_weight, channels, proj_weight):
    return pl.pallas_call(
        encode_body,
        grid=(SLOTS,),
        out_shape=(
            jax.ShapeDtypeStruct((SLOTS, T, LANES), bf16),
            jax.ShapeDtypeStruct((SLOTS, REACH, LANES), bf16),
            jax.ShapeDtypeStruct((SLOTS, REACH, LANES), bf16),
            jax.ShapeDtypeStruct((SLOTS, T, 2 * C), bf16),
            jax.ShapeDtypeStruct((SLOTS, T, C), f32),
            jax.ShapeDtypeStruct((SLOTS, T, C), f32),
            jax.ShapeDtypeStruct((SLOTS, T, C), f32),
            jax.ShapeDtypeStruct((SLOTS, T, 2 * LANES), f32),
        ),
        in_specs=[
            SMEM,
            by_slot(2 * T, C),
            whole(2 * C, C),
            whole(8, C),
            whole(C, GC),
        ],
        out_specs=(
            by_slot(T, LANES),
            by_slot(REACH, LANES),
            by_slot(REACH, LANES),
            by_slot(T, 2 * C),
            by_slot(T, C),
            by_slot(T, C),
            by_slot(T, C),
            by_slot(T, 2 * LANES),
        ),
        scratch_shapes=[
            pltpu.VMEM((C // LANES, 2 * T, LANES), f32),
            pltpu.VMEM((C, LANES), bf16),
            pltpu.VMEM((T, C), f32),
        ],
        compiler_params=params(),
        cost_estimate=cost(2 * SLOTS * T * C * (2 * C + LANES), 8 << 20, SLOTS * T * C * 2),
        name="encode",
    )(info, audio, conv_weight, channels, proj_weight)


def fill_ext(ext, low, own, high):
    ext[:REACH, :] = low.astype(f32)
    ext[REACH : REACH + T, :] = own.astype(f32)
    ext[REACH + T :, :] = high.astype(f32)


def fill_windows(windows, ext, first):
    rows = T + NEAR * (K // NEAR - 1)
    for r in range(NEAR):
        take = min(rows, EXT - first - r)
        windows[:take, r * LANES : (r + 1) * LANES] = ext[
            first + r : first + r + take, :
        ].astype(bf16)


def gathered(group):
    total = group[:T, :LANES]
    for p in range(1, PER_GROUP):
        total += group[NEAR * p : NEAR * p + T, p * LANES : (p + 1) * LANES]
    return total


def mix_body(
    info_ref,
    feat_ref,
    low_ref,
    high_ref,
    weight_ref,
    cot_ref,
    recv_ref,
    states_ref,
    slopes_ref,
    tail_ref,
    head_ref,
    ext,
    windows,
    back,
):
    slot = pl.program_id(0)
    living = alive(info_ref, slot)
    wide = PER_GROUP * LANES

    @pl.when(living)
    def _():
        own = feat_ref[0]
        fill_ext(ext, low_ref[0], own, high_ref[0])
        fill_windows(windows, ext, 0)
        back[...] = jnp.zeros_like(back)
        picked = info_ref[1] == slot
        back[:, :GC] = jnp.where(
            picked, recv_ref[...].astype(f32), cot_ref[0].astype(f32)
        )
        group = jnp.zeros((SPAN, wide), f32)
        for g in range(GROUPS):
            at = g * NEAR * PER_GROUP
            group += nn(windows[at : at + SPAN, :], weight_ref[:, g * wide : (g + 1) * wide])
        mixed = gathered(group)
        below = phi(mixed)
        mask = row_mask(info_ref, slot, 0, T)
        states = jnp.where(mask, own.astype(f32) + mixed * below, 0.0)
        states_ref[0] = states[:, :GC].astype(bf16)
        slopes = jnp.where(mask, back[...] * (below + mixed * bell(mixed)), 0.0)
        slopes_ref[0] = slopes.astype(bf16)

    @pl.when(jnp.logical_not(living))
    def _():
        states_ref[...] = jnp.zeros_like(states_ref)
        slopes_ref[...] = jnp.zeros_like(slopes_ref)

    tail_ref[0] = slopes_ref[0, T - REACH :, :]
    head_ref[0] = slopes_ref[0, :REACH, :]


def mix(info, features, low, high, weight, cotangent, received):
    return pl.pallas_call(
        mix_body,
        grid=(SLOTS,),
        out_shape=(
            jax.ShapeDtypeStruct((SLOTS, T, GC), bf16),
            jax.ShapeDtypeStruct((SLOTS, T, LANES), bf16),
            jax.ShapeDtypeStruct((SLOTS, REACH, LANES), bf16),
            jax.ShapeDtypeStruct((SLOTS, REACH, LANES), bf16),
        ),
        in_specs=[
            SMEM,
            by_slot(T, LANES),
            by_slot(REACH, LANES),
            by_slot(REACH, LANES),
            whole(*weight.shape),
            by_slot(T, GC),
            whole(T, GC),
        ],
        out_specs=(
            by_slot(T, GC),
            by_slot(T, LANES),
            by_slot(REACH, LANES),
            by_slot(REACH, LANES),
        ),
        scratch_shapes=[
            pltpu.VMEM((EXT, LANES), f32),
            pltpu.VMEM((T + NEAR * (K // NEAR - 1), NEAR * LANES), bf16),
            pltpu.VMEM((T, LANES), f32),
        ],
        compiler_params=params(),
        cost_estimate=cost(2 * SLOTS * SPAN * K * LANES * LANES, 6 << 20, SLOTS * T * LANES * 2),
        name="mix",
    )(info, features, low, high, weight, cotangent, received)


def taps_body(scale, info_ref, feat_ref, low_ref, high_ref, slopes_ref, keep_ref, send_ref, ext, stack, spread):
    living = jnp.logical_or(alive(info_ref, 0), alive(info_ref, 1))
    first_core = info_ref[4] == 0

    @pl.when(living)
    def _():
        for slot in range(SLOTS):
            fill_ext(ext, low_ref[slot], feat_ref[slot], high_ref[slot])
            for g in range(GROUPS):
                at = g * NEAR * PER_GROUP
                for r in range(NEAR):
                    stack[
                        g, slot * SPAN : (slot + 1) * SPAN, r * LANES : (r + 1) * LANES
                    ] = ext[at + r : at + r + SPAN, :].astype(bf16)
        spread[...] = jnp.zeros_like(spread)
        for slot in range(SLOTS):
            for p in range(PER_GROUP):
                at = slot * SPAN + NEAR * p
                spread[at : at + T, p * LANES : (p + 1) * LANES] = slopes_ref[slot]
        turned = spread[...].T
        half = 8 * LANES
        for g in range(GROUPS):
            for far in range(2):
                sums = nn(turned, stack[g, :, far * half : (far + 1) * half]) * scale
                for p in range(PER_GROUP):
                    cell = 2 * (g * PER_GROUP + p) + far
                    for x in range(4):
                        rows = slice(p * LANES, (p + 1) * LANES)
                        even = sums[rows, x * LANES : (x + 1) * LANES]
                        odd = sums[rows, (x + 4) * LANES : (x + 5) * LANES]
                        keep = jnp.where(first_core, even, odd).astype(bf16)
                        send = jnp.where(first_core, odd, even).astype(bf16)
                        for y in range(2):
                            part = slice(y * REACH, (y + 1) * REACH)
                            keep_ref[y * 4 + x, cell] = keep[part, :]
                            send_ref[y * 4 + x, cell] = send[part, :]

    @pl.when(jnp.logical_not(living))
    def _():
        keep_ref[...] = jnp.zeros_like(keep_ref)
        send_ref[...] = jnp.zeros_like(send_ref)


def taps(scale, info, features, low, high, slopes):
    shape = jax.ShapeDtypeStruct((8, 16, REACH, LANES), bf16)
    return pl.pallas_call(
        functools.partial(taps_body, scale),
        out_shape=(shape, shape),
        in_specs=[SMEM] + [VMEM] * 4,
        out_specs=(VMEM, VMEM),
        scratch_shapes=[
            pltpu.VMEM((EXT, LANES), f32),
            pltpu.VMEM((GROUPS, SLOTS * SPAN, NEAR * LANES), bf16),
            pltpu.VMEM((SLOTS * SPAN, PER_GROUP * LANES), bf16),
        ],
        compiler_params=params(),
        cost_estimate=cost(2 * SLOTS * SPAN * K * LANES * LANES, 6 << 20),
        name="taps",
    )(info, features, low, high, slopes)


def backward_body(
    scale,
    info_ref,
    slopes_ref,
    low_ref,
    high_ref,
    cot_ref,
    recv_ref,
    weight_ref,
    pair_ref,
    q_ref,
    slope_ref,
    m_ref,
    inv_ref,
    conv_ref,
    chan_ref,
    proj_ref,
    audio_grad_ref,
    keep_ref,
    send_ref,
    ext,
    windows,
    proj,
    feat_grad,
    normed,
    mid,
    wide,
    conv_sum,
    proj_sum,
    chan_sum,
):
    slot = pl.program_id(0)
    living = alive(info_ref, slot)
    span = PER_GROUP * LANES

    @pl.when(slot == 0)
    def _():
        proj[...] = jnp.zeros_like(proj)
        proj[:, :GC] = proj_ref[...]
        conv_sum[...] = jnp.zeros_like(conv_sum)
        proj_sum[...] = jnp.zeros_like(proj_sum)
        chan_sum[...] = jnp.zeros_like(chan_sum)

    @pl.when(living)
    def _():
        fill_ext(ext, low_ref[0], slopes_ref[0], high_ref[0])
        fill_windows(windows, ext, 1)
        group = jnp.zeros((SPAN, span), f32)
        for g in range(GROUPS):
            at = g * NEAR * PER_GROUP
            group += nt(windows[at : at + SPAN, :], weight_ref[g * span : (g + 1) * span, :])
        spread = gathered(group)
        wide[0, :T, :] = jnp.zeros((T, LANES), f32)
        picked = info_ref[1] == slot
        wide[0, :T, :GC] = jnp.where(picked, recv_ref[...].astype(f32), cot_ref[0].astype(f32))
        mask = row_mask(info_ref, slot, 0, T)
        feat_grad[...] = jnp.where(mask, wide[0, :T, :] + spread, 0.0).astype(bf16)
        gain = chan_ref[1:2, :]
        gain_two, shift_two = chan_ref[3:4, :], chan_ref[4:5, :]
        mid[...] = nt(feat_grad[...], proj[...])
        for at in range(0, T, CHUNK):
            rows = slice(at, at + CHUNK)
            m = m_ref[0, rows, :]
            normed[rows, :] = (m * gain_two + shift_two).astype(bf16)
            normed_grad = mid[rows, :]
            chan_sum[24:32, :] += jnp.sum((normed_grad * m).reshape(-1, 8, C), axis=0)
            chan_sum[32:40, :] += jnp.sum(normed_grad.reshape(-1, 8, C), axis=0)
            scaled = normed_grad * gain_two
            first = jnp.mean(scaled, axis=-1, keepdims=True)
            second = jnp.mean(scaled * m, axis=-1, keepdims=True)
            inverse_two = inv_ref[0, rows, LANES : LANES + 1]
            pre_grad = inverse_two * (scaled - first - m * second) * slope_ref[0, rows, :]
            q = q_ref[0, rows, :]
            chan_sum[8:16, :] += jnp.sum((pre_grad * q).reshape(-1, 8, C), axis=0)
            chan_sum[16:24, :] += jnp.sum(pre_grad.reshape(-1, 8, C), axis=0)
            scaled = pre_grad * gain
            first = jnp.mean(scaled, axis=-1, keepdims=True)
            second = jnp.mean(scaled * q, axis=-1, keepdims=True)
            inverse = inv_ref[0, rows, 0:1]
            conv_grad = inverse * (scaled - first - q * second)
            chan_sum[0:8, :] += jnp.sum(conv_grad.reshape(-1, 8, C), axis=0)
            mid[rows, :] = conv_grad
        operand = mid[...].astype(bf16)
        for tap in range(2):
            rows = slice(tap * C, (tap + 1) * C)
            audio_grad = nt(operand, conv_ref[rows, :])
            for c in range(C // LANES):
                wide[c, pl.ds(tap, T, stride=2), :] = audio_grad[:, c * LANES : (c + 1) * LANES]
            conv_sum[rows, :] += tn(pair_ref[0, :, rows], operand)
        for c in range(C // LANES):
            audio_grad_ref[0, :, c * LANES : (c + 1) * LANES] = wide[c].astype(bf16)
        proj_sum[...] += tn(normed[...], feat_grad[...])

    @pl.when(jnp.logical_not(living))
    def _():
        audio_grad_ref[...] = jnp.zeros_like(audio_grad_ref)

    @pl.when(slot == SLOTS - 1)
    def _():
        first_core = info_ref[4] == 0
        for cell in range(16):
            for y in range(2):
                for x in range(4):
                    parts = []
                    for odd in range(2):
                        at = (2 * cell + odd) * 32 + y * 16
                        parts.append(conv_sum[at : at + 16, x * LANES : (x + 1) * LANES] * scale)
                    even, odd = parts
                    keep_ref[y * 4 + x, cell, :16, :] = jnp.where(first_core, even, odd).astype(bf16)
                    send_ref[y * 4 + x, cell, :16, :] = jnp.where(first_core, odd, even).astype(bf16)
            even = proj_sum[cell * 32 : cell * 32 + 16, :] * scale
            odd = proj_sum[cell * 32 + 16 : cell * 32 + 32, :] * scale
            keep_ref[0, cell, 16:, :] = jnp.where(first_core, even, odd).astype(bf16)
            send_ref[0, cell, 16:, :] = jnp.where(first_core, odd, even).astype(bf16)
            tile = slice(cell // 4 * LANES, (cell // 4 + 1) * LANES)
            lines = [
                jnp.sum(chan_sum[8 * n : 8 * n + 8, tile], axis=0, keepdims=True) * scale
                for n in range(5)
            ]
            block = jnp.concatenate(lines + [jnp.zeros((11, LANES), f32)], axis=0).astype(bf16)
            keep_ref[1, cell, 16:, :] = block
            send_ref[1, cell, 16:, :] = block
            for rest in range(2, 8):
                keep_ref[rest, cell, 16:, :] = jnp.zeros((16, LANES), bf16)
                send_ref[rest, cell, 16:, :] = jnp.zeros((16, LANES), bf16)


def backward(
    scale, info, slopes, low, high, cotangent, received, weight, stored, conv_weight, channels, proj_weight
):
    pair, q, slope, m, inv = stored
    shape = jax.ShapeDtypeStruct((8, 16, 32, LANES), bf16)
    return pl.pallas_call(
        functools.partial(backward_body, scale),
        grid=(SLOTS,),
        out_shape=(jax.ShapeDtypeStruct((SLOTS, 2 * T, C), bf16), shape, shape),
        in_specs=[
            SMEM,
            by_slot(T, LANES),
            by_slot(REACH, LANES),
            by_slot(REACH, LANES),
            by_slot(T, GC),
            whole(T, GC),
            whole(*weight.shape),
            by_slot(T, 2 * C),
            by_slot(T, C),
            by_slot(T, C),
            by_slot(T, C),
            by_slot(T, 2 * LANES),
            whole(2 * C, C),
            whole(8, C),
            whole(C, GC),
        ],
        out_specs=(by_slot(2 * T, C), whole(*shape.shape), whole(*shape.shape)),
        scratch_shapes=[
            pltpu.VMEM((EXT, LANES), f32),
            pltpu.VMEM((T + NEAR * (K // NEAR - 1), NEAR * LANES), bf16),
            pltpu.VMEM((C, LANES), bf16),
            pltpu.VMEM((T, LANES), bf16),
            pltpu.VMEM((T, C), bf16),
            pltpu.VMEM((T, C), f32),
            pltpu.VMEM((C // LANES, 2 * T, LANES), f32),
            pltpu.VMEM((2 * C, C), f32),
            pltpu.VMEM((C, LANES), f32),
            pltpu.VMEM((40, C), f32),
        ],
        compiler_params=params(),
        cost_estimate=cost(
            2 * SLOTS * (SPAN * K * LANES * LANES + T * C * (4 * C + 2 * LANES)), 14 << 20
        ),
        name="backward",
    )(
        info,
        slopes,
        low,
        high,
        cotangent,
        received,
        weight,
        pair,
        q,
        slope,
        m,
        inv,
        conv_weight,
        channels,
        proj_weight,
    )


def join_body(a_ref, b_ref, c_ref, d_ref, out_ref):
    out_ref[0, :, :REACH, :] = (a_ref[0].astype(f32) + b_ref[0].astype(f32)).astype(bf16)
    out_ref[0, :, REACH:, :] = (c_ref[0].astype(f32) + d_ref[0].astype(f32)).astype(bf16)


def join(a, b, c, d):
    rows = REACH + 32
    return pl.pallas_call(
        join_body,
        grid=(8,),
        out_shape=jax.ShapeDtypeStruct((8, 16, rows, LANES), bf16),
        in_specs=[by_slot(16, REACH, LANES)] * 2 + [by_slot(16, 32, LANES)] * 2,
        out_specs=by_slot(16, rows, LANES),
        compiler_params=params(),
        cost_estimate=cost(0, 10 << 20),
        name="join",
    )(a, b, c, d)


def total_body(in_ref, out_ref):
    total = in_ref[0].astype(f32)
    for n in range(1, in_ref.shape[0]):
        total += in_ref[n].astype(f32)
    out_ref[...] = total.astype(bf16)


def total(parts):
    return pl.pallas_call(
        total_body,
        out_shape=jax.ShapeDtypeStruct(parts.shape[1:], bf16),
        in_specs=[VMEM],
        out_specs=VMEM,
        compiler_params=params(),
        cost_estimate=cost(0, 2 * parts.size),
        name="total",
    )(parts)


def finish_body(info_ref, in_ref, pos_ref, conv_ref, proj_ref, chan_ref, turned):
    for x in range(4):
        block = jnp.concatenate(
            [in_ref[x, :REACH, :].astype(f32), in_ref[4 + x, :REACH, :].astype(f32)], axis=0
        ).T
        pos_ref[x] = block[:GC, :GC]
        for y in range(2):
            conv_ref[y * 16 : (y + 1) * 16, x * LANES : (x + 1) * LANES] = in_ref[
                y * 4 + x, REACH : REACH + 16, :
            ].astype(f32)
    proj_ref[...] = in_ref[0, REACH + 16 :, :].astype(f32)[:, :GC]
    lines = in_ref[1, REACH + 16 :, :].astype(f32)
    turned[...] = jnp.concatenate([lines] * 8, axis=0).T
    at = pl.multiple_of(lax.rem(info_ref[5], 8) * 16, 16)
    chan_ref[...] = turned[pl.ds(at, 16), :][:, :5]


def finish(info, cells):
    return pl.pallas_call(
        finish_body,
        out_shape=(
            jax.ShapeDtypeStruct((4, GC, GC), f32),
            jax.ShapeDtypeStruct((32, C), f32),
            jax.ShapeDtypeStruct((16, GC), f32),
            jax.ShapeDtypeStruct((16, 5), f32),
        ),
        in_specs=[SMEM, VMEM],
        out_specs=(VMEM,) * 4,
        scratch_shapes=[pltpu.VMEM((LANES, LANES), f32)],
        compiler_params=params(),
        name="finish",
    )(info, cells)


def neighbours(tail, head):
    count = lax.axis_size("mp")
    forward = [(i, i + 1) for i in range(count - 1)]
    backward_route = [(i + 1, i) for i in range(count - 1)]
    return lax.ppermute(tail, "mp", forward), lax.ppermute(head, "mp", backward_route)


def per_device(
    audio, lengths, moved_slots, conv_weight, channel_params, proj_weight, pos_weight, cotangent
):
    data_size = lax.axis_size("dp")
    model_size = lax.axis_size("mp")
    half = data_size // 2
    data_index = lax.axis_index("dp")
    model_index = lax.axis_index("mp")
    scale = (SLOTS * data_size * T * model_size) ** -0.5
    chosen = lax.dynamic_index_in_dim(moved_slots[:, 0], data_index % half, 0, keepdims=False)
    own = lax.dynamic_slice_in_dim(lengths, data_index * SLOTS, SLOTS)
    info = jnp.stack(
        [model_index * T, chosen, own[0], own[1], data_index % 2, data_index, 0, 0]
    ).astype(jnp.int32)
    swap = [(i, i ^ half) for i in range(data_size)]
    core_swap = [(i, i ^ 1) for i in range(data_size)]
    channels = jnp.pad(channel_params.T, ((0, 3), (0, 0)))

    def picked(rows):
        return lax.dynamic_index_in_dim(rows, chosen, 0, keepdims=False)

    received = lax.ppermute(picked(cotangent), "dp", swap)
    features, tail, head, *stored = encode(info, audio, conv_weight, channels, proj_weight)
    low, high = neighbours(tail, head)
    forward_weight, backward_weight = arrange(pos_weight)
    states, slopes, tail, head = mix(
        info, features, low, high, forward_weight, cotangent, received
    )
    slope_low, slope_high = neighbours(tail, head)
    other = lax.ppermute(picked(states), "dp", swap)
    pos_keep, pos_send = taps(scale, info, features, low, high, slopes)
    pos_recv = lax.ppermute(pos_send, "dp", core_swap)
    audio_grad, keep, send = backward(
        scale,
        info,
        slopes,
        slope_low,
        slope_high,
        cotangent,
        received,
        backward_weight,
        stored,
        conv_weight,
        channels,
        proj_weight,
    )
    recv = lax.ppermute(send, "dp", core_swap)
    moved = (jnp.arange(SLOTS) == chosen)[:, None, None]
    hidden = jnp.where(moved, other[None], states)
    cells = join(pos_keep, pos_recv, keep, recv)
    cells = total(lax.all_to_all(cells, "mp", 0, 0, tiled=True))
    groups = [list(range(bit, data_size, 2)) for bit in range(2)]
    cells = total(
        lax.all_to_all(cells, "dp", 0, 0, axis_index_groups=groups, tiled=True)
    )
    copies = jnp.broadcast_to(cells[None], (model_size,) + cells.shape)
    cells = lax.all_to_all(copies, "mp", 0, 0, tiled=True)
    return (hidden, audio_grad) + tuple(finish(info, cells))


def solution(mesh):
    return jax.shard_map(
        per_device,
        mesh=mesh,
        in_specs=(P("dp", "mp", None), P(), P(), P(), P(), P(), P(), P("dp", "mp", None)),
        out_specs=(
            P("dp", "mp", None),
            P("dp", "mp", None),
            P("dp", None, None),
            P("dp", None),
            P("dp", None),
            P("dp", None),
        ),
        check_vma=False,
    )
```

time: 752 us -> 181 us (0.24)
  waiting for transfers between devices: 507 us -> 20.5 us
  Pallas kernels: 0 us -> 52.1 us
  other arithmetic: 45.9 us -> 0.78 us
  matrix products: 34.2 us -> 0 us
  local copies, waits for them, and re-layouts: 54.9 us -> 23.2 us
  starting transfers between devices: 55.2 us -> 34.9 us
  blocking collectives: 30 us -> 46.2 us
  between operations: 16.1 us -> 2.92 us
    reduce_scatter x2 -> x0, waiting for transfers between devices: 241 us -> none  [the longest x1 124 us: per_device(): lax.psum_scatter(scaled[0].astype(jnp.bfloat16), 'dp', scatter_dimension=...]
    unnamed x7 -> x0, waiting for transfers between devices: 222 us -> none
    pallas_call x0 -> x9, Pallas kernels: none -> 52.1 us  [the longest x1 11.6 us: backward(): pl.pallas_call(functools.partial(backward_body, scale), grid=(SLOTS,), ou...]
    all_to_all x0 -> x1, blocking collectives: none -> 46.2 us  [per_device(): cells = total(lax.all_to_all(cells, 'mp', 0, 0, tiled=True))]
    psum x1 -> x0, waiting for transfers between devices: 45.1 us -> none  [per_device(): lax.psum(shares[0].astype(jnp.bfloat16), 'mp').astype(jnp.float32)]
    psum x1 -> x0, blocking collectives: 30 us -> none  [per_device(): lax.psum(shares[2].astype(jnp.bfloat16), 'mp').astype(jnp.float32)]
    ppermute x6 -> x8, starting transfers between devices: 55 us -> 25.1 us  [the longest x1 7.28 us: per_device(): received = lax.ppermute(picked(cotangent), 'dp', swap)]
    conv_general_dilated x3 -> x0, matrix products: 26.9 us -> none  [the longest x1 9.89 us: mix_backward(): lax.conv_general_dilated(padded[:, :, None], slope_rows[:, None, :], (1,)...]
  transfers between devices with their start and end apart: 11 -> 10, of which waited for: 5 -> 4; matrix products, arithmetic and copies ran while one was open for 5% -> 9% of each run, Pallas kernels for 0% -> 15%
where the time goes in v1:
time: 181 us
  Pallas kernels  52.1 us (29%)
  blocking collectives  46.2 us (26%)
  starting transfers between devices  34.9 us (19%)
  local copies, waits for them, and re-layouts  23.2 us (13%)
  waiting for transfers between devices  20.5 us (11%)
  between operations  2.92 us (2%)
    all_to_all x1, blocking collectives, per_device(): cells = total(lax.all_to_all(cells, 'mp', 0, 0, tiled=True))  46.2 us
    unnamed x31, local copies, waits for them, and re-layouts  16.8 us
    pallas_call x1, Pallas kernels, backward(): pl.pallas_call(functools.partial(backward_body, scale), grid=(SLOTS,), ou...  11.6 us
    all_to_all x1, waiting for transfers between devices, per_device(): lax.all_to_all(cells, 'dp', 0, 0, axis_index_groups=groups, tiled=True)  9.5 us
    pallas_call x1, Pallas kernels, arrange(): pl.pallas_call(arrange_body, out_shape=(jax.ShapeDtypeStruct((deep, wide)...  7.92 us
    pallas_call x1, Pallas kernels, taps(): pl.pallas_call(functools.partial(taps_body, scale), out_shape=(shape, sha...  7.5 us
    ppermute x1, starting transfers between devices, per_device(): received = lax.ppermute(picked(cotangent), 'dp', swap)  7.28 us
    pallas_call x1, Pallas kernels, join(): pl.pallas_call(join_body, grid=(8,), out_shape=jax.ShapeDtypeStruct((8, 1...  6.88 us
  transfers between devices with their start and end apart: 10, of which 4 were waited for; matrix products, arithmetic and copies ran while one was open for 9% of the time, Pallas kernels for 15%

profile of v1, /device:TPU:2, one launch (start us, length us, event | category | flops | bytes accessed | tf_op | source)
XLA Modules:
  0.0 180.6 jit_solution(18283332474047872914)
XLA Ops:
  0.6 0.0 copy-start
  0.7 0.6 copy-done
  1.3 0.7 constant_dynamic-slice_fusion.1
  4.0 0.8 constant_dynamic-slice_fusion
  4.9 0.1 copy.16
  5.0 7.3 %collective-permute-start.2 = (bf16[256,120]{1,0:T(8,128)(2,1)S(1)}, bf16[256,120]{1,0:T(8,128)(2,1)S(1)}, u32[]{:S(2)}, u32[]{:S(2)}) collective-permute-start(bf16[256,120]{1,0:T(8,128)(2,1)S(1)} %bitcast.9), channel_id=1, source_target_pairs={{0,128},{8,136},{16,144},{24,152},{32,160},{40,168},{48,176},{56,1... | collective-permute-start | bytes 184328 | tf_op jit(solution)/shard_map/ppermute | solution.py:682
  12.3 1.7 copy.14.proj_ref
  13.9 0.7 dynamic_slice.18
  14.7 1.3 pad.4.chan_ref
  16.0 1.4 stack.16.info_ref
  17.3 5.6 %encode.1 = (bf16[2,256,128]{2,1,0:T(8,128)(2,1)}, bf16[2,64,128]{2,1,0:T(8,128)(2,1)}, bf16[2,64,128]{2,1,0:T(8,128)(2,1)}, bf16[2,256,1024]{2,1,0:T(8,128)(2,1...) custom-call(s32[8]{0:T(128)} %stack.16.info_ref, ...), custom_call_target="tpu_custom_call" | custom-call | flops 603979776 | bytes 8388608 | tf_op jit(solution)/shard_map/encode/pallas_call | solution.py:181
  23.0 3.4 %collective-permute-start = (bf16[2,64,128]{2,1,0:T(8,128)(2,1)}, bf16[2,64,128]{2,1,0:T(8,128)(2,1)S(1)}, u32[]{:S(2)}, u32[]{:S(2)}) collective-permute-start(bf16[2,64,128]{2,1,0:T(8,128)(2,1)} %get-tuple-element.30), channel_id=1, source_target_pairs={{0,1},{1,2},{2,3},{3,4},{4,5},{5,6},{6,7},{8,9},{9,10},{10,11},{11... | collective-permute-start | bytes 98312 | tf_op jit(solution)/shard_map/ppermute | solution.py:658
  26.4 2.4 %collective-permute-start.1 = (bf16[2,64,128]{2,1,0:T(8,128)(2,1)}, bf16[2,64,128]{2,1,0:T(8,128)(2,1)S(1)}, u32[]{:S(2)}, u32[]{:S(2)}) collective-permute-start(bf16[2,64,128]{2,1,0:T(8,128)(2,1)} %get-tuple-element.31), channel_id=1, source_target_pairs={{1,0},{2,1},{3,2},{4,3},{5,4},{6,5},{7,6},{9,8},{10,9},{11,10},{12... | collective-permute-start | bytes 98312 | tf_op jit(solution)/shard_map/ppermute | solution.py:658
  28.8 1.7 copy.17.cot_ref
  30.5 6.3 %copy.15.pos_ref = bf16[128,120,120]{2,1,0:T(8,128)(2,1)} copy(bf16[128,120,120]{0,2,1:T(8,128)(2,1)} %param.14) | data formatting | bytes 7372800 | tf_op args[6]
  36.8 7.9 %arrange.1 = (bf16[2048,1024]{1,0:T(8,128)(2,1)}, bf16[1024,2048]{1,0:T(8,128)(2,1)}) custom-call(bf16[128,120,120]{2,1,0:T(8,128)(2,1)} %copy.15.pos_ref), custom_call_target="tpu_custom_call" | custom-call | bytes 12582912 | tf_op jit(solution)/shard_map/arrange/pallas_call | solution.py:86
  44.7 0.0 collective-permute-done.low_ref
  44.7 0.0 copy-start.7
  44.7 0.0 collective-permute-done.1.high_ref
  44.7 0.0 copy-start.8
  44.7 0.0 collective-permute-done.2.recv_ref
  44.7 0.0 copy-start.6
  44.7 0.6 copy-done.7
  45.3 0.0 copy-done.8
  45.3 0.0 copy-done.6
  45.4 6.1 %mix.1 = (bf16[2,256,120]{2,1,0:T(8,128)(2,1)}, bf16[2,256,128]{2,1,0:T(8,128)(2,1)}, bf16[2,64,128]{2,1,0:T(8,128)(2,1)}, bf16[2,64,128]{2,1,0:T(8,128)(2,1)}) custom-call(s32[8]{0:T(128)} %stack.16.info_ref, bf16[2,256,128]{2,1,0:T(8,128)(2,1)} %get-tuple-element.29.feat_ref, bf16[2,64,128]{2,1,0:T(8,128)(2,1)} %copy-done.7, ...), custom_call_target="tpu_custom_call" | custom-call | flops 2550136832 | bytes 6291456 | tf_op jit(solution)/shard_map/mix/pallas_call | solution.py:296
  51.5 0.0 copy-start.12
  51.5 0.0 copy-start.10
  51.5 7.5 %taps.1 = (bf16[8,16,64,128]{3,2,1,0:T(8,128)(2,1)}, bf16[8,16,64,128]{3,2,1,0:T(8,128)(2,1)}) custom-call(s32[8]{0:T(128)} %stack.16.info_ref, bf16[2,256,128]{2,1,0:T(8,128)(2,1)} %get-tuple-element.29.feat_ref, bf16[2,64,128]{2,1,0:T(8,128)(2,1)} %copy-done.7, bf16[2,64,128]{2,1,0:T(8,128)(2,1)} %copy-done.8, ...), custom_call_target="tpu_custom_call" | custom-call | flops 2550136832 | bytes 6291456 | tf_op jit(solution)/shard_map/taps/pallas_call | solution.py:376
  59.0 0.0 collective-permute-start.6
  59.0 0.0 copy-done.12
  59.0 3.4 %collective-permute-start.4 = (bf16[2,64,128]{2,1,0:T(8,128)(2,1)S(1)}, bf16[2,64,128]{2,1,0:T(8,128)(2,1)S(1)}, u32[]{:S(2)}, u32[]{:S(2)}) collective-permute-start(bf16[2,64,128]{2,1,0:T(8,128)(2,1)S(1)} %copy-done.12), channel_id=1, source_target_pairs={{0,1},{1,2},{2,3},{3,4},{4,5},{5,6},{6,7},{8,9},{9,10},{10,11},{11... | collective-permute-start | bytes 98312 | tf_op jit(solution)/shard_map/ppermute | solution.py:658
  62.4 0.0 copy-done.10
  62.4 2.6 %collective-permute-start.5 = (bf16[2,64,128]{2,1,0:T(8,128)(2,1)S(1)}, bf16[2,64,128]{2,1,0:T(8,128)(2,1)S(1)}, u32[]{:S(2)}, u32[]{:S(2)}) collective-permute-start(bf16[2,64,128]{2,1,0:T(8,128)(2,1)S(1)} %copy-done.10), channel_id=1, source_target_pairs={{1,0},{2,1},{3,2},{4,3},{5,4},{6,5},{7,6},{9,8},{10,9},{11,10},{12... | collective-permute-start | bytes 98312 | tf_op jit(solution)/shard_map/ppermute | solution.py:658
  65.1 0.0 collective-permute-done.4.low_ref
  65.1 0.0 copy-start.9
  65.1 3.2 %collective-permute-done.5.high_ref = bf16[2,64,128]{2,1,0:T(8,128)(2,1)S(1)} collective-permute-done((bf16[2,64,128]{2,1,0:T(8,128)(2,1)S(1)}, bf16[2,64,128]{2,1,0:T(8,128)(2,1)S(1)}, u32[]{:S(2)}, u32[]{:S(2)}) %collective-permute-start.5) | collective-permute-done | bytes 32800 | tf_op jit(solution)/shard_map/ppermute | solution.py:658
  68.3 0.0 copy-done.9
  68.3 0.6 copy-done.11
  68.9 11.6 %backward.1 = (bf16[2,512,512]{2,1,0:T(8,128)(2,1)}, bf16[8,16,32,128]{3,2,1,0:T(8,128)(2,1)}, bf16[8,16,32,128]{3,2,1,0:T(8,128)(2,1)}) custom-call(s32[8]{0:T(128)} %stack.16.info_ref, bf16[2,256,128]{2,1,0:T(8,128)(2,1)} %get-tuple-element.34.slopes_ref, bf16[2,64,128]{2,1,0:T(8,128)(2,1)} %copy-done.9, bf16[2,64,128]{2,1,0:T(8,128)(2,1)} %copy-done.11, ...), custom_call_target="tpu_custom_call" | custom-call | flops 3758096384 | bytes 14680064 | tf_op jit(solution)/shard_map/backward/pallas_call | solution.py:524
  80.5 0.1 collective-permute-start.7
  80.6 2.9 %collective-permute-done.7.d_ref = bf16[8,16,32,128]{3,2,1,0:T(8,128)(2,1)S(1)} collective-permute-done((bf16[8,16,32,128]{3,2,1,0:T(8,128)(2,1)}, bf16[8,16,32,128]{3,2,1,0:T(8,128)(2,1)S(1)}, u32[]{:S(2)}, u32[]{:S(2)}) %collective-permute-start.7) | collective-permute-done | bytes 1048608 | tf_op jit(solution)/shard_map/ppermute | solution.py:707
  83.4 0.0 collective-permute-done.6.b_ref
  83.4 1.0 copy-done.3
  84.4 0.7 copy-done.1
  85.1 6.9 %join.1 = bf16[8,16,96,128]{3,2,1,0:T(8,128)(2,1)} custom-call(bf16[8,16,64,128]{3,2,1,0:T(8,128)(2,1)} %get-tuple-element.44.a_ref, bf16[8,16,64,128]{3,2,1,0:T(8,128)(2,1)} %copy-done.1, bf16[8,16,32,128]{3,2,1,0:T(8,128)(2,1)} %get-tuple-element.46.c_ref, bf16[8,16,32,128]{3,2,1,0:T(8,128)(2,1)} %copy-done.3), custom_call_target="tpu_custom_call" | custom-call | bytes 10485760 | tf_op jit(solution)/shard_map/join/pallas_call | solution.py:589
  92.0 46.2 %all_to_all.15.in_ref = bf16[8,16,96,128]{3,2,1,0:T(8,128)(2,1)} all-to-all(bf16[8,16,96,128]{3,2,1,0:T(8,128)(2,1)} %join.1), channel_id=1, replica_groups=mesh['dp'=32,'mp'=8] {'mp'}, dimensions={0} | all-to-all | bytes 6291456 | tf_op jit(solution)/shard_map/all_to_all | solution.py:711
  138.2 3.1 %total.2 = bf16[16,96,128]{2,1,0:T(8,128)(2,1)} custom-call(bf16[8,16,96,128]{3,2,1,0:T(8,128)(2,1)} %all_to_all.15.in_ref), custom_call_target="tpu_custom_call" | custom-call | bytes 3145728 | tf_op jit(solution)/shard_map/total/pallas_call | solution.py:609
  141.3 4.7 %all-to-all-start.1 = ((bf16[16,96,128]{2,1,0:T(8,128)(2,1)}), bf16[16,96,128]{2,1,0:T(8,128)(2,1)S(1)}, u32[]{:S(2)}, u32[]{:S(2)}) async-start(bf16[16,96,128]{2,1,0:T(8,128)(2,1)} %total.2), calls=%async_computation.1 | async-start | bytes 786432 | tf_op jit(solution)/shard_map/all_to_all | solution.py:714
  146.0 0.0 copy-done.5
  146.1 5.9 %collective-permute-start.3 = (bf16[256,120]{1,0:T(8,128)(2,1)S(1)}, bf16[256,120]{1,0:T(8,128)(2,1)S(1)}, u32[]{:S(2)}, u32[]{:S(2)}) collective-permute-start(bf16[256,120]{1,0:T(8,128)(2,1)S(1)} %dynamic-slice_bitcast_fusion), channel_id=1, source_target_pairs={{0,128},{8,136},{16,144},{24,152},{32,160},{40,168},{48,176},{56,1... | collective-permute-start | bytes 184328 | tf_op jit(solution)/shard_map/ppermute | solution.py:690
  152.0 0.7 iota_compare_fusion
  152.7 9.5 %all-to-all-done.1.in_ref = bf16[16,96,128]{2,1,0:T(8,128)(2,1)S(1)} async-done(((bf16[16,96,128]{2,1,0:T(8,128)(2,1)}), bf16[16,96,128]{2,1,0:T(8,128)(2,1)S(1)}, u32[]{:S(2)}, u32[]{:S(2)}) %all-to-all-start.1) | async-done | bytes 393248 | tf_op jit(solution)/shard_map/all_to_all | solution.py:714
  162.2 0.8 copy-done.2
  162.9 1.7 total.3
  164.6 1.4 broadcast_in_dim.26
  166.0 5.0 %all-to-all-start.2 = ((bf16[8,96,128]{2,1,0:T(8,128)(2,1)}), bf16[8,96,128]{2,1,0:T(8,128)(2,1)S(1)}, u32[]{:S(2)}, u32[]{:S(2)}) async-start(bf16[8,96,128]{2,1,0:T(8,128)(2,1)} %broadcast_in_dim.26), calls=%async_computation.2 | async-start | bytes 393216 | tf_op jit(solution)/shard_map/all_to_all | solution.py:717
  171.0 0.0 collective-permute-done.3
  171.1 0.1 broadcast_select_fusion
  171.1 0.8 copy.20
  171.9 5.0 %all-to-all-done.2.in_ref = bf16[8,96,128]{2,1,0:T(8,128)(2,1)S(1)} async-done(((bf16[8,96,128]{2,1,0:T(8,128)(2,1)}), bf16[8,96,128]{2,1,0:T(8,128)(2,1)S(1)}, u32[]{:S(2)}, u32[]{:S(2)}) %all-to-all-start.2) | async-done | bytes 196640 | tf_op jit(solution)/shard_map/all_to_all | solution.py:717
  176.9 0.7 copy-done.4
  177.5 1.7 finish.1
  179.3 1.4 copy.21
  (8 shorter events, 0.0 us)
Async XLA Ops:
  0.6 0.7 copy-start
  5.0 39.7 %collective-permute-start.2 = (bf16[256,120]{1,0:T(8,128)(2,1)S(1)}, bf16[256,120]{1,0:T(8,128)(2,1)S(1)}, u32[]{:S(2)}, u32[]{:S(2)}) collective-permute-start(bf16[256,120]{1,0:T(8,128)(2,1)S(1)} %bitcast.9), channel_id=1, source_target_pairs={{0,128},{8,136},{16,144},{24,152},{32,160},{40,168},{48,176},{56,1... | collective-permute-start | bytes 184328 | tf_op jit(solution)/shard_map/ppermute | solution.py:682
  23.0 21.7 %collective-permute-start = (bf16[2,64,128]{2,1,0:T(8,128)(2,1)}, bf16[2,64,128]{2,1,0:T(8,128)(2,1)S(1)}, u32[]{:S(2)}, u32[]{:S(2)}) collective-permute-start(bf16[2,64,128]{2,1,0:T(8,128)(2,1)} %get-tuple-element.30), channel_id=1, source_target_pairs={{0,1},{1,2},{2,3},{3,4},{4,5},{5,6},{6,7},{8,9},{9,10},{10,11},{11... | collective-permute-start | bytes 98312 | tf_op jit(solution)/shard_map/ppermute | solution.py:658
  26.4 18.3 %collective-permute-start.1 = (bf16[2,64,128]{2,1,0:T(8,128)(2,1)}, bf16[2,64,128]{2,1,0:T(8,128)(2,1)S(1)}, u32[]{:S(2)}, u32[]{:S(2)}) collective-permute-start(bf16[2,64,128]{2,1,0:T(8,128)(2,1)} %get-tuple-element.31), channel_id=1, source_target_pairs={{1,0},{2,1},{3,2},{4,3},{5,4},{6,5},{7,6},{9,8},{10,9},{11,10},{12... | collective-permute-start | bytes 98312 | tf_op jit(solution)/shard_map/ppermute | solution.py:658
  44.7 0.6 copy-start.7
  44.7 0.6 copy-start.8
  44.7 0.6 copy-start.6
  51.5 7.5 %copy-start.12 = (bf16[2,64,128]{2,1,0:T(8,128)(2,1)S(1)}, bf16[2,64,128]{2,1,0:T(8,128)(2,1)}, u32[]{:S(2)}) copy-start(bf16[2,64,128]{2,1,0:T(8,128)(2,1)} %get-tuple-element.35) | copy-start | bytes 98308
  51.5 10.9 %copy-start.10 = (bf16[2,64,128]{2,1,0:T(8,128)(2,1)S(1)}, bf16[2,64,128]{2,1,0:T(8,128)(2,1)}, u32[]{:S(2)}) copy-start(bf16[2,64,128]{2,1,0:T(8,128)(2,1)} %get-tuple-element.36) | copy-start | bytes 98308
  59.0 24.4 %collective-permute-start.6 = (bf16[8,16,64,128]{3,2,1,0:T(8,128)(2,1)}, bf16[8,16,64,128]{3,2,1,0:T(8,128)(2,1)S(1)}, u32[]{:S(2)}, u32[]{:S(2)}) collective-permute-start(bf16[8,16,64,128]{3,2,1,0:T(8,128)(2,1)} %get-tuple-element.45), channel_id=1, source_target_pairs={{0,8},{8,0},{16,24},{24,16},{32,40},{40,32},{48,56},{56,48},{64,72... | collective-permute-start | bytes 6291464 | tf_op jit(solution)/shard_map/ppermute | solution.py:692
  59.0 6.0 %collective-permute-start.4 = (bf16[2,64,128]{2,1,0:T(8,128)(2,1)S(1)}, bf16[2,64,128]{2,1,0:T(8,128)(2,1)S(1)}, u32[]{:S(2)}, u32[]{:S(2)}) collective-permute-start(bf16[2,64,128]{2,1,0:T(8,128)(2,1)S(1)} %copy-done.12), channel_id=1, source_target_pairs={{0,1},{1,2},{2,3},{3,4},{4,5},{5,6},{6,7},{8,9},{9,10},{10,11},{11... | collective-permute-start | bytes 98312 | tf_op jit(solution)/shard_map/ppermute | solution.py:658
  62.4 5.8 %collective-permute-start.5 = (bf16[2,64,128]{2,1,0:T(8,128)(2,1)S(1)}, bf16[2,64,128]{2,1,0:T(8,128)(2,1)S(1)}, u32[]{:S(2)}, u32[]{:S(2)}) collective-permute-start(bf16[2,64,128]{2,1,0:T(8,128)(2,1)S(1)} %copy-done.10), channel_id=1, source_target_pairs={{1,0},{2,1},{3,2},{4,3},{5,4},{6,5},{7,6},{9,8},{10,9},{11,10},{12... | collective-permute-start | bytes 98312 | tf_op jit(solution)/shard_map/ppermute | solution.py:658
  65.1 3.2 %copy-start.9 = (bf16[2,64,128]{2,1,0:T(8,128)(2,1)}, bf16[2,64,128]{2,1,0:T(8,128)(2,1)S(1)}, u32[]{:S(2)}) copy-start(bf16[2,64,128]{2,1,0:T(8,128)(2,1)S(1)} %collective-permute-done.4.low_ref) | copy-start | bytes 98308
  68.3 0.6 copy-start.11
  80.5 3.0 %collective-permute-start.7 = (bf16[8,16,32,128]{3,2,1,0:T(8,128)(2,1)}, bf16[8,16,32,128]{3,2,1,0:T(8,128)(2,1)S(1)}, u32[]{:S(2)}, u32[]{:S(2)}) collective-permute-start(bf16[8,16,32,128]{3,2,1,0:T(8,128)(2,1)} %get-tuple-element.47), channel_id=1, source_target_pairs={{0,8},{8,0},{16,24},{24,16},{32,40},{40,32},{48,56},{56,48},{64,72... | collective-permute-start | bytes 3145736 | tf_op jit(solution)/shard_map/ppermute | solution.py:707
  83.4 1.0 copy-start.3
  83.4 1.7 copy-start.1
  138.2 7.8 %copy-start.5 = (bf16[2,256,120]{2,1,0:T(8,128)(2,1)S(1)}, bf16[2,256,120]{2,1,0:T(8,128)(2,1)}, u32[]{:S(2)}) copy-start(bf16[2,256,120]{2,1,0:T(8,128)(2,1)} %get-tuple-element.33) | copy-start | bytes 368644
  141.3 20.9 %all-to-all-start.1 = ((bf16[16,96,128]{2,1,0:T(8,128)(2,1)}), bf16[16,96,128]{2,1,0:T(8,128)(2,1)S(1)}, u32[]{:S(2)}, u32[]{:S(2)}) async-start(bf16[16,96,128]{2,1,0:T(8,128)(2,1)} %total.2), calls=%async_computation.1 | async-start | bytes 786432 | tf_op jit(solution)/shard_map/all_to_all | solution.py:714
  146.1 25.0 %collective-permute-start.3 = (bf16[256,120]{1,0:T(8,128)(2,1)S(1)}, bf16[256,120]{1,0:T(8,128)(2,1)S(1)}, u32[]{:S(2)}, u32[]{:S(2)}) collective-permute-start(bf16[256,120]{1,0:T(8,128)(2,1)S(1)} %dynamic-slice_bitcast_fusion), channel_id=1, source_target_pairs={{0,128},{8,136},{16,144},{24,152},{32,160},{40,168},{48,176},{56,1... | collective-permute-start | bytes 184328 | tf_op jit(solution)/shard_map/ppermute | solution.py:690
  162.2 0.8 copy-start.2
  166.0 10.8 %all-to-all-start.2 = ((bf16[8,96,128]{2,1,0:T(8,128)(2,1)}), bf16[8,96,128]{2,1,0:T(8,128)(2,1)S(1)}, u32[]{:S(2)}, u32[]{:S(2)}) async-start(bf16[8,96,128]{2,1,0:T(8,128)(2,1)} %broadcast_in_dim.26), calls=%async_computation.2 | async-start | bytes 393216 | tf_op jit(solution)/shard_map/all_to_all | solution.py:717
  176.9 0.7 copy-start.4

commit v2 on v1

v2 whole, which is shorter than its diff:
```python
import functools

import jax
import jax.numpy as jnp
from jax import lax
from jax.experimental import pallas as pl
from jax.experimental.pallas import tpu as pltpu
from jax.sharding import PartitionSpec as P

epsilon = 1e-05
root_half = 0.7071067811865476
density = 0.3989422804014327

SLOTS = 2
T = 256
C = 512
GC = 120
LANES = 128
K = 128
REACH = 64
EXT = T + 2 * REACH
NEAR = 16
GROUPS = 2
PER_GROUP = 4
SPAN = T + NEAR * (PER_GROUP - 1)
CHUNK = 32
MP = 8
DP = 32
X = 4
CELLS = 16
PIECE = 2 * T + REACH
REST = CELLS + 2
VMEM_LIMIT = 56 * 1024 * 1024

f32 = jnp.float32
bf16 = jnp.bfloat16

VMEM = pl.BlockSpec(memory_space=pltpu.VMEM)
SMEM = pl.BlockSpec(memory_space=pltpu.SMEM)


def params(**more):
    return pltpu.CompilerParams(vmem_limit_bytes=VMEM_LIMIT, **more)


def cost(flops, moved, trans=0):
    return pl.CostEstimate(flops=flops, bytes_accessed=moved, transcendentals=trans)


def phi(values):
    return 0.5 * (1.0 + lax.erf(values * root_half))


def bell(values):
    return jnp.exp(-0.5 * values * values) * density


def nt(a, b):
    return lax.dot_general(a, b, (((1,), (1,)), ((), ())), preferred_element_type=f32)


def tn(a, b):
    return lax.dot_general(a, b, (((0,), (0,)), ((), ())), preferred_element_type=f32)


def nn(a, b):
    return jnp.dot(a, b, preferred_element_type=f32)


class Place:
    def __init__(self, dev_ref, len_ref, mov_ref):
        self.data = dev_ref[0] // MP
        self.model = lax.rem(dev_ref[0], MP)
        self.x = lax.rem(self.model, X)
        self.y = self.model // X
        self.core = lax.rem(self.data, 2)
        self.cell = self.data // 2
        self.first = self.model * T
        self.lengths = len_ref
        self.chosen = mov_ref[lax.rem(self.data, DP // 2)]

    def length(self, slot):
        return self.lengths[self.data * SLOTS + slot]

    def alive(self, slot):
        return self.first < self.length(slot)

    def mask(self, slot):
        ids = self.first + lax.broadcasted_iota(jnp.int32, (T, 1), 0)
        return ids < self.length(slot)


def by_slot(*dims):
    return pl.BlockSpec((1,) + dims, lambda s: (s,) + (0,) * len(dims))


def whole(*dims):
    return pl.BlockSpec(dims, lambda s: (0,) * len(dims))


def encode_body(
    dev_ref,
    len_ref,
    mov_ref,
    audio_ref,
    conv_ref,
    chan_ref,
    proj_ref,
    feat_ref,
    tail_ref,
    head_ref,
    pair_ref,
    q_ref,
    slope_ref,
    m_ref,
    inv_ref,
    wide,
    proj,
    mid,
    normed,
):
    place = Place(dev_ref, len_ref, mov_ref)
    slot = pl.program_id(0)

    @pl.when(slot == 0)
    def _():
        proj[...] = jnp.zeros_like(proj)
        proj[:GC, :] = proj_ref[...]

    living = place.alive(slot)

    @pl.when(living)
    def _():
        for c in range(C // LANES):
            wide[c] = audio_ref[0, :, c * LANES : (c + 1) * LANES].astype(f32)
            for tap in range(2):
                at = tap * C + c * LANES
                pair_ref[0, :, at : at + LANES] = wide[c, pl.ds(tap, T, stride=2), :].astype(bf16)
        mid[...] = nn(pair_ref[0], conv_ref[...])
        bias, gain, shift = chan_ref[0:1, :], chan_ref[1:2, :], chan_ref[2:3, :]
        gain_two, shift_two = chan_ref[3:4, :], chan_ref[4:5, :]
        for at in range(0, T, CHUNK):
            rows = slice(at, at + CHUNK)
            conv = mid[rows, :] + bias
            offset = conv - jnp.mean(conv, axis=-1, keepdims=True)
            inverse = lax.rsqrt(jnp.mean(offset * offset, axis=-1, keepdims=True) + epsilon)
            q = offset * inverse
            pre = q * gain + shift
            below = phi(pre)
            encoded = (pre * below).astype(bf16).astype(f32)
            slope_ref[0, rows, :] = below + pre * bell(pre)
            q_ref[0, rows, :] = q
            offset = encoded - jnp.mean(encoded, axis=-1, keepdims=True)
            inverse_two = lax.rsqrt(jnp.mean(offset * offset, axis=-1, keepdims=True) + epsilon)
            m = offset * inverse_two
            m_ref[0, rows, :] = m
            inv_ref[0, rows, :] = jnp.concatenate(
                [
                    jnp.broadcast_to(inverse, (CHUNK, LANES)),
                    jnp.broadcast_to(inverse_two, (CHUNK, LANES)),
                ],
                axis=1,
            )
            normed[rows, :] = (m * gain_two + shift_two).astype(bf16)
        projected = nt(normed[...], proj[...])
        feat_ref[0] = jnp.where(place.mask(slot), projected, 0.0).astype(bf16)

    @pl.when(jnp.logical_not(living))
    def _():
        feat_ref[...] = jnp.zeros_like(feat_ref)

    tail_ref[0] = feat_ref[0, T - REACH :, :]
    head_ref[0] = feat_ref[0, :REACH, :]


def encode(place, audio, conv_weight, channels, proj):
    return pl.pallas_call(
        encode_body,
        grid=(SLOTS,),
        out_shape=(
            jax.ShapeDtypeStruct((SLOTS, T, LANES), bf16),
            jax.ShapeDtypeStruct((SLOTS, REACH, LANES), bf16),
            jax.ShapeDtypeStruct((SLOTS, REACH, LANES), bf16),
            jax.ShapeDtypeStruct((SLOTS, T, 2 * C), bf16),
            jax.ShapeDtypeStruct((SLOTS, T, C), f32),
            jax.ShapeDtypeStruct((SLOTS, T, C), f32),
            jax.ShapeDtypeStruct((SLOTS, T, C), f32),
            jax.ShapeDtypeStruct((SLOTS, T, 2 * LANES), f32),
        ),
        in_specs=[SMEM] * 3
        + [
            by_slot(2 * T, C),
            whole(2 * C, C),
            whole(5, C),
            whole(GC, C),
        ],
        out_specs=(
            by_slot(T, LANES),
            by_slot(REACH, LANES),
            by_slot(REACH, LANES),
            by_slot(T, 2 * C),
            by_slot(T, C),
            by_slot(T, C),
            by_slot(T, C),
            by_slot(T, 2 * LANES),
        ),
        scratch_shapes=[
            pltpu.VMEM((C // LANES, 2 * T, LANES), f32),
            pltpu.VMEM((LANES, C), bf16),
            pltpu.VMEM((T, C), f32),
            pltpu.VMEM((T, C), bf16),
        ],
        compiler_params=params(),
        cost_estimate=cost(2 * SLOTS * T * C * (2 * C + LANES), 8 << 20, SLOTS * T * C * 2),
        name="encode",
    )(*place, audio, conv_weight, channels, proj)


def fill_ext(ext, low, own, high):
    ext[:REACH, :] = low.astype(f32)
    ext[REACH : REACH + T, :] = own.astype(f32)
    ext[REACH + T :, :] = high.astype(f32)


def fill_windows(windows, ext, first):
    rows = T + NEAR * (K // NEAR - 1)
    for r in range(NEAR):
        windows[:, r * LANES : (r + 1) * LANES] = ext[first + r : first + r + rows, :].astype(bf16)


def gathered(group):
    total = group[:T, :LANES]
    for p in range(1, PER_GROUP):
        total += group[NEAR * p : NEAR * p + T, p * LANES : (p + 1) * LANES]
    return total


def fill_back(turned, place, slot, cot_ref, recv_ref):
    turned[GC:, :] = jnp.zeros((LANES - GC, T), f32)
    turned[:GC, :] = jnp.where(
        place.chosen == slot, recv_ref[0].astype(f32), cot_ref[0].astype(f32)
    )


def mix_body(
    dev_ref,
    len_ref,
    mov_ref,
    feat_ref,
    low_ref,
    high_ref,
    pos_ref,
    cot_ref,
    recv_ref,
    states_ref,
    sent_ref,
    slopes_ref,
    tail_ref,
    head_ref,
    piece_ref,
    ext,
    windows,
    turned,
    weight,
):
    place = Place(dev_ref, len_ref, mov_ref)
    slot = pl.program_id(0)
    living = place.alive(slot)
    wide = PER_GROUP * LANES

    @pl.when(slot == 0)
    def _():
        fill_weight(weight, pos_ref, True)

    @pl.when(living)
    def _():
        own = feat_ref[0]
        fill_ext(ext, low_ref[0], own, high_ref[0])
        fill_windows(windows, ext, 0)
        fill_back(turned, place, slot, cot_ref, recv_ref)
        back = turned[...].T
        group = jnp.zeros((SPAN, wide), f32)
        for g in range(GROUPS):
            at = g * NEAR * PER_GROUP
            group += nn(windows[at : at + SPAN, :], weight[:, g * wide : (g + 1) * wide])
        mixed = gathered(group)
        below = phi(mixed)
        mask = place.mask(slot)
        states = jnp.where(mask, own.astype(f32) + mixed * below, 0.0)
        states_ref[0] = states.T[:GC, :].astype(bf16)
        slopes = jnp.where(mask, back * (below + mixed * bell(mixed)), 0.0)
        slopes_ref[0] = slopes.astype(bf16)
        edge = jnp.where(place.x < X // 2, low_ref[0].astype(f32), high_ref[0].astype(f32))
        for copy in range(X):
            piece_ref[copy, 0, :T, :] = own
            piece_ref[copy, 0, T : T + REACH, :] = edge.astype(bf16)
            piece_ref[copy, 0, T + REACH :, :] = slopes.astype(bf16)

    @pl.when(jnp.logical_not(living))
    def _():
        states_ref[...] = jnp.zeros_like(states_ref)
        slopes_ref[...] = jnp.zeros_like(slopes_ref)
        piece_ref[...] = jnp.zeros_like(piece_ref)

    @pl.when(place.chosen == slot)
    def _():
        sent_ref[...] = states_ref[0]

    tail_ref[0] = slopes_ref[0, T - REACH :, :]
    head_ref[0] = slopes_ref[0, :REACH, :]


def fill_weight(weight, pos_ref, ahead):
    size = LANES
    for q in range(K // NEAR):
        for r in range(NEAR):
            tap = q * NEAR + r
            if ahead:
                weight[r * size : (r + 1) * size, q * size : (q + 1) * size] = pos_ref[tap]
            else:
                weight[q * size : (q + 1) * size, r * size : (r + 1) * size] = pos_ref[K - 1 - tap]


def mix(place, features, low, high, pos, cotangent, received):
    return pl.pallas_call(
        mix_body,
        grid=(SLOTS,),
        out_shape=(
            jax.ShapeDtypeStruct((SLOTS, GC, T), bf16),
            jax.ShapeDtypeStruct((GC, T), bf16),
            jax.ShapeDtypeStruct((SLOTS, T, LANES), bf16),
            jax.ShapeDtypeStruct((SLOTS, REACH, LANES), bf16),
            jax.ShapeDtypeStruct((SLOTS, REACH, LANES), bf16),
            jax.ShapeDtypeStruct((X, SLOTS, PIECE, LANES), bf16),
        ),
        in_specs=[SMEM] * 3
        + [
            by_slot(T, LANES),
            by_slot(REACH, LANES),
            by_slot(REACH, LANES),
            whole(K, LANES, LANES),
            by_slot(GC, T),
            by_slot(GC, T),
        ],
        out_specs=(
            by_slot(GC, T),
            whole(GC, T),
            by_slot(T, LANES),
            by_slot(REACH, LANES),
            by_slot(REACH, LANES),
            pl.BlockSpec((X, 1, PIECE, LANES), lambda s: (0, s, 0, 0)),
        ),
        scratch_shapes=[
            pltpu.VMEM((EXT, LANES), f32),
            pltpu.VMEM((T + NEAR * (K // NEAR - 1), NEAR * LANES), bf16),
            pltpu.VMEM((LANES, T), f32),
            pltpu.VMEM((NEAR * LANES, K // NEAR * LANES), bf16),
        ],
        compiler_params=params(),
        cost_estimate=cost(2 * SLOTS * SPAN * K * LANES * LANES, 7 << 20, SLOTS * T * LANES * 2),
        name="mix",
    )(*place, features, low, high, pos, cotangent, received)


def taps_body(
    scale, dev_ref, len_ref, mov_ref, piece_ref, keep_ref, send_ref, ext, windows, turned, sums
):
    place = Place(dev_ref, len_ref, mov_ref)
    slot = pl.program_id(0)
    spread = X * T
    rows = spread + NEAR * (K // NEAR - 1)

    @pl.when(slot == 0)
    def _():
        sums[...] = jnp.zeros_like(sums)

    @pl.when(place.y * spread < place.length(slot))
    def _():
        ext[:REACH, :] = piece_ref[0, 0, T : T + REACH, :].astype(f32)
        ext[REACH + spread :, :] = piece_ref[X - 1, 0, T : T + REACH, :].astype(f32)
        for x in range(X):
            ext[REACH + x * T : REACH + (x + 1) * T, :] = piece_ref[x, 0, :T, :].astype(f32)
            turned[:, x * T : (x + 1) * T] = (
                piece_ref[x, 0, T + REACH :, :].astype(f32).T.astype(bf16)
            )
        for j in range(4):
            windows[:, j * LANES : (j + 1) * LANES] = ext[
                pl.ds(place.x + 4 * j, rows), :
            ].astype(bf16)
        for q in range(K // NEAR):
            sums[q] += nn(turned[...], windows[q * NEAR : q * NEAR + spread, :])

    @pl.when(slot == SLOTS - 1)
    def _():
        first_core = place.core == 0
        for q in range(K // NEAR):
            for far in range(2):
                even = sums[q, :, (2 * far) * LANES : (2 * far + 1) * LANES] * scale
                odd = sums[q, :, (2 * far + 1) * LANES : (2 * far + 2) * LANES] * scale
                keep = jnp.where(first_core, even, odd).astype(bf16)
                send = jnp.where(first_core, odd, even).astype(bf16)
                for y in range(2):
                    keep_ref[y, 2 * q + far] = keep[y * REACH : (y + 1) * REACH, :]
                    send_ref[y, 2 * q + far] = send[y * REACH : (y + 1) * REACH, :]


def taps(scale, place, pieces):
    shape = jax.ShapeDtypeStruct((2, CELLS, REACH, LANES), bf16)
    spread = X * T
    return pl.pallas_call(
        functools.partial(taps_body, scale),
        grid=(SLOTS,),
        out_shape=(shape, shape),
        in_specs=[SMEM] * 3 + [pl.BlockSpec((X, 1, PIECE, LANES), lambda s: (0, s, 0, 0))],
        out_specs=(whole(*shape.shape), whole(*shape.shape)),
        scratch_shapes=[
            pltpu.VMEM((spread + 2 * REACH, LANES), f32),
            pltpu.VMEM((spread + NEAR * (K // NEAR - 1), 4 * LANES), bf16),
            pltpu.VMEM((LANES, spread), bf16),
            pltpu.VMEM((K // NEAR, LANES, 4 * LANES), f32),
        ],
        compiler_params=params(),
        cost_estimate=cost(2 * SLOTS * SPAN * K * LANES * LANES, 4 << 20),
        name="taps",
    )(*place, pieces)


def backward_body(
    scale,
    dev_ref,
    len_ref,
    mov_ref,
    slopes_ref,
    low_ref,
    high_ref,
    cot_ref,
    recv_ref,
    pos_ref,
    pair_ref,
    q_ref,
    slope_ref,
    m_ref,
    inv_ref,
    conv_ref,
    chan_ref,
    proj_ref,
    audio_grad_ref,
    keep_ref,
    send_ref,
    ext,
    windows,
    turned,
    weight,
    proj,
    feat_grad,
    normed,
    mid,
    wide,
    conv_sum,
    proj_sum,
    chan_sum,
    columns,
):
    place = Place(dev_ref, len_ref, mov_ref)
    slot = pl.program_id(0)
    living = place.alive(slot)
    span = PER_GROUP * LANES

    @pl.when(slot == 0)
    def _():
        fill_weight(weight, pos_ref, False)
        proj[...] = jnp.zeros_like(proj)
        proj[:GC, :] = proj_ref[...]
        conv_sum[...] = jnp.zeros_like(conv_sum)
        proj_sum[...] = jnp.zeros_like(proj_sum)
        chan_sum[...] = jnp.zeros_like(chan_sum)

    @pl.when(living)
    def _():
        fill_ext(ext, low_ref[0], slopes_ref[0], high_ref[0])
        fill_windows(windows, ext, 1)
        fill_back(turned, place, slot, cot_ref, recv_ref)
        group = jnp.zeros((SPAN, span), f32)
        for g in range(GROUPS):
            at = g * NEAR * PER_GROUP
            group += nt(windows[at : at + SPAN, :], weight[g * span : (g + 1) * span, :])
        spread = gathered(group)
        feat_grad[...] = jnp.where(place.mask(slot), turned[...].T + spread, 0.0).astype(bf16)
        gain = chan_ref[1:2, :]
        gain_two, shift_two = chan_ref[3:4, :], chan_ref[4:5, :]
        mid[...] = nn(feat_grad[...], proj[...])
        for at in range(0, T, CHUNK):
            rows = slice(at, at + CHUNK)
            m = m_ref[0, rows, :]
            normed[rows, :] = (m * gain_two + shift_two).astype(bf16)
            normed_grad = mid[rows, :]
            chan_sum[24:32, :] += jnp.sum((normed_grad * m).reshape(-1, 8, C), axis=0)
            chan_sum[32:40, :] += jnp.sum(normed_grad.reshape(-1, 8, C), axis=0)
            scaled = normed_grad * gain_two
            first = jnp.mean(scaled, axis=-1, keepdims=True)
            second = jnp.mean(scaled * m, axis=-1, keepdims=True)
            inverse_two = inv_ref[0, rows, LANES : LANES + 1]
            pre_grad = inverse_two * (scaled - first - m * second) * slope_ref[0, rows, :]
            q = q_ref[0, rows, :]
            chan_sum[8:16, :] += jnp.sum((pre_grad * q).reshape(-1, 8, C), axis=0)
            chan_sum[16:24, :] += jnp.sum(pre_grad.reshape(-1, 8, C), axis=0)
            scaled = pre_grad * gain
            first = jnp.mean(scaled, axis=-1, keepdims=True)
            second = jnp.mean(scaled * q, axis=-1, keepdims=True)
            inverse = inv_ref[0, rows, 0:1]
            conv_grad = inverse * (scaled - first - q * second)
            chan_sum[0:8, :] += jnp.sum(conv_grad.reshape(-1, 8, C), axis=0)
            mid[rows, :] = conv_grad
        operand = mid[...].astype(bf16)
        for tap in range(2):
            rows = slice(tap * C, (tap + 1) * C)
            audio_grad = nt(operand, conv_ref[rows, :])
            for c in range(C // LANES):
                wide[c, pl.ds(tap, T, stride=2), :] = audio_grad[:, c * LANES : (c + 1) * LANES]
            conv_sum[rows, :] += tn(pair_ref[0, :, rows], operand)
        for c in range(C // LANES):
            audio_grad_ref[0, :, c * LANES : (c + 1) * LANES] = wide[c].astype(bf16)
        proj_sum[...] += tn(normed[...], feat_grad[...])

    @pl.when(jnp.logical_not(living))
    def _():
        audio_grad_ref[...] = jnp.zeros_like(audio_grad_ref)

    @pl.when(slot == SLOTS - 1)
    def _():
        first_core = place.core == 0
        columns[...] = jnp.zeros_like(columns)
        for n in range(5):
            columns[GC + n : GC + n + 1, :] = jnp.sum(
                chan_sum[8 * n : 8 * n + 8, :], axis=0, keepdims=True
            )
        proj_sum[...] += columns[...].T
        keep_ref[:, CELLS:, :, :] = jnp.zeros((MP, 2, 16, LANES), bf16)
        send_ref[:, CELLS:, :, :] = jnp.zeros((MP, 2, 16, LANES), bf16)

        def put(at, cell, even, odd):
            keep_ref[at, cell] = (jnp.where(first_core, even, odd) * scale).astype(bf16)
            send_ref[at, cell] = (jnp.where(first_core, odd, even) * scale).astype(bf16)

        for cell in range(CELLS):
            for y in range(2):
                for x in range(X):
                    at = 2 * cell * 32 + y * 16
                    lanes = slice(x * LANES, (x + 1) * LANES)
                    put(
                        y * X + x,
                        cell,
                        conv_sum[at : at + 16, lanes],
                        conv_sum[at + 32 : at + 48, lanes],
                    )
            at = cell * 32
            put(
                cell // 2,
                CELLS + cell % 2,
                proj_sum[at : at + 16, :],
                proj_sum[at + 16 : at + 32, :],
            )


def backward(
    scale, place, slopes, low, high, cotangent, received, pos, stored, conv_weight, channels, proj
):
    shape = jax.ShapeDtypeStruct((MP, REST, 16, LANES), bf16)
    return pl.pallas_call(
        functools.partial(backward_body, scale),
        grid=(SLOTS,),
        out_shape=(jax.ShapeDtypeStruct((SLOTS, 2 * T, C), bf16), shape, shape),
        in_specs=[SMEM] * 3
        + [
            by_slot(T, LANES),
            by_slot(REACH, LANES),
            by_slot(REACH, LANES),
            by_slot(GC, T),
            by_slot(GC, T),
            whole(K, LANES, LANES),
            by_slot(T, 2 * C),
            by_slot(T, C),
            by_slot(T, C),
            by_slot(T, C),
            by_slot(T, 2 * LANES),
            whole(2 * C, C),
            whole(5, C),
            whole(GC, C),
        ],
        out_specs=(by_slot(2 * T, C), whole(*shape.shape), whole(*shape.shape)),
        scratch_shapes=[
            pltpu.VMEM((EXT, LANES), f32),
            pltpu.VMEM((T + NEAR * (K // NEAR - 1), NEAR * LANES), bf16),
            pltpu.VMEM((LANES, T), f32),
            pltpu.VMEM((K // NEAR * LANES, NEAR * LANES), bf16),
            pltpu.VMEM((LANES, C), bf16),
            pltpu.VMEM((T, LANES), bf16),
            pltpu.VMEM((T, C), bf16),
            pltpu.VMEM((T, C), f32),
            pltpu.VMEM((C // LANES, 2 * T, LANES), f32),
            pltpu.VMEM((2 * C, C), f32),
            pltpu.VMEM((C, LANES), f32),
            pltpu.VMEM((40, C), f32),
            pltpu.VMEM((LANES, C), f32),
        ],
        compiler_params=params(),
        cost_estimate=cost(
            2 * SLOTS * (SPAN * K * LANES * LANES + T * C * (4 * C + 2 * LANES)), 14 << 20
        ),
        name="backward",
    )(
        *place,
        slopes,
        low,
        high,
        cotangent,
        received,
        pos,
        *stored,
        conv_weight,
        channels,
        proj,
    )


def cells_body(dev_ref, kept_ref, recv_ref, rest_ref, out_ref):
    model = lax.rem(dev_ref[0], MP)
    out_ref[:, :REACH, :] = (kept_ref[...].astype(f32) + recv_ref[...].astype(f32)).astype(bf16)
    rest = rest_ref[0].astype(f32)
    for n in range(1, MP):
        rest += rest_ref[n].astype(f32)
    out_ref[:, REACH : REACH + 16, :] = rest[:CELLS].astype(bf16)
    for cell in range(CELLS):
        small = jnp.where(model == cell // 2, rest[CELLS + cell % 2], 0.0)
        out_ref[cell, REACH + 16 :, :] = small.astype(bf16)


def make_cells(dev, kept, received, rest):
    return pl.pallas_call(
        cells_body,
        out_shape=jax.ShapeDtypeStruct((CELLS, REACH + 32, LANES), bf16),
        in_specs=[SMEM] + [VMEM] * 3,
        out_specs=VMEM,
        compiler_params=params(),
        cost_estimate=cost(0, 2 << 20),
        name="cells",
    )(dev, kept, received, rest)


def total_body(in_ref, out_ref):
    total = in_ref[0].astype(f32)
    for n in range(1, in_ref.shape[0]):
        total += in_ref[n].astype(f32)
    for copy in range(MP):
        out_ref[copy] = total.astype(bf16)


def total(parts):
    return pl.pallas_call(
        total_body,
        out_shape=jax.ShapeDtypeStruct((MP,) + parts.shape[1:], bf16),
        in_specs=[VMEM],
        out_specs=VMEM,
        compiler_params=params(),
        cost_estimate=cost(0, 2 * parts.size),
        name="total",
    )(parts)


def finish_body(
    dev_ref,
    len_ref,
    mov_ref,
    in_ref,
    states_ref,
    other_ref,
    hidden_ref,
    pos_ref,
    conv_ref,
    proj_ref,
    chan_ref,
):
    place = Place(dev_ref, len_ref, mov_ref)
    for slot in range(SLOTS):
        hidden_ref[slot] = jnp.where(
            place.chosen == slot, other_ref[...].astype(f32), states_ref[slot].astype(f32)
        ).astype(bf16)
    for x in range(X):
        block = jnp.concatenate(
            [in_ref[x, :REACH, :].astype(f32), in_ref[X + x, :REACH, :].astype(f32)], axis=0
        ).T
        pos_ref[x] = block[:GC, :GC]
        for y in range(2):
            conv_ref[y * 16 : (y + 1) * 16, x * LANES : (x + 1) * LANES] = in_ref[
                y * X + x, REACH : REACH + 16, :
            ].astype(f32)
    small = in_ref[place.cell // 2, REACH + 16 :, :].astype(f32)
    proj_ref[...] = small[:, :GC]
    chan_ref[...] = jnp.concatenate([small] * 8, axis=0).T[GC : GC + 5, :16]


def finish(place, cells, states, other):
    return pl.pallas_call(
        finish_body,
        out_shape=(
            jax.ShapeDtypeStruct((SLOTS, GC, T), bf16),
            jax.ShapeDtypeStruct((4, GC, GC), f32),
            jax.ShapeDtypeStruct((32, C), f32),
            jax.ShapeDtypeStruct((16, GC), f32),
            jax.ShapeDtypeStruct((5, 16), f32),
        ),
        in_specs=[SMEM] * 3 + [VMEM] * 3,
        out_specs=(VMEM,) * 5,
        compiler_params=params(),
        name="finish",
    )(*place, cells, states, other)


def neighbours(tail, head):
    count = lax.axis_size("mp")
    forward = [(i, i + 1) for i in range(count - 1)]
    backward_route = [(i + 1, i) for i in range(count - 1)]
    return lax.ppermute(tail, "mp", forward), lax.ppermute(head, "mp", backward_route)


def added(a, b):
    return (a.astype(f32) + b.astype(f32)).astype(bf16)


def per_device(
    audio, lengths, moved_slots, conv_weight, channel_params, proj_weight, pos_weight, cotangent
):
    data_index = lax.axis_index("dp")
    model_index = lax.axis_index("mp")
    scale = (SLOTS * DP * T * MP) ** -0.5
    dev = (data_index * MP + model_index).astype(jnp.int32).reshape(1)
    place = (dev, lengths, moved_slots.reshape(-1))
    swap = [(i, i ^ (DP // 2)) for i in range(DP)]
    core_swap = [(i, i ^ 1) for i in range(DP)]
    channels = channel_params.T
    proj = proj_weight.T
    cot = cotangent.transpose(0, 2, 1)
    pos = jnp.pad(pos_weight, ((0, 0), (0, LANES - GC), (0, LANES - GC)))

    received = lax.ppermute(cot, "dp", swap)
    features, tail, head, *stored = encode(place, audio, conv_weight, channels, proj)
    low, high = neighbours(tail, head)
    states, sent, slopes, tail, head, pieces = mix(
        place, features, low, high, pos, cot, received
    )
    slope_low, slope_high = neighbours(tail, head)
    rows = [list(range(X)), list(range(X, 2 * X))]
    pieces = lax.all_to_all(pieces, "mp", 0, 0, axis_index_groups=rows, tiled=True)
    other = lax.ppermute(sent, "dp", swap)
    audio_grad, keep, send = backward(
        scale,
        place,
        slopes,
        slope_low,
        slope_high,
        cot,
        received,
        pos,
        stored,
        conv_weight,
        channels,
        proj,
    )
    rest = added(keep, lax.ppermute(send, "dp", core_swap))
    pos_keep, pos_send = taps(scale, place, pieces)
    rest = lax.all_to_all(rest, "mp", 0, 0, tiled=True)
    pos_sum = added(pos_keep, lax.ppermute(pos_send, "dp", core_swap))
    low_half = model_index < X
    kept = jnp.where(low_half, pos_sum[0], pos_sum[1])
    leaving = jnp.where(low_half, pos_sum[1], pos_sum[0])
    coming = lax.ppermute(leaving, "mp", [(i, i ^ X) for i in range(MP)])
    cells = make_cells(dev, kept, coming, rest)
    groups = [list(range(bit, DP, 2)) for bit in range(2)]
    cells = lax.all_to_all(cells, "dp", 0, 0, axis_index_groups=groups, tiled=True)
    cells = lax.all_to_all(total(cells), "mp", 0, 0, tiled=True)
    hidden, grad_pos, grad_conv, grad_proj, grad_channels = finish(place, cells, states, other)
    return (
        hidden.transpose(0, 2, 1),
        audio_grad,
        grad_pos,
        grad_conv,
        grad_proj,
        grad_channels.T,
    )


def solution(mesh):
    return jax.shard_map(
        per_device,
        mesh=mesh,
        in_specs=(P("dp", "mp", None), P(), P(), P(), P(), P(), P(), P("dp", "mp", None)),
        out_specs=(
            P("dp", "mp", None),
            P("dp", "mp", None),
            P("dp", None, None),
            P("dp", None),
            P("dp", None),
            P("dp", None),
        ),
        check_vma=False,
    )
```

time: 181 us -> 141 us (0.78)
  blocking collectives: 46.2 us -> 24.6 us
  Pallas kernels: 52.1 us -> 37.1 us
  local copies, waits for them, and re-layouts: 23.2 us -> 15.2 us
  waiting for transfers between devices: 20.5 us -> 25.5 us
  between operations: 2.92 us -> 0.82 us
    all_to_all x1, blocking collectives: 46.2 us -> 24.6 us  [per_device(): lax.all_to_all(cells, 'dp', 0, 0, axis_index_groups=groups, tiled=True)]
    pallas_call x6 -> x4, Pallas kernels: 28.8 us -> 11.1 us  [the longest x1 5.33 us: taps(): pl.pallas_call(functools.partial(taps_body, scale), grid=(SLOTS,), out_sh...]
    ppermute x4 -> x5, waiting for transfers between devices: 2.87 us -> 10.7 us  [the longest x1 6.45 us: per_device(): other = lax.ppermute(sent, 'dp', swap)]
    unnamed x31, local copies, waits for them, and re-layouts: 16.8 us -> 9.9 us
    all_to_all x2 -> x3, waiting for transfers between devices: 14.5 us -> 7.75 us  [the longest x1 7.75 us: per_device(): rest = lax.all_to_all(rest, 'mp', 0, 0, tiled=True)]
    ppermute x2, waiting for transfers between devices: 0.01 us -> 5.39 us  [neighbours(): lax.ppermute(tail, 'mp', forward)]
    pad x1, local copies, waits for them, and re-layouts: 1.32 us -> 5.26 us  [per_device(): pos = jnp.pad(pos_weight, ((0, 0), (0, LANES - GC), (0, LANES - GC)))]
    all_to_all x2 -> x3, starting transfers between devices: 9.75 us -> 12.3 us  [the longest x1 5.12 us: per_device(): cells = lax.all_to_all(total(cells), 'mp', 0, 0, tiled=True)]
  transfers between devices with their start and end apart: 10 -> 12, of which waited for: 4 -> 5; matrix products, arithmetic and copies ran while one was open for 9% -> 10% of each run, Pallas kernels for 15% -> 17%
where the time goes in v2:
time: 141 us; the launch traced here: 140 us
  Pallas kernels  37.1 us (26%)
  starting transfers between devices  34.9 us (25%)
  waiting for transfers between devices  25.5 us (18%)
  blocking collectives  24.6 us (17%)
  local copies, waits for them, and re-layouts  15.2 us (11%)
  other arithmetic  1.89 us (1%)
    all_to_all x1, blocking collectives, per_device(): lax.all_to_all(cells, 'dp', 0, 0, axis_index_groups=groups, tiled=True)  24.6 us
    pallas_call x1, Pallas kernels, backward(): pl.pallas_call(functools.partial(backward_body, scale), grid=(SLOTS,), ou...  12.4 us
    unnamed x31, local copies, waits for them, and re-layouts  9.9 us
    pallas_call x1, Pallas kernels, mix(): pl.pallas_call(mix_body, grid=(SLOTS,), out_shape=(jax.ShapeDtypeStruct((...  7.88 us
    all_to_all x1, waiting for transfers between devices, per_device(): rest = lax.all_to_all(rest, 'mp', 0, 0, tiled=True)  7.75 us
    ppermute x1, starting transfers between devices, per_device(): received = lax.ppermute(cot, 'dp', swap)  7.28 us
    ppermute x2, starting transfers between devices, neighbours(): lax.ppermute(head, 'mp', backward_route)  6.64 us
    ppermute x1, waiting for transfers between devices, per_device(): other = lax.ppermute(sent, 'dp', swap)  6.45 us
  transfers between devices with their start and end apart: 12, of which 5 were waited for; matrix products, arithmetic and copies ran while one was open for 10% of the time, Pallas kernels for 17%

profile of v2, /device:TPU:2, one launch (start us, length us, event | category | flops | bytes accessed | tf_op | source)
XLA Modules:
  0.0 140.1 jit_solution(8477590180897755896)
XLA Ops:
  0.6 7.3 %collective-permute-start.2 = (bf16[2,120,256]{2,1,0:T(8,128)(2,1)}, bf16[2,120,256]{2,1,0:T(8,128)(2,1)S(1)}, u32[]{:S(2)}, u32[]{:S(2)}) collective-permute-start(bf16[2,120,256]{2,1,0:T(8,128)(2,1)} %bitcast.20), channel_id=1, source_target_pairs={{0,128},{8,136},{16,144},{24,152},{32,160},{40,168},{48,176},{56,1... | collective-permute-start | bytes 368648 | tf_op jit(solution)/shard_map/ppermute | solution.py:745
  7.9 5.8 %encode.1 = (bf16[2,256,128]{2,1,0:T(8,128)(2,1)}, bf16[2,64,128]{2,1,0:T(8,128)(2,1)}, bf16[2,64,128]{2,1,0:T(8,128)(2,1)}, bf16[2,256,1024]{2,1,0:T(8,128)(2,1...) custom-call(s32[1]{0:T(128)} %bitcast.dev_ref, ...), custom_call_target="tpu_custom_call" | custom-call | flops 603979776 | bytes 8388608 | tf_op jit(solution)/shard_map/encode/pallas_call | solution.py:177
  13.7 1.9 %collective-permute-start = (bf16[2,64,128]{2,1,0:T(8,128)(2,1)}, bf16[2,64,128]{2,1,0:T(8,128)(2,1)S(1)}, u32[]{:S(2)}, u32[]{:S(2)}) collective-permute-start(bf16[2,64,128]{2,1,0:T(8,128)(2,1)} %get-tuple-element.31), channel_id=1, source_target_pairs={{0,1},{1,2},{2,3},{3,4},{4,5},{5,6},{6,7},{8,9},{9,10},{10,11},{11... | collective-permute-start | bytes 98312 | tf_op jit(solution)/shard_map/ppermute | solution.py:723
  15.6 3.9 %collective-permute-start.1 = (bf16[2,64,128]{2,1,0:T(8,128)(2,1)}, bf16[2,64,128]{2,1,0:T(8,128)(2,1)S(1)}, u32[]{:S(2)}, u32[]{:S(2)}) collective-permute-start(bf16[2,64,128]{2,1,0:T(8,128)(2,1)} %get-tuple-element.32), channel_id=1, source_target_pairs={{1,0},{2,1},{3,2},{4,3},{5,4},{6,5},{7,6},{9,8},{10,9},{11,10},{12... | collective-permute-start | bytes 98312 | tf_op jit(solution)/shard_map/ppermute | solution.py:723
  19.5 6.2 %copy.14 = bf16[128,120,120]{2,1,0:T(8,128)(2,1)} copy(bf16[128,120,120]{0,2,1:T(8,128)(2,1)} %param.14) | data formatting | bytes 7372800 | tf_op args[6]
  25.8 5.3 %pad.4.pos_ref = bf16[128,128,128]{2,1,0:T(8,128)(2,1)} pad(bf16[128,120,120]{2,1,0:T(8,128)(2,1)} %copy.14, bf16[]{:T(256)} %constant.15.clone.1), padding=0_0x0_8x0_8 | pad | bytes 7880706 | tf_op jit(solution)/shard_map/jit(_pad)/pad | solution.py:743
  31.0 0.0 collective-permute-done.low_ref
  31.0 0.0 copy-start.9
  31.0 0.0 collective-permute-done.1.high_ref
  31.0 0.0 copy-start.12
  31.0 0.0 collective-permute-done.2.recv_ref
  31.0 0.0 copy-start.7
  31.1 0.6 copy-done.9
  31.6 0.0 copy-done.12
  31.6 0.1 copy-done.7
  31.7 7.9 %mix.1 = (bf16[2,120,256]{2,1,0:T(8,128)(2,1)}, bf16[120,256]{1,0:T(8,128)(2,1)}, bf16[2,256,128]{2,1,0:T(8,128)(2,1)}, bf16[2,64,128]{2,1,0:T(8,128)(2,1)}, bf1...) custom-call(s32[1]{0:T(128)} %bitcast.dev_ref, s32[64]{0:T(128)} %len_ref.9, s32[16]{0:T(128)} %bitcast.16, ...), custom_call_target="tpu_custom_call" | custom-call | flops 2550136832 | bytes 7340032 | tf_op jit(solution)/shard_map/mix/pallas_call | solution.py:325
  39.6 0.0 copy-start.13
  39.6 0.0 copy-start.10
  39.6 3.7 %all-to-all-start = ((bf16[4,2,576,128]{3,2,1,0:T(8,128)(2,1)}), bf16[4,2,576,128]{3,2,1,0:T(8,128)(2,1)S(1)}, u32[]{:S(2)}, u32[]{:S(2)}) async-start(bf16[4,2,576,128]{3,2,1,0:T(8,128)(2,1)} %get-tuple-element.33), calls=%async_computation | async-start | bytes 2359296 | tf_op jit(solution)/shard_map/all_to_all | solution.py:753
  43.3 0.0 copy-done.13
  43.3 3.1 %collective-permute-start.5 = (bf16[2,64,128]{2,1,0:T(8,128)(2,1)S(1)}, bf16[2,64,128]{2,1,0:T(8,128)(2,1)S(1)}, u32[]{:S(2)}, u32[]{:S(2)}) collective-permute-start(bf16[2,64,128]{2,1,0:T(8,128)(2,1)S(1)} %copy-done.13), channel_id=1, source_target_pairs={{0,1},{1,2},{2,3},{3,4},{4,5},{5,6},{6,7},{8,9},{9,10},{10,11},{11... | collective-permute-start | bytes 98312 | tf_op jit(solution)/shard_map/ppermute | solution.py:723
  46.4 0.0 copy-done.10
  46.4 2.7 %collective-permute-start.6 = (bf16[2,64,128]{2,1,0:T(8,128)(2,1)S(1)}, bf16[2,64,128]{2,1,0:T(8,128)(2,1)S(1)}, u32[]{:S(2)}, u32[]{:S(2)}) collective-permute-start(bf16[2,64,128]{2,1,0:T(8,128)(2,1)S(1)} %copy-done.10), channel_id=1, source_target_pairs={{1,0},{2,1},{3,2},{4,3},{5,4},{6,5},{7,6},{9,8},{10,9},{11,10},{12... | collective-permute-start | bytes 98312 | tf_op jit(solution)/shard_map/ppermute | solution.py:723
  49.1 5.4 %collective-permute-done.5.low_ref = bf16[2,64,128]{2,1,0:T(8,128)(2,1)S(1)} collective-permute-done((bf16[2,64,128]{2,1,0:T(8,128)(2,1)S(1)}, bf16[2,64,128]{2,1,0:T(8,128)(2,1)S(1)}, u32[]{:S(2)}, u32[]{:S(2)}) %collective-permute-start.5) | collective-permute-done | bytes 32800 | tf_op jit(solution)/shard_map/ppermute | solution.py:723
  54.5 0.0 copy-start.11
  54.5 1.7 %collective-permute-done.6.high_ref = bf16[2,64,128]{2,1,0:T(8,128)(2,1)S(1)} collective-permute-done((bf16[2,64,128]{2,1,0:T(8,128)(2,1)S(1)}, bf16[2,64,128]{2,1,0:T(8,128)(2,1)S(1)}, u32[]{:S(2)}, u32[]{:S(2)}) %collective-permute-start.6) | collective-permute-done | bytes 32800 | tf_op jit(solution)/shard_map/ppermute | solution.py:723
  56.3 0.0 copy-start.14
  56.3 0.0 copy-done.11
  56.3 0.6 copy-done.14
  56.9 12.4 %backward.1 = (bf16[2,512,512]{2,1,0:T(8,128)(2,1)}, bf16[8,18,16,128]{3,2,1,0:T(8,128)(2,1)}, bf16[8,18,16,128]{3,2,1,0:T(8,128)(2,1)}) custom-call(s32[1]{0:T(128)} %bitcast.dev_ref, s32[64]{0:T(128)} %len_ref.9, s32[16]{0:T(128)} %bitcast.17, bf16[2,256,128]{2,1,0:T(8,128)(2,1)} %get-tuple-element.36.slopes_ref, bf16[2,64,128]{2,1,0:T(8,128)(2,1)} %copy-done.11, ...), custom_call_target="tpu_custom_call" | custom-call | flops 3758096384 | bytes 14680064 | tf_op jit(solution)/shard_map/backward/pallas_call | solution.py:569
  69.3 0.0 copy-start.3
  69.3 0.1 collective-permute-start.7
  69.4 0.0 all-to-all-done.piece_ref
  69.4 0.0 copy-start.1
  69.4 1.0 copy-done.1
  70.4 5.3 %taps.1 = (bf16[2,16,64,128]{3,2,1,0:T(8,128)(2,1)}, bf16[2,16,64,128]{3,2,1,0:T(8,128)(2,1)}) custom-call(s32[1]{0:T(128)} %bitcast.dev_ref, s32[64]{0:T(128)} %len_ref.9, s32[16]{0:T(128)} %bitcast.18, bf16[4,2,576,128]{3,2,1,0:T(8,128)(2,1)} %copy-done.1), custom_call_target="tpu_custom_call" | custom-call | flops 2550136832 | bytes 4194304 | tf_op jit(solution)/shard_map/taps/pallas_call | solution.py:410
  75.7 0.5 collective-permute-start.3
  76.2 0.0 collective-permute-done.7
  76.2 0.0 copy-done.3
  76.2 0.0 copy-start.4
  76.2 1.0 add_convert_fusion
  77.2 3.5 %all-to-all-start.1 = ((bf16[8,18,16,128]{3,2,1,0:T(8,128)(2,1)}), bf16[8,18,16,128]{3,2,1,0:T(8,128)(2,1)S(1)}, u32[]{:S(2)}, u32[]{:S(2)}) async-start(bf16[8,18,16,128]{3,2,1,0:T(8,128)(2,1)} %add_convert_fusion), calls=%async_computation.1 | async-start | bytes 1179648 | tf_op jit(solution)/shard_map/all_to_all | solution.py:771
  80.7 0.0 collective-permute-done.3
  80.7 0.0 copy-done.4
  80.7 0.2 add_convert_fusion.1
  80.9 0.7 select_bitcast_fusion
  81.6 1.4 %collective-permute-start.4 = (bf16[16,64,128]{2,1,0:T(8,128)(2,1)S(1)}, bf16[16,64,128]{2,1,0:T(8,128)(2,1)S(1)}, u32[]{:S(2)}, u32[]{:S(2)}) collective-permute-start(bf16[16,64,128]{2,1,0:T(8,128)(2,1)S(1)} %get-tuple-element.54), channel_id=1, source_target_pairs={{0,4},{1,5},{2,6},{3,7},{4,0},{5,1},{6,2},{7,3},{8,12},{9,13},{10,... | collective-permute-start | bytes 786440 | tf_op jit(solution)/shard_map/ppermute | solution.py:776
  83.1 7.7 %all-to-all-done.1.rest_ref = bf16[8,18,16,128]{3,2,1,0:T(8,128)(2,1)S(1)} async-done(((bf16[8,18,16,128]{3,2,1,0:T(8,128)(2,1)}), bf16[8,18,16,128]{3,2,1,0:T(8,128)(2,1)S(1)}, u32[]{:S(2)}, u32[]{:S(2)}) %all-to-all-start.1) | async-done | bytes 589856 | tf_op jit(solution)/shard_map/all_to_all | solution.py:771
  90.8 0.0 copy-start
  90.8 4.2 %collective-permute-done.4.recv_ref = bf16[16,64,128]{2,1,0:T(8,128)(2,1)S(1)} collective-permute-done((bf16[16,64,128]{2,1,0:T(8,128)(2,1)S(1)}, bf16[16,64,128]{2,1,0:T(8,128)(2,1)S(1)}, u32[]{:S(2)}, u32[]{:S(2)}) %collective-permute-start.4) | collective-permute-done | bytes 262176 | tf_op jit(solution)/shard_map/ppermute | solution.py:776
  95.0 0.0 copy-start.5
  95.0 0.0 copy-done
  95.0 0.7 copy-done.5
  95.7 2.1 %cells.1 = bf16[16,96,128]{2,1,0:T(8,128)(2,1)} custom-call(s32[1]{0:T(128)} %bitcast.dev_ref, bf16[16,64,128]{2,1,0:T(8,128)(2,1)} %get-tuple-element.55.kept_ref, bf16[16,64,128]{2,1,0:T(8,128)(2,1)} %copy-done.5, bf16[8,18,16,128]{3,2,1,0:T(8,128)(2,1)} %copy-done), custom_call_target="tpu_custom_call" | custom-call | bytes 2097152 | tf_op jit(solution)/shard_map/cells/pallas_call | solution.py:639
  97.9 24.6 %all_to_all.20.in_ref = bf16[16,96,128]{2,1,0:T(8,128)(2,1)} all-to-all(bf16[16,96,128]{2,1,0:T(8,128)(2,1)} %cells.1), channel_id=1, replica_groups={{0,16,32,48,64,80,96,112,128,144,160,176,192,208,224,240},{8,24,40,56,7..., dimensions={0} | all-to-all | bytes 786432 | tf_op jit(solution)/shard_map/all_to_all | solution.py:779
  122.5 1.7 %total.1 = bf16[8,96,128]{2,1,0:T(8,128)(2,1)} custom-call(bf16[16,96,128]{2,1,0:T(8,128)(2,1)} %all_to_all.20.in_ref), custom_call_target="tpu_custom_call" | custom-call | bytes 393216 | tf_op jit(solution)/shard_map/total/pallas_call | solution.py:659
  124.2 5.1 %all-to-all-start.3 = ((bf16[8,96,128]{2,1,0:T(8,128)(2,1)}), bf16[8,96,128]{2,1,0:T(8,128)(2,1)S(1)}, u32[]{:S(2)}, u32[]{:S(2)}) async-start(bf16[8,96,128]{2,1,0:T(8,128)(2,1)} %total.1), calls=%async_computation.3 | async-start | bytes 393216 | tf_op jit(solution)/shard_map/all_to_all | solution.py:780
  129.4 0.0 copy-done.8
  129.4 1.7 %collective-permute-start.8 = (bf16[120,256]{1,0:T(8,128)(2,1)S(1)}, bf16[120,256]{1,0:T(8,128)(2,1)S(1)}, u32[]{:S(2)}, u32[]{:S(2)}) collective-permute-start(bf16[120,256]{1,0:T(8,128)(2,1)S(1)} %copy-done.8), channel_id=1, source_target_pairs={{0,128},{8,136},{16,144},{24,152},{32,160},{40,168},{48,176},{56,1... | collective-permute-start | bytes 184328 | tf_op jit(solution)/shard_map/ppermute | solution.py:754
  131.0 6.5 %collective-permute-done.8.other_ref = bf16[120,256]{1,0:T(8,128)(2,1)S(1)} collective-permute-done((bf16[120,256]{1,0:T(8,128)(2,1)S(1)}, bf16[120,256]{1,0:T(8,128)(2,1)S(1)}, u32[]{:S(2)}, u32[]{:S(2)}) %collective-permute-start.8) | collective-permute-done | bytes 61472 | tf_op jit(solution)/shard_map/ppermute | solution.py:754
  137.5 0.0 all-to-all-done.3.in_ref
  137.5 0.6 copy-done.6
  138.1 0.1 copy-done.2
  138.2 1.9 %finish.1 = (bf16[2,120,256]{2,1,0:T(8,128)(2,1)}, f32[4,120,120]{2,1,0:T(8,128)}, f32[32,512]{1,0:T(8,128)}, f32[16,120]{1,0:T(8,128)}, f32[5,16]{1,0:T(8,128)}) custom-call(s32[1]{0:T(128)} %bitcast.dev_ref, s32[64]{0:T(128)} %len_ref.9, s32[16]{0:T(128)} %bitcast.19, bf16[8,96,128]{2,1,0:T(8,128)(2,1)} %copy-done.2, ...), custom_call_target="tpu_custom_call" | custom-call | tf_op jit(solution)/shard_map/finish/pallas_call | solution.py:703
  (3 shorter events, 0.0 us)
Async XLA Ops:
  0.6 30.4 %collective-permute-start.2 = (bf16[2,120,256]{2,1,0:T(8,128)(2,1)}, bf16[2,120,256]{2,1,0:T(8,128)(2,1)S(1)}, u32[]{:S(2)}, u32[]{:S(2)}) collective-permute-start(bf16[2,120,256]{2,1,0:T(8,128)(2,1)} %bitcast.20), channel_id=1, source_target_pairs={{0,128},{8,136},{16,144},{24,152},{32,160},{40,168},{48,176},{56,1... | collective-permute-start | bytes 368648 | tf_op jit(solution)/shard_map/ppermute | solution.py:745
  13.7 17.3 %collective-permute-start = (bf16[2,64,128]{2,1,0:T(8,128)(2,1)}, bf16[2,64,128]{2,1,0:T(8,128)(2,1)S(1)}, u32[]{:S(2)}, u32[]{:S(2)}) collective-permute-start(bf16[2,64,128]{2,1,0:T(8,128)(2,1)} %get-tuple-element.31), channel_id=1, source_target_pairs={{0,1},{1,2},{2,3},{3,4},{4,5},{5,6},{6,7},{8,9},{9,10},{10,11},{11... | collective-permute-start | bytes 98312 | tf_op jit(solution)/shard_map/ppermute | solution.py:723
  15.6 15.4 %collective-permute-start.1 = (bf16[2,64,128]{2,1,0:T(8,128)(2,1)}, bf16[2,64,128]{2,1,0:T(8,128)(2,1)S(1)}, u32[]{:S(2)}, u32[]{:S(2)}) collective-permute-start(bf16[2,64,128]{2,1,0:T(8,128)(2,1)} %get-tuple-element.32), channel_id=1, source_target_pairs={{1,0},{2,1},{3,2},{4,3},{5,4},{6,5},{7,6},{9,8},{10,9},{11,10},{12... | collective-permute-start | bytes 98312 | tf_op jit(solution)/shard_map/ppermute | solution.py:723
  31.0 0.6 copy-start.9
  31.0 0.6 copy-start.12
  31.0 0.7 copy-start.7
  39.6 3.7 %copy-start.13 = (bf16[2,64,128]{2,1,0:T(8,128)(2,1)S(1)}, bf16[2,64,128]{2,1,0:T(8,128)(2,1)}, u32[]{:S(2)}) copy-start(bf16[2,64,128]{2,1,0:T(8,128)(2,1)} %get-tuple-element.37) | copy-start | bytes 98308
  39.6 6.8 %copy-start.10 = (bf16[2,64,128]{2,1,0:T(8,128)(2,1)S(1)}, bf16[2,64,128]{2,1,0:T(8,128)(2,1)}, u32[]{:S(2)}) copy-start(bf16[2,64,128]{2,1,0:T(8,128)(2,1)} %get-tuple-element.38) | copy-start | bytes 98308
  39.6 29.8 %all-to-all-start = ((bf16[4,2,576,128]{3,2,1,0:T(8,128)(2,1)}), bf16[4,2,576,128]{3,2,1,0:T(8,128)(2,1)S(1)}, u32[]{:S(2)}, u32[]{:S(2)}) async-start(bf16[4,2,576,128]{3,2,1,0:T(8,128)(2,1)} %get-tuple-element.33), calls=%async_computation | async-start | bytes 2359296 | tf_op jit(solution)/shard_map/all_to_all | solution.py:753
  43.3 11.3 %collective-permute-start.5 = (bf16[2,64,128]{2,1,0:T(8,128)(2,1)S(1)}, bf16[2,64,128]{2,1,0:T(8,128)(2,1)S(1)}, u32[]{:S(2)}, u32[]{:S(2)}) collective-permute-start(bf16[2,64,128]{2,1,0:T(8,128)(2,1)S(1)} %copy-done.13), channel_id=1, source_target_pairs={{0,1},{1,2},{2,3},{3,4},{4,5},{5,6},{6,7},{8,9},{9,10},{10,11},{11... | collective-permute-start | bytes 98312 | tf_op jit(solution)/shard_map/ppermute | solution.py:723
  46.4 9.8 %collective-permute-start.6 = (bf16[2,64,128]{2,1,0:T(8,128)(2,1)S(1)}, bf16[2,64,128]{2,1,0:T(8,128)(2,1)S(1)}, u32[]{:S(2)}, u32[]{:S(2)}) collective-permute-start(bf16[2,64,128]{2,1,0:T(8,128)(2,1)S(1)} %copy-done.10), channel_id=1, source_target_pairs={{1,0},{2,1},{3,2},{4,3},{5,4},{6,5},{7,6},{9,8},{10,9},{11,10},{12... | collective-permute-start | bytes 98312 | tf_op jit(solution)/shard_map/ppermute | solution.py:723
  54.5 1.7 %copy-start.11 = (bf16[2,64,128]{2,1,0:T(8,128)(2,1)}, bf16[2,64,128]{2,1,0:T(8,128)(2,1)S(1)}, u32[]{:S(2)}) copy-start(bf16[2,64,128]{2,1,0:T(8,128)(2,1)S(1)} %collective-permute-done.5.low_ref) | copy-start | bytes 98308
  56.3 0.6 copy-start.14
  69.3 7.0 %copy-start.3 = (bf16[8,18,16,128]{3,2,1,0:T(8,128)(2,1)S(1)}, bf16[8,18,16,128]{3,2,1,0:T(8,128)(2,1)}, u32[]{:S(2)}) copy-start(bf16[8,18,16,128]{3,2,1,0:T(8,128)(2,1)} %get-tuple-element.44) | copy-start | bytes 1769476
  69.3 7.0 %collective-permute-start.7 = (bf16[8,18,16,128]{3,2,1,0:T(8,128)(2,1)}, bf16[8,18,16,128]{3,2,1,0:T(8,128)(2,1)S(1)}, u32[]{:S(2)}, u32[]{:S(2)}) collective-permute-start(bf16[8,18,16,128]{3,2,1,0:T(8,128)(2,1)} %get-tuple-element.45), channel_id=1, source_target_pairs={{0,8},{8,0},{16,24},{24,16},{32,40},{40,32},{48,56},{56,48},{64,72... | collective-permute-start | bytes 1769480 | tf_op jit(solution)/shard_map/ppermute | solution.py:769
  69.4 1.0 copy-start.1
  75.7 5.0 %collective-permute-start.3 = (bf16[2,16,64,128]{3,2,1,0:T(8,128)(2,1)}, bf16[2,16,64,128]{3,2,1,0:T(8,128)(2,1)S(1)}, u32[]{:S(2)}, u32[]{:S(2)}) collective-permute-start(bf16[2,16,64,128]{3,2,1,0:T(8,128)(2,1)} %get-tuple-element.35), channel_id=1, source_target_pairs={{0,8},{8,0},{16,24},{24,16},{32,40},{40,32},{48,56},{56,48},{64,72... | collective-permute-start | bytes 1572872 | tf_op jit(solution)/shard_map/ppermute | solution.py:772
  76.2 4.5 %copy-start.4 = (bf16[2,16,64,128]{3,2,1,0:T(8,128)(2,1)S(1)}, bf16[2,16,64,128]{3,2,1,0:T(8,128)(2,1)}, u32[]{:S(2)}) copy-start(bf16[2,16,64,128]{3,2,1,0:T(8,128)(2,1)} %get-tuple-element.34) | copy-start | bytes 1572868
  77.2 13.6 %all-to-all-start.1 = ((bf16[8,18,16,128]{3,2,1,0:T(8,128)(2,1)}), bf16[8,18,16,128]{3,2,1,0:T(8,128)(2,1)S(1)}, u32[]{:S(2)}, u32[]{:S(2)}) async-start(bf16[8,18,16,128]{3,2,1,0:T(8,128)(2,1)} %add_convert_fusion), calls=%async_computation.1 | async-start | bytes 1179648 | tf_op jit(solution)/shard_map/all_to_all | solution.py:771
  81.6 13.4 %collective-permute-start.4 = (bf16[16,64,128]{2,1,0:T(8,128)(2,1)S(1)}, bf16[16,64,128]{2,1,0:T(8,128)(2,1)S(1)}, u32[]{:S(2)}, u32[]{:S(2)}) collective-permute-start(bf16[16,64,128]{2,1,0:T(8,128)(2,1)S(1)} %get-tuple-element.54), channel_id=1, source_target_pairs={{0,4},{1,5},{2,6},{3,7},{4,0},{5,1},{6,2},{7,3},{8,12},{9,13},{10,... | collective-permute-start | bytes 786440 | tf_op jit(solution)/shard_map/ppermute | solution.py:776
  90.8 4.2 %copy-start = (bf16[8,18,16,128]{3,2,1,0:T(8,128)(2,1)}, bf16[8,18,16,128]{3,2,1,0:T(8,128)(2,1)S(1)}, u32[]{:S(2)}) copy-start(bf16[8,18,16,128]{3,2,1,0:T(8,128)(2,1)S(1)} %all-to-all-done.1.rest_ref) | copy-start | bytes 1769476
  95.0 0.7 copy-start.5
  97.9 31.5 %copy-start.8 = (bf16[120,256]{1,0:T(8,128)(2,1)S(1)}, bf16[120,256]{1,0:T(8,128)(2,1)}, u32[]{:S(2)}) copy-start(bf16[120,256]{1,0:T(8,128)(2,1)} %get-tuple-element.47) | copy-start | bytes 184324
  124.2 13.3 %all-to-all-start.3 = ((bf16[8,96,128]{2,1,0:T(8,128)(2,1)}), bf16[8,96,128]{2,1,0:T(8,128)(2,1)S(1)}, u32[]{:S(2)}, u32[]{:S(2)}) async-start(bf16[8,96,128]{2,1,0:T(8,128)(2,1)} %total.1), calls=%async_computation.3 | async-start | bytes 393216 | tf_op jit(solution)/shard_map/all_to_all | solution.py:780
  129.4 8.1 %collective-permute-start.8 = (bf16[120,256]{1,0:T(8,128)(2,1)S(1)}, bf16[120,256]{1,0:T(8,128)(2,1)S(1)}, u32[]{:S(2)}, u32[]{:S(2)}) collective-permute-start(bf16[120,256]{1,0:T(8,128)(2,1)S(1)} %copy-done.8), channel_id=1, source_target_pairs={{0,128},{8,136},{16,144},{24,152},{32,160},{40,168},{48,176},{56,1... | collective-permute-start | bytes 184328 | tf_op jit(solution)/shard_map/ppermute | solution.py:754
  137.5 0.6 copy-start.6
  137.5 0.7 copy-start.2

commit v3 on v2

--- a/solution.py
+++ b/solution.py
@@ -30,7 +30,6 @@
 CELLS = 16
 PIECE = 2 * T + REACH
 REST = CELLS + 2
-VMEM_LIMIT = 56 * 1024 * 1024
 
 f32 = jnp.float32
 bf16 = jnp.bfloat16
@@ -39,8 +38,8 @@
 SMEM = pl.BlockSpec(memory_space=pltpu.SMEM)
 
 
-def params(**more):
-    return pltpu.CompilerParams(vmem_limit_bytes=VMEM_LIMIT, **more)
+def params(mebibytes):
+    return pltpu.CompilerParams(vmem_limit_bytes=mebibytes << 20)
 
 
 def cost(flops, moved, trans=0):
@@ -96,6 +95,52 @@
 
 def whole(*dims):
     return pl.BlockSpec(dims, lambda s: (0,) * len(dims))
+
+
+def once(*dims):
+    return pl.BlockSpec(dims, lambda s: (0,) * len(dims), pipeline_mode=pl.Buffered(1))
+
+
+def turn_body(in_ref, ahead_ref, behind_ref, rows):
+    block = pl.program_id(0)
+    blocks = pl.num_programs(0)
+    for n in range(NEAR):
+        tile = jnp.concatenate(
+            [in_ref[n].astype(f32), jnp.zeros((LANES - GC, K), f32)], axis=0
+        ).T
+        if n >= GC % NEAR:
+            tile = jnp.where(block == blocks - 1, 0.0, tile)
+        rows[pl.ds(n, K, stride=NEAR), :] = tile
+    far = K // NEAR
+    for q in range(far):
+        for r in range(NEAR):
+            at = (q * NEAR + r) * NEAR
+            tile = rows[at : at + NEAR, :].astype(bf16)
+            ahead_ref[r, :, q * LANES : (q + 1) * LANES] = tile
+            r_back = NEAR - 1 - r
+            behind_ref[far - 1 - q, :, r_back * LANES : (r_back + 1) * LANES] = tile
+
+
+def turn(pos):
+    far = K // NEAR
+    ahead, behind = pl.pallas_call(
+        turn_body,
+        grid=(LANES // NEAR,),
+        out_shape=(
+            jax.ShapeDtypeStruct((NEAR, LANES, far * LANES), bf16),
+            jax.ShapeDtypeStruct((far, LANES, NEAR * LANES), bf16),
+        ),
+        in_specs=[pl.BlockSpec((NEAR, GC, K), lambda b: (b, 0, 0))],
+        out_specs=(
+            pl.BlockSpec((NEAR, NEAR, far * LANES), lambda b: (0, b, 0)),
+            pl.BlockSpec((far, NEAR, NEAR * LANES), lambda b: (0, b, 0)),
+        ),
+        scratch_shapes=[pltpu.VMEM((K * NEAR, LANES), f32)],
+        compiler_params=params(10),
+        cost_estimate=cost(0, 12 << 20),
+        name="turn",
+    )(pos)
+    return ahead.reshape(NEAR * LANES, -1), behind.reshape(far * LANES, -1)
 
 
 def encode_body(
@@ -148,12 +193,12 @@
             pre = q * gain + shift
             below = phi(pre)
             encoded = (pre * below).astype(bf16).astype(f32)
-            slope_ref[0, rows, :] = below + pre * bell(pre)
-            q_ref[0, rows, :] = q
+            slope_ref[0, rows, :] = (below + pre * bell(pre)).astype(bf16)
+            q_ref[0, rows, :] = q.astype(bf16)
             offset = encoded - jnp.mean(encoded, axis=-1, keepdims=True)
             inverse_two = lax.rsqrt(jnp.mean(offset * offset, axis=-1, keepdims=True) + epsilon)
             m = offset * inverse_two
-            m_ref[0, rows, :] = m
+            m_ref[0, rows, :] = m.astype(bf16)
             inv_ref[0, rows, :] = jnp.concatenate(
                 [
                     jnp.broadcast_to(inverse, (CHUNK, LANES)),
@@ -182,15 +227,15 @@
             jax.ShapeDtypeStruct((SLOTS, REACH, LANES), bf16),
             jax.ShapeDtypeStruct((SLOTS, REACH, LANES), bf16),
             jax.ShapeDtypeStruct((SLOTS, T, 2 * C), bf16),
-            jax.ShapeDtypeStruct((SLOTS, T, C), f32),
-            jax.ShapeDtypeStruct((SLOTS, T, C), f32),
-            jax.ShapeDtypeStruct((SLOTS, T, C), f32),
+            jax.ShapeDtypeStruct((SLOTS, T, C), bf16),
+            jax.ShapeDtypeStruct((SLOTS, T, C), bf16),
+            jax.ShapeDtypeStruct((SLOTS, T, C), bf16),
             jax.ShapeDtypeStruct((SLOTS, T, 2 * LANES), f32),
         ),
         in_specs=[SMEM] * 3
         + [
             by_slot(2 * T, C),
-            whole(2 * C, C),
+            once(2 * C, C),
             whole(5, C),
             whole(GC, C),
         ],
@@ -210,7 +255,7 @@
             pltpu.VMEM((T, C), f32),
             pltpu.VMEM((T, C), bf16),
         ],
-        compiler_params=params(),
+        compiler_params=params(14),
         cost_estimate=cost(2 * SLOTS * T * C * (2 * C + LANES), 8 << 20, SLOTS * T * C * 2),
         name="encode",
     )(*place, audio, conv_weight, channels, proj)
@@ -249,7 +294,7 @@
     feat_ref,
     low_ref,
     high_ref,
-    pos_ref,
+    weight,
     cot_ref,
     recv_ref,
     states_ref,
@@ -261,16 +306,11 @@
     ext,
     windows,
     turned,
-    weight,
 ):
     place = Place(dev_ref, len_ref, mov_ref)
     slot = pl.program_id(0)
     living = place.alive(slot)
     wide = PER_GROUP * LANES
-
-    @pl.when(slot == 0)
-    def _():
-        fill_weight(weight, pos_ref, True)
 
     @pl.when(living)
     def _():
@@ -310,18 +350,7 @@
     head_ref[0] = slopes_ref[0, :REACH, :]
 
 
-def fill_weight(weight, pos_ref, ahead):
-    size = LANES
-    for q in range(K // NEAR):
-        for r in range(NEAR):
-            tap = q * NEAR + r
-            if ahead:
-                weight[r * size : (r + 1) * size, q * size : (q + 1) * size] = pos_ref[tap]
-            else:
-                weight[q * size : (q + 1) * size, r * size : (r + 1) * size] = pos_ref[K - 1 - tap]
-
-
-def mix(place, features, low, high, pos, cotangent, received):
+def mix(place, features, low, high, weight, cotangent, received):
     return pl.pallas_call(
         mix_body,
         grid=(SLOTS,),
@@ -338,7 +367,7 @@
             by_slot(T, LANES),
             by_slot(REACH, LANES),
             by_slot(REACH, LANES),
-            whole(K, LANES, LANES),
+            once(*weight.shape),
             by_slot(GC, T),
             by_slot(GC, T),
         ],
@@ -354,12 +383,11 @@
             pltpu.VMEM((EXT, LANES), f32),
             pltpu.VMEM((T + NEAR * (K // NEAR - 1), NEAR * LANES), bf16),
             pltpu.VMEM((LANES, T), f32),
-            pltpu.VMEM((NEAR * LANES, K // NEAR * LANES), bf16),
         ],
-        compiler_params=params(),
+        compiler_params=params(20),
         cost_estimate=cost(2 * SLOTS * SPAN * K * LANES * LANES, 7 << 20, SLOTS * T * LANES * 2),
         name="mix",
-    )(*place, features, low, high, pos, cotangent, received)
+    )(*place, features, low, high, weight, cotangent, received)
 
 
 def taps_body(
@@ -400,12 +428,12 @@
                 keep = jnp.where(first_core, even, odd).astype(bf16)
                 send = jnp.where(first_core, odd, even).astype(bf16)
                 for y in range(2):
-                    keep_ref[y, 2 * q + far] = keep[y * REACH : (y + 1) * REACH, :]
-                    send_ref[y, 2 * q + far] = send[y * REACH : (y + 1) * REACH, :]
+                    keep_ref[2 * (2 * q + far) + y] = keep[y * REACH : (y + 1) * REACH, :]
+                    send_ref[2 * (2 * q + far) + y] = send[y * REACH : (y + 1) * REACH, :]
 
 
 def taps(scale, place, pieces):
-    shape = jax.ShapeDtypeStruct((2, CELLS, REACH, LANES), bf16)
+    shape = jax.ShapeDtypeStruct((2 * CELLS, REACH, LANES), bf16)
     spread = X * T
     return pl.pallas_call(
         functools.partial(taps_body, scale),
@@ -419,7 +447,7 @@
             pltpu.VMEM((LANES, spread), bf16),
             pltpu.VMEM((K // NEAR, LANES, 4 * LANES), f32),
         ],
-        compiler_params=params(),
+        compiler_params=params(16),
         cost_estimate=cost(2 * SLOTS * SPAN * K * LANES * LANES, 4 << 20),
         name="taps",
     )(*place, pieces)
@@ -435,7 +463,7 @@
     high_ref,
     cot_ref,
     recv_ref,
-    pos_ref,
+    weight,
     pair_ref,
     q_ref,
     slope_ref,
@@ -450,7 +478,6 @@
     ext,
     windows,
     turned,
-    weight,
     proj,
     feat_grad,
     normed,
@@ -468,7 +495,6 @@
 
     @pl.when(slot == 0)
     def _():
-        fill_weight(weight, pos_ref, False)
         proj[...] = jnp.zeros_like(proj)
         proj[:GC, :] = proj_ref[...]
         conv_sum[...] = jnp.zeros_like(conv_sum)
@@ -491,7 +517,7 @@
         mid[...] = nn(feat_grad[...], proj[...])
         for at in range(0, T, CHUNK):
             rows = slice(at, at + CHUNK)
-            m = m_ref[0, rows, :]
+            m = m_ref[0, rows, :].astype(f32)
             normed[rows, :] = (m * gain_two + shift_two).astype(bf16)
             normed_grad = mid[rows, :]
             chan_sum[24:32, :] += jnp.sum((normed_grad * m).reshape(-1, 8, C), axis=0)
@@ -500,8 +526,10 @@
             first = jnp.mean(scaled, axis=-1, keepdims=True)
             second = jnp.mean(scaled * m, axis=-1, keepdims=True)
             inverse_two = inv_ref[0, rows, LANES : LANES + 1]
-            pre_grad = inverse_two * (scaled - first - m * second) * slope_ref[0, rows, :]
-            q = q_ref[0, rows, :]
+            pre_grad = inverse_two * (scaled - first - m * second) * slope_ref[
+                0, rows, :
+            ].astype(f32)
+            q = q_ref[0, rows, :].astype(f32)
             chan_sum[8:16, :] += jnp.sum((pre_grad * q).reshape(-1, 8, C), axis=0)
             chan_sum[16:24, :] += jnp.sum(pre_grad.reshape(-1, 8, C), axis=0)
             scaled = pre_grad * gain
@@ -563,7 +591,7 @@
 
 
 def backward(
-    scale, place, slopes, low, high, cotangent, received, pos, stored, conv_weight, channels, proj
+    scale, place, slopes, low, high, cotangent, received, weight, stored, conv_weight, channels, proj
 ):
     shape = jax.ShapeDtypeStruct((MP, REST, 16, LANES), bf16)
     return pl.pallas_call(
@@ -577,13 +605,13 @@
             by_slot(REACH, LANES),
             by_slot(GC, T),
             by_slot(GC, T),
-            whole(K, LANES, LANES),
+            once(*weight.shape),
             by_slot(T, 2 * C),
             by_slot(T, C),
             by_slot(T, C),
             by_slot(T, C),
             by_slot(T, 2 * LANES),
-            whole(2 * C, C),
+            once(2 * C, C),
             whole(5, C),
             whole(GC, C),
         ],
@@ -592,7 +620,6 @@
             pltpu.VMEM((EXT, LANES), f32),
             pltpu.VMEM((T + NEAR * (K // NEAR - 1), NEAR * LANES), bf16),
             pltpu.VMEM((LANES, T), f32),
-            pltpu.VMEM((K // NEAR * LANES, NEAR * LANES), bf16),
             pltpu.VMEM((LANES, C), bf16),
             pltpu.VMEM((T, LANES), bf16),
             pltpu.VMEM((T, C), bf16),
@@ -603,7 +630,7 @@
             pltpu.VMEM((40, C), f32),
             pltpu.VMEM((LANES, C), f32),
         ],
-        compiler_params=params(),
+        compiler_params=params(30),
         cost_estimate=cost(
             2 * SLOTS * (SPAN * K * LANES * LANES + T * C * (4 * C + 2 * LANES)), 14 << 20
         ),
@@ -615,7 +642,7 @@
         high,
         cotangent,
         received,
-        pos,
+        weight,
         *stored,
         conv_weight,
         channels,
@@ -623,48 +650,48 @@
     )
 
 
-def cells_body(dev_ref, kept_ref, recv_ref, rest_ref, out_ref):
+def cells_body(dev_ref, rest_ref, out_ref):
     model = lax.rem(dev_ref[0], MP)
-    out_ref[:, :REACH, :] = (kept_ref[...].astype(f32) + recv_ref[...].astype(f32)).astype(bf16)
     rest = rest_ref[0].astype(f32)
     for n in range(1, MP):
         rest += rest_ref[n].astype(f32)
-    out_ref[:, REACH : REACH + 16, :] = rest[:CELLS].astype(bf16)
+    out_ref[:, :16, :] = rest[:CELLS].astype(bf16)
     for cell in range(CELLS):
         small = jnp.where(model == cell // 2, rest[CELLS + cell % 2], 0.0)
-        out_ref[cell, REACH + 16 :, :] = small.astype(bf16)
-
-
-def make_cells(dev, kept, received, rest):
+        out_ref[cell, 16:, :] = small.astype(bf16)
+
+
+def make_cells(dev, rest):
     return pl.pallas_call(
         cells_body,
-        out_shape=jax.ShapeDtypeStruct((CELLS, REACH + 32, LANES), bf16),
-        in_specs=[SMEM] + [VMEM] * 3,
+        out_shape=jax.ShapeDtypeStruct((CELLS, 32, LANES), bf16),
+        in_specs=[SMEM, VMEM],
         out_specs=VMEM,
-        compiler_params=params(),
-        cost_estimate=cost(0, 2 << 20),
+        compiler_params=params(8),
+        cost_estimate=cost(0, 1 << 20),
         name="cells",
-    )(dev, kept, received, rest)
-
-
-def total_body(in_ref, out_ref):
-    total = in_ref[0].astype(f32)
-    for n in range(1, in_ref.shape[0]):
-        total += in_ref[n].astype(f32)
-    for copy in range(MP):
-        out_ref[copy] = total.astype(bf16)
-
-
-def total(parts):
+    )(dev, rest)
+
+
+def total_body(pos_ref, rest_ref, out_ref):
+    for at, parts_ref in ((0, pos_ref), (REACH, rest_ref)):
+        total = parts_ref[0].astype(f32)
+        for n in range(1, parts_ref.shape[0]):
+            total += parts_ref[n].astype(f32)
+        for copy in range(MP):
+            out_ref[copy, at : at + total.shape[0], :] = total.astype(bf16)
+
+
+def total(pos, rest):
     return pl.pallas_call(
         total_body,
-        out_shape=jax.ShapeDtypeStruct((MP,) + parts.shape[1:], bf16),
-        in_specs=[VMEM],
+        out_shape=jax.ShapeDtypeStruct((MP, REACH + 32, LANES), bf16),
+        in_specs=[VMEM] * 2,
         out_specs=VMEM,
-        compiler_params=params(),
-        cost_estimate=cost(0, 2 * parts.size),
+        compiler_params=params(8),
+        cost_estimate=cost(0, 2 << 20),
         name="total",
-    )(parts)
+    )(pos, rest)
 
 
 def finish_body(
@@ -711,7 +738,7 @@
         ),
         in_specs=[SMEM] * 3 + [VMEM] * 3,
         out_specs=(VMEM,) * 5,
-        compiler_params=params(),
+        compiler_params=params(8),
         name="finish",
     )(*place, cells, states, other)
 
@@ -740,15 +767,16 @@
     channels = channel_params.T
     proj = proj_weight.T
     cot = cotangent.transpose(0, 2, 1)
-    pos = jnp.pad(pos_weight, ((0, 0), (0, LANES - GC), (0, LANES - GC)))
 
     received = lax.ppermute(cot, "dp", swap)
     features, tail, head, *stored = encode(place, audio, conv_weight, channels, proj)
     low, high = neighbours(tail, head)
+    ahead, behind = turn(pos_weight.transpose(1, 2, 0))
     states, sent, slopes, tail, head, pieces = mix(
-        place, features, low, high, pos, cot, received
+        place, features, low, high, ahead, cot, received
     )
     slope_low, slope_high = neighbours(tail, head)
+    pieces, slope_low, slope_high = lax.optimization_barrier((pieces, slope_low, slope_high))
     rows = [list(range(X)), list(range(X, 2 * X))]
     pieces = lax.all_to_all(pieces, "mp", 0, 0, axis_index_groups=rows, tiled=True)
     other = lax.ppermute(sent, "dp", swap)
@@ -760,7 +788,7 @@
         slope_high,
         cot,
         received,
-        pos,
+        behind,
         stored,
         conv_weight,
         channels,
@@ -770,14 +798,25 @@
     pos_keep, pos_send = taps(scale, place, pieces)
     rest = lax.all_to_all(rest, "mp", 0, 0, tiled=True)
     pos_sum = added(pos_keep, lax.ppermute(pos_send, "dp", core_swap))
-    low_half = model_index < X
-    kept = jnp.where(low_half, pos_sum[0], pos_sum[1])
-    leaving = jnp.where(low_half, pos_sum[1], pos_sum[0])
-    coming = lax.ppermute(leaving, "mp", [(i, i ^ X) for i in range(MP)])
-    cells = make_cells(dev, kept, coming, rest)
+    links = [
+        [MP * (2 * cell + core) + X * y + x for cell in range(CELLS) for y in range(2)]
+        for core in range(2)
+        for x in range(X)
+    ]
+    pos_sum = lax.all_to_all(
+        pos_sum,
+        ("dp", "mp"),
+        0,
+        0,
+        axis_index_groups=links,
+        tiled=True,
+    )
+    rest, other = lax.optimization_barrier((rest, other))
     groups = [list(range(bit, DP, 2)) for bit in range(2)]
-    cells = lax.all_to_all(cells, "dp", 0, 0, axis_index_groups=groups, tiled=True)
-    cells = lax.all_to_all(total(cells), "mp", 0, 0, tiled=True)
+    rest = lax.all_to_all(
+        make_cells(dev, rest), "dp", 0, 0, axis_index_groups=groups, tiled=True
+    )
+    cells = lax.all_to_all(total(pos_sum, rest), "mp", 0, 0, tiled=True)
     hidden, grad_pos, grad_conv, grad_proj, grad_channels = finish(place, cells, states, other)
     return (
         hidden.transpose(0, 2, 1),

time: 141 us -> 145 us (1.028)
  starting transfers between devices: 34.9 us -> 52.6 us
  Pallas kernels: 37.1 us -> 21.4 us
  waiting for transfers between devices: 25.5 us -> 14.8 us
  local copies, waits for them, and re-layouts: 15.2 us -> 21.7 us
  blocking collectives: 24.6 us -> 29.2 us
    unnamed x31 -> x54, local copies, waits for them, and re-layouts: 9.9 us -> 21.7 us
    all_to_all x1, waiting for transfers between devices: 0.01 us -> 9.88 us  [per_device(): lax.all_to_all(make_cells(dev, rest), 'dp', 0, 0, axis_index_groups=group...]
    all_to_all x1, waiting for transfers between devices: 7.75 us -> 0.01 us  [per_device(): rest = lax.all_to_all(rest, 'mp', 0, 0, tiled=True)]
    pallas_call x1, Pallas kernels: 12.4 us -> 5.1 us  [backward(): pl.pallas_call(functools.partial(backward_body, scale), grid=(SLOTS,), ou...]
    all_to_all x1, starting transfers between devices: 5.12 us -> 11.7 us  [per_device(): lax.all_to_all(make_cells(dev, rest), 'dp', 0, 0, axis_index_groups=group...]
    ppermute x1, starting transfers between devices: 1.67 us -> 7.47 us  [per_device(): other = lax.ppermute(sent, 'dp', swap)]
    ppermute x2, waiting for transfers between devices: 5.39 us -> 0.01 us  [neighbours(): lax.ppermute(tail, 'mp', forward)]
    pad x1 -> x0, local copies, waits for them, and re-layouts: 5.26 us -> none  [per_device(): pos = jnp.pad(pos_weight, ((0, 0), (0, LANES - GC), (0, LANES - GC)))]
  transfers between devices with their start and end apart: 12 -> 11, of which waited for: 5 -> 3; matrix products, arithmetic and copies ran while one was open for 10% -> 2% of each run, Pallas kernels for 17% -> 12%
where the time goes in v3:
time: 145 us; the launch traced here: 144 us
  starting transfers between devices  52.6 us (36%)
  blocking collectives  29.2 us (20%)
  local copies, waits for them, and re-layouts  21.7 us (15%)
  Pallas kernels  21.4 us (15%)
  waiting for transfers between devices  14.8 us (10%)
  other arithmetic  3.28 us (2%)
    unnamed x54, local copies, waits for them, and re-layouts  21.7 us
    all_to_all x1, blocking collectives, per_device(): lax.all_to_all(pos_sum, ('dp', 'mp'), 0, 0, axis_index_groups=links, tile...  18.7 us
    all_to_all x1, starting transfers between devices, per_device(): lax.all_to_all(make_cells(dev, rest), 'dp', 0, 0, axis_index_groups=group...  11.7 us
    all_to_all x1, blocking collectives, per_device(): cells = lax.all_to_all(total(pos_sum, rest), 'mp', 0, 0, tiled=True)  10.4 us
    all_to_all x1, waiting for transfers between devices, per_device(): lax.all_to_all(make_cells(dev, rest), 'dp', 0, 0, axis_index_groups=group...  9.88 us
    ppermute x2, starting transfers between devices, neighbours(): lax.ppermute(head, 'mp', backward_route)  7.75 us
    all_to_all x1, starting transfers between devices, per_device(): lax.all_to_all(pieces, 'mp', 0, 0, axis_index_groups=rows, tiled=True)  7.57 us
    ppermute x1, starting transfers between devices, per_device(): other = lax.ppermute(sent, 'dp', swap)  7.47 us
  transfers between devices with their start and end apart: 11, of which 3 were waited for; matrix products, arithmetic and copies ran while one was open for 2% of the time, Pallas kernels for 12%

profile of v3, /device:TPU:2, one launch (start us, length us, event | category | flops | bytes accessed | tf_op | source)
XLA Modules:
  0.0 143.8 jit_solution(5551677238126751216)
XLA Ops:
  0.6 7.3 %collective-permute-start.2 = (bf16[2,120,256]{2,1,0:T(8,128)(2,1)}, bf16[2,120,256]{2,1,0:T(8,128)(2,1)S(1)}, u32[]{:S(2)}, u32[]{:S(2)}) collective-permute-start(bf16[2,120,256]{2,1,0:T(8,128)(2,1)} %bitcast.22), channel_id=1, source_target_pairs={{0,128},{8,136},{16,144},{24,152},{32,160},{40,168},{48,176},{56,1... | collective-permute-start | bytes 368648 | tf_op jit(solution)/shard_map/ppermute | solution.py:771
  7.9 1.2 copy-done.1
  9.1 1.2 copy-done.2
  10.4 0.9 copy-done.4
  11.3 0.7 copy-done.6
  12.0 0.7 copy-done.8
  12.6 0.7 copy-done.10
  13.3 2.1 %encode.1 = (bf16[2,256,128]{2,1,0:T(8,128)(2,1)S(1)}, bf16[2,64,128]{2,1,0:T(8,128)(2,1)S(1)}, bf16[2,64,128]{2,1,0:T(8,128)(2,1)S(1)}, bf16[2,256,1024]{2,1,0:...) custom-call(s32[1]{0:T(128)} %bitcast.dev_ref, ...), custom_call_target="tpu_custom_call" | custom-call | flops 603979776 | bytes 8388608 | tf_op jit(solution)/shard_map/encode/pallas_call | solution.py:222
  15.3 0.0 copy-start.16
  15.4 0.8 copy-done.16
  16.2 0.8 copy-done.18
  17.0 0.8 copy-done.20
  17.7 0.8 copy-done.22
  18.5 2.0 %collective-permute-start = (bf16[2,64,128]{2,1,0:T(8,128)(2,1)S(1)}, bf16[2,64,128]{2,1,0:T(8,128)(2,1)S(1)}, u32[]{:S(2)}, u32[]{:S(2)}) collective-permute-start(bf16[2,64,128]{2,1,0:T(8,128)(2,1)S(1)} %get-tuple-element.38), channel_id=1, source_target_pairs={{0,1},{1,2},{2,3},{3,4},{4,5},{5,6},{6,7},{8,9},{9,10},{10,11},{11... | collective-permute-start | bytes 98312 | tf_op jit(solution)/shard_map/ppermute | solution.py:750
  20.5 3.8 %collective-permute-start.1 = (bf16[2,64,128]{2,1,0:T(8,128)(2,1)S(1)}, bf16[2,64,128]{2,1,0:T(8,128)(2,1)S(1)}, u32[]{:S(2)}, u32[]{:S(2)}) collective-permute-start(bf16[2,64,128]{2,1,0:T(8,128)(2,1)S(1)} %get-tuple-element.39), channel_id=1, source_target_pairs={{1,0},{2,1},{3,2},{4,3},{5,4},{6,5},{7,6},{9,8},{10,9},{11,10},{12... | collective-permute-start | bytes 98312 | tf_op jit(solution)/shard_map/ppermute | solution.py:750
  24.4 0.0 copy-start
  24.4 2.0 %copy-done = bf16[128,120,120]{0,2,1:T(8,128)(2,1)S(1)} copy-done((bf16[128,120,120]{0,2,1:T(8,128)(2,1)S(1)}, bf16[128,120,120]{0,2,1:T(8,128)(2,1)}, u32[]{:S(2)}) %copy-start) | copy-done | bytes 3686424
  26.4 4.9 %turn.1 = (bf16[16,128,1024]{2,1,0:T(8,128)(2,1)S(1)}, bf16[8,128,2048]{2,1,0:T(8,128)(2,1)S(1)}) custom-call(bf16[120,120,128]{2,1,0:T(8,128)(2,1)S(1)} %bitcast.10), custom_call_target="tpu_custom_call" | custom-call | bytes 12582912 | tf_op jit(solution)/shard_map/turn/pallas_call | solution.py:126
  31.4 0.0 copy-done.14
  31.4 0.0 copy-start.12
  31.4 1.9 %copy-done.12 = bf16[8,128,2048]{2,1,0:T(8,128)(2,1)} copy-done((bf16[8,128,2048]{2,1,0:T(8,128)(2,1)}, bf16[8,128,2048]{2,1,0:T(8,128)(2,1)S(1)}, u32[]{:S(2)}) %copy-start.12) | copy-done | bytes 4194328
  33.3 0.0 collective-permute-done.low_ref
  33.3 0.0 collective-permute-done.1.high_ref
  33.3 0.0 collective-permute-done.2.recv_ref
  33.3 0.0 copy-done.9
  33.4 0.0 copy-done.11
  33.4 0.0 copy-done.24
  33.4 3.2 %mix.1 = (bf16[2,120,256]{2,1,0:T(8,128)(2,1)S(1)}, bf16[120,256]{1,0:T(8,128)(2,1)S(1)}, bf16[2,256,128]{2,1,0:T(8,128)(2,1)S(1)}, bf16[2,64,128]{2,1,0:T(8,128...) custom-call(s32[1]{0:T(128)} %bitcast.dev_ref, s32[64]{0:T(128)S(1)} %copy-done.9, ...), custom_call_target="tpu_custom_call" | custom-call | flops 2550136832 | bytes 7340032 | tf_op jit(solution)/shard_map/mix/pallas_call | solution.py:354
  36.6 0.7 copy-done.25
  37.2 1.9 %collective-permute-start.3 = (bf16[2,64,128]{2,1,0:T(8,128)(2,1)S(1)}, bf16[2,64,128]{2,1,0:T(8,128)(2,1)S(1)}, u32[]{:S(2)}, u32[]{:S(2)}) collective-permute-start(bf16[2,64,128]{2,1,0:T(8,128)(2,1)S(1)} %get-tuple-element.42), channel_id=1, source_target_pairs={{0,1},{1,2},{2,3},{3,4},{4,5},{5,6},{6,7},{8,9},{9,10},{10,11},{11... | collective-permute-start | bytes 98312 | tf_op jit(solution)/shard_map/ppermute | solution.py:750
  39.1 3.9 %collective-permute-start.4 = (bf16[2,64,128]{2,1,0:T(8,128)(2,1)S(1)}, bf16[2,64,128]{2,1,0:T(8,128)(2,1)S(1)}, u32[]{:S(2)}, u32[]{:S(2)}) collective-permute-start(bf16[2,64,128]{2,1,0:T(8,128)(2,1)S(1)} %get-tuple-element.43), channel_id=1, source_target_pairs={{1,0},{2,1},{3,2},{4,3},{5,4},{6,5},{7,6},{9,8},{10,9},{11,10},{12... | collective-permute-start | bytes 98312 | tf_op jit(solution)/shard_map/ppermute | solution.py:750
  43.1 0.0 collective-permute-done.3.low_ref
  43.1 1.9 %collective-permute-done.4.high_ref = bf16[2,64,128]{2,1,0:T(8,128)(2,1)S(1)} collective-permute-done((bf16[2,64,128]{2,1,0:T(8,128)(2,1)S(1)}, bf16[2,64,128]{2,1,0:T(8,128)(2,1)S(1)}, u32[]{:S(2)}, u32[]{:S(2)}) %collective-permute-start.4) | collective-permute-done | bytes 32800 | tf_op jit(solution)/shard_map/ppermute | solution.py:750
  45.0 7.6 %all-to-all-start = ((bf16[4,2,576,128]{3,2,1,0:T(8,128)(2,1)}), bf16[4,2,576,128]{3,2,1,0:T(8,128)(2,1)S(1)}, u32[]{:S(2)}, u32[]{:S(2)}) async-start(bf16[4,2,576,128]{3,2,1,0:T(8,128)(2,1)} %get-tuple-element.44), calls=%async_computation | async-start | bytes 2359296 | tf_op jit(solution)/shard_map/all_to_all | solution.py:781
  52.5 0.0 copy-done.3
  52.5 0.0 copy-done.5
  52.5 0.0 copy-done.7
  52.6 2.2 %copy-done.13 = bf16[8,128,2048]{2,1,0:T(8,128)(2,1)S(1)} copy-done((bf16[8,128,2048]{2,1,0:T(8,128)(2,1)S(1)}, bf16[8,128,2048]{2,1,0:T(8,128)(2,1)}, u32[]{:S(2)}) %copy-start.13) | copy-done | bytes 4194328
  54.7 1.2 copy-done.15
  56.0 1.0 copy-done.17
  57.0 1.0 copy-done.19
  58.0 1.0 copy-done.21
  59.1 1.0 copy-done.23
  60.1 0.9 copy-done.26
  61.0 5.1 %backward.1 = (bf16[2,512,512]{2,1,0:T(8,128)(2,1)}, bf16[8,18,16,128]{3,2,1,0:T(8,128)(2,1)S(1)}, bf16[8,18,16,128]{3,2,1,0:T(8,128)(2,1)}) custom-call(s32[1]{0:T(128)} %bitcast.dev_ref, s32[64]{0:T(128)S(1)} %copy-done.9, s32[16]{0:T(128)S(1)} %bitcast.17, bf16[2,256,128]{2,1,0:T(8,128)(2,1)S(1)} %copy-done.26, ...), custom_call_target="tpu_custom_call" | custom-call | flops 3758096384 | bytes 14680064 | tf_op jit(solution)/shard_map/backward/pallas_call | solution.py:597
  66.1 0.0 collective-permute-start.6
  66.1 0.0 all-to-all-done.piece_ref
  66.1 3.9 %taps.1 = (bf16[32,64,128]{2,1,0:T(8,128)(2,1)S(1)}, bf16[32,64,128]{2,1,0:T(8,128)(2,1)S(1)}) custom-call(s32[1]{0:T(128)} %bitcast.dev_ref, s32[64]{0:T(128)S(1)} %copy-done.9, s32[16]{0:T(128)S(1)} %bitcast.18, bf16[4,2,576,128]{3,2,1,0:T(8,128)(2,1)S(1)} %all-to-all-done.piece_ref), custom_call_target="tpu_custom_call" | custom-call | flops 2550136832 | bytes 4194304 | tf_op jit(solution)/shard_map/taps/pallas_call | solution.py:438
  70.0 0.6 collective-permute-start.5
  70.6 0.0 collective-permute-done.6
  70.6 2.1 %add_convert_fusion = bf16[8,18,16,128]{3,2,1,0:T(8,128)(2,1)} fusion(bf16[8,18,16,128]{3,2,1,0:T(8,128)(2,1)} %collective-permute-done.6, bf16[8,18,16,128]{3,2,1,0:T(8,128)(2,1)S(1)} %get-tuple-element.56), kind=kLoop, calls=%fused_computation | loop fusion | flops 1179648 | bytes 1769472 | tf_op jit(solution)/shard_map/convert_element_type | solution.py:754
  72.7 6.4 %all-to-all-start.2 = ((bf16[8,18,16,128]{3,2,1,0:T(8,128)(2,1)}), bf16[8,18,16,128]{3,2,1,0:T(8,128)(2,1)S(1)}, u32[]{:S(2)}, u32[]{:S(2)}) async-start(bf16[8,18,16,128]{3,2,1,0:T(8,128)(2,1)} %add_convert_fusion), calls=%async_computation.2 | async-start | bytes 1179648 | tf_op jit(solution)/shard_map/all_to_all | solution.py:799
  79.1 7.5 %collective-permute-start.7 = (bf16[120,256]{1,0:T(8,128)(2,1)S(1)}, bf16[120,256]{1,0:T(8,128)(2,1)S(1)}, u32[]{:S(2)}, u32[]{:S(2)}) collective-permute-start(bf16[120,256]{1,0:T(8,128)(2,1)S(1)} %get-tuple-element.58), channel_id=1, source_target_pairs={{0,128},{8,136},{16,144},{24,152},{32,160},{40,168},{48,176},{56,1... | collective-permute-start | bytes 184328 | tf_op jit(solution)/shard_map/ppermute | solution.py:782
  86.5 3.1 %collective-permute-done.7.other_ref = bf16[120,256]{1,0:T(8,128)(2,1)S(1)} collective-permute-done((bf16[120,256]{1,0:T(8,128)(2,1)S(1)}, bf16[120,256]{1,0:T(8,128)(2,1)S(1)}, u32[]{:S(2)}, u32[]{:S(2)}) %collective-permute-start.7) | collective-permute-done | bytes 61472 | tf_op jit(solution)/shard_map/ppermute | solution.py:782
  89.6 0.0 all-to-all-done.2.rest_ref
  89.6 0.7 cells.1
  90.3 11.7 %all-to-all-start.3 = ((bf16[16,32,128]{2,1,0:T(8,128)(2,1)}), bf16[16,32,128]{2,1,0:T(8,128)(2,1)S(1)}, u32[]{:S(2)}, u32[]{:S(2)}) async-start(bf16[16,32,128]{2,1,0:T(8,128)(2,1)} %cells.1), calls=%async_computation.3 | async-start | bytes 262144 | tf_op jit(solution)/shard_map/all_to_all | solution.py:816
  102.0 0.0 collective-permute-done.5
  102.0 1.2 add_convert_fusion.1
  103.2 9.9 %all-to-all-done.3.rest_ref = bf16[16,32,128]{2,1,0:T(8,128)(2,1)S(1)} async-done(((bf16[16,32,128]{2,1,0:T(8,128)(2,1)}), bf16[16,32,128]{2,1,0:T(8,128)(2,1)S(1)}, u32[]{:S(2)}, u32[]{:S(2)}) %all-to-all-start.3) | async-done | bytes 131104 | tf_op jit(solution)/shard_map/all_to_all | solution.py:816
  113.1 18.7 %all_to_all.25.pos_ref = bf16[32,64,128]{2,1,0:T(8,128)(2,1)S(1)} all-to-all(bf16[32,64,128]{2,1,0:T(8,128)(2,1)S(1)} %add_convert_fusion.1), channel_id=1, replica_groups={{0,4,16,20,32,36,48,52,64,68,80,84,96,100,112,116,128,132,144,148,160,1..., dimensions={0} | all-to-all | bytes 1048576 | tf_op jit(solution)/shard_map/all_to_all | solution.py:806
  131.8 0.1 total.1
  131.9 10.4 %all_to_all.26.in_ref = bf16[8,96,128]{2,1,0:T(8,128)(2,1)S(1)} all-to-all(bf16[8,96,128]{2,1,0:T(8,128)(2,1)S(1)} %total.1), channel_id=1, replica_groups=mesh['dp'=32,'mp'=8] {'mp'}, dimensions={0} | all-to-all | bytes 393216 | tf_op jit(solution)/shard_map/all_to_all | solution.py:819
  142.4 1.4 finish.1
  (24 shorter events, 0.0 us)
Async XLA Ops:
  0.6 32.7 %collective-permute-start.2 = (bf16[2,120,256]{2,1,0:T(8,128)(2,1)}, bf16[2,120,256]{2,1,0:T(8,128)(2,1)S(1)}, u32[]{:S(2)}, u32[]{:S(2)}) collective-permute-start(bf16[2,120,256]{2,1,0:T(8,128)(2,1)} %bitcast.22), channel_id=1, source_target_pairs={{0,128},{8,136},{16,144},{24,152},{32,160},{40,168},{48,176},{56,1... | collective-permute-start | bytes 368648 | tf_op jit(solution)/shard_map/ppermute | solution.py:771
  7.9 1.2 copy-start.1
  9.1 1.2 copy-start.2
  10.4 0.9 copy-start.4
  11.3 0.7 copy-start.6
  12.0 0.7 copy-start.8
  12.6 0.7 copy-start.10
  15.3 0.8 copy-start.16
  16.2 0.8 copy-start.18
  17.0 0.8 copy-start.20
  17.7 0.8 copy-start.22
  18.5 12.8 %copy-start.14 = (bf16[2,256,1024]{2,1,0:T(8,128)(2,1)}, bf16[2,256,1024]{2,1,0:T(8,128)(2,1)S(1)}, u32[]{:S(2)}) copy-start(bf16[2,256,1024]{2,1,0:T(8,128)(2,1)S(1)} %get-tuple-element.51.pair_ref) | copy-start | bytes 3145732
  18.5 14.8 %collective-permute-start = (bf16[2,64,128]{2,1,0:T(8,128)(2,1)S(1)}, bf16[2,64,128]{2,1,0:T(8,128)(2,1)S(1)}, u32[]{:S(2)}, u32[]{:S(2)}) collective-permute-start(bf16[2,64,128]{2,1,0:T(8,128)(2,1)S(1)} %get-tuple-element.38), channel_id=1, source_target_pairs={{0,1},{1,2},{2,3},{3,4},{4,5},{5,6},{6,7},{8,9},{9,10},{10,11},{11... | collective-permute-start | bytes 98312 | tf_op jit(solution)/shard_map/ppermute | solution.py:750
  20.5 12.8 %collective-permute-start.1 = (bf16[2,64,128]{2,1,0:T(8,128)(2,1)S(1)}, bf16[2,64,128]{2,1,0:T(8,128)(2,1)S(1)}, u32[]{:S(2)}, u32[]{:S(2)}) collective-permute-start(bf16[2,64,128]{2,1,0:T(8,128)(2,1)S(1)} %get-tuple-element.39), channel_id=1, source_target_pairs={{1,0},{2,1},{3,2},{4,3},{5,4},{6,5},{7,6},{9,8},{10,9},{11,10},{12... | collective-permute-start | bytes 98312 | tf_op jit(solution)/shard_map/ppermute | solution.py:750
  24.4 2.0 %copy-start = (bf16[128,120,120]{0,2,1:T(8,128)(2,1)S(1)}, bf16[128,120,120]{0,2,1:T(8,128)(2,1)}, u32[]{:S(2)}) copy-start(bf16[128,120,120]{0,2,1:T(8,128)(2,1)} %param.14) | copy-start | bytes 11059204
  26.4 6.9 %copy-start.9 = (s32[64]{0:T(128)S(1)}, s32[64]{0:T(128)}, u32[]{:S(2)}) copy-start(s32[64]{0:T(128)} %len_ref.9) | copy-start | bytes 772
  26.4 6.9 %copy-start.11 = (s32[16,1]{0,1:T(1,128)S(1)}, s32[16,1]{0,1:T(1,128)}, u32[]{:S(2)}) copy-start(s32[16,1]{0,1:T(1,128)} %param.10) | copy-start | bytes 196
  26.4 6.9 %copy-start.24 = (bf16[2,256,120]{1,2,0:T(8,128)(2,1)S(1)}, bf16[2,256,120]{1,2,0:T(8,128)(2,1)}, u32[]{:S(2)}) copy-start(bf16[2,256,120]{1,2,0:T(8,128)(2,1)} %param.15) | copy-start | bytes 368644
  31.4 2.0 %copy-start.12 = (bf16[8,128,2048]{2,1,0:T(8,128)(2,1)}, bf16[8,128,2048]{2,1,0:T(8,128)(2,1)S(1)}, u32[]{:S(2)}) copy-start(bf16[8,128,2048]{2,1,0:T(8,128)(2,1)S(1)} %get-tuple-element.50) | copy-start | bytes 12582916
  36.6 0.7 copy-start.25
  37.2 5.8 %collective-permute-start.3 = (bf16[2,64,128]{2,1,0:T(8,128)(2,1)S(1)}, bf16[2,64,128]{2,1,0:T(8,128)(2,1)S(1)}, u32[]{:S(2)}, u32[]{:S(2)}) collective-permute-start(bf16[2,64,128]{2,1,0:T(8,128)(2,1)S(1)} %get-tuple-element.42), channel_id=1, source_target_pairs={{0,1},{1,2},{2,3},{3,4},{4,5},{5,6},{6,7},{8,9},{9,10},{10,11},{11... | collective-permute-start | bytes 98312 | tf_op jit(solution)/shard_map/ppermute | solution.py:750
  39.1 5.8 %collective-permute-start.4 = (bf16[2,64,128]{2,1,0:T(8,128)(2,1)S(1)}, bf16[2,64,128]{2,1,0:T(8,128)(2,1)S(1)}, u32[]{:S(2)}, u32[]{:S(2)}) collective-permute-start(bf16[2,64,128]{2,1,0:T(8,128)(2,1)S(1)} %get-tuple-element.43), channel_id=1, source_target_pairs={{1,0},{2,1},{3,2},{4,3},{5,4},{6,5},{7,6},{9,8},{10,9},{11,10},{12... | collective-permute-start | bytes 98312 | tf_op jit(solution)/shard_map/ppermute | solution.py:750
  45.0 7.6 %copy-start.3 = (bf16[1024,512]{1,0:T(8,128)(2,1)S(1)}, bf16[1024,512]{1,0:T(8,128)(2,1)}, u32[]{:S(2)}) copy-start(bf16[1024,512]{1,0:T(8,128)(2,1)} %conv_ref.3) | copy-start | bytes 3145732
  45.0 7.6 %copy-start.5 = (bf16[512,120]{0,1:T(8,128)(2,1)S(1)}, bf16[512,120]{0,1:T(8,128)(2,1)}, u32[]{:S(2)}) copy-start(bf16[512,120]{0,1:T(8,128)(2,1)} %param.13) | copy-start | bytes 368644
  45.0 7.6 %copy-start.7 = (f32[512,5]{0,1:T(8,128)S(1)}, f32[512,5]{0,1:T(8,128)}, u32[]{:S(2)}) copy-start(f32[512,5]{0,1:T(8,128)} %param.12) | copy-start | bytes 30724
  45.0 21.2 %all-to-all-start = ((bf16[4,2,576,128]{3,2,1,0:T(8,128)(2,1)}), bf16[4,2,576,128]{3,2,1,0:T(8,128)(2,1)S(1)}, u32[]{:S(2)}, u32[]{:S(2)}) async-start(bf16[4,2,576,128]{3,2,1,0:T(8,128)(2,1)} %get-tuple-element.44), calls=%async_computation | async-start | bytes 2359296 | tf_op jit(solution)/shard_map/all_to_all | solution.py:781
  52.5 2.2 %copy-start.13 = (bf16[8,128,2048]{2,1,0:T(8,128)(2,1)S(1)}, bf16[8,128,2048]{2,1,0:T(8,128)(2,1)}, u32[]{:S(2)}) copy-start(bf16[8,128,2048]{2,1,0:T(8,128)(2,1)} %copy-done.12) | copy-start | bytes 12582916
  54.7 1.2 copy-start.15
  56.0 1.0 copy-start.17
  57.0 1.0 copy-start.19
  58.0 1.0 copy-start.21
  59.1 1.0 copy-start.23
  60.1 0.9 copy-start.26
  66.1 4.5 %collective-permute-start.6 = (bf16[8,18,16,128]{3,2,1,0:T(8,128)(2,1)}, bf16[8,18,16,128]{3,2,1,0:T(8,128)(2,1)}, u32[]{:S(2)}, u32[]{:S(2)}) collective-permute-start(bf16[8,18,16,128]{3,2,1,0:T(8,128)(2,1)} %get-tuple-element.57), channel_id=1, source_target_pairs={{0,8},{8,0},{16,24},{24,16},{32,40},{40,32},{48,56},{56,48},{64,72... | collective-permute-start | bytes 1769480 | tf_op jit(solution)/shard_map/ppermute | solution.py:797
  70.0 32.0 %collective-permute-start.5 = (bf16[32,64,128]{2,1,0:T(8,128)(2,1)S(1)}, bf16[32,64,128]{2,1,0:T(8,128)(2,1)}, u32[]{:S(2)}, u32[]{:S(2)}) collective-permute-start(bf16[32,64,128]{2,1,0:T(8,128)(2,1)S(1)} %get-tuple-element.46), channel_id=1, source_target_pairs={{0,8},{8,0},{16,24},{24,16},{32,40},{40,32},{48,56},{56,48},{64,72... | collective-permute-start | bytes 1572872 | tf_op jit(solution)/shard_map/ppermute | solution.py:800
  72.7 16.9 %all-to-all-start.2 = ((bf16[8,18,16,128]{3,2,1,0:T(8,128)(2,1)}), bf16[8,18,16,128]{3,2,1,0:T(8,128)(2,1)S(1)}, u32[]{:S(2)}, u32[]{:S(2)}) async-start(bf16[8,18,16,128]{3,2,1,0:T(8,128)(2,1)} %add_convert_fusion), calls=%async_computation.2 | async-start | bytes 1179648 | tf_op jit(solution)/shard_map/all_to_all | solution.py:799
  79.1 10.5 %collective-permute-start.7 = (bf16[120,256]{1,0:T(8,128)(2,1)S(1)}, bf16[120,256]{1,0:T(8,128)(2,1)S(1)}, u32[]{:S(2)}, u32[]{:S(2)}) collective-permute-start(bf16[120,256]{1,0:T(8,128)(2,1)S(1)} %get-tuple-element.58), channel_id=1, source_target_pairs={{0,128},{8,136},{16,144},{24,152},{32,160},{40,168},{48,176},{56,1... | collective-permute-start | bytes 184328 | tf_op jit(solution)/shard_map/ppermute | solution.py:782
  90.3 22.8 %all-to-all-start.3 = ((bf16[16,32,128]{2,1,0:T(8,128)(2,1)}), bf16[16,32,128]{2,1,0:T(8,128)(2,1)S(1)}, u32[]{:S(2)}, u32[]{:S(2)}) async-start(bf16[16,32,128]{2,1,0:T(8,128)(2,1)} %cells.1), calls=%async_computation.3 | async-start | bytes 262144 | tf_op jit(solution)/shard_map/all_to_all | solution.py:816

commit v4 on v3

--- a/solution.py
+++ b/solution.py
@@ -28,7 +28,7 @@
 DP = 32
 X = 4
 CELLS = 16
-PIECE = 2 * T + REACH
+PIECE = T + REACH
 REST = CELLS + 2
 
 f32 = jnp.float32
@@ -84,6 +84,18 @@
     def alive(self, slot):
         return self.first < self.length(slot)
 
+    def seam(self, rows):
+        return jnp.where(self.x == 0, rows[:REACH, :], rows[T - REACH :, :]).astype(bf16)
+
+    def extended(self, ext, edge, pieces):
+        own = pieces[self.x, 0, :T, :].astype(f32)
+        before = pieces[jnp.maximum(self.x - 1, 0), 0, T - REACH : T, :].astype(f32)
+        after = pieces[jnp.minimum(self.x + 1, X - 1), 0, :REACH, :].astype(f32)
+        ext[:REACH, :] = jnp.where(self.x == 0, edge, before)
+        ext[REACH : REACH + T, :] = own
+        ext[REACH + T :, :] = jnp.where(self.x == X - 1, edge, after)
+        return own
+
     def mask(self, slot):
         ids = self.first + lax.broadcasted_iota(jnp.int32, (T, 1), 0)
         return ids < self.length(slot)
@@ -95,6 +107,10 @@
 
 def whole(*dims):
     return pl.BlockSpec(dims, lambda s: (0,) * len(dims))
+
+
+def all_x(rows):
+    return pl.BlockSpec((X, 1, rows, LANES), lambda s: (0, s, 0, 0))
 
 
 def once(*dims):
@@ -136,7 +152,7 @@
             pl.BlockSpec((far, NEAR, NEAR * LANES), lambda b: (0, b, 0)),
         ),
         scratch_shapes=[pltpu.VMEM((K * NEAR, LANES), f32)],
-        compiler_params=params(10),
+        compiler_params=params(56),
         cost_estimate=cost(0, 12 << 20),
         name="turn",
     )(pos)
@@ -152,8 +168,7 @@
     chan_ref,
     proj_ref,
     feat_ref,
-    tail_ref,
-    head_ref,
+    edge_ref,
     pair_ref,
     q_ref,
     slope_ref,
@@ -208,14 +223,15 @@
             )
             normed[rows, :] = (m * gain_two + shift_two).astype(bf16)
         projected = nt(normed[...], proj[...])
-        feat_ref[0] = jnp.where(place.mask(slot), projected, 0.0).astype(bf16)
+        features = jnp.where(place.mask(slot), projected, 0.0)
+        for copy in range(X):
+            feat_ref[copy, 0] = features.astype(bf16)
+        edge_ref[0] = place.seam(features)
 
     @pl.when(jnp.logical_not(living))
     def _():
         feat_ref[...] = jnp.zeros_like(feat_ref)
-
-    tail_ref[0] = feat_ref[0, T - REACH :, :]
-    head_ref[0] = feat_ref[0, :REACH, :]
+        edge_ref[...] = jnp.zeros_like(edge_ref)
 
 
 def encode(place, audio, conv_weight, channels, proj):
@@ -223,8 +239,7 @@
         encode_body,
         grid=(SLOTS,),
         out_shape=(
-            jax.ShapeDtypeStruct((SLOTS, T, LANES), bf16),
-            jax.ShapeDtypeStruct((SLOTS, REACH, LANES), bf16),
+            jax.ShapeDtypeStruct((X, SLOTS, T, LANES), bf16),
             jax.ShapeDtypeStruct((SLOTS, REACH, LANES), bf16),
             jax.ShapeDtypeStruct((SLOTS, T, 2 * C), bf16),
             jax.ShapeDtypeStruct((SLOTS, T, C), bf16),
@@ -240,8 +255,7 @@
             whole(GC, C),
         ],
         out_specs=(
-            by_slot(T, LANES),
-            by_slot(REACH, LANES),
+            all_x(T),
             by_slot(REACH, LANES),
             by_slot(T, 2 * C),
             by_slot(T, C),
@@ -255,16 +269,10 @@
             pltpu.VMEM((T, C), f32),
             pltpu.VMEM((T, C), bf16),
         ],
-        compiler_params=params(14),
+        compiler_params=params(56),
         cost_estimate=cost(2 * SLOTS * T * C * (2 * C + LANES), 8 << 20, SLOTS * T * C * 2),
         name="encode",
     )(*place, audio, conv_weight, channels, proj)
-
-
-def fill_ext(ext, low, own, high):
-    ext[:REACH, :] = low.astype(f32)
-    ext[REACH : REACH + T, :] = own.astype(f32)
-    ext[REACH + T :, :] = high.astype(f32)
 
 
 def fill_windows(windows, ext, first):
@@ -292,17 +300,14 @@
     len_ref,
     mov_ref,
     feat_ref,
-    low_ref,
-    high_ref,
+    edge_ref,
     weight,
     cot_ref,
     recv_ref,
     states_ref,
     sent_ref,
-    slopes_ref,
-    tail_ref,
-    head_ref,
     piece_ref,
+    seam_ref,
     ext,
     windows,
     turned,
@@ -314,8 +319,8 @@
 
     @pl.when(living)
     def _():
-        own = feat_ref[0]
-        fill_ext(ext, low_ref[0], own, high_ref[0])
+        edge = edge_ref[0].astype(f32)
+        own = place.extended(ext, edge, feat_ref)
         fill_windows(windows, ext, 0)
         fill_back(turned, place, slot, cot_ref, recv_ref)
         back = turned[...].T
@@ -326,46 +331,38 @@
         mixed = gathered(group)
         below = phi(mixed)
         mask = place.mask(slot)
-        states = jnp.where(mask, own.astype(f32) + mixed * below, 0.0)
+        states = jnp.where(mask, own + mixed * below, 0.0)
         states_ref[0] = states.T[:GC, :].astype(bf16)
         slopes = jnp.where(mask, back * (below + mixed * bell(mixed)), 0.0)
-        slopes_ref[0] = slopes.astype(bf16)
-        edge = jnp.where(place.x < X // 2, low_ref[0].astype(f32), high_ref[0].astype(f32))
         for copy in range(X):
-            piece_ref[copy, 0, :T, :] = own
-            piece_ref[copy, 0, T : T + REACH, :] = edge.astype(bf16)
-            piece_ref[copy, 0, T + REACH :, :] = slopes.astype(bf16)
+            piece_ref[copy, 0, :T, :] = slopes.astype(bf16)
+            piece_ref[copy, 0, T:, :] = edge.astype(bf16)
+        seam_ref[0] = place.seam(slopes)
 
     @pl.when(jnp.logical_not(living))
     def _():
         states_ref[...] = jnp.zeros_like(states_ref)
-        slopes_ref[...] = jnp.zeros_like(slopes_ref)
         piece_ref[...] = jnp.zeros_like(piece_ref)
+        seam_ref[...] = jnp.zeros_like(seam_ref)
 
     @pl.when(place.chosen == slot)
     def _():
         sent_ref[...] = states_ref[0]
 
-    tail_ref[0] = slopes_ref[0, T - REACH :, :]
-    head_ref[0] = slopes_ref[0, :REACH, :]
-
-
-def mix(place, features, low, high, weight, cotangent, received):
+
+def mix(place, features, edge, weight, cotangent, received):
     return pl.pallas_call(
         mix_body,
         grid=(SLOTS,),
         out_shape=(
             jax.ShapeDtypeStruct((SLOTS, GC, T), bf16),
             jax.ShapeDtypeStruct((GC, T), bf16),
-            jax.ShapeDtypeStruct((SLOTS, T, LANES), bf16),
+            jax.ShapeDtypeStruct((X, SLOTS, PIECE, LANES), bf16),
             jax.ShapeDtypeStruct((SLOTS, REACH, LANES), bf16),
-            jax.ShapeDtypeStruct((SLOTS, REACH, LANES), bf16),
-            jax.ShapeDtypeStruct((X, SLOTS, PIECE, LANES), bf16),
         ),
         in_specs=[SMEM] * 3
         + [
-            by_slot(T, LANES),
-            by_slot(REACH, LANES),
+            all_x(T),
             by_slot(REACH, LANES),
             once(*weight.shape),
             by_slot(GC, T),
@@ -374,24 +371,22 @@
         out_specs=(
             by_slot(GC, T),
             whole(GC, T),
-            by_slot(T, LANES),
+            all_x(PIECE),
             by_slot(REACH, LANES),
-            by_slot(REACH, LANES),
-            pl.BlockSpec((X, 1, PIECE, LANES), lambda s: (0, s, 0, 0)),
         ),
         scratch_shapes=[
             pltpu.VMEM((EXT, LANES), f32),
             pltpu.VMEM((T + NEAR * (K // NEAR - 1), NEAR * LANES), bf16),
             pltpu.VMEM((LANES, T), f32),
         ],
-        compiler_params=params(20),
+        compiler_params=params(56),
         cost_estimate=cost(2 * SLOTS * SPAN * K * LANES * LANES, 7 << 20, SLOTS * T * LANES * 2),
         name="mix",
-    )(*place, features, low, high, weight, cotangent, received)
+    )(*place, features, edge, weight, cotangent, received)
 
 
 def taps_body(
-    scale, dev_ref, len_ref, mov_ref, piece_ref, keep_ref, send_ref, ext, windows, turned, sums
+    scale, dev_ref, len_ref, mov_ref, feat_ref, piece_ref, keep_ref, send_ref, ext, windows, turned, sums
 ):
     place = Place(dev_ref, len_ref, mov_ref)
     slot = pl.program_id(0)
@@ -404,12 +399,12 @@
 
     @pl.when(place.y * spread < place.length(slot))
     def _():
-        ext[:REACH, :] = piece_ref[0, 0, T : T + REACH, :].astype(f32)
-        ext[REACH + spread :, :] = piece_ref[X - 1, 0, T : T + REACH, :].astype(f32)
+        ext[:REACH, :] = piece_ref[0, 0, T:, :].astype(f32)
+        ext[REACH + spread :, :] = piece_ref[X - 1, 0, T:, :].astype(f32)
         for x in range(X):
-            ext[REACH + x * T : REACH + (x + 1) * T, :] = piece_ref[x, 0, :T, :].astype(f32)
+            ext[REACH + x * T : REACH + (x + 1) * T, :] = feat_ref[x, 0].astype(f32)
             turned[:, x * T : (x + 1) * T] = (
-                piece_ref[x, 0, T + REACH :, :].astype(f32).T.astype(bf16)
+                piece_ref[x, 0, :T, :].astype(f32).T.astype(bf16)
             )
         for j in range(4):
             windows[:, j * LANES : (j + 1) * LANES] = ext[
@@ -428,18 +423,18 @@
                 keep = jnp.where(first_core, even, odd).astype(bf16)
                 send = jnp.where(first_core, odd, even).astype(bf16)
                 for y in range(2):
-                    keep_ref[2 * (2 * q + far) + y] = keep[y * REACH : (y + 1) * REACH, :]
-                    send_ref[2 * (2 * q + far) + y] = send[y * REACH : (y + 1) * REACH, :]
-
-
-def taps(scale, place, pieces):
-    shape = jax.ShapeDtypeStruct((2 * CELLS, REACH, LANES), bf16)
+                    keep_ref[y, 2 * q + far] = keep[y * REACH : (y + 1) * REACH, :]
+                    send_ref[y, 2 * q + far] = send[y * REACH : (y + 1) * REACH, :]
+
+
+def taps(scale, place, features, pieces):
+    shape = jax.ShapeDtypeStruct((2, CELLS, REACH, LANES), bf16)
     spread = X * T
     return pl.pallas_call(
         functools.partial(taps_body, scale),
         grid=(SLOTS,),
         out_shape=(shape, shape),
-        in_specs=[SMEM] * 3 + [pl.BlockSpec((X, 1, PIECE, LANES), lambda s: (0, s, 0, 0))],
+        in_specs=[SMEM] * 3 + [all_x(T), all_x(PIECE)],
         out_specs=(whole(*shape.shape), whole(*shape.shape)),
         scratch_shapes=[
             pltpu.VMEM((spread + 2 * REACH, LANES), f32),
@@ -450,7 +445,7 @@
         compiler_params=params(16),
         cost_estimate=cost(2 * SLOTS * SPAN * K * LANES * LANES, 4 << 20),
         name="taps",
-    )(*place, pieces)
+    )(*place, features, pieces)
 
 
 def backward_body(
@@ -458,9 +453,8 @@
     dev_ref,
     len_ref,
     mov_ref,
-    slopes_ref,
-    low_ref,
-    high_ref,
+    piece_ref,
+    edge_ref,
     cot_ref,
     recv_ref,
     weight,
@@ -503,7 +497,7 @@
 
     @pl.when(living)
     def _():
-        fill_ext(ext, low_ref[0], slopes_ref[0], high_ref[0])
+        place.extended(ext, edge_ref[0].astype(f32), piece_ref)
         fill_windows(windows, ext, 1)
         fill_back(turned, place, slot, cot_ref, recv_ref)
         group = jnp.zeros((SPAN, span), f32)
@@ -591,7 +585,7 @@
 
 
 def backward(
-    scale, place, slopes, low, high, cotangent, received, weight, stored, conv_weight, channels, proj
+    scale, place, pieces, edge, cotangent, received, weight, stored, conv_weight, channels, proj
 ):
     shape = jax.ShapeDtypeStruct((MP, REST, 16, LANES), bf16)
     return pl.pallas_call(
@@ -600,8 +594,7 @@
         out_shape=(jax.ShapeDtypeStruct((SLOTS, 2 * T, C), bf16), shape, shape),
         in_specs=[SMEM] * 3
         + [
-            by_slot(T, LANES),
-            by_slot(REACH, LANES),
+            all_x(PIECE),
             by_slot(REACH, LANES),
             by_slot(GC, T),
             by_slot(GC, T),
@@ -630,16 +623,15 @@
             pltpu.VMEM((40, C), f32),
             pltpu.VMEM((LANES, C), f32),
         ],
-        compiler_params=params(30),
+        compiler_params=params(56),
         cost_estimate=cost(
             2 * SLOTS * (SPAN * K * LANES * LANES + T * C * (4 * C + 2 * LANES)), 14 << 20
         ),
         name="backward",
     )(
         *place,
-        slopes,
-        low,
-        high,
+        pieces,
+        edge,
         cotangent,
         received,
         weight,
@@ -650,48 +642,48 @@
     )
 
 
-def cells_body(dev_ref, rest_ref, out_ref):
+def cells_body(dev_ref, kept_ref, recv_ref, rest_ref, out_ref):
     model = lax.rem(dev_ref[0], MP)
+    out_ref[:, :REACH, :] = (kept_ref[...].astype(f32) + recv_ref[...].astype(f32)).astype(bf16)
     rest = rest_ref[0].astype(f32)
     for n in range(1, MP):
         rest += rest_ref[n].astype(f32)
-    out_ref[:, :16, :] = rest[:CELLS].astype(bf16)
+    out_ref[:, REACH : REACH + 16, :] = rest[:CELLS].astype(bf16)
     for cell in range(CELLS):
         small = jnp.where(model == cell // 2, rest[CELLS + cell % 2], 0.0)
-        out_ref[cell, 16:, :] = small.astype(bf16)
-
-
-def make_cells(dev, rest):
+        out_ref[cell, REACH + 16 :, :] = small.astype(bf16)
+
+
+def make_cells(dev, kept, received, rest):
     return pl.pallas_call(
         cells_body,
-        out_shape=jax.ShapeDtypeStruct((CELLS, 32, LANES), bf16),
-        in_specs=[SMEM, VMEM],
+        out_shape=jax.ShapeDtypeStruct((CELLS, REACH + 32, LANES), bf16),
+        in_specs=[SMEM] + [VMEM] * 3,
         out_specs=VMEM,
-        compiler_params=params(8),
-        cost_estimate=cost(0, 1 << 20),
+        compiler_params=params(10),
+        cost_estimate=cost(0, 2 << 20),
         name="cells",
-    )(dev, rest)
-
-
-def total_body(pos_ref, rest_ref, out_ref):
-    for at, parts_ref in ((0, pos_ref), (REACH, rest_ref)):
-        total = parts_ref[0].astype(f32)
-        for n in range(1, parts_ref.shape[0]):
-            total += parts_ref[n].astype(f32)
-        for copy in range(MP):
-            out_ref[copy, at : at + total.shape[0], :] = total.astype(bf16)
-
-
-def total(pos, rest):
+    )(dev, kept, received, rest)
+
+
+def total_body(in_ref, out_ref):
+    total = in_ref[0].astype(f32)
+    for n in range(1, in_ref.shape[0]):
+        total += in_ref[n].astype(f32)
+    for copy in range(MP):
+        out_ref[copy] = total.astype(bf16)
+
+
+def total(parts):
     return pl.pallas_call(
         total_body,
-        out_shape=jax.ShapeDtypeStruct((MP, REACH + 32, LANES), bf16),
-        in_specs=[VMEM] * 2,
+        out_shape=jax.ShapeDtypeStruct((MP,) + parts.shape[1:], bf16),
+        in_specs=[VMEM],
         out_specs=VMEM,
-        compiler_params=params(8),
-        cost_estimate=cost(0, 2 << 20),
+        compiler_params=params(10),
+        cost_estimate=cost(0, 2 * parts.size),
         name="total",
-    )(pos, rest)
+    )(parts)
 
 
 def finish_body(
@@ -743,13 +735,6 @@
     )(*place, cells, states, other)
 
 
-def neighbours(tail, head):
-    count = lax.axis_size("mp")
-    forward = [(i, i + 1) for i in range(count - 1)]
-    backward_route = [(i + 1, i) for i in range(count - 1)]
-    return lax.ppermute(tail, "mp", forward), lax.ppermute(head, "mp", backward_route)
-
-
 def added(a, b):
     return (a.astype(f32) + b.astype(f32)).astype(bf16)
 
@@ -768,24 +753,29 @@
     proj = proj_weight.T
     cot = cotangent.transpose(0, 2, 1)
 
+    rows = [list(range(X)), list(range(X, 2 * X))]
+    seam = [(X - 1, X), (X, X - 1)]
+
+    def over_x(copies):
+        return lax.all_to_all(copies, "mp", 0, 0, axis_index_groups=rows, tiled=True)
+
     received = lax.ppermute(cot, "dp", swap)
-    features, tail, head, *stored = encode(place, audio, conv_weight, channels, proj)
-    low, high = neighbours(tail, head)
+    features, edge, *stored = encode(place, audio, conv_weight, channels, proj)
+    features = over_x(features)
+    edge = lax.ppermute(edge, "mp", seam)
     ahead, behind = turn(pos_weight.transpose(1, 2, 0))
-    states, sent, slopes, tail, head, pieces = mix(
-        place, features, low, high, ahead, cot, received
-    )
-    slope_low, slope_high = neighbours(tail, head)
-    pieces, slope_low, slope_high = lax.optimization_barrier((pieces, slope_low, slope_high))
-    rows = [list(range(X)), list(range(X, 2 * X))]
-    pieces = lax.all_to_all(pieces, "mp", 0, 0, axis_index_groups=rows, tiled=True)
+    states, sent, pieces, edge = mix(place, features, edge, ahead, cot, received)
+    pieces = over_x(pieces)
+    edge = lax.ppermute(edge, "mp", seam)
     other = lax.ppermute(sent, "dp", swap)
+    pos_keep, pos_send = taps(scale, place, features, pieces)
+    pos_send, edge = lax.optimization_barrier((pos_send, edge))
+    pos_recv = lax.ppermute(pos_send, "dp", core_swap)
     audio_grad, keep, send = backward(
         scale,
         place,
-        slopes,
-        slope_low,
-        slope_high,
+        pieces,
+        edge,
         cot,
         received,
         behind,
@@ -795,28 +785,17 @@
         proj,
     )
     rest = added(keep, lax.ppermute(send, "dp", core_swap))
-    pos_keep, pos_send = taps(scale, place, pieces)
     rest = lax.all_to_all(rest, "mp", 0, 0, tiled=True)
-    pos_sum = added(pos_keep, lax.ppermute(pos_send, "dp", core_swap))
-    links = [
-        [MP * (2 * cell + core) + X * y + x for cell in range(CELLS) for y in range(2)]
-        for core in range(2)
-        for x in range(X)
-    ]
-    pos_sum = lax.all_to_all(
-        pos_sum,
-        ("dp", "mp"),
-        0,
-        0,
-        axis_index_groups=links,
-        tiled=True,
-    )
+    pos_sum = added(pos_keep, pos_recv)
+    low_half = model_index < X
+    kept = jnp.where(low_half, pos_sum[0], pos_sum[1])
+    leaving = jnp.where(low_half, pos_sum[1], pos_sum[0])
+    coming = lax.ppermute(leaving, "mp", [(i, i ^ X) for i in range(MP)])
     rest, other = lax.optimization_barrier((rest, other))
+    cells = make_cells(dev, kept, coming, rest)
     groups = [list(range(bit, DP, 2)) for bit in range(2)]
-    rest = lax.all_to_all(
-        make_cells(dev, rest), "dp", 0, 0, axis_index_groups=groups, tiled=True
-    )
-    cells = lax.all_to_all(total(pos_sum, rest), "mp", 0, 0, tiled=True)
+    cells = lax.all_to_all(cells, "dp", 0, 0, axis_index_groups=groups, tiled=True)
+    cells = lax.all_to_all(total(cells), "mp", 0, 0, tiled=True)
     hidden, grad_pos, grad_conv, grad_proj, grad_channels = finish(place, cells, states, other)
     return (
         hidden.transpose(0, 2, 1),

time: 145 us -> 124 us (0.86); the launches traced: 144 us -> 124 us
  starting transfers between devices: 52.6 us -> 23.5 us
  local copies, waits for them, and re-layouts: 21.7 us -> 2.49 us
  Pallas kernels: 21.4 us -> 37.5 us
  waiting for transfers between devices: 14.8 us -> 24.2 us
  blocking collectives: 29.2 us -> 33.6 us
    unnamed x54 -> x24, local copies, waits for them, and re-layouts: 21.7 us -> 2.49 us
    all_to_all x2, starting transfers between devices: 19.2 us -> 9.3 us  [over_x(): lax.all_to_all(copies, 'mp', 0, 0, axis_index_groups=rows, tiled=True)]
    ppermute x5 -> x4, starting transfers between devices: 12.2 us -> 3.25 us  [the longest x1 1.55 us: per_device(): coming = lax.ppermute(leaving, 'mp', [(i, i ^ X) for i in range(MP)])]
    ppermute x1, starting transfers between devices: 7.47 us -> 0.01 us  [per_device(): other = lax.ppermute(sent, 'dp', swap)]
    pallas_call x1, Pallas kernels: 5.1 us -> 10.8 us  [backward(): pl.pallas_call(functools.partial(backward_body, scale), grid=(SLOTS,), ou...]
    ppermute x1, waiting for transfers between devices: 3.05 us -> 8.17 us  [per_device(): other = lax.ppermute(sent, 'dp', swap)]
    all_to_all x2, blocking collectives: 29.2 us -> 33.6 us  [the longest x1 22.5 us: per_device(): lax.all_to_all(cells, 'dp', 0, 0, axis_index_groups=groups, tiled=True)]
    pallas_call x1, Pallas kernels: 4.93 us -> 9.1 us  [turn(): pl.pallas_call(turn_body, grid=(LANES // NEAR,), out_shape=(jax.ShapeDtyp...]
  transfers between devices with their start and end apart: 11 -> 10, of which waited for: 3 -> 5; matrix products, arithmetic and copies ran while one was open for 2% -> 2% of each run, Pallas kernels for 12% -> 10%
where the time goes in v4:
time: 124 us
  Pallas kernels  37.5 us (30%)
  blocking collectives  33.6 us (27%)
  waiting for transfers between devices  24.2 us (20%)
  starting transfers between devices  23.5 us (19%)
  local copies, waits for them, and re-layouts  2.49 us (2%)
  other arithmetic  2.25 us (2%)
    all_to_all x1, blocking collectives, per_device(): lax.all_to_all(cells, 'dp', 0, 0, axis_index_groups=groups, tiled=True)  22.5 us
    all_to_all x1, blocking collectives, per_device(): cells = lax.all_to_all(total(cells), 'mp', 0, 0, tiled=True)  11.1 us
    pallas_call x1, Pallas kernels, backward(): pl.pallas_call(functools.partial(backward_body, scale), grid=(SLOTS,), ou...  10.8 us
    all_to_all x2, waiting for transfers between devices, over_x(): lax.all_to_all(copies, 'mp', 0, 0, axis_index_groups=rows, tiled=True)  9.98 us
    all_to_all x2, starting transfers between devices, over_x(): lax.all_to_all(copies, 'mp', 0, 0, axis_index_groups=rows, tiled=True)  9.3 us
    pallas_call x1, Pallas kernels, turn(): pl.pallas_call(turn_body, grid=(LANES // NEAR,), out_shape=(jax.ShapeDtyp...  9.1 us
    ppermute x1, waiting for transfers between devices, per_device(): other = lax.ppermute(sent, 'dp', swap)  8.17 us
    pallas_call x1, Pallas kernels, mix(): pl.pallas_call(mix_body, grid=(SLOTS,), out_shape=(jax.ShapeDtypeStruct((...  6.47 us
  transfers between devices with their start and end apart: 10, of which 5 were waited for; matrix products, arithmetic and copies ran while one was open for 2% of the time, Pallas kernels for 10%

profile of v4, /device:TPU:2, one launch (start us, length us, event | category | flops | bytes accessed | tf_op | source)
XLA Modules:
  0.0 124.2 jit_solution(10903266467271967509)
XLA Ops:
  0.6 5.6 %encode.1 = (bf16[4,2,256,128]{3,2,1,0:T(8,128)(2,1)}, bf16[2,64,128]{2,1,0:T(8,128)(2,1)}, bf16[2,256,1024]{2,1,0:T(8,128)(2,1)}, bf16[2,256,512]{2,1,0:T(8,128...) custom-call(s32[1]{0:T(128)} %bitcast.dev_ref, s32[64]{0:T(128)} %len_ref.9, ...), custom_call_target="tpu_custom_call" | custom-call | flops 603979776 | bytes 8388608 | tf_op jit(solution)/shard_map/encode/pallas_call | solution.py:238
  6.2 5.7 %all-to-all-start = ((bf16[4,2,256,128]{3,2,1,0:T(8,128)(2,1)}), bf16[4,2,256,128]{3,2,1,0:T(8,128)(2,1)S(1)}, u32[]{:S(2)}, u32[]{:S(2)}) async-start(bf16[4,2,256,128]{3,2,1,0:T(8,128)(2,1)} %get-tuple-element.33), calls=%async_computation | async-start | bytes 1048576 | tf_op jit(solution)/shard_map/all_to_all | solution.py:760
  12.0 5.5 %collective-permute-start.1 = (bf16[2,120,256]{2,1,0:T(8,128)(2,1)}, bf16[2,120,256]{2,1,0:T(8,128)(2,1)S(1)}, u32[]{:S(2)}, u32[]{:S(2)}) collective-permute-start(bf16[2,120,256]{2,1,0:T(8,128)(2,1)} %bitcast.26), channel_id=1, source_target_pairs={{0,128},{8,136},{16,144},{24,152},{32,160},{40,168},{48,176},{56,1... | collective-permute-start | bytes 368648 | tf_op jit(solution)/shard_map/ppermute | solution.py:762
  17.4 0.7 collective-permute-start
  18.1 9.1 %turn.1 = (bf16[16,128,1024]{2,1,0:T(8,128)(2,1)}, bf16[8,128,2048]{2,1,0:T(8,128)(2,1)}) custom-call(bf16[120,120,128]{2,1,0:T(8,128)(2,1)} %bitcast.19), custom_call_target="tpu_custom_call" | custom-call | bytes 12582912 | tf_op jit(solution)/shard_map/turn/pallas_call | solution.py:142
  27.2 0.0 collective-permute-done.edge_ref
  27.2 0.0 copy-start.11
  27.2 0.0 collective-permute-done.1.recv_ref
  27.2 0.0 copy-start.8
  27.2 0.0 all-to-all-done.feat_ref
  27.2 0.0 copy-start.1
  27.2 0.6 copy-done.11
  27.8 0.1 copy-done.8
  27.8 0.2 copy-done.1
  28.0 0.0 copy-start.4
  28.0 0.0 copy-start.6
  28.0 6.5 %mix.1 = (bf16[2,120,256]{2,1,0:T(8,128)(2,1)}, bf16[120,256]{1,0:T(8,128)(2,1)}, bf16[4,2,320,128]{3,2,1,0:T(8,128)(2,1)}, bf16[2,64,128]{2,1,0:T(8,128)(2,1)}) custom-call(s32[1]{0:T(128)} %bitcast.dev_ref, s32[64]{0:T(128)} %len_ref.9, s32[16]{0:T(128)} %bitcast.15, bf16[4,2,256,128]{3,2,1,0:T(8,128)(2,1)} %copy-done.1, bf16[2,64,128]{2,1,0:T(8,128)(2,1)} %copy-done.11, ...), custom_call_target="tpu_custom_call" | custom-call | flops 2550136832 | bytes 7340032 | tf_op jit(solution)/shard_map/mix/pallas_call | solution.py:354
  34.5 3.6 %all-to-all-start.1 = ((bf16[4,2,320,128]{3,2,1,0:T(8,128)(2,1)}), bf16[4,2,320,128]{3,2,1,0:T(8,128)(2,1)S(1)}, u32[]{:S(2)}, u32[]{:S(2)}) async-start(bf16[4,2,320,128]{3,2,1,0:T(8,128)(2,1)} %get-tuple-element.36), calls=%async_computation.1 | async-start | bytes 1310720 | tf_op jit(solution)/shard_map/all_to_all | solution.py:760
  38.1 0.7 collective-permute-start.2
  38.8 10.0 %all-to-all-done.1.piece_ref = bf16[4,2,320,128]{3,2,1,0:T(8,128)(2,1)S(1)} async-done(((bf16[4,2,320,128]{3,2,1,0:T(8,128)(2,1)}), bf16[4,2,320,128]{3,2,1,0:T(8,128)(2,1)S(1)}, u32[]{:S(2)}, u32[]{:S(2)}) %all-to-all-start.1) | async-done | bytes 655392 | tf_op jit(solution)/shard_map/all_to_all | solution.py:760
  48.7 0.0 copy-done.4
  48.7 0.0 copy-done.6
  48.7 0.0 copy-start.2
  48.7 1.0 copy-done.2
  49.8 0.0 copy-start
  49.8 3.9 %taps.1 = (bf16[2,16,64,128]{3,2,1,0:T(8,128)(2,1)S(1)}, bf16[2,16,64,128]{3,2,1,0:T(8,128)(2,1)S(1)}) custom-call(s32[1]{0:T(128)} %bitcast.dev_ref, s32[64]{0:T(128)S(1)} %copy-done.4, s32[16]{0:T(128)S(1)} %bitcast.17, bf16[4,2,256,128]{3,2,1,0:T(8,128)(2,1)S(1)} %copy-done.2, bf16[4,2,320,128]{3,2,1,0:T(8,128)(2,1)S(1)} %all-to-all-done.1.piece_ref), custom_call_target="tpu_custom_call" | custom-call | flops 2550136832 | bytes 4194304 | tf_op jit(solution)/shard_map/taps/pallas_call | solution.py:433
  53.7 0.0 copy-done
  53.7 0.0 collective-permute-done.2.edge_ref
  53.7 0.0 copy-start.10
  53.7 0.6 copy-done.10
  54.3 10.8 %backward.1 = (bf16[2,512,512]{2,1,0:T(8,128)(2,1)}, bf16[8,18,16,128]{3,2,1,0:T(8,128)(2,1)}, bf16[8,18,16,128]{3,2,1,0:T(8,128)(2,1)}) custom-call(s32[1]{0:T(128)} %bitcast.dev_ref, s32[64]{0:T(128)} %len_ref.9, s32[16]{0:T(128)} %bitcast.16, bf16[4,2,320,128]{3,2,1,0:T(8,128)(2,1)} %copy-done, bf16[2,64,128]{2,1,0:T(8,128)(2,1)} %copy-done.10, ...), custom_call_target="tpu_custom_call" | custom-call | flops 3758096384 | bytes 14680064 | tf_op jit(solution)/shard_map/backward/pallas_call | solution.py:591
  65.1 0.0 copy-start.9
  65.2 0.2 collective-permute-start.5
  65.3 0.4 collective-permute-start.3
  65.7 1.7 %collective-permute-done.5 = bf16[8,18,16,128]{3,2,1,0:T(8,128)(2,1)S(1)} collective-permute-done((bf16[8,18,16,128]{3,2,1,0:T(8,128)(2,1)}, bf16[8,18,16,128]{3,2,1,0:T(8,128)(2,1)S(1)}, u32[]{:S(2)}, u32[]{:S(2)}) %collective-permute-start.5) | collective-permute-done | bytes 589856 | tf_op jit(solution)/shard_map/ppermute | solution.py:787
  67.5 2.0 %add_convert_fusion = bf16[8,18,16,128]{3,2,1,0:T(8,128)(2,1)} fusion(bf16[8,18,16,128]{3,2,1,0:T(8,128)(2,1)S(1)} %collective-permute-done.5, bf16[8,18,16,128]{3,2,1,0:T(8,128)(2,1)} %get-tuple-element.48), kind=kLoop, calls=%fused_computation | loop fusion | flops 1179648 | bytes 1769472 | tf_op jit(solution)/shard_map/convert_element_type | solution.py:739
  69.5 0.0 copy-start.3
  69.5 0.0 copy-start.5
  69.5 0.0 copy-start.7
  69.5 5.3 %all-to-all-start.2 = ((bf16[8,18,16,128]{3,2,1,0:T(8,128)(2,1)}), bf16[8,18,16,128]{3,2,1,0:T(8,128)(2,1)S(1)}, u32[]{:S(2)}, u32[]{:S(2)}) async-start(bf16[8,18,16,128]{3,2,1,0:T(8,128)(2,1)} %add_convert_fusion), calls=%async_computation.2 | async-start | bytes 1179648 | tf_op jit(solution)/shard_map/all_to_all | solution.py:788
  74.8 0.0 collective-permute-done.3
  74.8 0.2 add_convert_fusion.1
  75.0 1.6 %collective-permute-start.4 = (bf16[16,64,128]{2,1,0:T(8,128)(2,1)S(1)}, bf16[16,64,128]{2,1,0:T(8,128)(2,1)S(1)}, u32[]{:S(2)}, u32[]{:S(2)}) collective-permute-start(bf16[16,64,128]{2,1,0:T(8,128)(2,1)S(1)} %get-tuple-element.60), channel_id=1, source_target_pairs={{0,4},{1,5},{2,6},{3,7},{4,0},{5,1},{6,2},{7,3},{8,12},{9,13},{10,... | collective-permute-start | bytes 786440 | tf_op jit(solution)/shard_map/ppermute | solution.py:793
  76.6 0.0 copy-done.9
  76.6 0.0 collective-permute-start.6
  76.6 8.2 %collective-permute-done.6.other_ref = bf16[120,256]{1,0:T(8,128)(2,1)S(1)} collective-permute-done((bf16[120,256]{1,0:T(8,128)(2,1)S(1)}, bf16[120,256]{1,0:T(8,128)(2,1)S(1)}, u32[]{:S(2)}, u32[]{:S(2)}) %collective-permute-start.6) | collective-permute-done | bytes 61472 | tf_op jit(solution)/shard_map/ppermute | solution.py:770
  84.7 0.2 all-to-all-done.2.rest_ref
  85.0 4.1 %collective-permute-done.4.recv_ref = bf16[16,64,128]{2,1,0:T(8,128)(2,1)S(1)} collective-permute-done((bf16[16,64,128]{2,1,0:T(8,128)(2,1)S(1)}, bf16[16,64,128]{2,1,0:T(8,128)(2,1)S(1)}, u32[]{:S(2)}, u32[]{:S(2)}) %collective-permute-start.4) | collective-permute-done | bytes 262176 | tf_op jit(solution)/shard_map/ppermute | solution.py:793
  89.0 0.1 cells.1
  89.2 22.5 %all_to_all.25.in_ref = bf16[16,96,128]{2,1,0:T(8,128)(2,1)S(1)} all-to-all(bf16[16,96,128]{2,1,0:T(8,128)(2,1)S(1)} %cells.1), channel_id=1, replica_groups={{0,16,32,48,64,80,96,112,128,144,160,176,192,208,224,240},{8,24,40,56,7..., dimensions={0} | all-to-all | bytes 786432 | tf_op jit(solution)/shard_map/all_to_all | solution.py:797
  111.6 0.1 total.1
  111.7 11.1 %all_to_all.26.in_ref = bf16[8,96,128]{2,1,0:T(8,128)(2,1)S(1)} all-to-all(bf16[8,96,128]{2,1,0:T(8,128)(2,1)S(1)} %total.1), channel_id=1, replica_groups=mesh['dp'=32,'mp'=8] {'mp'}, dimensions={0} | all-to-all | bytes 393216 | tf_op jit(solution)/shard_map/all_to_all | solution.py:798
  122.8 0.0 copy-done.3
  122.8 0.0 copy-done.5
  122.8 0.0 copy-done.7
  122.8 1.4 %finish.1 = (bf16[2,120,256]{2,1,0:T(8,128)(2,1)}, f32[4,120,120]{2,1,0:T(8,128)}, f32[32,512]{1,0:T(8,128)}, f32[16,120]{1,0:T(8,128)}, f32[5,16]{1,0:T(8,128)}) custom-call(s32[1]{0:T(128)} %bitcast.dev_ref, s32[64]{0:T(128)S(1)} %copy-done.5, s32[16]{0:T(128)S(1)} %bitcast.18, bf16[8,96,128]{2,1,0:T(8,128)(2,1)S(1)} %all_to_all.26.in_ref, ...), custom_call_target="tpu_custom_call" | custom-call | tf_op jit(solution)/shard_map/finish/pallas_call | solution.py:722
  (1 shorter events, 0.0 us)
Async XLA Ops:
  6.2 21.0 %all-to-all-start = ((bf16[4,2,256,128]{3,2,1,0:T(8,128)(2,1)}), bf16[4,2,256,128]{3,2,1,0:T(8,128)(2,1)S(1)}, u32[]{:S(2)}, u32[]{:S(2)}) async-start(bf16[4,2,256,128]{3,2,1,0:T(8,128)(2,1)} %get-tuple-element.33), calls=%async_computation | async-start | bytes 1048576 | tf_op jit(solution)/shard_map/all_to_all | solution.py:760
  12.0 15.2 %collective-permute-start.1 = (bf16[2,120,256]{2,1,0:T(8,128)(2,1)}, bf16[2,120,256]{2,1,0:T(8,128)(2,1)S(1)}, u32[]{:S(2)}, u32[]{:S(2)}) collective-permute-start(bf16[2,120,256]{2,1,0:T(8,128)(2,1)} %bitcast.26), channel_id=1, source_target_pairs={{0,128},{8,136},{16,144},{24,152},{32,160},{40,168},{48,176},{56,1... | collective-permute-start | bytes 368648 | tf_op jit(solution)/shard_map/ppermute | solution.py:762
  17.4 9.8 %collective-permute-start = (bf16[2,64,128]{2,1,0:T(8,128)(2,1)}, bf16[2,64,128]{2,1,0:T(8,128)(2,1)S(1)}, u32[]{:S(2)}, u32[]{:S(2)}) collective-permute-start(bf16[2,64,128]{2,1,0:T(8,128)(2,1)} %get-tuple-element.34), channel_id=1, source_target_pairs={{3,4},{4,3},{11,12},{12,11},{19,20},{20,19},{27,28},{28,27},{35,36... | collective-permute-start | bytes 98312 | tf_op jit(solution)/shard_map/ppermute | solution.py:765
  27.2 0.6 copy-start.11
  27.2 0.7 copy-start.8
  27.2 0.8 copy-start.1
  28.0 20.7 %copy-start.4 = (s32[64]{0:T(128)S(1)}, s32[64]{0:T(128)}, u32[]{:S(2)}) copy-start(s32[64]{0:T(128)} %len_ref.9) | copy-start | bytes 772
  28.0 20.7 %copy-start.6 = (s32[16,1]{0,1:T(1,128)S(1)}, s32[16,1]{0,1:T(1,128)}, u32[]{:S(2)}) copy-start(s32[16,1]{0,1:T(1,128)} %param.10) | copy-start | bytes 196
  34.5 14.2 %all-to-all-start.1 = ((bf16[4,2,320,128]{3,2,1,0:T(8,128)(2,1)}), bf16[4,2,320,128]{3,2,1,0:T(8,128)(2,1)S(1)}, u32[]{:S(2)}, u32[]{:S(2)}) async-start(bf16[4,2,320,128]{3,2,1,0:T(8,128)(2,1)} %get-tuple-element.36), calls=%async_computation.1 | async-start | bytes 1310720 | tf_op jit(solution)/shard_map/all_to_all | solution.py:760
  38.1 15.6 %collective-permute-start.2 = (bf16[2,64,128]{2,1,0:T(8,128)(2,1)}, bf16[2,64,128]{2,1,0:T(8,128)(2,1)S(1)}, u32[]{:S(2)}, u32[]{:S(2)}) collective-permute-start(bf16[2,64,128]{2,1,0:T(8,128)(2,1)} %get-tuple-element.39), channel_id=1, source_target_pairs={{3,4},{4,3},{11,12},{12,11},{19,20},{20,19},{27,28},{28,27},{35,36... | collective-permute-start | bytes 98312 | tf_op jit(solution)/shard_map/ppermute | solution.py:769
  48.7 1.0 copy-start.2
  49.8 3.9 %copy-start = (bf16[4,2,320,128]{3,2,1,0:T(8,128)(2,1)}, bf16[4,2,320,128]{3,2,1,0:T(8,128)(2,1)S(1)}, u32[]{:S(2)}) copy-start(bf16[4,2,320,128]{3,2,1,0:T(8,128)(2,1)S(1)} %all-to-all-done.1.piece_ref) | copy-start | bytes 1966084
  53.7 0.6 copy-start.10
  65.1 11.4 %copy-start.9 = (bf16[120,256]{1,0:T(8,128)(2,1)S(1)}, bf16[120,256]{1,0:T(8,128)(2,1)}, u32[]{:S(2)}) copy-start(bf16[120,256]{1,0:T(8,128)(2,1)} %get-tuple-element.50) | copy-start | bytes 184324
  65.2 2.3 %collective-permute-start.5 = (bf16[8,18,16,128]{3,2,1,0:T(8,128)(2,1)}, bf16[8,18,16,128]{3,2,1,0:T(8,128)(2,1)S(1)}, u32[]{:S(2)}, u32[]{:S(2)}) collective-permute-start(bf16[8,18,16,128]{3,2,1,0:T(8,128)(2,1)} %get-tuple-element.49), channel_id=1, source_target_pairs={{0,8},{8,0},{16,24},{24,16},{32,40},{40,32},{48,56},{56,48},{64,72... | collective-permute-start | bytes 1769480 | tf_op jit(solution)/shard_map/ppermute | solution.py:787
  65.3 9.4 %collective-permute-start.3 = (bf16[2,16,64,128]{3,2,1,0:T(8,128)(2,1)S(1)}, bf16[2,16,64,128]{3,2,1,0:T(8,128)(2,1)S(1)}, u32[]{:S(2)}, u32[]{:S(2)}) collective-permute-start(bf16[2,16,64,128]{3,2,1,0:T(8,128)(2,1)S(1)} %get-tuple-element.40), channel_id=1, source_target_pairs={{0,8},{8,0},{16,24},{24,16},{32,40},{40,32},{48,56},{56,48},{64,72... | collective-permute-start | bytes 1572872 | tf_op jit(solution)/shard_map/ppermute | solution.py:773
  69.5 53.3 %copy-start.3 = (bf16[2,120,256]{2,1,0:T(8,128)(2,1)S(1)}, bf16[2,120,256]{2,1,0:T(8,128)(2,1)}, u32[]{:S(2)}) copy-start(bf16[2,120,256]{2,1,0:T(8,128)(2,1)} %get-tuple-element.52.states_ref) | copy-start | bytes 368644
  69.5 53.3 %copy-start.5 = (s32[64]{0:T(128)S(1)}, s32[64]{0:T(128)}, u32[]{:S(2)}) copy-start(s32[64]{0:T(128)} %len_ref.9) | copy-start | bytes 772
  69.5 53.3 %copy-start.7 = (s32[16,1]{0,1:T(1,128)S(1)}, s32[16,1]{0,1:T(1,128)}, u32[]{:S(2)}) copy-start(s32[16,1]{0,1:T(1,128)} %param.10) | copy-start | bytes 196
  69.5 15.5 %all-to-all-start.2 = ((bf16[8,18,16,128]{3,2,1,0:T(8,128)(2,1)}), bf16[8,18,16,128]{3,2,1,0:T(8,128)(2,1)S(1)}, u32[]{:S(2)}, u32[]{:S(2)}) async-start(bf16[8,18,16,128]{3,2,1,0:T(8,128)(2,1)} %add_convert_fusion), calls=%async_computation.2 | async-start | bytes 1179648 | tf_op jit(solution)/shard_map/all_to_all | solution.py:788
  75.0 14.0 %collective-permute-start.4 = (bf16[16,64,128]{2,1,0:T(8,128)(2,1)S(1)}, bf16[16,64,128]{2,1,0:T(8,128)(2,1)S(1)}, u32[]{:S(2)}, u32[]{:S(2)}) collective-permute-start(bf16[16,64,128]{2,1,0:T(8,128)(2,1)S(1)} %get-tuple-element.60), channel_id=1, source_target_pairs={{0,4},{1,5},{2,6},{3,7},{4,0},{5,1},{6,2},{7,3},{8,12},{9,13},{10,... | collective-permute-start | bytes 786440 | tf_op jit(solution)/shard_map/ppermute | solution.py:793
  76.6 8.2 %collective-permute-start.6 = (bf16[120,256]{1,0:T(8,128)(2,1)S(1)}, bf16[120,256]{1,0:T(8,128)(2,1)S(1)}, u32[]{:S(2)}, u32[]{:S(2)}) collective-permute-start(bf16[120,256]{1,0:T(8,128)(2,1)S(1)} %copy-done.9), channel_id=1, source_target_pairs={{0,128},{8,136},{16,144},{24,152},{32,160},{40,168},{48,176},{56,1... | collective-permute-start | bytes 184328 | tf_op jit(solution)/shard_map/ppermute | solution.py:770

commit v5 on v4

--- a/solution.py
+++ b/solution.py
@@ -29,7 +29,10 @@
 X = 4
 CELLS = 16
 PIECE = T + REACH
-REST = CELLS + 2
+HALF = GC // 2
+SPARE = REACH - HALF
+CONV_ROWS = CELLS * 32
+REST = CONV_ROWS + CELLS * SPARE
 
 f32 = jnp.float32
 bf16 = jnp.bfloat16
@@ -117,7 +120,7 @@
     return pl.BlockSpec(dims, lambda s: (0,) * len(dims), pipeline_mode=pl.Buffered(1))
 
 
-def turn_body(in_ref, ahead_ref, behind_ref, rows):
+def turn_body(in_ref, ahead_ref, rows):
     block = pl.program_id(0)
     blocks = pl.num_programs(0)
     for n in range(NEAR):
@@ -131,32 +134,44 @@
     for q in range(far):
         for r in range(NEAR):
             at = (q * NEAR + r) * NEAR
-            tile = rows[at : at + NEAR, :].astype(bf16)
-            ahead_ref[r, :, q * LANES : (q + 1) * LANES] = tile
-            r_back = NEAR - 1 - r
-            behind_ref[far - 1 - q, :, r_back * LANES : (r_back + 1) * LANES] = tile
+            ahead_ref[r, :, q * LANES : (q + 1) * LANES] = rows[at : at + NEAR, :].astype(bf16)
 
 
 def turn(pos):
     far = K // NEAR
-    ahead, behind = pl.pallas_call(
+    ahead = pl.pallas_call(
         turn_body,
         grid=(LANES // NEAR,),
-        out_shape=(
-            jax.ShapeDtypeStruct((NEAR, LANES, far * LANES), bf16),
-            jax.ShapeDtypeStruct((far, LANES, NEAR * LANES), bf16),
-        ),
+        out_shape=jax.ShapeDtypeStruct((NEAR, LANES, far * LANES), bf16),
         in_specs=[pl.BlockSpec((NEAR, GC, K), lambda b: (b, 0, 0))],
-        out_specs=(
-            pl.BlockSpec((NEAR, NEAR, far * LANES), lambda b: (0, b, 0)),
-            pl.BlockSpec((far, NEAR, NEAR * LANES), lambda b: (0, b, 0)),
-        ),
+        out_specs=pl.BlockSpec((NEAR, NEAR, far * LANES), lambda b: (0, b, 0)),
         scratch_shapes=[pltpu.VMEM((K * NEAR, LANES), f32)],
-        compiler_params=params(56),
-        cost_estimate=cost(0, 12 << 20),
+        compiler_params=params(10),
+        cost_estimate=cost(0, 8 << 20),
         name="turn",
     )(pos)
-    return ahead.reshape(NEAR * LANES, -1), behind.reshape(far * LANES, -1)
+    return ahead.reshape(NEAR * LANES, -1)
+
+
+def flip_body(in_ref, out_ref):
+    for r in range(NEAR):
+        out_ref[:, r * LANES : (r + 1) * LANES] = in_ref[
+            (NEAR - 1 - r) * LANES : (NEAR - r) * LANES, :
+        ]
+
+
+def flip(ahead):
+    far = K // NEAR
+    return pl.pallas_call(
+        flip_body,
+        grid=(far,),
+        out_shape=jax.ShapeDtypeStruct((far * LANES, NEAR * LANES), bf16),
+        in_specs=[pl.BlockSpec((NEAR * LANES, LANES), lambda q: (0, far - 1 - q))],
+        out_specs=pl.BlockSpec((LANES, NEAR * LANES), lambda q: (q, 0)),
+        compiler_params=params(8),
+        cost_estimate=cost(0, 8 << 20),
+        name="flip",
+    )(ahead)
 
 
 def encode_body(
@@ -379,14 +394,14 @@
             pltpu.VMEM((T + NEAR * (K // NEAR - 1), NEAR * LANES), bf16),
             pltpu.VMEM((LANES, T), f32),
         ],
-        compiler_params=params(56),
+        compiler_params=params(20),
         cost_estimate=cost(2 * SLOTS * SPAN * K * LANES * LANES, 7 << 20, SLOTS * T * LANES * 2),
         name="mix",
     )(*place, features, edge, weight, cotangent, received)
 
 
 def taps_body(
-    scale, dev_ref, len_ref, mov_ref, feat_ref, piece_ref, keep_ref, send_ref, ext, windows, turned, sums
+    scale, dev_ref, len_ref, mov_ref, feat_ref, piece_ref, own_ref, core_ref, low_ref, both_ref, ext, windows, turned, sums
 ):
     place = Place(dev_ref, len_ref, mov_ref)
     slot = pl.program_id(0)
@@ -416,26 +431,30 @@
     @pl.when(slot == SLOTS - 1)
     def _():
         first_core = place.core == 0
+        first_half = place.y == 0
         for q in range(K // NEAR):
             for far in range(2):
-                even = sums[q, :, (2 * far) * LANES : (2 * far + 1) * LANES] * scale
-                odd = sums[q, :, (2 * far + 1) * LANES : (2 * far + 2) * LANES] * scale
-                keep = jnp.where(first_core, even, odd).astype(bf16)
-                send = jnp.where(first_core, odd, even).astype(bf16)
-                for y in range(2):
-                    keep_ref[y, 2 * q + far] = keep[y * REACH : (y + 1) * REACH, :]
-                    send_ref[y, 2 * q + far] = send[y * REACH : (y + 1) * REACH, :]
+                at = 2 * far * LANES
+                even = sums[q, :, at : at + LANES] * scale
+                odd = sums[q, :, at + LANES : at + 2 * LANES] * scale
+                keep = jnp.where(first_core, even, odd)
+                send = jnp.where(first_core, odd, even)
+                cell = 2 * q + far
+                for mine, other, rows in ((own_ref, low_ref, keep), (core_ref, both_ref, send)):
+                    one, two = rows[:REACH, :], rows[HALF : HALF + REACH, :]
+                    mine[cell] = jnp.where(first_half, one, two).astype(bf16)
+                    other[cell] = jnp.where(first_half, two, one).astype(bf16)
 
 
 def taps(scale, place, features, pieces):
-    shape = jax.ShapeDtypeStruct((2, CELLS, REACH, LANES), bf16)
+    shape = jax.ShapeDtypeStruct((CELLS, REACH, LANES), bf16)
     spread = X * T
     return pl.pallas_call(
         functools.partial(taps_body, scale),
         grid=(SLOTS,),
-        out_shape=(shape, shape),
+        out_shape=(shape,) * 4,
         in_specs=[SMEM] * 3 + [all_x(T), all_x(PIECE)],
-        out_specs=(whole(*shape.shape), whole(*shape.shape)),
+        out_specs=(whole(*shape.shape),) * 4,
         scratch_shapes=[
             pltpu.VMEM((spread + 2 * REACH, LANES), f32),
             pltpu.VMEM((spread + NEAR * (K // NEAR - 1), 4 * LANES), bf16),
@@ -557,37 +576,38 @@
                 chan_sum[8 * n : 8 * n + 8, :], axis=0, keepdims=True
             )
         proj_sum[...] += columns[...].T
-        keep_ref[:, CELLS:, :, :] = jnp.zeros((MP, 2, 16, LANES), bf16)
-        send_ref[:, CELLS:, :, :] = jnp.zeros((MP, 2, 16, LANES), bf16)
-
-        def put(at, cell, even, odd):
-            keep_ref[at, cell] = (jnp.where(first_core, even, odd) * scale).astype(bf16)
-            send_ref[at, cell] = (jnp.where(first_core, odd, even) * scale).astype(bf16)
-
-        for cell in range(CELLS):
-            for y in range(2):
-                for x in range(X):
-                    at = 2 * cell * 32 + y * 16
-                    lanes = slice(x * LANES, (x + 1) * LANES)
-                    put(
-                        y * X + x,
-                        cell,
-                        conv_sum[at : at + 16, lanes],
-                        conv_sum[at + 32 : at + 48, lanes],
+        for x in range(X):
+            lanes = slice(x * LANES, (x + 1) * LANES)
+            for cell in range(CELLS):
+                at = 2 * cell * 32
+                even = conv_sum[at : at + 32, lanes]
+                odd = conv_sum[at + 32 : at + 64, lanes]
+                rows = slice(cell * 32, (cell + 1) * 32)
+                keep_ref[x, rows, :] = (jnp.where(first_core, even, odd) * scale).astype(bf16)
+                send_ref[x, rows, :] = (jnp.where(first_core, odd, even) * scale).astype(bf16)
+            for four in range(CELLS // 4):
+                even, odd = [
+                    jnp.concatenate(
+                        [
+                            proj_sum[at : at + SPARE, :]
+                            for at in (
+                                (2 * cell + odd) * 16 + x * SPARE
+                                for cell in range(4 * four, 4 * four + 4)
+                            )
+                        ],
+                        axis=0,
                     )
-            at = cell * 32
-            put(
-                cell // 2,
-                CELLS + cell % 2,
-                proj_sum[at : at + 16, :],
-                proj_sum[at + 16 : at + 32, :],
-            )
+                    for odd in range(2)
+                ]
+                rows = slice(CONV_ROWS + four * 16, CONV_ROWS + (four + 1) * 16)
+                keep_ref[x, rows, :] = (jnp.where(first_core, even, odd) * scale).astype(bf16)
+                send_ref[x, rows, :] = (jnp.where(first_core, odd, even) * scale).astype(bf16)
 
 
 def backward(
     scale, place, pieces, edge, cotangent, received, weight, stored, conv_weight, channels, proj
 ):
-    shape = jax.ShapeDtypeStruct((MP, REST, 16, LANES), bf16)
+    shape = jax.ShapeDtypeStruct((X, REST, LANES), bf16)
     return pl.pallas_call(
         functools.partial(backward_body, scale),
         grid=(SLOTS,),
@@ -642,28 +662,58 @@
     )
 
 
-def cells_body(dev_ref, kept_ref, recv_ref, rest_ref, out_ref):
-    model = lax.rem(dev_ref[0], MP)
-    out_ref[:, :REACH, :] = (kept_ref[...].astype(f32) + recv_ref[...].astype(f32)).astype(bf16)
-    rest = rest_ref[0].astype(f32)
-    for n in range(1, MP):
-        rest += rest_ref[n].astype(f32)
-    out_ref[:, REACH : REACH + 16, :] = rest[:CELLS].astype(bf16)
-    for cell in range(CELLS):
-        small = jnp.where(model == cell // 2, rest[CELLS + cell % 2], 0.0)
-        out_ref[cell, REACH + 16 :, :] = small.astype(bf16)
-
-
-def make_cells(dev, kept, received, rest):
+def join_body(dev_ref, keep_ref, recv_ref, *out_refs):
+    x = lax.rem(dev_ref[0], X)
+    for step, out_ref in enumerate(out_refs):
+        at = lax.rem(x + step, X)
+        out_ref[...] = (keep_ref[at].astype(f32) + recv_ref[at].astype(f32)).astype(bf16)
+
+
+def join(dev, keep, received):
+    shape = jax.ShapeDtypeStruct((REST, LANES), bf16)
+    return pl.pallas_call(
+        join_body,
+        out_shape=(shape,) * X,
+        in_specs=[SMEM] + [VMEM] * 2,
+        out_specs=(VMEM,) * X,
+        compiler_params=params(8),
+        cost_estimate=cost(0, 2 << 20),
+        name="join",
+    )(dev, keep, received)
+
+
+def cells_body(*refs):
+    pos_refs, rest_refs, out_ref, rows = refs[:4], refs[4:8], refs[8], refs[9]
+
+    def summed(parts, *at):
+        result = parts[0][at].astype(f32)
+        for part in parts[1:]:
+            result += part[at].astype(f32)
+        return result
+
+    for four in range(CELLS // 4):
+        at = CONV_ROWS + four * 16
+        small = summed(rest_refs, slice(at, at + 16), slice(None))
+        for n in range(4):
+            cell = 4 * four + n
+            rows[...] = summed(pos_refs, cell)
+            rows[HALF:, :] = small[n * SPARE : (n + 1) * SPARE, :]
+            out_ref[cell, :REACH, :] = rows[...].astype(bf16)
+            conv = summed(rest_refs, slice(cell * 32, cell * 32 + 32), slice(None))
+            out_ref[cell, REACH:, :] = conv.astype(bf16)
+
+
+def make_cells(pos_parts, rest_parts):
     return pl.pallas_call(
         cells_body,
         out_shape=jax.ShapeDtypeStruct((CELLS, REACH + 32, LANES), bf16),
-        in_specs=[SMEM] + [VMEM] * 3,
+        in_specs=[VMEM] * 8,
         out_specs=VMEM,
-        compiler_params=params(10),
+        scratch_shapes=[pltpu.VMEM((REACH, LANES), f32)],
+        compiler_params=params(8),
         cost_estimate=cost(0, 2 << 20),
         name="cells",
-    )(dev, kept, received, rest)
+    )(*pos_parts, *rest_parts)
 
 
 def total_body(in_ref, out_ref):
@@ -704,16 +754,17 @@
         hidden_ref[slot] = jnp.where(
             place.chosen == slot, other_ref[...].astype(f32), states_ref[slot].astype(f32)
         ).astype(bf16)
+    small = []
     for x in range(X):
+        low, high = in_ref[x].astype(f32), in_ref[X + x].astype(f32)
         block = jnp.concatenate(
-            [in_ref[x, :REACH, :].astype(f32), in_ref[X + x, :REACH, :].astype(f32)], axis=0
+            [low[:HALF, :], high[:HALF, :], jnp.zeros((LANES - GC, LANES), f32)], axis=0
         ).T
         pos_ref[x] = block[:GC, :GC]
-        for y in range(2):
-            conv_ref[y * 16 : (y + 1) * 16, x * LANES : (x + 1) * LANES] = in_ref[
-                y * X + x, REACH : REACH + 16, :
-            ].astype(f32)
-    small = in_ref[place.cell // 2, REACH + 16 :, :].astype(f32)
+        both = low[HALF:, :] + high[HALF:, :]
+        small.append(both[:SPARE, :])
+        conv_ref[:, x * LANES : (x + 1) * LANES] = both[SPARE:, :]
+    small = jnp.concatenate(small, axis=0)
     proj_ref[...] = small[:, :GC]
     chan_ref[...] = jnp.concatenate([small] * 8, axis=0).T[GC : GC + 5, :16]
 
@@ -735,10 +786,6 @@
     )(*place, cells, states, other)
 
 
-def added(a, b):
-    return (a.astype(f32) + b.astype(f32)).astype(bf16)
-
-
 def per_device(
     audio, lengths, moved_slots, conv_weight, channel_params, proj_weight, pos_weight, cotangent
 ):
@@ -763,14 +810,23 @@
     features, edge, *stored = encode(place, audio, conv_weight, channels, proj)
     features = over_x(features)
     edge = lax.ppermute(edge, "mp", seam)
-    ahead, behind = turn(pos_weight.transpose(1, 2, 0))
+    ahead = turn(pos_weight.transpose(1, 2, 0))
     states, sent, pieces, edge = mix(place, features, edge, ahead, cot, received)
+    pieces, ahead = lax.optimization_barrier((pieces, ahead))
     pieces = over_x(pieces)
     edge = lax.ppermute(edge, "mp", seam)
     other = lax.ppermute(sent, "dp", swap)
-    pos_keep, pos_send = taps(scale, place, features, pieces)
-    pos_send, edge = lax.optimization_barrier((pos_send, edge))
-    pos_recv = lax.ppermute(pos_send, "dp", core_swap)
+    behind = flip(ahead)
+    own, to_core, to_low, to_both = taps(scale, place, features, pieces)
+    to_core, to_low, to_both, edge = lax.optimization_barrier((to_core, to_low, to_both, edge))
+    low_swap = [(i, i ^ X) for i in range(MP)]
+    both_swap = [(i, i ^ MP ^ X) for i in range(DP * MP)]
+    pos_parts = (
+        own,
+        lax.ppermute(to_core, "dp", core_swap),
+        lax.ppermute(to_low, "mp", low_swap),
+        lax.ppermute(to_both, ("dp", "mp"), both_swap),
+    )
     audio_grad, keep, send = backward(
         scale,
         place,
@@ -784,17 +840,16 @@
         channels,
         proj,
     )
-    rest = added(keep, lax.ppermute(send, "dp", core_swap))
-    rest = lax.all_to_all(rest, "mp", 0, 0, tiled=True)
-    pos_sum = added(pos_keep, pos_recv)
-    low_half = model_index < X
-    kept = jnp.where(low_half, pos_sum[0], pos_sum[1])
-    leaving = jnp.where(low_half, pos_sum[1], pos_sum[0])
-    coming = lax.ppermute(leaving, "mp", [(i, i ^ X) for i in range(MP)])
-    rest, other = lax.optimization_barrier((rest, other))
-    cells = make_cells(dev, kept, coming, rest)
+    send, pos_parts = lax.optimization_barrier((send, pos_parts))
+    chunks = join(dev, keep, lax.ppermute(send, "dp", core_swap))
+    rest_parts = [chunks[0]]
+    for step in (2, 1, 3):
+        route = [(X * y + x, X * y + (x + step) % X) for y in range(2) for x in range(X)]
+        rest_parts.append(lax.ppermute(chunks[step], "mp", route))
+    cells = make_cells(pos_parts, rest_parts)
     groups = [list(range(bit, DP, 2)) for bit in range(2)]
     cells = lax.all_to_all(cells, "dp", 0, 0, axis_index_groups=groups, tiled=True)
+    cells, other = lax.optimization_barrier((cells, other))
     cells = lax.all_to_all(total(cells), "mp", 0, 0, tiled=True)
     hidden, grad_pos, grad_conv, grad_proj, grad_channels = finish(place, cells, states, other)
     return (

time: 124 us -> 118 us (0.952)
  blocking collectives: 33.6 us -> 11.2 us
  starting transfers between devices: 23.5 us -> 39.8 us
  local copies, waits for them, and re-layouts: 2.49 us -> 11.4 us
  Pallas kernels: 37.5 us -> 28.7 us
  other arithmetic: 2.25 us -> 0 us
  waiting for transfers between devices: 24.2 us -> 25.6 us
    all_to_all x1 -> x0, blocking collectives: 22.5 us -> none  [per_device(): lax.all_to_all(cells, 'dp', 0, 0, axis_index_groups=groups, tiled=True)]
    unnamed x24 -> x28, local copies, waits for them, and re-layouts: 2.49 us -> 11.4 us
    all_to_all x2, waiting for transfers between devices: 9.98 us -> 3.63 us  [over_x(): lax.all_to_all(copies, 'mp', 0, 0, axis_index_groups=rows, tiled=True)]
    ppermute x1, starting transfers between devices: 0.01 us -> 5.84 us  [per_device(): other = lax.ppermute(sent, 'dp', swap)]
    ppermute x3 -> x7, starting transfers between devices: 2.15 us -> 7.97 us  [the longest x3 4.91 us: per_device(): rest_parts.append(lax.ppermute(chunks[step], 'mp', route))]
    ppermute x3 -> x7, waiting for transfers between devices: 5.77 us -> 11.2 us  [the longest x3 5.94 us: per_device(): rest_parts.append(lax.ppermute(chunks[step], 'mp', route))]
    pallas_call x1, Pallas kernels: 6.47 us -> 3.08 us  [mix(): pl.pallas_call(mix_body, grid=(SLOTS,), out_shape=(jax.ShapeDtypeStruct((...]
    all_to_all x2, starting transfers between devices: 9.3 us -> 12.4 us  [over_x(): lax.all_to_all(copies, 'mp', 0, 0, axis_index_groups=rows, tiled=True)]
  transfers between devices with their start and end apart: 10 -> 14, of which waited for: 5 -> 7; matrix products, arithmetic and copies ran while one was open for 2% -> 0% of each run, Pallas kernels for 10% -> 16%
where the time goes in v5:
time: 118 us
  starting transfers between devices  39.8 us (34%)
  Pallas kernels  28.7 us (24%)
  waiting for transfers between devices  25.6 us (22%)
  local copies, waits for them, and re-layouts  11.4 us (10%)
  blocking collectives  11.2 us (9%)
    all_to_all x2, starting transfers between devices, over_x(): lax.all_to_all(copies, 'mp', 0, 0, axis_index_groups=rows, tiled=True)  12.4 us
    unnamed x28, local copies, waits for them, and re-layouts  11.4 us
    all_to_all x1, blocking collectives, per_device(): cells = lax.all_to_all(total(cells), 'mp', 0, 0, tiled=True)  11.2 us
    ppermute x1, waiting for transfers between devices, per_device(): other = lax.ppermute(sent, 'dp', swap)  10.8 us
    pallas_call x1, Pallas kernels, backward(): pl.pallas_call(functools.partial(backward_body, scale), grid=(SLOTS,), ou...  8.24 us
    all_to_all x1, starting transfers between devices, per_device(): lax.all_to_all(cells, 'dp', 0, 0, axis_index_groups=groups, tiled=True)  6.82 us
    ppermute x3, waiting for transfers between devices, per_device(): rest_parts.append(lax.ppermute(chunks[step], 'mp', route))  5.94 us
    ppermute x1, starting transfers between devices, per_device(): other = lax.ppermute(sent, 'dp', swap)  5.84 us
  transfers between devices with their start and end apart: 14, of which 7 were waited for; matrix products, arithmetic and copies ran while one was open for 0% of the time, Pallas kernels for 16%

profile of v5, /device:TPU:2, one launch (start us, length us, event | category | flops | bytes accessed | tf_op | source)
XLA Modules:
  0.0 117.5 jit_solution(10823793012956903335)
XLA Ops:
  0.6 4.3 %encode.1 = (bf16[4,2,256,128]{3,2,1,0:T(8,128)(2,1)}, bf16[2,64,128]{2,1,0:T(8,128)(2,1)}, bf16[2,256,1024]{2,1,0:T(8,128)(2,1)}, bf16[2,256,512]{2,1,0:T(8,128...) custom-call(s32[1]{0:T(128)} %bitcast.dev_ref, s32[64]{0:T(128)} %len_ref.9, ...), custom_call_target="tpu_custom_call" | custom-call | flops 603979776 | bytes 8388608 | tf_op jit(solution)/shard_map/encode/pallas_call | solution.py:253
  4.9 0.0 copy-start.11
  4.9 7.2 %all-to-all-start = ((bf16[4,2,256,128]{3,2,1,0:T(8,128)(2,1)}), bf16[4,2,256,128]{3,2,1,0:T(8,128)(2,1)S(1)}, u32[]{:S(2)}, u32[]{:S(2)}) async-start(bf16[4,2,256,128]{3,2,1,0:T(8,128)(2,1)} %get-tuple-element.46), calls=%async_computation | async-start | bytes 1048576 | tf_op jit(solution)/shard_map/all_to_all | solution.py:807
  12.1 0.0 copy-start.7
  12.1 0.0 copy-start.9
  12.1 5.5 %collective-permute-start.1 = (bf16[2,120,256]{2,1,0:T(8,128)(2,1)}, bf16[2,120,256]{2,1,0:T(8,128)(2,1)S(1)}, u32[]{:S(2)}, u32[]{:S(2)}) collective-permute-start(bf16[2,120,256]{2,1,0:T(8,128)(2,1)} %bitcast.17), channel_id=1, source_target_pairs={{0,128},{8,136},{16,144},{24,152},{32,160},{40,168},{48,176},{56,1... | collective-permute-start | bytes 368648 | tf_op jit(solution)/shard_map/ppermute | solution.py:809
  17.6 0.7 collective-permute-start
  18.2 0.0 copy-start.4
  18.2 2.0 %copy-done.4 = bf16[128,120,120]{0,2,1:T(8,128)(2,1)S(1)} copy-done((bf16[128,120,120]{0,2,1:T(8,128)(2,1)S(1)}, bf16[128,120,120]{0,2,1:T(8,128)(2,1)}, u32[]{:S(2)}) %copy-start.4) | copy-done | bytes 3686424
  20.3 4.0 %turn.1 = bf16[16,128,1024]{2,1,0:T(8,128)(2,1)S(1)} custom-call(bf16[120,120,128]{2,1,0:T(8,128)(2,1)S(1)} %bitcast.11), custom_call_target="tpu_custom_call" | custom-call | bytes 8388608 | tf_op jit(solution)/shard_map/turn/pallas_call | solution.py:142
  24.3 0.0 copy-start
  24.3 2.0 %copy-done = bf16[16,128,1024]{2,1,0:T(8,128)(2,1)} copy-done((bf16[16,128,1024]{2,1,0:T(8,128)(2,1)}, bf16[16,128,1024]{2,1,0:T(8,128)(2,1)S(1)}, u32[]{:S(2)}) %copy-start) | copy-done | bytes 4194328
  26.2 0.0 collective-permute-done.edge_ref
  26.2 0.0 collective-permute-done.1.recv_ref
  26.2 0.0 all-to-all-done.feat_ref
  26.2 0.0 copy-done.11
  26.3 0.0 copy-done.7
  26.3 0.0 copy-done.9
  26.3 0.0 copy-start.1
  26.3 2.2 %copy-done.1 = bf16[16,128,1024]{2,1,0:T(8,128)(2,1)S(1)} copy-done((bf16[16,128,1024]{2,1,0:T(8,128)(2,1)S(1)}, bf16[16,128,1024]{2,1,0:T(8,128)(2,1)}, u32[]{:S(2)}) %copy-start.1) | copy-done | bytes 4194328
  28.5 3.1 %mix.1 = (bf16[2,120,256]{2,1,0:T(8,128)(2,1)S(1)}, bf16[120,256]{1,0:T(8,128)(2,1)S(1)}, bf16[4,2,320,128]{3,2,1,0:T(8,128)(2,1)}, bf16[2,64,128]{2,1,0:T(8,128)(2,1)S(1)}) custom-call(s32[1]{0:T(128)} %bitcast.dev_ref, s32[64]{0:T(128)S(1)} %copy-done.7, s32[16]{0:T(128)S(1)} %bitcast.14, bf16[4,2,256,128]{3,2,1,0:T(8,128)(2,1)S(1)} %all-to-all-done.feat_ref, ...), custom_call_target="tpu_custom_call" | custom-call | flops 2550136832 | bytes 7340032 | tf_op jit(solution)/shard_map/mix/pallas_call | solution.py:369
  31.6 0.0 copy-done.12
  31.6 5.2 %all-to-all-start.1 = ((bf16[4,2,320,128]{3,2,1,0:T(8,128)(2,1)}), bf16[4,2,320,128]{3,2,1,0:T(8,128)(2,1)S(1)}, u32[]{:S(2)}, u32[]{:S(2)}) async-start(bf16[4,2,320,128]{3,2,1,0:T(8,128)(2,1)} %get-tuple-element.49), calls=%async_computation.1 | async-start | bytes 1310720 | tf_op jit(solution)/shard_map/all_to_all | solution.py:807
  36.8 0.7 collective-permute-start.2
  37.4 0.0 copy-start.2
  37.4 2.2 %copy-done.2 = bf16[16,128,1024]{2,1,0:T(8,128)(2,1)S(1)} copy-done((bf16[16,128,1024]{2,1,0:T(8,128)(2,1)S(1)}, bf16[16,128,1024]{2,1,0:T(8,128)(2,1)}, u32[]{:S(2)}) %copy-start.2) | copy-done | bytes 4194328
  39.6 2.2 %flip.1.weight = bf16[1024,2048]{1,0:T(8,128)(2,1)S(1)} custom-call(bf16[2048,1024]{1,0:T(8,128)(2,1)S(1)} %bitcast.10), custom_call_target="tpu_custom_call" | custom-call | bytes 8388608 | tf_op jit(solution)/shard_map/flip/pallas_call | solution.py:165
  41.8 0.0 copy-start.3
  41.8 2.0 %copy-done.3 = bf16[1024,2048]{1,0:T(8,128)(2,1)} copy-done((bf16[1024,2048]{1,0:T(8,128)(2,1)}, bf16[1024,2048]{1,0:T(8,128)(2,1)S(1)}, u32[]{:S(2)}) %copy-start.3) | copy-done | bytes 4194328
  43.8 3.6 %all-to-all-done.1.piece_ref = bf16[4,2,320,128]{3,2,1,0:T(8,128)(2,1)S(1)} async-done(((bf16[4,2,320,128]{3,2,1,0:T(8,128)(2,1)}), bf16[4,2,320,128]{3,2,1,0:T(8,128)(2,1)S(1)}, u32[]{:S(2)}, u32[]{:S(2)}) %all-to-all-start.1) | async-done | bytes 655392 | tf_op jit(solution)/shard_map/all_to_all | solution.py:807
  47.4 4.3 %taps.1 = (bf16[16,64,128]{2,1,0:T(8,128)(2,1)S(1)}, bf16[16,64,128]{2,1,0:T(8,128)(2,1)S(1)}, bf16[16,64,128]{2,1,0:T(8,128)(2,1)S(1)}, bf16[16,64,128]{2,1,0:T(8,128)(2,1)S(1)}) custom-call(s32[1]{0:T(128)} %bitcast.dev_ref, s32[64]{0:T(128)S(1)} %copy-done.7, s32[16]{0:T(128)S(1)} %bitcast.15, bf16[4,2,256,128]{3,2,1,0:T(8,128)(2,1)S(1)} %all-to-all-done.feat_ref, ...), custom_call_target="tpu_custom_call" | custom-call | flops 2550136832 | bytes 4194304 | tf_op jit(solution)/shard_map/taps/pallas_call | solution.py:452
  51.7 0.0 copy-done.5
  51.7 0.0 collective-permute-done.2.edge_ref
  51.8 0.0 copy-start.13
  51.8 0.2 collective-permute-start.3
  52.0 2.5 %collective-permute-start.4 = (bf16[16,64,128]{2,1,0:T(8,128)(2,1)S(1)}, bf16[16,64,128]{2,1,0:T(8,128)(2,1)S(1)}, u32[]{:S(2)}, u32[]{:S(2)}) collective-permute-start(bf16[16,64,128]{2,1,0:T(8,128)(2,1)S(1)} %get-tuple-element.64), channel_id=1, source_target_pairs={{0,4},{1,5},{2,6},{3,7},{4,0},{5,1},{6,2},{7,3},{8,12},{9,13},{10,... | collective-permute-start | bytes 786440 | tf_op jit(solution)/shard_map/ppermute | solution.py:827
  54.5 0.0 collective-permute-start.5
  54.5 0.0 copy-done.13
  54.5 8.2 %backward.1 = (bf16[2,512,512]{2,1,0:T(8,128)(2,1)}, bf16[4,576,128]{2,1,0:T(8,128)(2,1)}, bf16[4,576,128]{2,1,0:T(8,128)(2,1)}) custom-call(s32[1]{0:T(128)} %bitcast.dev_ref, s32[64]{0:T(128)} %len_ref.9, s32[16]{0:T(128)} %bitcast.13, bf16[4,2,320,128]{3,2,1,0:T(8,128)(2,1)} %copy-done.5, bf16[2,64,128]{2,1,0:T(8,128)(2,1)} %copy-done.13, ...), custom_call_target="tpu_custom_call" | custom-call | flops 3758096384 | bytes 14680064 | tf_op jit(solution)/shard_map/backward/pallas_call | solution.py:611
  62.7 0.0 copy-start.8
  62.7 0.0 copy-start.10
  62.8 0.0 collective-permute-done.3.refs_1_
  62.8 0.0 collective-permute-done.4.refs_2_
  62.8 3.4 %collective-permute-done.5.refs_3_ = bf16[16,64,128]{2,1,0:T(8,128)(2,1)S(1)} collective-permute-done((bf16[16,64,128]{2,1,0:T(8,128)(2,1)S(1)}, bf16[16,64,128]{2,1,0:T(8,128)(2,1)S(1)}, u32[]{:S(2)}, u32[]{:S(2)}) %collective-permute-start.5) | collective-permute-done | bytes 262176 | tf_op jit(solution)/shard_map/ppermute | solution.py:828
  66.1 0.3 collective-permute-start.6
  66.5 1.9 %collective-permute-done.6.recv_ref = bf16[4,576,128]{2,1,0:T(8,128)(2,1)S(1)} collective-permute-done((bf16[4,576,128]{2,1,0:T(8,128)(2,1)}, bf16[4,576,128]{2,1,0:T(8,128)(2,1)S(1)}, u32[]{:S(2)}, u32[]{:S(2)}) %collective-permute-start.6) | collective-permute-done | bytes 589856 | tf_op jit(solution)/shard_map/ppermute | solution.py:844
  68.4 1.1 copy-done.6
  69.4 0.1 join.1
  69.6 2.9 %collective-permute-start.7 = (bf16[576,128]{1,0:T(8,128)(2,1)S(1)}, bf16[576,128]{1,0:T(8,128)(2,1)S(1)}, u32[]{:S(2)}, u32[]{:S(2)}) collective-permute-start(bf16[576,128]{1,0:T(8,128)(2,1)S(1)} %get-tuple-element.73), channel_id=1, source_target_pairs={{0,2},{1,3},{2,0},{3,1},{4,6},{5,7},{6,4},{7,5},{8,10},{9,11},{10,... | collective-permute-start | bytes 442376 | tf_op jit(solution)/shard_map/ppermute | solution.py:848
  72.4 0.1 collective-permute-start.8
  72.6 1.9 %collective-permute-start.9 = (bf16[576,128]{1,0:T(8,128)(2,1)S(1)}, bf16[576,128]{1,0:T(8,128)(2,1)S(1)}, u32[]{:S(2)}, u32[]{:S(2)}) collective-permute-start(bf16[576,128]{1,0:T(8,128)(2,1)S(1)} %get-tuple-element.75), channel_id=1, source_target_pairs={{0,3},{1,0},{2,1},{3,2},{4,7},{5,4},{6,5},{7,6},{8,11},{9,8},{10,9... | collective-permute-start | bytes 442376 | tf_op jit(solution)/shard_map/ppermute | solution.py:848
  74.5 3.4 %collective-permute-done.7.refs_5_ = bf16[576,128]{1,0:T(8,128)(2,1)S(1)} collective-permute-done((bf16[576,128]{1,0:T(8,128)(2,1)S(1)}, bf16[576,128]{1,0:T(8,128)(2,1)S(1)}, u32[]{:S(2)}, u32[]{:S(2)}) %collective-permute-start.7) | collective-permute-done | bytes 147488 | tf_op jit(solution)/shard_map/ppermute | solution.py:848
  77.8 1.1 collective-permute-done.8.refs_6_
  78.9 1.5 %collective-permute-done.9.refs_7_ = bf16[576,128]{1,0:T(8,128)(2,1)S(1)} collective-permute-done((bf16[576,128]{1,0:T(8,128)(2,1)S(1)}, bf16[576,128]{1,0:T(8,128)(2,1)S(1)}, u32[]{:S(2)}, u32[]{:S(2)}) %collective-permute-start.9) | collective-permute-done | bytes 147488 | tf_op jit(solution)/shard_map/ppermute | solution.py:848
  80.4 1.0 cells.1
  81.4 6.8 %all-to-all-start.2 = ((bf16[16,96,128]{2,1,0:T(8,128)(2,1)}), bf16[16,96,128]{2,1,0:T(8,128)(2,1)S(1)}, u32[]{:S(2)}, u32[]{:S(2)}) async-start(bf16[16,96,128]{2,1,0:T(8,128)(2,1)} %cells.1), calls=%async_computation.2 | async-start | bytes 786432 | tf_op jit(solution)/shard_map/all_to_all | solution.py:851
  88.2 5.8 %collective-permute-start.10 = (bf16[120,256]{1,0:T(8,128)(2,1)S(1)}, bf16[120,256]{1,0:T(8,128)(2,1)S(1)}, u32[]{:S(2)}, u32[]{:S(2)}) collective-permute-start(bf16[120,256]{1,0:T(8,128)(2,1)S(1)} %get-tuple-element.76), channel_id=1, source_target_pairs={{0,128},{8,136},{16,144},{24,152},{32,160},{40,168},{48,176},{56,1... | collective-permute-start | bytes 184328 | tf_op jit(solution)/shard_map/ppermute | solution.py:818
  94.1 10.8 %collective-permute-done.10.other_ref = bf16[120,256]{1,0:T(8,128)(2,1)S(1)} collective-permute-done((bf16[120,256]{1,0:T(8,128)(2,1)S(1)}, bf16[120,256]{1,0:T(8,128)(2,1)S(1)}, u32[]{:S(2)}, u32[]{:S(2)}) %collective-permute-start.10) | collective-permute-done | bytes 61472 | tf_op jit(solution)/shard_map/ppermute | solution.py:818
  104.9 0.0 all-to-all-done.2.in_ref
  104.9 0.1 total.1
  104.9 11.2 %all_to_all.20.in_ref = bf16[8,96,128]{2,1,0:T(8,128)(2,1)S(1)} all-to-all(bf16[8,96,128]{2,1,0:T(8,128)(2,1)S(1)} %total.1), channel_id=1, replica_groups=mesh['dp'=32,'mp'=8] {'mp'}, dimensions={0} | all-to-all | bytes 393216 | tf_op jit(solution)/shard_map/all_to_all | solution.py:853
  116.1 0.0 copy-done.8
  116.1 0.0 copy-done.10
  116.1 1.4 %finish.1 = (bf16[2,120,256]{2,1,0:T(8,128)(2,1)}, f32[4,120,120]{2,1,0:T(8,128)}, f32[32,512]{1,0:T(8,128)}, f32[16,120]{1,0:T(8,128)}, f32[5,16]{1,0:T(8,128)}) custom-call(s32[1]{0:T(128)} %bitcast.dev_ref, s32[64]{0:T(128)S(1)} %copy-done.8, s32[16]{0:T(128)S(1)} %bitcast.16, bf16[8,96,128]{2,1,0:T(8,128)(2,1)S(1)} %all_to_all.20.in_ref, ...), custom_call_target="tpu_custom_call" | custom-call | tf_op jit(solution)/shard_map/finish/pallas_call | solution.py:773
  (3 shorter events, 0.0 us)
Async XLA Ops:
  4.9 21.3 %copy-start.11 = (bf16[2,256,120]{1,2,0:T(8,128)(2,1)S(1)}, bf16[2,256,120]{1,2,0:T(8,128)(2,1)}, u32[]{:S(2)}) copy-start(bf16[2,256,120]{1,2,0:T(8,128)(2,1)} %param.15) | copy-start | bytes 368644
  4.9 21.3 %all-to-all-start = ((bf16[4,2,256,128]{3,2,1,0:T(8,128)(2,1)}), bf16[4,2,256,128]{3,2,1,0:T(8,128)(2,1)S(1)}, u32[]{:S(2)}, u32[]{:S(2)}) async-start(bf16[4,2,256,128]{3,2,1,0:T(8,128)(2,1)} %get-tuple-element.46), calls=%async_computation | async-start | bytes 1048576 | tf_op jit(solution)/shard_map/all_to_all | solution.py:807
  12.1 14.2 %copy-start.7 = (s32[64]{0:T(128)S(1)}, s32[64]{0:T(128)}, u32[]{:S(2)}) copy-start(s32[64]{0:T(128)} %len_ref.9) | copy-start | bytes 772
  12.1 14.2 %copy-start.9 = (s32[16,1]{0,1:T(1,128)S(1)}, s32[16,1]{0,1:T(1,128)}, u32[]{:S(2)}) copy-start(s32[16,1]{0,1:T(1,128)} %param.10) | copy-start | bytes 196
  12.1 14.1 %collective-permute-start.1 = (bf16[2,120,256]{2,1,0:T(8,128)(2,1)}, bf16[2,120,256]{2,1,0:T(8,128)(2,1)S(1)}, u32[]{:S(2)}, u32[]{:S(2)}) collective-permute-start(bf16[2,120,256]{2,1,0:T(8,128)(2,1)} %bitcast.17), channel_id=1, source_target_pairs={{0,128},{8,136},{16,144},{24,152},{32,160},{40,168},{48,176},{56,1... | collective-permute-start | bytes 368648 | tf_op jit(solution)/shard_map/ppermute | solution.py:809
  17.6 8.7 %collective-permute-start = (bf16[2,64,128]{2,1,0:T(8,128)(2,1)}, bf16[2,64,128]{2,1,0:T(8,128)(2,1)S(1)}, u32[]{:S(2)}, u32[]{:S(2)}) collective-permute-start(bf16[2,64,128]{2,1,0:T(8,128)(2,1)} %get-tuple-element.47), channel_id=1, source_target_pairs={{3,4},{4,3},{11,12},{12,11},{19,20},{20,19},{27,28},{28,27},{35,36... | collective-permute-start | bytes 98312 | tf_op jit(solution)/shard_map/ppermute | solution.py:812
  18.2 2.0 %copy-start.4 = (bf16[128,120,120]{0,2,1:T(8,128)(2,1)S(1)}, bf16[128,120,120]{0,2,1:T(8,128)(2,1)}, u32[]{:S(2)}) copy-start(bf16[128,120,120]{0,2,1:T(8,128)(2,1)} %param.14) | copy-start | bytes 11059204
  24.3 2.0 %copy-start = (bf16[16,128,1024]{2,1,0:T(8,128)(2,1)}, bf16[16,128,1024]{2,1,0:T(8,128)(2,1)S(1)}, u32[]{:S(2)}) copy-start(bf16[16,128,1024]{2,1,0:T(8,128)(2,1)S(1)} %turn.1) | copy-start | bytes 12582916
  26.2 5.3 %copy-start.12 = (bf16[2,120,256]{2,1,0:T(8,128)(2,1)}, bf16[2,120,256]{2,1,0:T(8,128)(2,1)S(1)}, u32[]{:S(2)}) copy-start(bf16[2,120,256]{2,1,0:T(8,128)(2,1)S(1)} %collective-permute-done.1.recv_ref) | copy-start | bytes 368644
  26.3 2.2 %copy-start.1 = (bf16[16,128,1024]{2,1,0:T(8,128)(2,1)S(1)}, bf16[16,128,1024]{2,1,0:T(8,128)(2,1)}, u32[]{:S(2)}) copy-start(bf16[16,128,1024]{2,1,0:T(8,128)(2,1)} %copy-done) | copy-start | bytes 12582916
  31.6 15.9 %all-to-all-start.1 = ((bf16[4,2,320,128]{3,2,1,0:T(8,128)(2,1)}), bf16[4,2,320,128]{3,2,1,0:T(8,128)(2,1)S(1)}, u32[]{:S(2)}, u32[]{:S(2)}) async-start(bf16[4,2,320,128]{3,2,1,0:T(8,128)(2,1)} %get-tuple-element.49), calls=%async_computation.1 | async-start | bytes 1310720 | tf_op jit(solution)/shard_map/all_to_all | solution.py:807
  36.8 15.0 %collective-permute-start.2 = (bf16[2,64,128]{2,1,0:T(8,128)(2,1)S(1)}, bf16[2,64,128]{2,1,0:T(8,128)(2,1)S(1)}, u32[]{:S(2)}, u32[]{:S(2)}) collective-permute-start(bf16[2,64,128]{2,1,0:T(8,128)(2,1)S(1)} %get-tuple-element.53), channel_id=1, source_target_pairs={{3,4},{4,3},{11,12},{12,11},{19,20},{20,19},{27,28},{28,27},{35,36... | collective-permute-start | bytes 98312 | tf_op jit(solution)/shard_map/ppermute | solution.py:817
  37.4 2.2 %copy-start.2 = (bf16[16,128,1024]{2,1,0:T(8,128)(2,1)S(1)}, bf16[16,128,1024]{2,1,0:T(8,128)(2,1)}, u32[]{:S(2)}) copy-start(bf16[16,128,1024]{2,1,0:T(8,128)(2,1)} %copy-done) | copy-start | bytes 12582916
  41.8 2.0 %copy-start.3 = (bf16[1024,2048]{1,0:T(8,128)(2,1)}, bf16[1024,2048]{1,0:T(8,128)(2,1)S(1)}, u32[]{:S(2)}) copy-start(bf16[1024,2048]{1,0:T(8,128)(2,1)S(1)} %flip.1.weight) | copy-start | bytes 12582916
  47.4 4.3 %copy-start.5 = (bf16[4,2,320,128]{3,2,1,0:T(8,128)(2,1)}, bf16[4,2,320,128]{3,2,1,0:T(8,128)(2,1)S(1)}, u32[]{:S(2)}) copy-start(bf16[4,2,320,128]{3,2,1,0:T(8,128)(2,1)S(1)} %all-to-all-done.1.piece_ref) | copy-start | bytes 1966084
  51.8 2.7 %copy-start.13 = (bf16[2,64,128]{2,1,0:T(8,128)(2,1)}, bf16[2,64,128]{2,1,0:T(8,128)(2,1)S(1)}, u32[]{:S(2)}) copy-start(bf16[2,64,128]{2,1,0:T(8,128)(2,1)S(1)} %collective-permute-done.2.edge_ref) | copy-start | bytes 98308
  51.8 11.0 %collective-permute-start.3 = (bf16[16,64,128]{2,1,0:T(8,128)(2,1)S(1)}, bf16[16,64,128]{2,1,0:T(8,128)(2,1)S(1)}, u32[]{:S(2)}, u32[]{:S(2)}) collective-permute-start(bf16[16,64,128]{2,1,0:T(8,128)(2,1)S(1)} %get-tuple-element.63), channel_id=1, source_target_pairs={{0,8},{8,0},{16,24},{24,16},{32,40},{40,32},{48,56},{56,48},{64,72... | collective-permute-start | bytes 786440 | tf_op jit(solution)/shard_map/ppermute | solution.py:826
  52.0 10.8 %collective-permute-start.4 = (bf16[16,64,128]{2,1,0:T(8,128)(2,1)S(1)}, bf16[16,64,128]{2,1,0:T(8,128)(2,1)S(1)}, u32[]{:S(2)}, u32[]{:S(2)}) collective-permute-start(bf16[16,64,128]{2,1,0:T(8,128)(2,1)S(1)} %get-tuple-element.64), channel_id=1, source_target_pairs={{0,4},{1,5},{2,6},{3,7},{4,0},{5,1},{6,2},{7,3},{8,12},{9,13},{10,... | collective-permute-start | bytes 786440 | tf_op jit(solution)/shard_map/ppermute | solution.py:827
  54.5 11.7 %collective-permute-start.5 = (bf16[16,64,128]{2,1,0:T(8,128)(2,1)S(1)}, bf16[16,64,128]{2,1,0:T(8,128)(2,1)S(1)}, u32[]{:S(2)}, u32[]{:S(2)}) collective-permute-start(bf16[16,64,128]{2,1,0:T(8,128)(2,1)S(1)} %get-tuple-element.65), channel_id=1, source_target_pairs={{0,12},{1,13},{2,14},{3,15},{4,8},{5,9},{6,10},{7,11},{8,4},{9,5},... | collective-permute-start | bytes 786440 | tf_op jit(solution)/shard_map/ppermute | solution.py:828
  62.7 53.4 %copy-start.8 = (s32[64]{0:T(128)S(1)}, s32[64]{0:T(128)}, u32[]{:S(2)}) copy-start(s32[64]{0:T(128)} %len_ref.9) | copy-start | bytes 772
  62.7 53.4 %copy-start.10 = (s32[16,1]{0,1:T(1,128)S(1)}, s32[16,1]{0,1:T(1,128)}, u32[]{:S(2)}) copy-start(s32[16,1]{0,1:T(1,128)} %param.10) | copy-start | bytes 196
  66.1 2.2 %collective-permute-start.6 = (bf16[4,576,128]{2,1,0:T(8,128)(2,1)}, bf16[4,576,128]{2,1,0:T(8,128)(2,1)S(1)}, u32[]{:S(2)}, u32[]{:S(2)}) collective-permute-start(bf16[4,576,128]{2,1,0:T(8,128)(2,1)} %get-tuple-element.71), channel_id=1, source_target_pairs={{0,8},{8,0},{16,24},{24,16},{32,40},{40,32},{48,56},{56,48},{64,72... | collective-permute-start | bytes 1769480 | tf_op jit(solution)/shard_map/ppermute | solution.py:844
  68.4 1.1 copy-start.6
  69.6 8.3 %collective-permute-start.7 = (bf16[576,128]{1,0:T(8,128)(2,1)S(1)}, bf16[576,128]{1,0:T(8,128)(2,1)S(1)}, u32[]{:S(2)}, u32[]{:S(2)}) collective-permute-start(bf16[576,128]{1,0:T(8,128)(2,1)S(1)} %get-tuple-element.73), channel_id=1, source_target_pairs={{0,2},{1,3},{2,0},{3,1},{4,6},{5,7},{6,4},{7,5},{8,10},{9,11},{10,... | collective-permute-start | bytes 442376 | tf_op jit(solution)/shard_map/ppermute | solution.py:848
  72.4 6.5 %collective-permute-start.8 = (bf16[576,128]{1,0:T(8,128)(2,1)S(1)}, bf16[576,128]{1,0:T(8,128)(2,1)S(1)}, u32[]{:S(2)}, u32[]{:S(2)}) collective-permute-start(bf16[576,128]{1,0:T(8,128)(2,1)S(1)} %get-tuple-element.74), channel_id=1, source_target_pairs={{0,1},{1,2},{2,3},{3,0},{4,5},{5,6},{6,7},{7,4},{8,9},{9,10},{10,1... | collective-permute-start | bytes 442376 | tf_op jit(solution)/shard_map/ppermute | solution.py:848
  72.6 7.8 %collective-permute-start.9 = (bf16[576,128]{1,0:T(8,128)(2,1)S(1)}, bf16[576,128]{1,0:T(8,128)(2,1)S(1)}, u32[]{:S(2)}, u32[]{:S(2)}) collective-permute-start(bf16[576,128]{1,0:T(8,128)(2,1)S(1)} %get-tuple-element.75), channel_id=1, source_target_pairs={{0,3},{1,0},{2,1},{3,2},{4,7},{5,4},{6,5},{7,6},{8,11},{9,8},{10,9... | collective-permute-start | bytes 442376 | tf_op jit(solution)/shard_map/ppermute | solution.py:848
  81.4 23.5 %all-to-all-start.2 = ((bf16[16,96,128]{2,1,0:T(8,128)(2,1)}), bf16[16,96,128]{2,1,0:T(8,128)(2,1)S(1)}, u32[]{:S(2)}, u32[]{:S(2)}) async-start(bf16[16,96,128]{2,1,0:T(8,128)(2,1)} %cells.1), calls=%async_computation.2 | async-start | bytes 786432 | tf_op jit(solution)/shard_map/all_to_all | solution.py:851
  88.2 16.7 %collective-permute-start.10 = (bf16[120,256]{1,0:T(8,128)(2,1)S(1)}, bf16[120,256]{1,0:T(8,128)(2,1)S(1)}, u32[]{:S(2)}, u32[]{:S(2)}) collective-permute-start(bf16[120,256]{1,0:T(8,128)(2,1)S(1)} %get-tuple-element.76), channel_id=1, source_target_pairs={{0,128},{8,136},{16,144},{24,152},{32,160},{40,168},{48,176},{56,1... | collective-permute-start | bytes 184328 | tf_op jit(solution)/shard_map/ppermute | solution.py:818

commit v6 on v5

--- a/solution.py
+++ b/solution.py
@@ -28,7 +28,7 @@
 DP = 32
 X = 4
 CELLS = 16
-PIECE = T + REACH
+PIECE = 2 * T + REACH
 HALF = GC // 2
 SPARE = REACH - HALF
 CONV_ROWS = CELLS * 32
@@ -87,18 +87,6 @@
     def alive(self, slot):
         return self.first < self.length(slot)
 
-    def seam(self, rows):
-        return jnp.where(self.x == 0, rows[:REACH, :], rows[T - REACH :, :]).astype(bf16)
-
-    def extended(self, ext, edge, pieces):
-        own = pieces[self.x, 0, :T, :].astype(f32)
-        before = pieces[jnp.maximum(self.x - 1, 0), 0, T - REACH : T, :].astype(f32)
-        after = pieces[jnp.minimum(self.x + 1, X - 1), 0, :REACH, :].astype(f32)
-        ext[:REACH, :] = jnp.where(self.x == 0, edge, before)
-        ext[REACH : REACH + T, :] = own
-        ext[REACH + T :, :] = jnp.where(self.x == X - 1, edge, after)
-        return own
-
     def mask(self, slot):
         ids = self.first + lax.broadcasted_iota(jnp.int32, (T, 1), 0)
         return ids < self.length(slot)
@@ -112,15 +100,11 @@
     return pl.BlockSpec(dims, lambda s: (0,) * len(dims))
 
 
-def all_x(rows):
-    return pl.BlockSpec((X, 1, rows, LANES), lambda s: (0, s, 0, 0))
-
-
 def once(*dims):
     return pl.BlockSpec(dims, lambda s: (0,) * len(dims), pipeline_mode=pl.Buffered(1))
 
 
-def turn_body(in_ref, ahead_ref, rows):
+def turn_body(in_ref, ahead_ref, behind_ref, rows):
     block = pl.program_id(0)
     blocks = pl.num_programs(0)
     for n in range(NEAR):
@@ -134,44 +118,32 @@
     for q in range(far):
         for r in range(NEAR):
             at = (q * NEAR + r) * NEAR
-            ahead_ref[r, :, q * LANES : (q + 1) * LANES] = rows[at : at + NEAR, :].astype(bf16)
+            tile = rows[at : at + NEAR, :].astype(bf16)
+            ahead_ref[r, :, q * LANES : (q + 1) * LANES] = tile
+            r_back = NEAR - 1 - r
+            behind_ref[far - 1 - q, :, r_back * LANES : (r_back + 1) * LANES] = tile
 
 
 def turn(pos):
     far = K // NEAR
-    ahead = pl.pallas_call(
+    ahead, behind = pl.pallas_call(
         turn_body,
         grid=(LANES // NEAR,),
-        out_shape=jax.ShapeDtypeStruct((NEAR, LANES, far * LANES), bf16),
+        out_shape=(
+            jax.ShapeDtypeStruct((NEAR, LANES, far * LANES), bf16),
+            jax.ShapeDtypeStruct((far, LANES, NEAR * LANES), bf16),
+        ),
         in_specs=[pl.BlockSpec((NEAR, GC, K), lambda b: (b, 0, 0))],
-        out_specs=pl.BlockSpec((NEAR, NEAR, far * LANES), lambda b: (0, b, 0)),
+        out_specs=(
+            pl.BlockSpec((NEAR, NEAR, far * LANES), lambda b: (0, b, 0)),
+            pl.BlockSpec((far, NEAR, NEAR * LANES), lambda b: (0, b, 0)),
+        ),
         scratch_shapes=[pltpu.VMEM((K * NEAR, LANES), f32)],
-        compiler_params=params(10),
-        cost_estimate=cost(0, 8 << 20),
+        compiler_params=params(56),
+        cost_estimate=cost(0, 12 << 20),
         name="turn",
     )(pos)
-    return ahead.reshape(NEAR * LANES, -1)
-
-
-def flip_body(in_ref, out_ref):
-    for r in range(NEAR):
-        out_ref[:, r * LANES : (r + 1) * LANES] = in_ref[
-            (NEAR - 1 - r) * LANES : (NEAR - r) * LANES, :
-        ]
-
-
-def flip(ahead):
-    far = K // NEAR
-    return pl.pallas_call(
-        flip_body,
-        grid=(far,),
-        out_shape=jax.ShapeDtypeStruct((far * LANES, NEAR * LANES), bf16),
-        in_specs=[pl.BlockSpec((NEAR * LANES, LANES), lambda q: (0, far - 1 - q))],
-        out_specs=pl.BlockSpec((LANES, NEAR * LANES), lambda q: (q, 0)),
-        compiler_params=params(8),
-        cost_estimate=cost(0, 8 << 20),
-        name="flip",
-    )(ahead)
+    return ahead.reshape(NEAR * LANES, -1), behind.reshape(far * LANES, -1)
 
 
 def encode_body(
@@ -183,7 +155,8 @@
     chan_ref,
     proj_ref,
     feat_ref,
-    edge_ref,
+    tail_ref,
+    head_ref,
     pair_ref,
     q_ref,
     slope_ref,
@@ -238,15 +211,14 @@
             )
             normed[rows, :] = (m * gain_two + shift_two).astype(bf16)
         projected = nt(normed[...], proj[...])
-        features = jnp.where(place.mask(slot), projected, 0.0)
-        for copy in range(X):
-            feat_ref[copy, 0] = features.astype(bf16)
-        edge_ref[0] = place.seam(features)
+        feat_ref[0] = jnp.where(place.mask(slot), projected, 0.0).astype(bf16)
 
     @pl.when(jnp.logical_not(living))
     def _():
         feat_ref[...] = jnp.zeros_like(feat_ref)
-        edge_ref[...] = jnp.zeros_like(edge_ref)
+
+    tail_ref[0] = feat_ref[0, T - REACH :, :]
+    head_ref[0] = feat_ref[0, :REACH, :]
 
 
 def encode(place, audio, conv_weight, channels, proj):
@@ -254,7 +226,8 @@
         encode_body,
         grid=(SLOTS,),
         out_shape=(
-            jax.ShapeDtypeStruct((X, SLOTS, T, LANES), bf16),
+            jax.ShapeDtypeStruct((SLOTS, T, LANES), bf16),
+            jax.ShapeDtypeStruct((SLOTS, REACH, LANES), bf16),
             jax.ShapeDtypeStruct((SLOTS, REACH, LANES), bf16),
             jax.ShapeDtypeStruct((SLOTS, T, 2 * C), bf16),
             jax.ShapeDtypeStruct((SLOTS, T, C), bf16),
@@ -270,7 +243,8 @@
             whole(GC, C),
         ],
         out_specs=(
-            all_x(T),
+            by_slot(T, LANES),
+            by_slot(REACH, LANES),
             by_slot(REACH, LANES),
             by_slot(T, 2 * C),
             by_slot(T, C),
@@ -290,6 +264,12 @@
     )(*place, audio, conv_weight, channels, proj)
 
 
+def fill_ext(ext, low, own, high):
+    ext[:REACH, :] = low.astype(f32)
+    ext[REACH : REACH + T, :] = own.astype(f32)
+    ext[REACH + T :, :] = high.astype(f32)
+
+
 def fill_windows(windows, ext, first):
     rows = T + NEAR * (K // NEAR - 1)
     for r in range(NEAR):
@@ -315,14 +295,17 @@
     len_ref,
     mov_ref,
     feat_ref,
-    edge_ref,
+    low_ref,
+    high_ref,
     weight,
     cot_ref,
     recv_ref,
     states_ref,
     sent_ref,
+    slopes_ref,
+    tail_ref,
+    head_ref,
     piece_ref,
-    seam_ref,
     ext,
     windows,
     turned,
@@ -334,8 +317,8 @@
 
     @pl.when(living)
     def _():
-        edge = edge_ref[0].astype(f32)
-        own = place.extended(ext, edge, feat_ref)
+        own = feat_ref[0].astype(f32)
+        fill_ext(ext, low_ref[0], own, high_ref[0])
         fill_windows(windows, ext, 0)
         fill_back(turned, place, slot, cot_ref, recv_ref)
         back = turned[...].T
@@ -349,35 +332,42 @@
         states = jnp.where(mask, own + mixed * below, 0.0)
         states_ref[0] = states.T[:GC, :].astype(bf16)
         slopes = jnp.where(mask, back * (below + mixed * bell(mixed)), 0.0)
-        for copy in range(X):
-            piece_ref[copy, 0, :T, :] = slopes.astype(bf16)
-            piece_ref[copy, 0, T:, :] = edge.astype(bf16)
-        seam_ref[0] = place.seam(slopes)
+        slopes_ref[0] = slopes.astype(bf16)
+        edge = jnp.where(place.x < X // 2, low_ref[0].astype(f32), high_ref[0].astype(f32))
+        piece_ref[0, :T, :] = feat_ref[0]
+        piece_ref[0, T : T + REACH, :] = edge.astype(bf16)
+        piece_ref[0, T + REACH :, :] = slopes.astype(bf16)
 
     @pl.when(jnp.logical_not(living))
     def _():
         states_ref[...] = jnp.zeros_like(states_ref)
+        slopes_ref[...] = jnp.zeros_like(slopes_ref)
         piece_ref[...] = jnp.zeros_like(piece_ref)
-        seam_ref[...] = jnp.zeros_like(seam_ref)
+
+    tail_ref[0] = slopes_ref[0, T - REACH :, :]
+    head_ref[0] = slopes_ref[0, :REACH, :]
 
     @pl.when(place.chosen == slot)
     def _():
         sent_ref[...] = states_ref[0]
 
 
-def mix(place, features, edge, weight, cotangent, received):
+def mix(place, features, low, high, weight, cotangent, received):
     return pl.pallas_call(
         mix_body,
         grid=(SLOTS,),
         out_shape=(
             jax.ShapeDtypeStruct((SLOTS, GC, T), bf16),
             jax.ShapeDtypeStruct((GC, T), bf16),
-            jax.ShapeDtypeStruct((X, SLOTS, PIECE, LANES), bf16),
+            jax.ShapeDtypeStruct((SLOTS, T, LANES), bf16),
             jax.ShapeDtypeStruct((SLOTS, REACH, LANES), bf16),
+            jax.ShapeDtypeStruct((SLOTS, REACH, LANES), bf16),
+            jax.ShapeDtypeStruct((SLOTS, PIECE, LANES), bf16),
         ),
         in_specs=[SMEM] * 3
         + [
-            all_x(T),
+            by_slot(T, LANES),
+            by_slot(REACH, LANES),
             by_slot(REACH, LANES),
             once(*weight.shape),
             by_slot(GC, T),
@@ -386,8 +376,10 @@
         out_specs=(
             by_slot(GC, T),
             whole(GC, T),
-            all_x(PIECE),
+            by_slot(T, LANES),
             by_slot(REACH, LANES),
+            by_slot(REACH, LANES),
+            by_slot(PIECE, LANES),
         ),
         scratch_shapes=[
             pltpu.VMEM((EXT, LANES), f32),
@@ -397,12 +389,12 @@
         compiler_params=params(20),
         cost_estimate=cost(2 * SLOTS * SPAN * K * LANES * LANES, 7 << 20, SLOTS * T * LANES * 2),
         name="mix",
-    )(*place, features, edge, weight, cotangent, received)
-
-
-def taps_body(
-    scale, dev_ref, len_ref, mov_ref, feat_ref, piece_ref, own_ref, core_ref, low_ref, both_ref, ext, windows, turned, sums
-):
+    )(*place, features, low, high, weight, cotangent, received)
+
+
+def taps_body(scale, dev_ref, len_ref, mov_ref, *refs):
+    piece_refs, (keep_ref, send_ref) = refs[:X], refs[X : X + 2]
+    ext, windows, turned, sums = refs[X + 2 :]
     place = Place(dev_ref, len_ref, mov_ref)
     slot = pl.program_id(0)
     spread = X * T
@@ -414,13 +406,20 @@
 
     @pl.when(place.y * spread < place.length(slot))
     def _():
-        ext[:REACH, :] = piece_ref[0, 0, T:, :].astype(f32)
-        ext[REACH + spread :, :] = piece_ref[X - 1, 0, T:, :].astype(f32)
-        for x in range(X):
-            ext[REACH + x * T : REACH + (x + 1) * T, :] = feat_ref[x, 0].astype(f32)
-            turned[:, x * T : (x + 1) * T] = (
-                piece_ref[x, 0, :T, :].astype(f32).T.astype(bf16)
-            )
+        for step, piece_ref in enumerate(piece_refs):
+            x = lax.rem(place.x + (X - step), X)
+            at = pl.multiple_of(x * T, T)
+            ext[pl.ds(REACH + at, T), :] = piece_ref[0, :T, :].astype(f32)
+            turned[:, pl.ds(at, T)] = piece_ref[0, T + REACH :, :].astype(f32).T.astype(bf16)
+
+            @pl.when(x == 0)
+            def _():
+                ext[:REACH, :] = piece_ref[0, T : T + REACH, :].astype(f32)
+
+            @pl.when(x == X - 1)
+            def _():
+                ext[REACH + spread :, :] = piece_ref[0, T : T + REACH, :].astype(f32)
+
         for j in range(4):
             windows[:, j * LANES : (j + 1) * LANES] = ext[
                 pl.ds(place.x + 4 * j, rows), :
@@ -431,7 +430,6 @@
     @pl.when(slot == SLOTS - 1)
     def _():
         first_core = place.core == 0
-        first_half = place.y == 0
         for q in range(K // NEAR):
             for far in range(2):
                 at = 2 * far * LANES
@@ -439,22 +437,21 @@
                 odd = sums[q, :, at + LANES : at + 2 * LANES] * scale
                 keep = jnp.where(first_core, even, odd)
                 send = jnp.where(first_core, odd, even)
-                cell = 2 * q + far
-                for mine, other, rows in ((own_ref, low_ref, keep), (core_ref, both_ref, send)):
-                    one, two = rows[:REACH, :], rows[HALF : HALF + REACH, :]
-                    mine[cell] = jnp.where(first_half, one, two).astype(bf16)
-                    other[cell] = jnp.where(first_half, two, one).astype(bf16)
-
-
-def taps(scale, place, features, pieces):
-    shape = jax.ShapeDtypeStruct((CELLS, REACH, LANES), bf16)
+                for y in range(2):
+                    rows = slice(y * HALF, y * HALF + REACH)
+                    keep_ref[y, 2 * q + far] = keep[rows, :].astype(bf16)
+                    send_ref[y, 2 * q + far] = send[rows, :].astype(bf16)
+
+
+def taps(scale, place, pieces):
+    shape = jax.ShapeDtypeStruct((2, CELLS, REACH, LANES), bf16)
     spread = X * T
     return pl.pallas_call(
         functools.partial(taps_body, scale),
         grid=(SLOTS,),
-        out_shape=(shape,) * 4,
-        in_specs=[SMEM] * 3 + [all_x(T), all_x(PIECE)],
-        out_specs=(whole(*shape.shape),) * 4,
+        out_shape=(shape,) * 2,
+        in_specs=[SMEM] * 3 + [by_slot(PIECE, LANES)] * X,
+        out_specs=(whole(*shape.shape),) * 2,
         scratch_shapes=[
             pltpu.VMEM((spread + 2 * REACH, LANES), f32),
             pltpu.VMEM((spread + NEAR * (K // NEAR - 1), 4 * LANES), bf16),
@@ -464,7 +461,7 @@
         compiler_params=params(16),
         cost_estimate=cost(2 * SLOTS * SPAN * K * LANES * LANES, 4 << 20),
         name="taps",
-    )(*place, features, pieces)
+    )(*place, *pieces)
 
 
 def backward_body(
@@ -472,8 +469,9 @@
     dev_ref,
     len_ref,
     mov_ref,
-    piece_ref,
-    edge_ref,
+    slopes_ref,
+    low_ref,
+    high_ref,
     cot_ref,
     recv_ref,
     weight,
@@ -516,7 +514,7 @@
 
     @pl.when(living)
     def _():
-        place.extended(ext, edge_ref[0].astype(f32), piece_ref)
+        fill_ext(ext, low_ref[0], slopes_ref[0], high_ref[0])
         fill_windows(windows, ext, 1)
         fill_back(turned, place, slot, cot_ref, recv_ref)
         group = jnp.zeros((SPAN, span), f32)
@@ -605,7 +603,7 @@
 
 
 def backward(
-    scale, place, pieces, edge, cotangent, received, weight, stored, conv_weight, channels, proj
+    scale, place, slopes, low, high, cotangent, received, weight, stored, conv_weight, channels, proj
 ):
     shape = jax.ShapeDtypeStruct((X, REST, LANES), bf16)
     return pl.pallas_call(
@@ -614,7 +612,8 @@
         out_shape=(jax.ShapeDtypeStruct((SLOTS, 2 * T, C), bf16), shape, shape),
         in_specs=[SMEM] * 3
         + [
-            all_x(PIECE),
+            by_slot(T, LANES),
+            by_slot(REACH, LANES),
             by_slot(REACH, LANES),
             by_slot(GC, T),
             by_slot(GC, T),
@@ -650,8 +649,9 @@
         name="backward",
     )(
         *place,
-        pieces,
-        edge,
+        slopes,
+        low,
+        high,
         cotangent,
         received,
         weight,
@@ -660,6 +660,25 @@
         channels,
         proj,
     )
+
+
+def halve_body(dev_ref, keep_ref, recv_ref, stay_ref, leave_ref):
+    y = lax.rem(dev_ref[0], MP) // X
+    for out_ref, at in ((stay_ref, y), (leave_ref, 1 - y)):
+        out_ref[...] = (keep_ref[at].astype(f32) + recv_ref[at].astype(f32)).astype(bf16)
+
+
+def halve(dev, keep, received):
+    shape = jax.ShapeDtypeStruct(keep.shape[1:], bf16)
+    return pl.pallas_call(
+        halve_body,
+        out_shape=(shape,) * 2,
+        in_specs=[SMEM] + [VMEM] * 2,
+        out_specs=(VMEM,) * 2,
+        compiler_params=params(8),
+        cost_estimate=cost(0, 2 << 20),
+        name="halve",
+    )(dev, keep, received)
 
 
 def join_body(dev_ref, keep_ref, recv_ref, *out_refs):
@@ -683,7 +702,7 @@
 
 
 def cells_body(*refs):
-    pos_refs, rest_refs, out_ref, rows = refs[:4], refs[4:8], refs[8], refs[9]
+    pos_refs, rest_refs, out_ref, rows = refs[:2], refs[2:6], refs[6], refs[7]
 
     def summed(parts, *at):
         result = parts[0][at].astype(f32)
@@ -707,7 +726,7 @@
     return pl.pallas_call(
         cells_body,
         out_shape=jax.ShapeDtypeStruct((CELLS, REACH + 32, LANES), bf16),
-        in_specs=[VMEM] * 8,
+        in_specs=[VMEM] * 6,
         out_specs=VMEM,
         scratch_shapes=[pltpu.VMEM((REACH, LANES), f32)],
         compiler_params=params(8),
@@ -786,6 +805,17 @@
     )(*place, cells, states, other)
 
 
+def neighbours(tail, head):
+    forward = [(i, i + 1) for i in range(MP - 1)]
+    backward_route = [(i + 1, i) for i in range(MP - 1)]
+    return lax.ppermute(tail, "mp", forward), lax.ppermute(head, "mp", backward_route)
+
+
+def along_x(block, step):
+    route = [(X * y + x, X * y + (x + step) % X) for y in range(2) for x in range(X)]
+    return lax.ppermute(block, "mp", route)
+
+
 def per_device(
     audio, lengths, moved_slots, conv_weight, channel_params, proj_weight, pos_weight, cotangent
 ):
@@ -800,38 +830,24 @@
     proj = proj_weight.T
     cot = cotangent.transpose(0, 2, 1)
 
-    rows = [list(range(X)), list(range(X, 2 * X))]
-    seam = [(X - 1, X), (X, X - 1)]
-
-    def over_x(copies):
-        return lax.all_to_all(copies, "mp", 0, 0, axis_index_groups=rows, tiled=True)
-
     received = lax.ppermute(cot, "dp", swap)
-    features, edge, *stored = encode(place, audio, conv_weight, channels, proj)
-    features = over_x(features)
-    edge = lax.ppermute(edge, "mp", seam)
-    ahead = turn(pos_weight.transpose(1, 2, 0))
-    states, sent, pieces, edge = mix(place, features, edge, ahead, cot, received)
-    pieces, ahead = lax.optimization_barrier((pieces, ahead))
-    pieces = over_x(pieces)
-    edge = lax.ppermute(edge, "mp", seam)
+    features, tail, head, *stored = encode(place, audio, conv_weight, channels, proj)
+    low, high = neighbours(tail, head)
+    ahead, behind = turn(pos_weight.transpose(1, 2, 0))
+    states, sent, slopes, tail, head, piece = mix(
+        place, features, low, high, ahead, cot, received
+    )
+    low, high = neighbours(tail, head)
     other = lax.ppermute(sent, "dp", swap)
-    behind = flip(ahead)
-    own, to_core, to_low, to_both = taps(scale, place, features, pieces)
-    to_core, to_low, to_both, edge = lax.optimization_barrier((to_core, to_low, to_both, edge))
-    low_swap = [(i, i ^ X) for i in range(MP)]
-    both_swap = [(i, i ^ MP ^ X) for i in range(DP * MP)]
-    pos_parts = (
-        own,
-        lax.ppermute(to_core, "dp", core_swap),
-        lax.ppermute(to_low, "mp", low_swap),
-        lax.ppermute(to_both, ("dp", "mp"), both_swap),
-    )
+    piece, low, high = lax.optimization_barrier((piece, low, high))
+    far = along_x(piece, 2)
+    pieces = (piece, along_x(piece, 1), far, along_x(piece, 3))
     audio_grad, keep, send = backward(
         scale,
         place,
-        pieces,
-        edge,
+        slopes,
+        low,
+        high,
         cot,
         received,
         behind,
@@ -840,16 +856,16 @@
         channels,
         proj,
     )
-    send, pos_parts = lax.optimization_barrier((send, pos_parts))
-    chunks = join(dev, keep, lax.ppermute(send, "dp", core_swap))
-    rest_parts = [chunks[0]]
-    for step in (2, 1, 3):
-        route = [(X * y + x, X * y + (x + step) % X) for y in range(2) for x in range(X)]
-        rest_parts.append(lax.ppermute(chunks[step], "mp", route))
+    send, pieces, other = lax.optimization_barrier((send, pieces, other))
+    recv, pieces = lax.optimization_barrier((lax.ppermute(send, "dp", core_swap), pieces))
+    chunks = join(dev, keep, recv)
+    rest_parts = [chunks[0]] + [along_x(chunks[step], step) for step in (2, 1, 3)]
+    pos_keep, pos_send = taps(scale, place, pieces)
+    stay, leave = halve(dev, pos_keep, lax.ppermute(pos_send, "dp", core_swap))
+    pos_parts = (stay, lax.ppermute(leave, "mp", [(i, i ^ X) for i in range(MP)]))
     cells = make_cells(pos_parts, rest_parts)
     groups = [list(range(bit, DP, 2)) for bit in range(2)]
     cells = lax.all_to_all(cells, "dp", 0, 0, axis_index_groups=groups, tiled=True)
-    cells, other = lax.optimization_barrier((cells, other))
     cells = lax.all_to_all(total(cells), "mp", 0, 0, tiled=True)
     hidden, grad_pos, grad_conv, grad_proj, grad_channels = finish(place, cells, states, other)
     return (

time: 118 us -> 120 us (1.017)
  blocking collectives: 11.2 us -> 38.3 us
  waiting for transfers between devices: 25.6 us -> 13.6 us
  starting transfers between devices: 39.8 us -> 32 us
  local copies, waits for them, and re-layouts: 11.4 us -> 3.8 us
  Pallas kernels: 28.7 us -> 30.5 us
    all_to_all x0 -> x1, blocking collectives: none -> 28.9 us  [per_device(): lax.all_to_all(cells, 'dp', 0, 0, axis_index_groups=groups, tiled=True)]
    all_to_all x3 -> x0, starting transfers between devices: 19.2 us -> none  [the longest x2 12.4 us: over_x(): lax.all_to_all(copies, 'mp', 0, 0, axis_index_groups=rows, tiled=True)]
    ppermute x9 -> x13, starting transfers between devices: 9.27 us -> 24.6 us  [the longest x6 12.6 us: along_x(): return lax.ppermute(block, 'mp', route)]
    ppermute x1, waiting for transfers between devices: 10.8 us -> 0.01 us  [per_device(): other = lax.ppermute(sent, 'dp', swap)]
    unnamed x28 -> x24, local copies, waits for them, and re-layouts: 11.4 us -> 3.8 us
    ppermute x1, starting transfers between devices: 5.84 us -> 0.13 us  [per_device(): other = lax.ppermute(sent, 'dp', swap)]
    all_to_all x3 -> x0, waiting for transfers between devices: 3.63 us -> none  [the longest x2 3.63 us: over_x(): lax.all_to_all(copies, 'mp', 0, 0, axis_index_groups=rows, tiled=True)]
    pallas_call x2, Pallas kernels: 6.21 us -> 9.27 us  [the longest x1 9.15 us: turn(): pl.pallas_call(turn_body, grid=(LANES // NEAR,), out_shape=(jax.ShapeDtyp...]
  transfers between devices with their start and end apart: 14 -> 15, of which waited for: 7 -> 7; matrix products, arithmetic and copies ran while one was open for 0% -> 0% of each run, Pallas kernels for 16% -> 18%
where the time goes in v6:
time: 120 us; the launch traced here: 119 us
  blocking collectives  38.3 us (32%)
  starting transfers between devices  32 us (27%)
  Pallas kernels  30.5 us (25%)
  waiting for transfers between devices  13.6 us (11%)
  local copies, waits for them, and re-layouts  3.8 us (3%)
    all_to_all x1, blocking collectives, per_device(): lax.all_to_all(cells, 'dp', 0, 0, axis_index_groups=groups, tiled=True)  28.9 us
    ppermute x6, starting transfers between devices, along_x(): return lax.ppermute(block, 'mp', route)  12.6 us
    all_to_all x1, blocking collectives, per_device(): cells = lax.all_to_all(total(cells), 'mp', 0, 0, tiled=True)  9.4 us
    pallas_call x1, Pallas kernels, turn(): pl.pallas_call(turn_body, grid=(LANES // NEAR,), out_shape=(jax.ShapeDtyp...  9.15 us
    pallas_call x1, Pallas kernels, backward(): pl.pallas_call(functools.partial(backward_body, scale), grid=(SLOTS,), ou...  8.32 us
    ppermute x6, waiting for transfers between devices, along_x(): return lax.ppermute(block, 'mp', route)  7.85 us
    ppermute x2, starting transfers between devices, neighbours(): lax.ppermute(head, 'mp', backward_route)  7.37 us
    ppermute x1, starting transfers between devices, per_device(): received = lax.ppermute(cot, 'dp', swap)  7.28 us
  transfers between devices with their start and end apart: 15, of which 7 were waited for; matrix products, arithmetic and copies ran while one was open for 0% of the time, Pallas kernels for 18%

profile of v6, /device:TPU:2, one launch (start us, length us, event | category | flops | bytes accessed | tf_op | source)
XLA Modules:
  0.0 119.0 jit_solution(14103356929140786043)
XLA Ops:
  0.6 0.0 copy-start.7
  0.6 0.0 copy-start.1
  0.7 0.0 copy-start.3
  0.7 7.3 %collective-permute-start.2 = (bf16[2,120,256]{2,1,0:T(8,128)(2,1)}, bf16[2,120,256]{2,1,0:T(8,128)(2,1)S(1)}, u32[]{:S(2)}, u32[]{:S(2)}) collective-permute-start(bf16[2,120,256]{2,1,0:T(8,128)(2,1)} %bitcast.16), channel_id=1, source_target_pairs={{0,128},{8,136},{16,144},{24,152},{32,160},{40,168},{48,176},{56,1... | collective-permute-start | bytes 368648 | tf_op jit(solution)/shard_map/ppermute | solution.py:833
  7.9 4.2 %encode.1 = (bf16[2,256,128]{2,1,0:T(8,128)(2,1)}, bf16[2,64,128]{2,1,0:T(8,128)(2,1)}, bf16[2,64,128]{2,1,0:T(8,128)(2,1)}, bf16[2,256,1024]{2,1,0:T(8,128)(2,1...) custom-call(s32[1]{0:T(128)} %bitcast.dev_ref, ...), custom_call_target="tpu_custom_call" | custom-call | flops 603979776 | bytes 8388608 | tf_op jit(solution)/shard_map/encode/pallas_call | solution.py:225
  12.2 2.4 %collective-permute-start = (bf16[2,64,128]{2,1,0:T(8,128)(2,1)}, bf16[2,64,128]{2,1,0:T(8,128)(2,1)S(1)}, u32[]{:S(2)}, u32[]{:S(2)}) collective-permute-start(bf16[2,64,128]{2,1,0:T(8,128)(2,1)} %get-tuple-element.53), channel_id=1, source_target_pairs={{0,1},{1,2},{2,3},{3,4},{4,5},{5,6},{6,7},{8,9},{9,10},{10,11},{11... | collective-permute-start | bytes 98312 | tf_op jit(solution)/shard_map/ppermute | solution.py:811
  14.5 3.5 %collective-permute-start.1 = (bf16[2,64,128]{2,1,0:T(8,128)(2,1)}, bf16[2,64,128]{2,1,0:T(8,128)(2,1)S(1)}, u32[]{:S(2)}, u32[]{:S(2)}) collective-permute-start(bf16[2,64,128]{2,1,0:T(8,128)(2,1)} %get-tuple-element.54), channel_id=1, source_target_pairs={{1,0},{2,1},{3,2},{4,3},{5,4},{6,5},{7,6},{9,8},{10,9},{11,10},{12... | collective-permute-start | bytes 98312 | tf_op jit(solution)/shard_map/ppermute | solution.py:811
  18.0 9.2 %turn.1 = (bf16[16,128,1024]{2,1,0:T(8,128)(2,1)}, bf16[8,128,2048]{2,1,0:T(8,128)(2,1)}) custom-call(bf16[120,120,128]{2,1,0:T(8,128)(2,1)} %bitcast.19), custom_call_target="tpu_custom_call" | custom-call | bytes 12582912 | tf_op jit(solution)/shard_map/turn/pallas_call | solution.py:129
  27.2 0.0 collective-permute-done.low_ref
  27.2 0.0 collective-permute-done.1.high_ref
  27.2 0.0 collective-permute-done.2.recv_ref
  27.2 0.0 copy-start.8
  27.2 0.0 copy-done.7
  27.2 0.0 copy-done.1
  27.2 0.0 copy-done.3
  27.2 0.0 copy-start.5
  27.2 2.2 %copy-done.5 = bf16[16,128,1024]{2,1,0:T(8,128)(2,1)S(1)} copy-done((bf16[16,128,1024]{2,1,0:T(8,128)(2,1)S(1)}, bf16[16,128,1024]{2,1,0:T(8,128)(2,1)}, u32[]{:S(2)}) %copy-start.5) | copy-done | bytes 4194328
  29.4 0.0 copy-start.6
  29.4 0.9 copy-done.6
  30.3 2.3 %mix.1 = (bf16[2,120,256]{2,1,0:T(8,128)(2,1)S(1)}, bf16[120,256]{1,0:T(8,128)(2,1)S(1)}, bf16[2,256,128]{2,1,0:T(8,128)(2,1)S(1)}, bf16[2,64,128]{2,1,0:T(8,128...) custom-call(s32[1]{0:T(128)} %bitcast.dev_ref, s32[64]{0:T(128)S(1)} %copy-done.1, ...), custom_call_target="tpu_custom_call" | custom-call | flops 2550136832 | bytes 7340032 | tf_op jit(solution)/shard_map/mix/pallas_call | solution.py:356
  32.7 0.0 copy-done.8
  32.7 0.0 copy-start.9
  32.7 0.6 copy-done.9
  33.4 1.9 %collective-permute-start.3 = (bf16[2,64,128]{2,1,0:T(8,128)(2,1)S(1)}, bf16[2,64,128]{2,1,0:T(8,128)(2,1)S(1)}, u32[]{:S(2)}, u32[]{:S(2)}) collective-permute-start(bf16[2,64,128]{2,1,0:T(8,128)(2,1)S(1)} %get-tuple-element.58), channel_id=1, source_target_pairs={{0,1},{1,2},{2,3},{3,4},{4,5},{5,6},{6,7},{8,9},{9,10},{10,11},{11... | collective-permute-start | bytes 98312 | tf_op jit(solution)/shard_map/ppermute | solution.py:811
  35.3 3.9 %collective-permute-start.4 = (bf16[2,64,128]{2,1,0:T(8,128)(2,1)S(1)}, bf16[2,64,128]{2,1,0:T(8,128)(2,1)S(1)}, u32[]{:S(2)}, u32[]{:S(2)}) collective-permute-start(bf16[2,64,128]{2,1,0:T(8,128)(2,1)S(1)} %get-tuple-element.59), channel_id=1, source_target_pairs={{1,0},{2,1},{3,2},{4,3},{5,4},{6,5},{7,6},{9,8},{10,9},{11,10},{12... | collective-permute-start | bytes 98312 | tf_op jit(solution)/shard_map/ppermute | solution.py:811
  39.2 0.1 collective-permute-start.8
  39.3 0.0 collective-permute-done.3.low_ref
  39.3 0.0 copy-start.10
  39.3 1.7 %collective-permute-done.4.high_ref = bf16[2,64,128]{2,1,0:T(8,128)(2,1)S(1)} collective-permute-done((bf16[2,64,128]{2,1,0:T(8,128)(2,1)S(1)}, bf16[2,64,128]{2,1,0:T(8,128)(2,1)S(1)}, u32[]{:S(2)}, u32[]{:S(2)}) %collective-permute-start.4) | collective-permute-done | bytes 32800 | tf_op jit(solution)/shard_map/ppermute | solution.py:811
  41.1 0.0 copy-start.11
  41.1 2.0 %collective-permute-start.7 = (bf16[2,576,128]{2,1,0:T(8,128)(2,1)S(1)}, bf16[2,576,128]{2,1,0:T(8,128)(2,1)S(1)}, u32[]{:S(2)}, u32[]{:S(2)}) collective-permute-start(bf16[2,576,128]{2,1,0:T(8,128)(2,1)S(1)} %get-tuple-element.76.refs_0_), channel_id=1, source_target_pairs={{0,3},{1,0},{2,1},{3,2},{4,7},{5,4},{6,5},{7,6},{8,11},{9,8},{10,9... | collective-permute-start | bytes 884744 | tf_op jit(solution)/shard_map/ppermute | solution.py:816
  43.1 3.2 %collective-permute-start.6 = (bf16[2,576,128]{2,1,0:T(8,128)(2,1)S(1)}, bf16[2,576,128]{2,1,0:T(8,128)(2,1)S(1)}, u32[]{:S(2)}, u32[]{:S(2)}) collective-permute-start(bf16[2,576,128]{2,1,0:T(8,128)(2,1)S(1)} %get-tuple-element.76.refs_0_), channel_id=1, source_target_pairs={{0,2},{1,3},{2,0},{3,1},{4,6},{5,7},{6,4},{7,5},{8,10},{9,11},{10,... | collective-permute-start | bytes 884744 | tf_op jit(solution)/shard_map/ppermute | solution.py:816
  46.3 2.6 %collective-permute-start.5 = (bf16[2,576,128]{2,1,0:T(8,128)(2,1)S(1)}, bf16[2,576,128]{2,1,0:T(8,128)(2,1)S(1)}, u32[]{:S(2)}, u32[]{:S(2)}) collective-permute-start(bf16[2,576,128]{2,1,0:T(8,128)(2,1)S(1)} %get-tuple-element.76.refs_0_), channel_id=1, source_target_pairs={{0,1},{1,2},{2,3},{3,0},{4,5},{5,6},{6,7},{7,4},{8,9},{9,10},{10,1... | collective-permute-start | bytes 884744 | tf_op jit(solution)/shard_map/ppermute | solution.py:816
  48.9 0.0 copy-done.10
  48.9 0.0 copy-done.11
  48.9 0.0 copy-start.2
  48.9 8.3 %backward.1 = (bf16[2,512,512]{2,1,0:T(8,128)(2,1)}, bf16[4,576,128]{2,1,0:T(8,128)(2,1)}, bf16[4,576,128]{2,1,0:T(8,128)(2,1)}) custom-call(s32[1]{0:T(128)} %bitcast.dev_ref, s32[64]{0:T(128)} %len_ref.9, s32[16]{0:T(128)} %bitcast.11, bf16[2,256,128]{2,1,0:T(8,128)(2,1)} %copy-done.9, bf16[2,64,128]{2,1,0:T(8,128)(2,1)} %copy-done.10, ...), custom_call_target="tpu_custom_call" | custom-call | flops 3758096384 | bytes 14680064 | tf_op jit(solution)/shard_map/backward/pallas_call | solution.py:609
  57.2 0.0 collective-permute-done.8.other_ref
  57.3 0.0 collective-permute-done.7.refs_3_
  57.3 1.0 collective-permute-done.6.refs_2_
  58.3 0.9 collective-permute-done.5.refs_1_
  59.2 0.0 collective-permute-start.9
  59.2 2.2 %collective-permute-done.9.recv_ref = bf16[4,576,128]{2,1,0:T(8,128)(2,1)S(1)} collective-permute-done((bf16[4,576,128]{2,1,0:T(8,128)(2,1)}, bf16[4,576,128]{2,1,0:T(8,128)(2,1)S(1)}, u32[]{:S(2)}, u32[]{:S(2)}) %collective-permute-start.9) | collective-permute-done | bytes 589856 | tf_op jit(solution)/shard_map/ppermute | solution.py:860
  61.4 0.0 copy-done.2
  61.5 0.0 copy-done.4
  61.5 4.6 %taps.1 = (bf16[2,16,64,128]{3,2,1,0:T(8,128)(2,1)S(1)}, bf16[2,16,64,128]{3,2,1,0:T(8,128)(2,1)S(1)}) custom-call(s32[1]{0:T(128)} %bitcast.dev_ref, s32[64]{0:T(128)S(1)} %copy-done.2, s32[16]{0:T(128)S(1)} %bitcast.13, bf16[2,576,128]{2,1,0:T(8,128)(2,1)S(1)} %get-tuple-element.76.refs_0_, bf16[2,576,128]{2,1,0:T(8,128)(2,1)S(1)} %collective-permute-done.5.refs_1_, ...), custom_call_target="tpu_custom_call" | custom-call | flops 2550136832 | bytes 4194304 | tf_op jit(solution)/shard_map/taps/pallas_call | solution.py:449
  66.1 0.2 collective-permute-start.10
  66.3 1.8 %collective-permute-done.10.recv_ref = bf16[2,16,64,128]{3,2,1,0:T(8,128)(2,1)S(1)} collective-permute-done((bf16[2,16,64,128]{3,2,1,0:T(8,128)(2,1)S(1)}, bf16[2,16,64,128]{3,2,1,0:T(8,128)(2,1)S(1)}, u32[]{:S(2)}, u32[]{:S(2)}) %collective-permute-start.10) | collective-permute-done | bytes 524320 | tf_op jit(solution)/shard_map/ppermute | solution.py:864
  68.1 0.1 halve.1
  68.2 0.1 collective-permute-start.11
  68.3 0.0 copy-done
  68.3 0.1 join.1
  68.4 2.7 %collective-permute-start.12 = (bf16[576,128]{1,0:T(8,128)(2,1)S(1)}, bf16[576,128]{1,0:T(8,128)(2,1)S(1)}, u32[]{:S(2)}, u32[]{:S(2)}) collective-permute-start(bf16[576,128]{1,0:T(8,128)(2,1)S(1)} %get-tuple-element.87), channel_id=1, source_target_pairs={{0,2},{1,3},{2,0},{3,1},{4,6},{5,7},{6,4},{7,5},{8,10},{9,11},{10,... | collective-permute-start | bytes 442376 | tf_op jit(solution)/shard_map/ppermute | solution.py:816
  71.2 1.7 %collective-permute-start.13 = (bf16[576,128]{1,0:T(8,128)(2,1)S(1)}, bf16[576,128]{1,0:T(8,128)(2,1)S(1)}, u32[]{:S(2)}, u32[]{:S(2)}) collective-permute-start(bf16[576,128]{1,0:T(8,128)(2,1)S(1)} %get-tuple-element.88), channel_id=1, source_target_pairs={{0,1},{1,2},{2,3},{3,0},{4,5},{5,6},{6,7},{7,4},{8,9},{9,10},{10,1... | collective-permute-start | bytes 442376 | tf_op jit(solution)/shard_map/ppermute | solution.py:816
  72.9 0.3 collective-permute-start.14
  73.2 3.5 %collective-permute-done.12.refs_3_ = bf16[576,128]{1,0:T(8,128)(2,1)S(1)} collective-permute-done((bf16[576,128]{1,0:T(8,128)(2,1)S(1)}, bf16[576,128]{1,0:T(8,128)(2,1)S(1)}, u32[]{:S(2)}, u32[]{:S(2)}) %collective-permute-start.12) | collective-permute-done | bytes 147488 | tf_op jit(solution)/shard_map/ppermute | solution.py:816
  76.7 2.3 %collective-permute-done.13.refs_4_ = bf16[576,128]{1,0:T(8,128)(2,1)S(1)} collective-permute-done((bf16[576,128]{1,0:T(8,128)(2,1)S(1)}, bf16[576,128]{1,0:T(8,128)(2,1)S(1)}, u32[]{:S(2)}, u32[]{:S(2)}) %collective-permute-start.13) | collective-permute-done | bytes 147488 | tf_op jit(solution)/shard_map/ppermute | solution.py:816
  79.0 0.0 collective-permute-done.14.refs_5_
  79.1 0.0 collective-permute-done.11.refs_1_
  79.1 0.2 cells.1
  79.3 28.9 %all_to_all.10.in_ref = bf16[16,96,128]{2,1,0:T(8,128)(2,1)S(1)} all-to-all(bf16[16,96,128]{2,1,0:T(8,128)(2,1)S(1)} %cells.1), channel_id=1, replica_groups={{0,16,32,48,64,80,96,112,128,144,160,176,192,208,224,240},{8,24,40,56,7..., dimensions={0} | all-to-all | bytes 786432 | tf_op jit(solution)/shard_map/all_to_all | solution.py:868
  108.2 0.1 total.1
  108.2 9.4 %all_to_all.11.in_ref = bf16[8,96,128]{2,1,0:T(8,128)(2,1)S(1)} all-to-all(bf16[8,96,128]{2,1,0:T(8,128)(2,1)S(1)} %total.1), channel_id=1, replica_groups=mesh['dp'=32,'mp'=8] {'mp'}, dimensions={0} | all-to-all | bytes 393216 | tf_op jit(solution)/shard_map/all_to_all | solution.py:869
  117.6 1.4 %finish.1 = (bf16[2,120,256]{2,1,0:T(8,128)(2,1)}, f32[4,120,120]{2,1,0:T(8,128)}, f32[32,512]{1,0:T(8,128)}, f32[16,120]{1,0:T(8,128)}, f32[5,16]{1,0:T(8,128)}) custom-call(s32[1]{0:T(128)} %bitcast.dev_ref, s32[64]{0:T(128)S(1)} %copy-done.2, s32[16]{0:T(128)S(1)} %bitcast.14, bf16[8,96,128]{2,1,0:T(8,128)(2,1)S(1)} %all_to_all.11.in_ref, ...), custom_call_target="tpu_custom_call" | custom-call | tf_op jit(solution)/shard_map/finish/pallas_call | solution.py:792
  (2 shorter events, 0.0 us)
Async XLA Ops:
  0.6 26.6 %copy-start.7 = (bf16[2,256,120]{1,2,0:T(8,128)(2,1)S(1)}, bf16[2,256,120]{1,2,0:T(8,128)(2,1)}, u32[]{:S(2)}) copy-start(bf16[2,256,120]{1,2,0:T(8,128)(2,1)} %param.15) | copy-start | bytes 368644
  0.6 26.6 %copy-start.1 = (s32[64]{0:T(128)S(1)}, s32[64]{0:T(128)}, u32[]{:S(2)}) copy-start(s32[64]{0:T(128)} %len_ref.9) | copy-start | bytes 772
  0.7 26.6 %copy-start.3 = (s32[16,1]{0,1:T(1,128)S(1)}, s32[16,1]{0,1:T(1,128)}, u32[]{:S(2)}) copy-start(s32[16,1]{0,1:T(1,128)} %param.10) | copy-start | bytes 196
  0.7 26.5 %collective-permute-start.2 = (bf16[2,120,256]{2,1,0:T(8,128)(2,1)}, bf16[2,120,256]{2,1,0:T(8,128)(2,1)S(1)}, u32[]{:S(2)}, u32[]{:S(2)}) collective-permute-start(bf16[2,120,256]{2,1,0:T(8,128)(2,1)} %bitcast.16), channel_id=1, source_target_pairs={{0,128},{8,136},{16,144},{24,152},{32,160},{40,168},{48,176},{56,1... | collective-permute-start | bytes 368648 | tf_op jit(solution)/shard_map/ppermute | solution.py:833
  12.2 15.0 %collective-permute-start = (bf16[2,64,128]{2,1,0:T(8,128)(2,1)}, bf16[2,64,128]{2,1,0:T(8,128)(2,1)S(1)}, u32[]{:S(2)}, u32[]{:S(2)}) collective-permute-start(bf16[2,64,128]{2,1,0:T(8,128)(2,1)} %get-tuple-element.53), channel_id=1, source_target_pairs={{0,1},{1,2},{2,3},{3,4},{4,5},{5,6},{6,7},{8,9},{9,10},{10,11},{11... | collective-permute-start | bytes 98312 | tf_op jit(solution)/shard_map/ppermute | solution.py:811
  14.5 12.6 %collective-permute-start.1 = (bf16[2,64,128]{2,1,0:T(8,128)(2,1)}, bf16[2,64,128]{2,1,0:T(8,128)(2,1)S(1)}, u32[]{:S(2)}, u32[]{:S(2)}) collective-permute-start(bf16[2,64,128]{2,1,0:T(8,128)(2,1)} %get-tuple-element.54), channel_id=1, source_target_pairs={{1,0},{2,1},{3,2},{4,3},{5,4},{6,5},{7,6},{9,8},{10,9},{11,10},{12... | collective-permute-start | bytes 98312 | tf_op jit(solution)/shard_map/ppermute | solution.py:811
  27.2 5.5 %copy-start.8 = (bf16[2,120,256]{2,1,0:T(8,128)(2,1)}, bf16[2,120,256]{2,1,0:T(8,128)(2,1)S(1)}, u32[]{:S(2)}) copy-start(bf16[2,120,256]{2,1,0:T(8,128)(2,1)S(1)} %collective-permute-done.2.recv_ref) | copy-start | bytes 368644
  27.2 2.2 %copy-start.5 = (bf16[16,128,1024]{2,1,0:T(8,128)(2,1)S(1)}, bf16[16,128,1024]{2,1,0:T(8,128)(2,1)}, u32[]{:S(2)}) copy-start(bf16[16,128,1024]{2,1,0:T(8,128)(2,1)} %get-tuple-element.55) | copy-start | bytes 12582916
  29.4 0.9 copy-start.6
  32.7 0.7 copy-start.9
  33.4 6.0 %collective-permute-start.3 = (bf16[2,64,128]{2,1,0:T(8,128)(2,1)S(1)}, bf16[2,64,128]{2,1,0:T(8,128)(2,1)S(1)}, u32[]{:S(2)}, u32[]{:S(2)}) collective-permute-start(bf16[2,64,128]{2,1,0:T(8,128)(2,1)S(1)} %get-tuple-element.58), channel_id=1, source_target_pairs={{0,1},{1,2},{2,3},{3,4},{4,5},{5,6},{6,7},{8,9},{9,10},{10,11},{11... | collective-permute-start | bytes 98312 | tf_op jit(solution)/shard_map/ppermute | solution.py:811
  35.3 5.8 %collective-permute-start.4 = (bf16[2,64,128]{2,1,0:T(8,128)(2,1)S(1)}, bf16[2,64,128]{2,1,0:T(8,128)(2,1)S(1)}, u32[]{:S(2)}, u32[]{:S(2)}) collective-permute-start(bf16[2,64,128]{2,1,0:T(8,128)(2,1)S(1)} %get-tuple-element.59), channel_id=1, source_target_pairs={{1,0},{2,1},{3,2},{4,3},{5,4},{6,5},{7,6},{9,8},{10,9},{11,10},{12... | collective-permute-start | bytes 98312 | tf_op jit(solution)/shard_map/ppermute | solution.py:811
  39.2 18.1 %collective-permute-start.8 = (bf16[120,256]{1,0:T(8,128)(2,1)S(1)}, bf16[120,256]{1,0:T(8,128)(2,1)S(1)}, u32[]{:S(2)}, u32[]{:S(2)}) collective-permute-start(bf16[120,256]{1,0:T(8,128)(2,1)S(1)} %get-tuple-element.70), channel_id=1, source_target_pairs={{0,128},{8,136},{16,144},{24,152},{32,160},{40,168},{48,176},{56,1... | collective-permute-start | bytes 184328 | tf_op jit(solution)/shard_map/ppermute | solution.py:841
  39.3 9.6 %copy-start.10 = (bf16[2,64,128]{2,1,0:T(8,128)(2,1)}, bf16[2,64,128]{2,1,0:T(8,128)(2,1)S(1)}, u32[]{:S(2)}) copy-start(bf16[2,64,128]{2,1,0:T(8,128)(2,1)S(1)} %collective-permute-done.3.low_ref) | copy-start | bytes 98308
  41.1 7.8 %copy-start.11 = (bf16[2,64,128]{2,1,0:T(8,128)(2,1)}, bf16[2,64,128]{2,1,0:T(8,128)(2,1)S(1)}, u32[]{:S(2)}) copy-start(bf16[2,64,128]{2,1,0:T(8,128)(2,1)S(1)} %collective-permute-done.4.high_ref) | copy-start | bytes 98308
  41.1 16.2 %collective-permute-start.7 = (bf16[2,576,128]{2,1,0:T(8,128)(2,1)S(1)}, bf16[2,576,128]{2,1,0:T(8,128)(2,1)S(1)}, u32[]{:S(2)}, u32[]{:S(2)}) collective-permute-start(bf16[2,576,128]{2,1,0:T(8,128)(2,1)S(1)} %get-tuple-element.76.refs_0_), channel_id=1, source_target_pairs={{0,3},{1,0},{2,1},{3,2},{4,7},{5,4},{6,5},{7,6},{8,11},{9,8},{10,9... | collective-permute-start | bytes 884744 | tf_op jit(solution)/shard_map/ppermute | solution.py:816
  43.1 15.2 %collective-permute-start.6 = (bf16[2,576,128]{2,1,0:T(8,128)(2,1)S(1)}, bf16[2,576,128]{2,1,0:T(8,128)(2,1)S(1)}, u32[]{:S(2)}, u32[]{:S(2)}) collective-permute-start(bf16[2,576,128]{2,1,0:T(8,128)(2,1)S(1)} %get-tuple-element.76.refs_0_), channel_id=1, source_target_pairs={{0,2},{1,3},{2,0},{3,1},{4,6},{5,7},{6,4},{7,5},{8,10},{9,11},{10,... | collective-permute-start | bytes 884744 | tf_op jit(solution)/shard_map/ppermute | solution.py:816
  46.3 13.0 %collective-permute-start.5 = (bf16[2,576,128]{2,1,0:T(8,128)(2,1)S(1)}, bf16[2,576,128]{2,1,0:T(8,128)(2,1)S(1)}, u32[]{:S(2)}, u32[]{:S(2)}) collective-permute-start(bf16[2,576,128]{2,1,0:T(8,128)(2,1)S(1)} %get-tuple-element.76.refs_0_), channel_id=1, source_target_pairs={{0,1},{1,2},{2,3},{3,0},{4,5},{5,6},{6,7},{7,4},{8,9},{9,10},{10,1... | collective-permute-start | bytes 884744 | tf_op jit(solution)/shard_map/ppermute | solution.py:816
  48.9 12.5 %copy-start.2 = (s32[64]{0:T(128)S(1)}, s32[64]{0:T(128)}, u32[]{:S(2)}) copy-start(s32[64]{0:T(128)} %len_ref.9) | copy-start | bytes 772
  48.9 12.5 %copy-start.4 = (s32[16,1]{0,1:T(1,128)S(1)}, s32[16,1]{0,1:T(1,128)}, u32[]{:S(2)}) copy-start(s32[16,1]{0,1:T(1,128)} %param.10) | copy-start | bytes 196
  59.2 9.1 %copy-start = (bf16[4,576,128]{2,1,0:T(8,128)(2,1)S(1)}, bf16[4,576,128]{2,1,0:T(8,128)(2,1)}, u32[]{:S(2)}) copy-start(bf16[4,576,128]{2,1,0:T(8,128)(2,1)} %get-tuple-element.84.keep_ref) | copy-start | bytes 1769476
  59.2 2.2 %collective-permute-start.9 = (bf16[4,576,128]{2,1,0:T(8,128)(2,1)}, bf16[4,576,128]{2,1,0:T(8,128)(2,1)S(1)}, u32[]{:S(2)}, u32[]{:S(2)}) collective-permute-start(bf16[4,576,128]{2,1,0:T(8,128)(2,1)} %get-tuple-element.71), channel_id=1, source_target_pairs={{0,8},{8,0},{16,24},{24,16},{32,40},{40,32},{48,56},{56,48},{64,72... | collective-permute-start | bytes 1769480 | tf_op jit(solution)/shard_map/ppermute | solution.py:860
  66.1 2.0 %collective-permute-start.10 = (bf16[2,16,64,128]{3,2,1,0:T(8,128)(2,1)S(1)}, bf16[2,16,64,128]{3,2,1,0:T(8,128)(2,1)S(1)}, u32[]{:S(2)}, u32[]{:S(2)}) collective-permute-start(bf16[2,16,64,128]{3,2,1,0:T(8,128)(2,1)S(1)} %get-tuple-element.81), channel_id=1, source_target_pairs={{0,8},{8,0},{16,24},{24,16},{32,40},{40,32},{48,56},{56,48},{64,72... | collective-permute-start | bytes 1572872 | tf_op jit(solution)/shard_map/ppermute | solution.py:864
  68.2 10.9 %collective-permute-start.11 = (bf16[16,64,128]{2,1,0:T(8,128)(2,1)S(1)}, bf16[16,64,128]{2,1,0:T(8,128)(2,1)S(1)}, u32[]{:S(2)}, u32[]{:S(2)}) collective-permute-start(bf16[16,64,128]{2,1,0:T(8,128)(2,1)S(1)} %get-tuple-element.83), channel_id=1, source_target_pairs={{0,4},{1,5},{2,6},{3,7},{4,0},{5,1},{6,2},{7,3},{8,12},{9,13},{10,... | collective-permute-start | bytes 786440 | tf_op jit(solution)/shard_map/ppermute | solution.py:865
  68.4 8.3 %collective-permute-start.12 = (bf16[576,128]{1,0:T(8,128)(2,1)S(1)}, bf16[576,128]{1,0:T(8,128)(2,1)S(1)}, u32[]{:S(2)}, u32[]{:S(2)}) collective-permute-start(bf16[576,128]{1,0:T(8,128)(2,1)S(1)} %get-tuple-element.87), channel_id=1, source_target_pairs={{0,2},{1,3},{2,0},{3,1},{4,6},{5,7},{6,4},{7,5},{8,10},{9,11},{10,... | collective-permute-start | bytes 442376 | tf_op jit(solution)/shard_map/ppermute | solution.py:816
  71.2 7.9 %collective-permute-start.13 = (bf16[576,128]{1,0:T(8,128)(2,1)S(1)}, bf16[576,128]{1,0:T(8,128)(2,1)S(1)}, u32[]{:S(2)}, u32[]{:S(2)}) collective-permute-start(bf16[576,128]{1,0:T(8,128)(2,1)S(1)} %get-tuple-element.88), channel_id=1, source_target_pairs={{0,1},{1,2},{2,3},{3,0},{4,5},{5,6},{6,7},{7,4},{8,9},{9,10},{10,1... | collective-permute-start | bytes 442376 | tf_op jit(solution)/shard_map/ppermute | solution.py:816
  72.9 6.2 %collective-permute-start.14 = (bf16[576,128]{1,0:T(8,128)(2,1)S(1)}, bf16[576,128]{1,0:T(8,128)(2,1)S(1)}, u32[]{:S(2)}, u32[]{:S(2)}) collective-permute-start(bf16[576,128]{1,0:T(8,128)(2,1)S(1)} %get-tuple-element.89), channel_id=1, source_target_pairs={{0,3},{1,0},{2,1},{3,2},{4,7},{5,4},{6,5},{7,6},{8,11},{9,8},{10,9... | collective-permute-start | bytes 442376 | tf_op jit(solution)/shard_map/ppermute | solution.py:816

commit v7 on v6

--- a/solution.py
+++ b/solution.py
@@ -28,7 +28,7 @@
 DP = 32
 X = 4
 CELLS = 16
-PIECE = 2 * T + REACH
+PIECE = T + REACH
 HALF = GC // 2
 SPARE = REACH - HALF
 CONV_ROWS = CELLS * 32
@@ -39,6 +39,7 @@
 
 VMEM = pl.BlockSpec(memory_space=pltpu.VMEM)
 SMEM = pl.BlockSpec(memory_space=pltpu.SMEM)
+HBM = pl.BlockSpec(memory_space=pltpu.HBM)
 
 
 def params(mebibytes):
@@ -70,7 +71,7 @@
 
 
 class Place:
-    def __init__(self, dev_ref, len_ref, mov_ref):
+    def __init__(self, dev_ref, len_ref, mov_ref=None):
         self.data = dev_ref[0] // MP
         self.model = lax.rem(dev_ref[0], MP)
         self.x = lax.rem(self.model, X)
@@ -79,7 +80,8 @@
         self.cell = self.data // 2
         self.first = self.model * T
         self.lengths = len_ref
-        self.chosen = mov_ref[lax.rem(self.data, DP // 2)]
+        if mov_ref is not None:
+            self.chosen = mov_ref[lax.rem(self.data, DP // 2)]
 
     def length(self, slot):
         return self.lengths[self.data * SLOTS + slot]
@@ -104,12 +106,29 @@
     return pl.BlockSpec(dims, lambda s: (0,) * len(dims), pipeline_mode=pl.Buffered(1))
 
 
-def turn_body(in_ref, ahead_ref, behind_ref, rows):
+def turn_body(in_ref, ahead_ref, behind_ref, rows, held, sems):
     block = pl.program_id(0)
-    blocks = pl.num_programs(0)
+    blocks = LANES // NEAR
+
+    def fetch(n):
+        count = min(NEAR, GC - n * NEAR)
+        part = pl.ds(n * NEAR, count)
+        return pltpu.make_async_copy(in_ref.at[part], held.at[part], sems.at[n])
+
+    @pl.when(block == 0)
+    def _():
+        for n in range(blocks):
+            fetch(n).start()
+
+    for n in range(blocks):
+
+        @pl.when(block == n)
+        def _():
+            fetch(n).wait()
+
     for n in range(NEAR):
         tile = jnp.concatenate(
-            [in_ref[n].astype(f32), jnp.zeros((LANES - GC, K), f32)], axis=0
+            [held[block * NEAR + n].astype(f32), jnp.zeros((LANES - GC, K), f32)], axis=0
         ).T
         if n >= GC % NEAR:
             tile = jnp.where(block == blocks - 1, 0.0, tile)
@@ -133,13 +152,17 @@
             jax.ShapeDtypeStruct((NEAR, LANES, far * LANES), bf16),
             jax.ShapeDtypeStruct((far, LANES, NEAR * LANES), bf16),
         ),
-        in_specs=[pl.BlockSpec((NEAR, GC, K), lambda b: (b, 0, 0))],
+        in_specs=[HBM],
         out_specs=(
             pl.BlockSpec((NEAR, NEAR, far * LANES), lambda b: (0, b, 0)),
             pl.BlockSpec((far, NEAR, NEAR * LANES), lambda b: (0, b, 0)),
         ),
-        scratch_shapes=[pltpu.VMEM((K * NEAR, LANES), f32)],
-        compiler_params=params(56),
+        scratch_shapes=[
+            pltpu.VMEM((K * NEAR, LANES), f32),
+            pltpu.VMEM((LANES, GC, K), bf16),
+            pltpu.SemaphoreType.DMA((LANES // NEAR,)),
+        ],
+        compiler_params=params(16),
         cost_estimate=cost(0, 12 << 20),
         name="turn",
     )(pos)
@@ -148,12 +171,11 @@
 
 def encode_body(
     dev_ref,
-    len_ref,
-    mov_ref,
-    audio_ref,
-    conv_ref,
-    chan_ref,
-    proj_ref,
+    len_hbm,
+    audio_hbm,
+    conv_hbm,
+    chan_hbm,
+    proj_hbm,
     feat_ref,
     tail_ref,
     head_ref,
@@ -166,21 +188,46 @@
     proj,
     mid,
     normed,
+    len_ref,
+    audio_ref,
+    conv_ref,
+    chan_ref,
+    sems,
 ):
-    place = Place(dev_ref, len_ref, mov_ref)
     slot = pl.program_id(0)
+    copies = [
+        pltpu.make_async_copy(source, target, sems.at[n])
+        for n, (source, target) in enumerate(
+            (
+                (len_hbm, len_ref),
+                (audio_hbm.at[0], audio_ref.at[0]),
+                (conv_hbm, conv_ref),
+                (chan_hbm, chan_ref),
+                (proj_hbm, proj.at[pl.ds(0, GC)]),
+                (audio_hbm.at[1], audio_ref.at[1]),
+            )
+        )
+    ]
 
     @pl.when(slot == 0)
     def _():
-        proj[...] = jnp.zeros_like(proj)
-        proj[:GC, :] = proj_ref[...]
-
+        proj[GC - 8 :, :] = jnp.zeros((LANES - GC + 8, C), bf16)
+        for copy in copies:
+            copy.start()
+        for copy in copies[:-1]:
+            copy.wait()
+
+    @pl.when(slot == SLOTS - 1)
+    def _():
+        copies[-1].wait()
+
+    place = Place(dev_ref, len_ref)
     living = place.alive(slot)
 
     @pl.when(living)
     def _():
         for c in range(C // LANES):
-            wide[c] = audio_ref[0, :, c * LANES : (c + 1) * LANES].astype(f32)
+            wide[c] = audio_ref[slot, :, c * LANES : (c + 1) * LANES].astype(f32)
             for tap in range(2):
                 at = tap * C + c * LANES
                 pair_ref[0, :, at : at + LANES] = wide[c, pl.ds(tap, T, stride=2), :].astype(bf16)
@@ -235,13 +282,7 @@
             jax.ShapeDtypeStruct((SLOTS, T, C), bf16),
             jax.ShapeDtypeStruct((SLOTS, T, 2 * LANES), f32),
         ),
-        in_specs=[SMEM] * 3
-        + [
-            by_slot(2 * T, C),
-            once(2 * C, C),
-            whole(5, C),
-            whole(GC, C),
-        ],
+        in_specs=[SMEM] + [HBM] * 5,
         out_specs=(
             by_slot(T, LANES),
             by_slot(REACH, LANES),
@@ -257,11 +298,16 @@
             pltpu.VMEM((LANES, C), bf16),
             pltpu.VMEM((T, C), f32),
             pltpu.VMEM((T, C), bf16),
+            pltpu.SMEM((DP * SLOTS,), jnp.int32),
+            pltpu.VMEM((SLOTS, 2 * T, C), bf16),
+            pltpu.VMEM((2 * C, C), bf16),
+            pltpu.VMEM((5, C), f32),
+            pltpu.SemaphoreType.DMA((6,)),
         ],
-        compiler_params=params(56),
+        compiler_params=params(50),
         cost_estimate=cost(2 * SLOTS * T * C * (2 * C + LANES), 8 << 20, SLOTS * T * C * 2),
         name="encode",
-    )(*place, audio, conv_weight, channels, proj)
+    )(*place[:2], audio, conv_weight, channels, proj)
 
 
 def fill_ext(ext, low, own, high):
@@ -334,9 +380,8 @@
         slopes = jnp.where(mask, back * (below + mixed * bell(mixed)), 0.0)
         slopes_ref[0] = slopes.astype(bf16)
         edge = jnp.where(place.x < X // 2, low_ref[0].astype(f32), high_ref[0].astype(f32))
-        piece_ref[0, :T, :] = feat_ref[0]
-        piece_ref[0, T : T + REACH, :] = edge.astype(bf16)
-        piece_ref[0, T + REACH :, :] = slopes.astype(bf16)
+        piece_ref[0, :T, :] = slopes.astype(bf16)
+        piece_ref[0, T:, :] = edge.astype(bf16)
 
     @pl.when(jnp.logical_not(living))
     def _():
@@ -393,8 +438,8 @@
 
 
 def taps_body(scale, dev_ref, len_ref, mov_ref, *refs):
-    piece_refs, (keep_ref, send_ref) = refs[:X], refs[X : X + 2]
-    ext, windows, turned, sums = refs[X + 2 :]
+    feat_refs, piece_refs, (keep_ref, send_ref) = refs[:X], refs[X : 2 * X], refs[2 * X : 2 * X + 2]
+    ext, windows, turned, sums = refs[2 * X + 2 :]
     place = Place(dev_ref, len_ref, mov_ref)
     slot = pl.program_id(0)
     spread = X * T
@@ -406,19 +451,19 @@
 
     @pl.when(place.y * spread < place.length(slot))
     def _():
-        for step, piece_ref in enumerate(piece_refs):
+        for step, (feat_ref, piece_ref) in enumerate(zip(feat_refs, piece_refs)):
             x = lax.rem(place.x + (X - step), X)
             at = pl.multiple_of(x * T, T)
-            ext[pl.ds(REACH + at, T), :] = piece_ref[0, :T, :].astype(f32)
-            turned[:, pl.ds(at, T)] = piece_ref[0, T + REACH :, :].astype(f32).T.astype(bf16)
+            ext[pl.ds(REACH + at, T), :] = feat_ref[0].astype(f32)
+            turned[:, pl.ds(at, T)] = piece_ref[0, :T, :].astype(f32).T.astype(bf16)
 
             @pl.when(x == 0)
             def _():
-                ext[:REACH, :] = piece_ref[0, T : T + REACH, :].astype(f32)
+                ext[:REACH, :] = piece_ref[0, T:, :].astype(f32)
 
             @pl.when(x == X - 1)
             def _():
-                ext[REACH + spread :, :] = piece_ref[0, T : T + REACH, :].astype(f32)
+                ext[REACH + spread :, :] = piece_ref[0, T:, :].astype(f32)
 
         for j in range(4):
             windows[:, j * LANES : (j + 1) * LANES] = ext[
@@ -443,14 +488,14 @@
                     send_ref[y, 2 * q + far] = send[rows, :].astype(bf16)
 
 
-def taps(scale, place, pieces):
+def taps(scale, place, features, pieces):
     shape = jax.ShapeDtypeStruct((2, CELLS, REACH, LANES), bf16)
     spread = X * T
     return pl.pallas_call(
         functools.partial(taps_body, scale),
         grid=(SLOTS,),
         out_shape=(shape,) * 2,
-        in_specs=[SMEM] * 3 + [by_slot(PIECE, LANES)] * X,
+        in_specs=[SMEM] * 3 + [by_slot(T, LANES)] * X + [by_slot(PIECE, LANES)] * X,
         out_specs=(whole(*shape.shape),) * 2,
         scratch_shapes=[
             pltpu.VMEM((spread + 2 * REACH, LANES), f32),
@@ -461,7 +506,7 @@
         compiler_params=params(16),
         cost_estimate=cost(2 * SLOTS * SPAN * K * LANES * LANES, 4 << 20),
         name="taps",
-    )(*place, *pieces)
+    )(*place, *features, *pieces)
 
 
 def backward_body(
@@ -642,7 +687,7 @@
             pltpu.VMEM((40, C), f32),
             pltpu.VMEM((LANES, C), f32),
         ],
-        compiler_params=params(56),
+        compiler_params=params(30),
         cost_estimate=cost(
             2 * SLOTS * (SPAN * K * LANES * LANES + T * C * (4 * C + 2 * LANES)), 14 << 20
         ),
@@ -816,6 +861,11 @@
     return lax.ppermute(block, "mp", route)
 
 
+def around_x(block):
+    far = along_x(block, 2)
+    return (block, along_x(block, 1), far, along_x(block, 3))
+
+
 def per_device(
     audio, lengths, moved_slots, conv_weight, channel_params, proj_weight, pos_weight, cotangent
 ):
@@ -833,15 +883,17 @@
     received = lax.ppermute(cot, "dp", swap)
     features, tail, head, *stored = encode(place, audio, conv_weight, channels, proj)
     low, high = neighbours(tail, head)
+    all_features = around_x(features)
     ahead, behind = turn(pos_weight.transpose(1, 2, 0))
     states, sent, slopes, tail, head, piece = mix(
         place, features, low, high, ahead, cot, received
     )
     low, high = neighbours(tail, head)
     other = lax.ppermute(sent, "dp", swap)
-    piece, low, high = lax.optimization_barrier((piece, low, high))
-    far = along_x(piece, 2)
-    pieces = (piece, along_x(piece, 1), far, along_x(piece, 3))
+    piece, low, high, all_features = lax.optimization_barrier(
+        (piece, low, high, all_features)
+    )
+    pieces = around_x(piece)
     audio_grad, keep, send = backward(
         scale,
         place,
@@ -856,11 +908,11 @@
         channels,
         proj,
     )
-    send, pieces, other = lax.optimization_barrier((send, pieces, other))
-    recv, pieces = lax.optimization_barrier((lax.ppermute(send, "dp", core_swap), pieces))
-    chunks = join(dev, keep, recv)
+    send, other, pieces = lax.optimization_barrier((send, other, pieces))
+    chunks = join(dev, keep, lax.ppermute(send, "dp", core_swap))
+    chunks, pieces = lax.optimization_barrier((chunks, pieces))
     rest_parts = [chunks[0]] + [along_x(chunks[step], step) for step in (2, 1, 3)]
-    pos_keep, pos_send = taps(scale, place, pieces)
+    pos_keep, pos_send = taps(scale, place, all_features, pieces)
     stay, leave = halve(dev, pos_keep, lax.ppermute(pos_send, "dp", core_swap))
     pos_parts = (stay, lax.ppermute(leave, "mp", [(i, i ^ X) for i in range(MP)]))
     cells = make_cells(pos_parts, rest_parts)

time: 120 us -> 113 us (0.942)
  Pallas kernels: 30.5 us -> 18.5 us
  starting transfers between devices: 32 us -> 42.3 us
  blocking collectives: 38.3 us -> 32 us
  waiting for transfers between devices: 13.6 us -> 15.2 us
    all_to_all x1, blocking collectives: 28.9 us -> 22.4 us  [per_device(): lax.all_to_all(cells, 'dp', 0, 0, axis_index_groups=groups, tiled=True)]
    pallas_call x1, Pallas kernels: 8.32 us -> 2.03 us  [backward(): pl.pallas_call(functools.partial(backward_body, scale), grid=(SLOTS,), ou...]
    ppermute x1, starting transfers between devices: 0.01 us -> 5.17 us  [per_device(): chunks = join(dev, keep, lax.ppermute(send, 'dp', core_swap))]
    ppermute x6 -> x9, waiting for transfers between devices: 7.85 us -> 10.5 us  [along_x(): return lax.ppermute(block, 'mp', route)]
    pallas_call x1, Pallas kernels: 4.22 us -> 1.67 us  [encode(): pl.pallas_call(encode_body, grid=(SLOTS,), out_shape=(jax.ShapeDtypeStruc...]
    ppermute x6 -> x9, starting transfers between devices: 12.6 us -> 14.8 us  [along_x(): return lax.ppermute(block, 'mp', route)]
    ppermute x2, starting transfers between devices: 7.37 us -> 8.98 us  [neighbours(): lax.ppermute(head, 'mp', backward_route)]
    pallas_call x1, Pallas kernels: 2.33 us -> 0.73 us  [mix(): pl.pallas_call(mix_body, grid=(SLOTS,), out_shape=(jax.ShapeDtypeStruct((...]
  transfers between devices with their start and end apart: 15 -> 18, of which waited for: 7 -> 7; matrix products, arithmetic and copies ran while one was open for 0% -> 0% of each run, Pallas kernels for 18% -> 11%
where the time goes in v7:
time: 113 us
  starting transfers between devices  42.3 us (37%)
  blocking collectives  32 us (28%)
  Pallas kernels  18.5 us (16%)
  waiting for transfers between devices  15.2 us (13%)
  local copies, waits for them, and re-layouts  4.33 us (4%)
    all_to_all x1, blocking collectives, per_device(): lax.all_to_all(cells, 'dp', 0, 0, axis_index_groups=groups, tiled=True)  22.4 us
    ppermute x9, starting transfers between devices, along_x(): return lax.ppermute(block, 'mp', route)  14.8 us
    ppermute x9, waiting for transfers between devices, along_x(): return lax.ppermute(block, 'mp', route)  10.5 us
    all_to_all x1, blocking collectives, per_device(): cells = lax.all_to_all(total(cells), 'mp', 0, 0, tiled=True)  9.57 us
    ppermute x2, starting transfers between devices, neighbours(): lax.ppermute(head, 'mp', backward_route)  8.98 us
    pallas_call x1, Pallas kernels, turn(): pl.pallas_call(turn_body, grid=(LANES // NEAR,), out_shape=(jax.ShapeDtyp...  7.57 us
    ppermute x1, starting transfers between devices, per_device(): received = lax.ppermute(cot, 'dp', swap)  7.28 us
    ppermute x2, starting transfers between devices, neighbours(): lax.ppermute(tail, 'mp', forward)  5.32 us
  transfers between devices with their start and end apart: 18, of which 7 were waited for; matrix products, arithmetic and copies ran while one was open for 0% of the time, Pallas kernels for 11%

profile of v7, /device:TPU:2, one launch (start us, length us, event | category | flops | bytes accessed | tf_op | source)
XLA Modules:
  0.0 113.1 jit_solution(6651275506124739442)
XLA Ops:
  0.6 0.0 copy-start.5
  0.6 7.3 %collective-permute-start.2 = (bf16[2,120,256]{2,1,0:T(8,128)(2,1)}, bf16[2,120,256]{2,1,0:T(8,128)(2,1)S(1)}, u32[]{:S(2)}, u32[]{:S(2)}) collective-permute-start(bf16[2,120,256]{2,1,0:T(8,128)(2,1)} %bitcast.21), channel_id=1, source_target_pairs={{0,128},{8,136},{16,144},{24,152},{32,160},{40,168},{48,176},{56,1... | collective-permute-start | bytes 368648 | tf_op jit(solution)/shard_map/ppermute | solution.py:883
  7.9 0.0 copy-start.2
  7.9 0.9 copy-done.2
  8.8 0.0 copy-start.3
  8.8 0.7 copy-done.3
  9.5 0.0 copy-start.4
  9.5 0.7 copy-done.4
  10.2 0.0 copy-start.6
  10.2 1.7 %encode.1 = (bf16[2,256,128]{2,1,0:T(8,128)(2,1)S(1)}, bf16[2,64,128]{2,1,0:T(8,128)(2,1)S(1)}, bf16[2,64,128]{2,1,0:T(8,128)(2,1)S(1)}, bf16[2,256,1024]{2,1,0:...) custom-call(s32[1]{0:T(128)} %bitcast.dev_ref, ...), custom_call_target="tpu_custom_call" | custom-call | flops 603979776 | bytes 8388608 | tf_op jit(solution)/shard_map/encode/pallas_call | solution.py:272
  11.9 3.4 %collective-permute-start = (bf16[2,64,128]{2,1,0:T(8,128)(2,1)S(1)}, bf16[2,64,128]{2,1,0:T(8,128)(2,1)S(1)}, u32[]{:S(2)}, u32[]{:S(2)}) collective-permute-start(bf16[2,64,128]{2,1,0:T(8,128)(2,1)S(1)} %get-tuple-element.60), channel_id=1, source_target_pairs={{0,1},{1,2},{2,3},{3,4},{4,5},{5,6},{6,7},{8,9},{9,10},{10,11},{11... | collective-permute-start | bytes 98312 | tf_op jit(solution)/shard_map/ppermute | solution.py:856
  15.3 3.0 %collective-permute-start.1 = (bf16[2,64,128]{2,1,0:T(8,128)(2,1)S(1)}, bf16[2,64,128]{2,1,0:T(8,128)(2,1)S(1)}, u32[]{:S(2)}, u32[]{:S(2)}) collective-permute-start(bf16[2,64,128]{2,1,0:T(8,128)(2,1)S(1)} %get-tuple-element.61), channel_id=1, source_target_pairs={{1,0},{2,1},{3,2},{4,3},{5,4},{6,5},{7,6},{9,8},{10,9},{11,10},{12... | collective-permute-start | bytes 98312 | tf_op jit(solution)/shard_map/ppermute | solution.py:856
  18.3 1.0 collective-permute-start.5
  19.3 0.7 collective-permute-start.6
  20.0 0.0 copy-start
  20.0 2.0 %copy-done = bf16[128,120,120]{0,2,1:T(8,128)(2,1)S(1)} copy-done((bf16[128,120,120]{0,2,1:T(8,128)(2,1)S(1)}, bf16[128,120,120]{0,2,1:T(8,128)(2,1)}, u32[]{:S(2)}) %copy-start) | copy-done | bytes 3686424
  22.1 7.6 %turn.1 = (bf16[16,128,1024]{2,1,0:T(8,128)(2,1)S(1)}, bf16[8,128,2048]{2,1,0:T(8,128)(2,1)S(1)}) custom-call(bf16[120,120,128]{2,1,0:T(8,128)(2,1)S(1)} %bitcast.10), custom_call_target="tpu_custom_call" | custom-call | bytes 12582912 | tf_op jit(solution)/shard_map/turn/pallas_call | solution.py:148
  29.6 0.0 collective-permute-done.low_ref
  29.7 2.6 %collective-permute-start.7 = (bf16[2,256,128]{2,1,0:T(8,128)(2,1)S(1)}, bf16[2,256,128]{2,1,0:T(8,128)(2,1)S(1)}, u32[]{:S(2)}, u32[]{:S(2)}) collective-permute-start(bf16[2,256,128]{2,1,0:T(8,128)(2,1)S(1)} %get-tuple-element.66.feat_ref.refs_0_), channel_id=1, source_target_pairs={{0,3},{1,0},{2,1},{3,2},{4,7},{5,4},{6,5},{7,6},{8,11},{9,8},{10,9... | collective-permute-start | bytes 393224 | tf_op jit(solution)/shard_map/ppermute | solution.py:861
  32.3 0.0 collective-permute-done.1.high_ref
  32.3 0.0 collective-permute-done.2.recv_ref
  32.3 0.0 copy-done.5
  32.3 0.0 copy-done.6
  32.3 0.0 copy-start.1
  32.3 0.7 mix.1
  33.0 1.9 %collective-permute-start.3 = (bf16[2,64,128]{2,1,0:T(8,128)(2,1)S(1)}, bf16[2,64,128]{2,1,0:T(8,128)(2,1)S(1)}, u32[]{:S(2)}, u32[]{:S(2)}) collective-permute-start(bf16[2,64,128]{2,1,0:T(8,128)(2,1)S(1)} %get-tuple-element.64), channel_id=1, source_target_pairs={{0,1},{1,2},{2,3},{3,4},{4,5},{5,6},{6,7},{8,9},{9,10},{10,11},{11... | collective-permute-start | bytes 98312 | tf_op jit(solution)/shard_map/ppermute | solution.py:856
  35.0 6.0 %collective-permute-start.4 = (bf16[2,64,128]{2,1,0:T(8,128)(2,1)S(1)}, bf16[2,64,128]{2,1,0:T(8,128)(2,1)S(1)}, u32[]{:S(2)}, u32[]{:S(2)}) collective-permute-start(bf16[2,64,128]{2,1,0:T(8,128)(2,1)S(1)} %get-tuple-element.65), channel_id=1, source_target_pairs={{1,0},{2,1},{3,2},{4,3},{5,4},{6,5},{7,6},{9,8},{10,9},{11,10},{12... | collective-permute-start | bytes 98312 | tf_op jit(solution)/shard_map/ppermute | solution.py:856
  41.0 0.0 collective-permute-done.5.refs_1_
  41.0 0.1 collective-permute-start.8
  41.1 0.0 collective-permute-done.6.refs_2_
  41.1 0.0 collective-permute-done.7.refs_3_
  41.1 0.0 collective-permute-done.3.low_ref
  41.1 1.4 %collective-permute-done.4.high_ref = bf16[2,64,128]{2,1,0:T(8,128)(2,1)S(1)} collective-permute-done((bf16[2,64,128]{2,1,0:T(8,128)(2,1)S(1)}, bf16[2,64,128]{2,1,0:T(8,128)(2,1)S(1)}, u32[]{:S(2)}, u32[]{:S(2)}) %collective-permute-start.4) | collective-permute-done | bytes 32800 | tf_op jit(solution)/shard_map/ppermute | solution.py:856
  42.5 4.9 %collective-permute-start.10 = (bf16[2,320,128]{2,1,0:T(8,128)(2,1)S(1)}, bf16[2,320,128]{2,1,0:T(8,128)(2,1)S(1)}, u32[]{:S(2)}, u32[]{:S(2)}) collective-permute-start(bf16[2,320,128]{2,1,0:T(8,128)(2,1)S(1)} %get-tuple-element.92.refs_4_), channel_id=1, source_target_pairs={{0,2},{1,3},{2,0},{3,1},{4,6},{5,7},{6,4},{7,5},{8,10},{9,11},{10,... | collective-permute-start | bytes 491528 | tf_op jit(solution)/shard_map/ppermute | solution.py:861
  47.4 0.0 collective-permute-start.11
  47.4 2.0 %collective-permute-start.9 = (bf16[2,320,128]{2,1,0:T(8,128)(2,1)S(1)}, bf16[2,320,128]{2,1,0:T(8,128)(2,1)S(1)}, u32[]{:S(2)}, u32[]{:S(2)}) collective-permute-start(bf16[2,320,128]{2,1,0:T(8,128)(2,1)S(1)} %get-tuple-element.92.refs_4_), channel_id=1, source_target_pairs={{0,1},{1,2},{2,3},{3,0},{4,5},{5,6},{6,7},{7,4},{8,9},{9,10},{10,1... | collective-permute-start | bytes 491528 | tf_op jit(solution)/shard_map/ppermute | solution.py:861
  49.4 0.0 copy-done.1
  49.4 2.0 %backward.1 = (bf16[2,512,512]{2,1,0:T(8,128)(2,1)}, bf16[4,576,128]{2,1,0:T(8,128)(2,1)S(1)}, bf16[4,576,128]{2,1,0:T(8,128)(2,1)S(1)}) custom-call(s32[1]{0:T(128)} %bitcast.dev_ref, s32[64]{0:T(128)S(1)} %copy-done.4, s32[16]{0:T(128)S(1)} %bitcast.16, bf16[2,256,128]{2,1,0:T(8,128)(2,1)S(1)} %get-tuple-element.70.slopes_ref, ...), custom_call_target="tpu_custom_call" | custom-call | flops 3758096384 | bytes 14680064 | tf_op jit(solution)/shard_map/backward/pallas_call | solution.py:654
  51.5 0.0 collective-permute-done.8.other_ref
  51.5 0.0 collective-permute-done.10.refs_6_
  51.5 3.3 %collective-permute-done.11.refs_7_ = bf16[2,320,128]{2,1,0:T(8,128)(2,1)S(1)} collective-permute-done((bf16[2,320,128]{2,1,0:T(8,128)(2,1)S(1)}, bf16[2,320,128]{2,1,0:T(8,128)(2,1)S(1)}, u32[]{:S(2)}, u32[]{:S(2)}) %collective-permute-start.11) | collective-permute-done | bytes 163872 | tf_op jit(solution)/shard_map/ppermute | solution.py:861
  54.7 0.0 collective-permute-done.9.refs_5_
  54.7 5.2 %collective-permute-start.12 = (bf16[4,576,128]{2,1,0:T(8,128)(2,1)S(1)}, bf16[4,576,128]{2,1,0:T(8,128)(2,1)S(1)}, u32[]{:S(2)}, u32[]{:S(2)}) collective-permute-start(bf16[4,576,128]{2,1,0:T(8,128)(2,1)S(1)} %get-tuple-element.83), channel_id=1, source_target_pairs={{0,8},{8,0},{16,24},{24,16},{32,40},{40,32},{48,56},{56,48},{64,72... | collective-permute-start | bytes 1769480 | tf_op jit(solution)/shard_map/ppermute | solution.py:912
  59.9 1.6 %collective-permute-done.12.recv_ref = bf16[4,576,128]{2,1,0:T(8,128)(2,1)S(1)} collective-permute-done((bf16[4,576,128]{2,1,0:T(8,128)(2,1)S(1)}, bf16[4,576,128]{2,1,0:T(8,128)(2,1)S(1)}, u32[]{:S(2)}, u32[]{:S(2)}) %collective-permute-start.12) | collective-permute-done | bytes 589856 | tf_op jit(solution)/shard_map/ppermute | solution.py:912
  61.5 0.1 join.1
  61.7 4.6 %taps.1 = (bf16[2,16,64,128]{3,2,1,0:T(8,128)(2,1)S(1)}, bf16[2,16,64,128]{3,2,1,0:T(8,128)(2,1)S(1)}) custom-call(s32[1]{0:T(128)} %bitcast.dev_ref, s32[64]{0:T(128)S(1)} %copy-done.4, s32[16]{0:T(128)S(1)} %bitcast.17, bf16[2,256,128]{2,1,0:T(8,128)(2,1)S(1)} %get-tuple-element.66.feat_ref.refs_0_, ...), custom_call_target="tpu_custom_call" | custom-call | flops 2550136832 | bytes 4194304 | tf_op jit(solution)/shard_map/taps/pallas_call | solution.py:494
  66.3 0.5 collective-permute-start.13
  66.8 1.5 %collective-permute-done.13.recv_ref = bf16[2,16,64,128]{3,2,1,0:T(8,128)(2,1)S(1)} collective-permute-done((bf16[2,16,64,128]{3,2,1,0:T(8,128)(2,1)S(1)}, bf16[2,16,64,128]{3,2,1,0:T(8,128)(2,1)S(1)}, u32[]{:S(2)}, u32[]{:S(2)}) %collective-permute-start.13) | collective-permute-done | bytes 524320 | tf_op jit(solution)/shard_map/ppermute | solution.py:916
  68.3 0.1 halve.1
  68.4 0.1 collective-permute-start.14
  68.5 1.6 %collective-permute-start.15 = (bf16[576,128]{1,0:T(8,128)(2,1)S(1)}, bf16[576,128]{1,0:T(8,128)(2,1)S(1)}, u32[]{:S(2)}, u32[]{:S(2)}) collective-permute-start(bf16[576,128]{1,0:T(8,128)(2,1)S(1)} %get-tuple-element.101), channel_id=1, source_target_pairs={{0,2},{1,3},{2,0},{3,1},{4,6},{5,7},{6,4},{7,5},{8,10},{9,11},{10,... | collective-permute-start | bytes 442376 | tf_op jit(solution)/shard_map/ppermute | solution.py:861
  70.1 0.2 collective-permute-start.16
  70.3 1.8 %collective-permute-start.17 = (bf16[576,128]{1,0:T(8,128)(2,1)S(1)}, bf16[576,128]{1,0:T(8,128)(2,1)S(1)}, u32[]{:S(2)}, u32[]{:S(2)}) collective-permute-start(bf16[576,128]{1,0:T(8,128)(2,1)S(1)} %get-tuple-element.103), channel_id=1, source_target_pairs={{0,3},{1,0},{2,1},{3,2},{4,7},{5,4},{6,5},{7,6},{8,11},{9,8},{10,9... | collective-permute-start | bytes 442376 | tf_op jit(solution)/shard_map/ppermute | solution.py:861
  72.1 4.7 %collective-permute-done.15.refs_3_ = bf16[576,128]{1,0:T(8,128)(2,1)S(1)} collective-permute-done((bf16[576,128]{1,0:T(8,128)(2,1)S(1)}, bf16[576,128]{1,0:T(8,128)(2,1)S(1)}, u32[]{:S(2)}, u32[]{:S(2)}) %collective-permute-start.15) | collective-permute-done | bytes 147488 | tf_op jit(solution)/shard_map/ppermute | solution.py:861
  76.8 1.5 %collective-permute-done.16.refs_4_ = bf16[576,128]{1,0:T(8,128)(2,1)S(1)} collective-permute-done((bf16[576,128]{1,0:T(8,128)(2,1)S(1)}, bf16[576,128]{1,0:T(8,128)(2,1)S(1)}, u32[]{:S(2)}, u32[]{:S(2)}) %collective-permute-start.16) | collective-permute-done | bytes 147488 | tf_op jit(solution)/shard_map/ppermute | solution.py:861
  78.3 1.1 collective-permute-done.17.refs_5_
  79.4 0.0 collective-permute-done.14.refs_1_
  79.4 0.2 cells.1
  79.6 22.4 %all_to_all.10.in_ref = bf16[16,96,128]{2,1,0:T(8,128)(2,1)S(1)} all-to-all(bf16[16,96,128]{2,1,0:T(8,128)(2,1)S(1)} %cells.1), channel_id=1, replica_groups={{0,16,32,48,64,80,96,112,128,144,160,176,192,208,224,240},{8,24,40,56,7..., dimensions={0} | all-to-all | bytes 786432 | tf_op jit(solution)/shard_map/all_to_all | solution.py:920
  102.0 0.1 total.1
  102.1 9.6 %all_to_all.11.in_ref = bf16[8,96,128]{2,1,0:T(8,128)(2,1)S(1)} all-to-all(bf16[8,96,128]{2,1,0:T(8,128)(2,1)S(1)} %total.1), channel_id=1, replica_groups=mesh['dp'=32,'mp'=8] {'mp'}, dimensions={0} | all-to-all | bytes 393216 | tf_op jit(solution)/shard_map/all_to_all | solution.py:921
  111.6 1.4 %finish.1 = (bf16[2,120,256]{2,1,0:T(8,128)(2,1)}, f32[4,120,120]{2,1,0:T(8,128)}, f32[32,512]{1,0:T(8,128)}, f32[16,120]{1,0:T(8,128)}, f32[5,16]{1,0:T(8,128)}) custom-call(s32[1]{0:T(128)} %bitcast.dev_ref, s32[64]{0:T(128)S(1)} %copy-done.4, s32[16]{0:T(128)S(1)} %bitcast.18, bf16[8,96,128]{2,1,0:T(8,128)(2,1)S(1)} %all_to_all.11.in_ref, ...), custom_call_target="tpu_custom_call" | custom-call | tf_op jit(solution)/shard_map/finish/pallas_call | solution.py:837
Async XLA Ops:
  0.6 31.6 %copy-start.5 = (s32[16,1]{0,1:T(1,128)S(1)}, s32[16,1]{0,1:T(1,128)}, u32[]{:S(2)}) copy-start(s32[16,1]{0,1:T(1,128)} %param.10) | copy-start | bytes 196
  0.6 31.6 %collective-permute-start.2 = (bf16[2,120,256]{2,1,0:T(8,128)(2,1)}, bf16[2,120,256]{2,1,0:T(8,128)(2,1)S(1)}, u32[]{:S(2)}, u32[]{:S(2)}) collective-permute-start(bf16[2,120,256]{2,1,0:T(8,128)(2,1)} %bitcast.21), channel_id=1, source_target_pairs={{0,128},{8,136},{16,144},{24,152},{32,160},{40,168},{48,176},{56,1... | collective-permute-start | bytes 368648 | tf_op jit(solution)/shard_map/ppermute | solution.py:883
  7.9 0.9 copy-start.2
  8.8 0.7 copy-start.3
  9.5 0.7 copy-start.4
  10.2 22.1 %copy-start.6 = (bf16[2,256,120]{1,2,0:T(8,128)(2,1)S(1)}, bf16[2,256,120]{1,2,0:T(8,128)(2,1)}, u32[]{:S(2)}) copy-start(bf16[2,256,120]{1,2,0:T(8,128)(2,1)} %param.15) | copy-start | bytes 368644
  11.9 17.8 %collective-permute-start = (bf16[2,64,128]{2,1,0:T(8,128)(2,1)S(1)}, bf16[2,64,128]{2,1,0:T(8,128)(2,1)S(1)}, u32[]{:S(2)}, u32[]{:S(2)}) collective-permute-start(bf16[2,64,128]{2,1,0:T(8,128)(2,1)S(1)} %get-tuple-element.60), channel_id=1, source_target_pairs={{0,1},{1,2},{2,3},{3,4},{4,5},{5,6},{6,7},{8,9},{9,10},{10,11},{11... | collective-permute-start | bytes 98312 | tf_op jit(solution)/shard_map/ppermute | solution.py:856
  15.3 17.0 %collective-permute-start.1 = (bf16[2,64,128]{2,1,0:T(8,128)(2,1)S(1)}, bf16[2,64,128]{2,1,0:T(8,128)(2,1)S(1)}, u32[]{:S(2)}, u32[]{:S(2)}) collective-permute-start(bf16[2,64,128]{2,1,0:T(8,128)(2,1)S(1)} %get-tuple-element.61), channel_id=1, source_target_pairs={{1,0},{2,1},{3,2},{4,3},{5,4},{6,5},{7,6},{9,8},{10,9},{11,10},{12... | collective-permute-start | bytes 98312 | tf_op jit(solution)/shard_map/ppermute | solution.py:856
  18.3 22.7 %collective-permute-start.5 = (bf16[2,256,128]{2,1,0:T(8,128)(2,1)S(1)}, bf16[2,256,128]{2,1,0:T(8,128)(2,1)S(1)}, u32[]{:S(2)}, u32[]{:S(2)}) collective-permute-start(bf16[2,256,128]{2,1,0:T(8,128)(2,1)S(1)} %get-tuple-element.66.feat_ref.refs_0_), channel_id=1, source_target_pairs={{0,1},{1,2},{2,3},{3,0},{4,5},{5,6},{6,7},{7,4},{8,9},{9,10},{10,1... | collective-permute-start | bytes 393224 | tf_op jit(solution)/shard_map/ppermute | solution.py:861
  19.3 21.8 %collective-permute-start.6 = (bf16[2,256,128]{2,1,0:T(8,128)(2,1)S(1)}, bf16[2,256,128]{2,1,0:T(8,128)(2,1)S(1)}, u32[]{:S(2)}, u32[]{:S(2)}) collective-permute-start(bf16[2,256,128]{2,1,0:T(8,128)(2,1)S(1)} %get-tuple-element.66.feat_ref.refs_0_), channel_id=1, source_target_pairs={{0,2},{1,3},{2,0},{3,1},{4,6},{5,7},{6,4},{7,5},{8,10},{9,11},{10,... | collective-permute-start | bytes 393224 | tf_op jit(solution)/shard_map/ppermute | solution.py:861
  20.0 2.0 %copy-start = (bf16[128,120,120]{0,2,1:T(8,128)(2,1)S(1)}, bf16[128,120,120]{0,2,1:T(8,128)(2,1)}, u32[]{:S(2)}) copy-start(bf16[128,120,120]{0,2,1:T(8,128)(2,1)} %param.14) | copy-start | bytes 11059204
  29.7 11.4 %collective-permute-start.7 = (bf16[2,256,128]{2,1,0:T(8,128)(2,1)S(1)}, bf16[2,256,128]{2,1,0:T(8,128)(2,1)S(1)}, u32[]{:S(2)}, u32[]{:S(2)}) collective-permute-start(bf16[2,256,128]{2,1,0:T(8,128)(2,1)S(1)} %get-tuple-element.66.feat_ref.refs_0_), channel_id=1, source_target_pairs={{0,3},{1,0},{2,1},{3,2},{4,7},{5,4},{6,5},{7,6},{8,11},{9,8},{10,9... | collective-permute-start | bytes 393224 | tf_op jit(solution)/shard_map/ppermute | solution.py:861
  32.3 17.1 %copy-start.1 = (bf16[1024,512]{1,0:T(8,128)(2,1)S(1)}, bf16[1024,512]{1,0:T(8,128)(2,1)}, u32[]{:S(2)}) copy-start(bf16[1024,512]{1,0:T(8,128)(2,1)} %conv_ref.1) | copy-start | bytes 3145732
  33.0 8.1 %collective-permute-start.3 = (bf16[2,64,128]{2,1,0:T(8,128)(2,1)S(1)}, bf16[2,64,128]{2,1,0:T(8,128)(2,1)S(1)}, u32[]{:S(2)}, u32[]{:S(2)}) collective-permute-start(bf16[2,64,128]{2,1,0:T(8,128)(2,1)S(1)} %get-tuple-element.64), channel_id=1, source_target_pairs={{0,1},{1,2},{2,3},{3,4},{4,5},{5,6},{6,7},{8,9},{9,10},{10,11},{11... | collective-permute-start | bytes 98312 | tf_op jit(solution)/shard_map/ppermute | solution.py:856
  35.0 7.6 %collective-permute-start.4 = (bf16[2,64,128]{2,1,0:T(8,128)(2,1)S(1)}, bf16[2,64,128]{2,1,0:T(8,128)(2,1)S(1)}, u32[]{:S(2)}, u32[]{:S(2)}) collective-permute-start(bf16[2,64,128]{2,1,0:T(8,128)(2,1)S(1)} %get-tuple-element.65), channel_id=1, source_target_pairs={{1,0},{2,1},{3,2},{4,3},{5,4},{6,5},{7,6},{9,8},{10,9},{11,10},{12... | collective-permute-start | bytes 98312 | tf_op jit(solution)/shard_map/ppermute | solution.py:856
  41.0 10.5 %collective-permute-start.8 = (bf16[120,256]{1,0:T(8,128)(2,1)S(1)}, bf16[120,256]{1,0:T(8,128)(2,1)S(1)}, u32[]{:S(2)}, u32[]{:S(2)}) collective-permute-start(bf16[120,256]{1,0:T(8,128)(2,1)S(1)} %get-tuple-element.81), channel_id=1, source_target_pairs={{0,128},{8,136},{16,144},{24,152},{32,160},{40,168},{48,176},{56,1... | collective-permute-start | bytes 184328 | tf_op jit(solution)/shard_map/ppermute | solution.py:892
  42.5 8.9 %collective-permute-start.10 = (bf16[2,320,128]{2,1,0:T(8,128)(2,1)S(1)}, bf16[2,320,128]{2,1,0:T(8,128)(2,1)S(1)}, u32[]{:S(2)}, u32[]{:S(2)}) collective-permute-start(bf16[2,320,128]{2,1,0:T(8,128)(2,1)S(1)} %get-tuple-element.92.refs_4_), channel_id=1, source_target_pairs={{0,2},{1,3},{2,0},{3,1},{4,6},{5,7},{6,4},{7,5},{8,10},{9,11},{10,... | collective-permute-start | bytes 491528 | tf_op jit(solution)/shard_map/ppermute | solution.py:861
  47.4 7.3 %collective-permute-start.11 = (bf16[2,320,128]{2,1,0:T(8,128)(2,1)S(1)}, bf16[2,320,128]{2,1,0:T(8,128)(2,1)S(1)}, u32[]{:S(2)}, u32[]{:S(2)}) collective-permute-start(bf16[2,320,128]{2,1,0:T(8,128)(2,1)S(1)} %get-tuple-element.92.refs_4_), channel_id=1, source_target_pairs={{0,3},{1,0},{2,1},{3,2},{4,7},{5,4},{6,5},{7,6},{8,11},{9,8},{10,9... | collective-permute-start | bytes 491528 | tf_op jit(solution)/shard_map/ppermute | solution.py:861
  47.4 7.3 %collective-permute-start.9 = (bf16[2,320,128]{2,1,0:T(8,128)(2,1)S(1)}, bf16[2,320,128]{2,1,0:T(8,128)(2,1)S(1)}, u32[]{:S(2)}, u32[]{:S(2)}) collective-permute-start(bf16[2,320,128]{2,1,0:T(8,128)(2,1)S(1)} %get-tuple-element.92.refs_4_), channel_id=1, source_target_pairs={{0,1},{1,2},{2,3},{3,0},{4,5},{5,6},{6,7},{7,4},{8,9},{9,10},{10,1... | collective-permute-start | bytes 491528 | tf_op jit(solution)/shard_map/ppermute | solution.py:861
  54.7 6.8 %collective-permute-start.12 = (bf16[4,576,128]{2,1,0:T(8,128)(2,1)S(1)}, bf16[4,576,128]{2,1,0:T(8,128)(2,1)S(1)}, u32[]{:S(2)}, u32[]{:S(2)}) collective-permute-start(bf16[4,576,128]{2,1,0:T(8,128)(2,1)S(1)} %get-tuple-element.83), channel_id=1, source_target_pairs={{0,8},{8,0},{16,24},{24,16},{32,40},{40,32},{48,56},{56,48},{64,72... | collective-permute-start | bytes 1769480 | tf_op jit(solution)/shard_map/ppermute | solution.py:912
  66.3 2.0 %collective-permute-start.13 = (bf16[2,16,64,128]{3,2,1,0:T(8,128)(2,1)S(1)}, bf16[2,16,64,128]{3,2,1,0:T(8,128)(2,1)S(1)}, u32[]{:S(2)}, u32[]{:S(2)}) collective-permute-start(bf16[2,16,64,128]{3,2,1,0:T(8,128)(2,1)S(1)} %get-tuple-element.97), channel_id=1, source_target_pairs={{0,8},{8,0},{16,24},{24,16},{32,40},{40,32},{48,56},{56,48},{64,72... | collective-permute-start | bytes 1572872 | tf_op jit(solution)/shard_map/ppermute | solution.py:916
  68.4 11.0 %collective-permute-start.14 = (bf16[16,64,128]{2,1,0:T(8,128)(2,1)S(1)}, bf16[16,64,128]{2,1,0:T(8,128)(2,1)S(1)}, u32[]{:S(2)}, u32[]{:S(2)}) collective-permute-start(bf16[16,64,128]{2,1,0:T(8,128)(2,1)S(1)} %get-tuple-element.99), channel_id=1, source_target_pairs={{0,4},{1,5},{2,6},{3,7},{4,0},{5,1},{6,2},{7,3},{8,12},{9,13},{10,... | collective-permute-start | bytes 786440 | tf_op jit(solution)/shard_map/ppermute | solution.py:917
  68.5 8.3 %collective-permute-start.15 = (bf16[576,128]{1,0:T(8,128)(2,1)S(1)}, bf16[576,128]{1,0:T(8,128)(2,1)S(1)}, u32[]{:S(2)}, u32[]{:S(2)}) collective-permute-start(bf16[576,128]{1,0:T(8,128)(2,1)S(1)} %get-tuple-element.101), channel_id=1, source_target_pairs={{0,2},{1,3},{2,0},{3,1},{4,6},{5,7},{6,4},{7,5},{8,10},{9,11},{10,... | collective-permute-start | bytes 442376 | tf_op jit(solution)/shard_map/ppermute | solution.py:861
  70.1 8.2 %collective-permute-start.16 = (bf16[576,128]{1,0:T(8,128)(2,1)S(1)}, bf16[576,128]{1,0:T(8,128)(2,1)S(1)}, u32[]{:S(2)}, u32[]{:S(2)}) collective-permute-start(bf16[576,128]{1,0:T(8,128)(2,1)S(1)} %get-tuple-element.102), channel_id=1, source_target_pairs={{0,1},{1,2},{2,3},{3,0},{4,5},{5,6},{6,7},{7,4},{8,9},{9,10},{10,1... | collective-permute-start | bytes 442376 | tf_op jit(solution)/shard_map/ppermute | solution.py:861
  70.3 9.1 %collective-permute-start.17 = (bf16[576,128]{1,0:T(8,128)(2,1)S(1)}, bf16[576,128]{1,0:T(8,128)(2,1)S(1)}, u32[]{:S(2)}, u32[]{:S(2)}) collective-permute-start(bf16[576,128]{1,0:T(8,128)(2,1)S(1)} %get-tuple-element.103), channel_id=1, source_target_pairs={{0,3},{1,0},{2,1},{3,2},{4,7},{5,4},{6,5},{7,6},{8,11},{9,8},{10,9... | collective-permute-start | bytes 442376 | tf_op jit(solution)/shard_map/ppermute | solution.py:861

commit v8 on v5

--- a/solution.py
+++ b/solution.py
@@ -39,6 +39,7 @@
 
 VMEM = pl.BlockSpec(memory_space=pltpu.VMEM)
 SMEM = pl.BlockSpec(memory_space=pltpu.SMEM)
+HBM = pl.BlockSpec(memory_space=pltpu.HBM)
 
 
 def params(mebibytes):
@@ -70,7 +71,7 @@
 
 
 class Place:
-    def __init__(self, dev_ref, len_ref, mov_ref):
+    def __init__(self, dev_ref, len_ref, mov_ref=None):
         self.data = dev_ref[0] // MP
         self.model = lax.rem(dev_ref[0], MP)
         self.x = lax.rem(self.model, X)
@@ -79,7 +80,8 @@
         self.cell = self.data // 2
         self.first = self.model * T
         self.lengths = len_ref
-        self.chosen = mov_ref[lax.rem(self.data, DP // 2)]
+        if mov_ref is not None:
+            self.chosen = mov_ref[lax.rem(self.data, DP // 2)]
 
     def length(self, slot):
         return self.lengths[self.data * SLOTS + slot]
@@ -120,7 +122,7 @@
     return pl.BlockSpec(dims, lambda s: (0,) * len(dims), pipeline_mode=pl.Buffered(1))
 
 
-def turn_body(in_ref, ahead_ref, rows):
+def turn_body(forward, in_ref, out_ref, rows):
     block = pl.program_id(0)
     blocks = pl.num_programs(0)
     for n in range(NEAR):
@@ -134,54 +136,37 @@
     for q in range(far):
         for r in range(NEAR):
             at = (q * NEAR + r) * NEAR
-            ahead_ref[r, :, q * LANES : (q + 1) * LANES] = rows[at : at + NEAR, :].astype(bf16)
-
-
-def turn(pos):
-    far = K // NEAR
-    ahead = pl.pallas_call(
-        turn_body,
+            tile = rows[at : at + NEAR, :].astype(bf16)
+            if forward:
+                out_ref[r, :, q * LANES : (q + 1) * LANES] = tile
+            else:
+                back = NEAR - 1 - r
+                out_ref[far - 1 - q, :, back * LANES : (back + 1) * LANES] = tile
+
+
+def turn(pos, forward):
+    outer, inner = (NEAR, K // NEAR) if forward else (K // NEAR, NEAR)
+    weight = pl.pallas_call(
+        functools.partial(turn_body, forward),
         grid=(LANES // NEAR,),
-        out_shape=jax.ShapeDtypeStruct((NEAR, LANES, far * LANES), bf16),
+        out_shape=jax.ShapeDtypeStruct((outer, LANES, inner * LANES), bf16),
         in_specs=[pl.BlockSpec((NEAR, GC, K), lambda b: (b, 0, 0))],
-        out_specs=pl.BlockSpec((NEAR, NEAR, far * LANES), lambda b: (0, b, 0)),
+        out_specs=pl.BlockSpec((outer, NEAR, inner * LANES), lambda b: (0, b, 0)),
         scratch_shapes=[pltpu.VMEM((K * NEAR, LANES), f32)],
-        compiler_params=params(10),
+        compiler_params=params(56),
         cost_estimate=cost(0, 8 << 20),
-        name="turn",
+        name="ahead" if forward else "behind",
     )(pos)
-    return ahead.reshape(NEAR * LANES, -1)
-
-
-def flip_body(in_ref, out_ref):
-    for r in range(NEAR):
-        out_ref[:, r * LANES : (r + 1) * LANES] = in_ref[
-            (NEAR - 1 - r) * LANES : (NEAR - r) * LANES, :
-        ]
-
-
-def flip(ahead):
-    far = K // NEAR
-    return pl.pallas_call(
-        flip_body,
-        grid=(far,),
-        out_shape=jax.ShapeDtypeStruct((far * LANES, NEAR * LANES), bf16),
-        in_specs=[pl.BlockSpec((NEAR * LANES, LANES), lambda q: (0, far - 1 - q))],
-        out_specs=pl.BlockSpec((LANES, NEAR * LANES), lambda q: (q, 0)),
-        compiler_params=params(8),
-        cost_estimate=cost(0, 8 << 20),
-        name="flip",
-    )(ahead)
+    return weight.reshape(outer * LANES, -1)
 
 
 def encode_body(
     dev_ref,
-    len_ref,
-    mov_ref,
-    audio_ref,
-    conv_ref,
-    chan_ref,
-    proj_ref,
+    len_hbm,
+    audio_hbm,
+    conv_hbm,
+    chan_hbm,
+    proj_hbm,
     feat_ref,
     edge_ref,
     pair_ref,
@@ -193,21 +178,46 @@
     proj,
     mid,
     normed,
+    len_ref,
+    audio_ref,
+    conv_ref,
+    chan_ref,
+    sems,
 ):
-    place = Place(dev_ref, len_ref, mov_ref)
     slot = pl.program_id(0)
+    copies = [
+        pltpu.make_async_copy(source, target, sems.at[n])
+        for n, (source, target) in enumerate(
+            (
+                (len_hbm, len_ref),
+                (audio_hbm.at[0], audio_ref.at[0]),
+                (conv_hbm, conv_ref),
+                (chan_hbm, chan_ref),
+                (proj_hbm, proj.at[pl.ds(0, GC)]),
+                (audio_hbm.at[1], audio_ref.at[1]),
+            )
+        )
+    ]
 
     @pl.when(slot == 0)
     def _():
-        proj[...] = jnp.zeros_like(proj)
-        proj[:GC, :] = proj_ref[...]
-
+        proj[GC - 8 :, :] = jnp.zeros((LANES - GC + 8, C), bf16)
+        for copy in copies:
+            copy.start()
+        for copy in copies[:-1]:
+            copy.wait()
+
+    @pl.when(slot == SLOTS - 1)
+    def _():
+        copies[-1].wait()
+
+    place = Place(dev_ref, len_ref)
     living = place.alive(slot)
 
     @pl.when(living)
     def _():
         for c in range(C // LANES):
-            wide[c] = audio_ref[0, :, c * LANES : (c + 1) * LANES].astype(f32)
+            wide[c] = audio_ref[slot, :, c * LANES : (c + 1) * LANES].astype(f32)
             for tap in range(2):
                 at = tap * C + c * LANES
                 pair_ref[0, :, at : at + LANES] = wide[c, pl.ds(tap, T, stride=2), :].astype(bf16)
@@ -231,8 +241,8 @@
             m_ref[0, rows, :] = m.astype(bf16)
             inv_ref[0, rows, :] = jnp.concatenate(
                 [
-                    jnp.broadcast_to(inverse, (CHUNK, LANES)),
-                    jnp.broadcast_to(inverse_two, (CHUNK, LANES)),
+                    jnp.broadcast_to(inverse, (CHUNK, LANES // 2)),
+                    jnp.broadcast_to(inverse_two, (CHUNK, LANES // 2)),
                 ],
                 axis=1,
             )
@@ -260,15 +270,9 @@
             jax.ShapeDtypeStruct((SLOTS, T, C), bf16),
             jax.ShapeDtypeStruct((SLOTS, T, C), bf16),
             jax.ShapeDtypeStruct((SLOTS, T, C), bf16),
-            jax.ShapeDtypeStruct((SLOTS, T, 2 * LANES), f32),
+            jax.ShapeDtypeStruct((SLOTS, T, LANES), f32),
         ),
-        in_specs=[SMEM] * 3
-        + [
-            by_slot(2 * T, C),
-            once(2 * C, C),
-            whole(5, C),
-            whole(GC, C),
-        ],
+        in_specs=[SMEM] + [HBM] * 5,
         out_specs=(
             all_x(T),
             by_slot(REACH, LANES),
@@ -276,18 +280,23 @@
             by_slot(T, C),
             by_slot(T, C),
             by_slot(T, C),
-            by_slot(T, 2 * LANES),
+            by_slot(T, LANES),
         ),
         scratch_shapes=[
             pltpu.VMEM((C // LANES, 2 * T, LANES), f32),
             pltpu.VMEM((LANES, C), bf16),
             pltpu.VMEM((T, C), f32),
             pltpu.VMEM((T, C), bf16),
+            pltpu.SMEM((DP * SLOTS,), jnp.int32),
+            pltpu.VMEM((SLOTS, 2 * T, C), bf16),
+            pltpu.VMEM((2 * C, C), bf16),
+            pltpu.VMEM((5, C), f32),
+            pltpu.SemaphoreType.DMA((6,)),
         ],
-        compiler_params=params(56),
+        compiler_params=params(52),
         cost_estimate=cost(2 * SLOTS * T * C * (2 * C + LANES), 8 << 20, SLOTS * T * C * 2),
         name="encode",
-    )(*place, audio, conv_weight, channels, proj)
+    )(*place[:2], audio, conv_weight, channels, proj)
 
 
 def fill_windows(windows, ext, first):
@@ -394,14 +403,14 @@
             pltpu.VMEM((T + NEAR * (K // NEAR - 1), NEAR * LANES), bf16),
             pltpu.VMEM((LANES, T), f32),
         ],
-        compiler_params=params(20),
+        compiler_params=params(50),
         cost_estimate=cost(2 * SLOTS * SPAN * K * LANES * LANES, 7 << 20, SLOTS * T * LANES * 2),
         name="mix",
     )(*place, features, edge, weight, cotangent, received)
 
 
 def taps_body(
-    scale, dev_ref, len_ref, mov_ref, feat_ref, piece_ref, own_ref, core_ref, low_ref, both_ref, ext, windows, turned, sums
+    scale, dev_ref, len_ref, mov_ref, feat_ref, piece_ref, keep_ref, send_ref, ext, windows, turned, sums
 ):
     place = Place(dev_ref, len_ref, mov_ref)
     slot = pl.program_id(0)
@@ -431,7 +440,6 @@
     @pl.when(slot == SLOTS - 1)
     def _():
         first_core = place.core == 0
-        first_half = place.y == 0
         for q in range(K // NEAR):
             for far in range(2):
                 at = 2 * far * LANES
@@ -439,22 +447,21 @@
                 odd = sums[q, :, at + LANES : at + 2 * LANES] * scale
                 keep = jnp.where(first_core, even, odd)
                 send = jnp.where(first_core, odd, even)
-                cell = 2 * q + far
-                for mine, other, rows in ((own_ref, low_ref, keep), (core_ref, both_ref, send)):
-                    one, two = rows[:REACH, :], rows[HALF : HALF + REACH, :]
-                    mine[cell] = jnp.where(first_half, one, two).astype(bf16)
-                    other[cell] = jnp.where(first_half, two, one).astype(bf16)
+                for y in range(2):
+                    rows = slice(y * HALF, y * HALF + REACH)
+                    keep_ref[y, 2 * q + far] = keep[rows, :].astype(bf16)
+                    send_ref[y, 2 * q + far] = send[rows, :].astype(bf16)
 
 
 def taps(scale, place, features, pieces):
-    shape = jax.ShapeDtypeStruct((CELLS, REACH, LANES), bf16)
+    shape = jax.ShapeDtypeStruct((2, CELLS, REACH, LANES), bf16)
     spread = X * T
     return pl.pallas_call(
         functools.partial(taps_body, scale),
         grid=(SLOTS,),
-        out_shape=(shape,) * 4,
+        out_shape=(shape,) * 2,
         in_specs=[SMEM] * 3 + [all_x(T), all_x(PIECE)],
-        out_specs=(whole(*shape.shape),) * 4,
+        out_specs=(whole(*shape.shape),) * 2,
         scratch_shapes=[
             pltpu.VMEM((spread + 2 * REACH, LANES), f32),
             pltpu.VMEM((spread + NEAR * (K // NEAR - 1), 4 * LANES), bf16),
@@ -538,7 +545,7 @@
             scaled = normed_grad * gain_two
             first = jnp.mean(scaled, axis=-1, keepdims=True)
             second = jnp.mean(scaled * m, axis=-1, keepdims=True)
-            inverse_two = inv_ref[0, rows, LANES : LANES + 1]
+            inverse_two = inv_ref[0, rows, LANES // 2 : LANES // 2 + 1]
             pre_grad = inverse_two * (scaled - first - m * second) * slope_ref[
                 0, rows, :
             ].astype(f32)
@@ -623,7 +630,7 @@
             by_slot(T, C),
             by_slot(T, C),
             by_slot(T, C),
-            by_slot(T, 2 * LANES),
+            by_slot(T, LANES),
             once(2 * C, C),
             whole(5, C),
             whole(GC, C),
@@ -643,7 +650,7 @@
             pltpu.VMEM((40, C), f32),
             pltpu.VMEM((LANES, C), f32),
         ],
-        compiler_params=params(56),
+        compiler_params=params(50),
         cost_estimate=cost(
             2 * SLOTS * (SPAN * K * LANES * LANES + T * C * (4 * C + 2 * LANES)), 14 << 20
         ),
@@ -662,6 +669,25 @@
     )
 
 
+def halve_body(dev_ref, keep_ref, recv_ref, stay_ref, leave_ref):
+    y = lax.rem(dev_ref[0], MP) // X
+    for out_ref, at in ((stay_ref, y), (leave_ref, 1 - y)):
+        out_ref[...] = (keep_ref[at].astype(f32) + recv_ref[at].astype(f32)).astype(bf16)
+
+
+def halve(dev, keep, received):
+    shape = jax.ShapeDtypeStruct(keep.shape[1:], bf16)
+    return pl.pallas_call(
+        halve_body,
+        out_shape=(shape,) * 2,
+        in_specs=[SMEM] + [VMEM] * 2,
+        out_specs=(VMEM,) * 2,
+        compiler_params=params(8),
+        cost_estimate=cost(0, 2 << 20),
+        name="halve",
+    )(dev, keep, received)
+
+
 def join_body(dev_ref, keep_ref, recv_ref, *out_refs):
     x = lax.rem(dev_ref[0], X)
     for step, out_ref in enumerate(out_refs):
@@ -683,7 +709,7 @@
 
 
 def cells_body(*refs):
-    pos_refs, rest_refs, out_ref, rows = refs[:4], refs[4:8], refs[8], refs[9]
+    pos_refs, rest_refs, out_ref, rows = refs[:2], refs[2:6], refs[6], refs[7]
 
     def summed(parts, *at):
         result = parts[0][at].astype(f32)
@@ -707,7 +733,7 @@
     return pl.pallas_call(
         cells_body,
         out_shape=jax.ShapeDtypeStruct((CELLS, REACH + 32, LANES), bf16),
-        in_specs=[VMEM] * 8,
+        in_specs=[VMEM] * 6,
         out_specs=VMEM,
         scratch_shapes=[pltpu.VMEM((REACH, LANES), f32)],
         compiler_params=params(8),
@@ -786,6 +812,11 @@
     )(*place, cells, states, other)
 
 
+def along_x(block, step):
+    route = [(X * y + x, X * y + (x + step) % X) for y in range(2) for x in range(X)]
+    return lax.ppermute(block, "mp", route)
+
+
 def per_device(
     audio, lengths, moved_slots, conv_weight, channel_params, proj_weight, pos_weight, cotangent
 ):
@@ -802,6 +833,7 @@
 
     rows = [list(range(X)), list(range(X, 2 * X))]
     seam = [(X - 1, X), (X, X - 1)]
+    natural = pos_weight.transpose(1, 2, 0)
 
     def over_x(copies):
         return lax.all_to_all(copies, "mp", 0, 0, axis_index_groups=rows, tiled=True)
@@ -810,23 +842,17 @@
     features, edge, *stored = encode(place, audio, conv_weight, channels, proj)
     features = over_x(features)
     edge = lax.ppermute(edge, "mp", seam)
-    ahead = turn(pos_weight.transpose(1, 2, 0))
+    ahead = turn(natural, True)
     states, sent, pieces, edge = mix(place, features, edge, ahead, cot, received)
-    pieces, ahead = lax.optimization_barrier((pieces, ahead))
+    pieces, natural = lax.optimization_barrier((pieces, natural))
     pieces = over_x(pieces)
     edge = lax.ppermute(edge, "mp", seam)
     other = lax.ppermute(sent, "dp", swap)
-    behind = flip(ahead)
-    own, to_core, to_low, to_both = taps(scale, place, features, pieces)
-    to_core, to_low, to_both, edge = lax.optimization_barrier((to_core, to_low, to_both, edge))
-    low_swap = [(i, i ^ X) for i in range(MP)]
-    both_swap = [(i, i ^ MP ^ X) for i in range(DP * MP)]
-    pos_parts = (
-        own,
-        lax.ppermute(to_core, "dp", core_swap),
-        lax.ppermute(to_low, "mp", low_swap),
-        lax.ppermute(to_both, ("dp", "mp"), both_swap),
-    )
+    behind = turn(natural, False)
+    pieces, other, behind = lax.optimization_barrier((pieces, other, behind))
+    pos_keep, pos_send = taps(scale, place, features, pieces)
+    pos_send, edge = lax.optimization_barrier((pos_send, edge))
+    pos_recv = lax.ppermute(pos_send, "dp", core_swap)
     audio_grad, keep, send = backward(
         scale,
         place,
@@ -840,16 +866,14 @@
         channels,
         proj,
     )
-    send, pos_parts = lax.optimization_barrier((send, pos_parts))
+    send, pos_recv = lax.optimization_barrier((send, pos_recv))
     chunks = join(dev, keep, lax.ppermute(send, "dp", core_swap))
-    rest_parts = [chunks[0]]
-    for step in (2, 1, 3):
-        route = [(X * y + x, X * y + (x + step) % X) for y in range(2) for x in range(X)]
-        rest_parts.append(lax.ppermute(chunks[step], "mp", route))
+    rest_parts = [chunks[0]] + [along_x(chunks[step], step) for step in (2, 1, 3)]
+    stay, leave = halve(dev, pos_keep, pos_recv)
+    pos_parts = (stay, lax.ppermute(leave, "mp", [(i, i ^ X) for i in range(MP)]))
     cells = make_cells(pos_parts, rest_parts)
     groups = [list(range(bit, DP, 2)) for bit in range(2)]
     cells = lax.all_to_all(cells, "dp", 0, 0, axis_index_groups=groups, tiled=True)
-    cells, other = lax.optimization_barrier((cells, other))
     cells = lax.all_to_all(total(cells), "mp", 0, 0, tiled=True)
     hidden, grad_pos, grad_conv, grad_proj, grad_channels = finish(place, cells, states, other)
     return (

time: 118 us -> 118 us (level)
  blocking collectives: 11.2 us -> 40.2 us
  waiting for transfers between devices: 25.6 us -> 9.9 us
  starting transfers between devices: 39.8 us -> 27.7 us
  local copies, waits for them, and re-layouts: 11.4 us -> 2.29 us
  Pallas kernels: 28.7 us -> 37.6 us
    all_to_all x0 -> x1, blocking collectives: none -> 29 us  [per_device(): lax.all_to_all(cells, 'dp', 0, 0, axis_index_groups=groups, tiled=True)]
    ppermute x1, waiting for transfers between devices: 10.8 us -> 0.01 us  [per_device(): other = lax.ppermute(sent, 'dp', swap)]
    pallas_call x2 -> x3, Pallas kernels: 6.21 us -> 16 us  [the longest x2 15.8 us: turn(): pl.pallas_call(functools.partial(turn_body, forward), grid=(LANES // NEAR...]
    unnamed x28 -> x18, local copies, waits for them, and re-layouts: 11.4 us -> 2.29 us
    all_to_all x1 -> x0, starting transfers between devices: 6.82 us -> none  [per_device(): lax.all_to_all(cells, 'dp', 0, 0, axis_index_groups=groups, tiled=True)]
    ppermute x6 -> x5, starting transfers between devices: 7.62 us -> 2.58 us  [the longest x3 2.21 us: along_x(): return lax.ppermute(block, 'mp', route)]
    all_to_all x2, waiting for transfers between devices: 3.63 us -> 0.01 us  [over_x(): lax.all_to_all(copies, 'mp', 0, 0, axis_index_groups=rows, tiled=True)]
    ppermute x1, starting transfers between devices: 5.84 us -> 2.76 us  [per_device(): other = lax.ppermute(sent, 'dp', swap)]
  transfers between devices with their start and end apart: 14 -> 12, of which waited for: 7 -> 4; matrix products, arithmetic and copies ran while one was open for 0% -> 0% of each run, Pallas kernels for 16% -> 23%
where the time goes in v8:
time: 118 us; the launch traced here: 119 us
  blocking collectives  40.2 us (34%)
  Pallas kernels  37.6 us (32%)
  starting transfers between devices  27.7 us (23%)
  waiting for transfers between devices  9.9 us (8%)
  local copies, waits for them, and re-layouts  2.29 us (2%)
    all_to_all x1, blocking collectives, per_device(): lax.all_to_all(cells, 'dp', 0, 0, axis_index_groups=groups, tiled=True)  29 us
    pallas_call x2, Pallas kernels, turn(): pl.pallas_call(functools.partial(turn_body, forward), grid=(LANES // NEAR...  15.8 us
    all_to_all x2, starting transfers between devices, over_x(): lax.all_to_all(copies, 'mp', 0, 0, axis_index_groups=rows, tiled=True)  12.2 us
    all_to_all x1, blocking collectives, per_device(): cells = lax.all_to_all(total(cells), 'mp', 0, 0, tiled=True)  11.2 us
    pallas_call x1, Pallas kernels, backward(): pl.pallas_call(functools.partial(backward_body, scale), grid=(SLOTS,), ou...  7.15 us
    ppermute x1, starting transfers between devices, per_device(): received = lax.ppermute(cot, 'dp', swap)  5.45 us
    pallas_call x1, Pallas kernels, mix(): pl.pallas_call(mix_body, grid=(SLOTS,), out_shape=(jax.ShapeDtypeStruct((...  4.72 us
    ppermute x1, waiting for transfers between devices, per_device(): lax.ppermute(leave, 'mp', [(i, i ^ X) for i in range(MP)])  4.64 us
  transfers between devices with their start and end apart: 12, of which 4 were waited for; matrix products, arithmetic and copies ran while one was open for 0% of the time, Pallas kernels for 23%

profile of v8, /device:TPU:2, one launch (start us, length us, event | category | flops | bytes accessed | tf_op | source)
XLA Modules:
  0.0 118.5 jit_solution(13901515021883577178)
XLA Ops:
  0.6 0.0 copy-start
  0.6 0.9 copy-done
  1.5 0.0 copy-start.2
  1.5 0.7 copy-done.2
  2.3 0.0 copy-start.4
  2.3 0.7 copy-done.4
  2.9 4.0 %encode.1 = (bf16[4,2,256,128]{3,2,1,0:T(8,128)(2,1)}, bf16[2,64,128]{2,1,0:T(8,128)(2,1)S(1)}, bf16[2,256,1024]{2,1,0:T(8,128)(2,1)}, bf16[2,256,512]{2,1,0:T(8...) custom-call(s32[1]{0:T(128)} %bitcast.dev_ref, ...), custom_call_target="tpu_custom_call" | custom-call | flops 603979776 | bytes 8388608 | tf_op jit(solution)/shard_map/encode/pallas_call | solution.py:263
  6.9 7.0 %all-to-all-start = ((bf16[4,2,256,128]{3,2,1,0:T(8,128)(2,1)}), bf16[4,2,256,128]{3,2,1,0:T(8,128)(2,1)S(1)}, u32[]{:S(2)}, u32[]{:S(2)}) async-start(bf16[4,2,256,128]{3,2,1,0:T(8,128)(2,1)} %get-tuple-element.42), calls=%async_computation | async-start | bytes 1048576 | tf_op jit(solution)/shard_map/all_to_all | solution.py:839
  13.9 0.0 copy-start.5
  13.9 0.0 copy-start.6
  13.9 0.0 copy-start.8
  13.9 5.5 %collective-permute-start.1 = (bf16[2,120,256]{2,1,0:T(8,128)(2,1)}, bf16[2,120,256]{2,1,0:T(8,128)(2,1)S(1)}, u32[]{:S(2)}, u32[]{:S(2)}) collective-permute-start(bf16[2,120,256]{2,1,0:T(8,128)(2,1)} %bitcast.18), channel_id=1, source_target_pairs={{0,128},{8,136},{16,144},{24,152},{32,160},{40,168},{48,176},{56,1... | collective-permute-start | bytes 368648 | tf_op jit(solution)/shard_map/ppermute | solution.py:841
  19.4 0.7 collective-permute-start
  20.0 8.0 %ahead.1 = bf16[16,128,1024]{2,1,0:T(8,128)(2,1)} custom-call(bf16[120,120,128]{2,1,0:T(8,128)(2,1)} %bitcast.21), custom_call_target="tpu_custom_call" | custom-call | bytes 8388608 | tf_op jit(solution)/shard_map/ahead/pallas_call | solution.py:149
  28.0 0.0 collective-permute-done.edge_ref
  28.0 0.0 collective-permute-done.1.recv_ref
  28.0 0.0 all-to-all-done.feat_ref
  28.0 0.0 copy-done.5
  28.1 0.0 copy-done.6
  28.1 0.0 copy-done.8
  28.1 4.7 %mix.1 = (bf16[2,120,256]{2,1,0:T(8,128)(2,1)S(1)}, bf16[120,256]{1,0:T(8,128)(2,1)S(1)}, bf16[4,2,320,128]{3,2,1,0:T(8,128)(2,1)}, bf16[2,64,128]{2,1,0:T(8,128)(2,1)S(1)}) custom-call(s32[1]{0:T(128)} %bitcast.dev_ref, s32[64]{0:T(128)S(1)} %copy-done.5, s32[16]{0:T(128)S(1)} %bitcast.14, bf16[4,2,256,128]{3,2,1,0:T(8,128)(2,1)S(1)} %all-to-all-done.feat_ref, ...), custom_call_target="tpu_custom_call" | custom-call | flops 2550136832 | bytes 7340032 | tf_op jit(solution)/shard_map/mix/pallas_call | solution.py:378
  32.8 5.1 %all-to-all-start.1 = ((bf16[4,2,320,128]{3,2,1,0:T(8,128)(2,1)}), bf16[4,2,320,128]{3,2,1,0:T(8,128)(2,1)S(1)}, u32[]{:S(2)}, u32[]{:S(2)}) async-start(bf16[4,2,320,128]{3,2,1,0:T(8,128)(2,1)} %get-tuple-element.45), calls=%async_computation.1 | async-start | bytes 1310720 | tf_op jit(solution)/shard_map/all_to_all | solution.py:839
  37.9 2.8 %collective-permute-start.2 = (bf16[120,256]{1,0:T(8,128)(2,1)S(1)}, bf16[120,256]{1,0:T(8,128)(2,1)S(1)}, u32[]{:S(2)}, u32[]{:S(2)}) collective-permute-start(bf16[120,256]{1,0:T(8,128)(2,1)S(1)} %get-tuple-element.46), channel_id=1, source_target_pairs={{0,128},{8,136},{16,144},{24,152},{32,160},{40,168},{48,176},{56,1... | collective-permute-start | bytes 184328 | tf_op jit(solution)/shard_map/ppermute | solution.py:850
  40.7 0.7 collective-permute-start.3
  41.4 7.9 %behind.1 = bf16[8,128,2048]{2,1,0:T(8,128)(2,1)} custom-call(bf16[120,120,128]{2,1,0:T(8,128)(2,1)} %bitcast.22), custom_call_target="tpu_custom_call" | custom-call | bytes 8388608 | tf_op jit(solution)/shard_map/behind/pallas_call | solution.py:149
  49.2 0.0 collective-permute-done.2.other_ref
  49.2 0.0 all-to-all-done.1.piece_ref
  49.2 0.0 copy-start.1
  49.2 0.0 copy-start.3
  49.2 0.0 copy-start.7
  49.2 4.0 %taps.1 = (bf16[2,16,64,128]{3,2,1,0:T(8,128)(2,1)S(1)}, bf16[2,16,64,128]{3,2,1,0:T(8,128)(2,1)S(1)}) custom-call(s32[1]{0:T(128)} %bitcast.dev_ref, s32[64]{0:T(128)S(1)} %copy-done.5, s32[16]{0:T(128)S(1)} %bitcast.15, bf16[4,2,256,128]{3,2,1,0:T(8,128)(2,1)S(1)} %all-to-all-done.feat_ref, bf16[4,2,320,128]{3,2,1,0:T(8,128)(2,1)S(1)} %all-to-all-done.1.piece_ref), custom_call_target="tpu_custom_call" | custom-call | flops 2550136832 | bytes 4194304 | tf_op jit(solution)/shard_map/taps/pallas_call | solution.py:459
  53.3 0.0 collective-permute-done.3.edge_ref
  53.3 0.1 collective-permute-start.4
  53.4 0.0 copy-done.1
  53.4 0.0 copy-done.3
  53.4 0.0 copy-done.7
  53.4 7.2 %backward.1 = (bf16[2,512,512]{2,1,0:T(8,128)(2,1)}, bf16[4,576,128]{2,1,0:T(8,128)(2,1)S(1)}, bf16[4,576,128]{2,1,0:T(8,128)(2,1)S(1)}) custom-call(s32[1]{0:T(128)} %bitcast.dev_ref, s32[64]{0:T(128)S(1)} %copy-done.5, s32[16]{0:T(128)S(1)} %bitcast.16, bf16[4,2,320,128]{3,2,1,0:T(8,128)(2,1)S(1)} %all-to-all-done.1.piece_ref, ...), custom_call_target="tpu_custom_call" | custom-call | flops 3758096384 | bytes 14680064 | tf_op jit(solution)/shard_map/backward/pallas_call | solution.py:618
  60.6 0.0 collective-permute-done.4.recv_ref
  60.6 3.4 %collective-permute-start.6 = (bf16[4,576,128]{2,1,0:T(8,128)(2,1)S(1)}, bf16[4,576,128]{2,1,0:T(8,128)(2,1)S(1)}, u32[]{:S(2)}, u32[]{:S(2)}) collective-permute-start(bf16[4,576,128]{2,1,0:T(8,128)(2,1)S(1)} %get-tuple-element.65), channel_id=1, source_target_pairs={{0,8},{8,0},{16,24},{24,16},{32,40},{40,32},{48,56},{56,48},{64,72... | collective-permute-start | bytes 1769480 | tf_op jit(solution)/shard_map/ppermute | solution.py:870
  64.0 0.1 halve.1
  64.1 0.3 collective-permute-start.5
  64.4 1.2 %collective-permute-done.6.recv_ref = bf16[4,576,128]{2,1,0:T(8,128)(2,1)S(1)} collective-permute-done((bf16[4,576,128]{2,1,0:T(8,128)(2,1)S(1)}, bf16[4,576,128]{2,1,0:T(8,128)(2,1)S(1)}, u32[]{:S(2)}, u32[]{:S(2)}) %collective-permute-start.6) | collective-permute-done | bytes 589856 | tf_op jit(solution)/shard_map/ppermute | solution.py:870
  65.6 0.1 join.1
  65.8 0.1 collective-permute-start.7
  65.9 1.6 %collective-permute-start.8 = (bf16[576,128]{1,0:T(8,128)(2,1)S(1)}, bf16[576,128]{1,0:T(8,128)(2,1)S(1)}, u32[]{:S(2)}, u32[]{:S(2)}) collective-permute-start(bf16[576,128]{1,0:T(8,128)(2,1)S(1)} %get-tuple-element.68), channel_id=1, source_target_pairs={{0,1},{1,2},{2,3},{3,0},{4,5},{5,6},{6,7},{7,4},{8,9},{9,10},{10,1... | collective-permute-start | bytes 442376 | tf_op jit(solution)/shard_map/ppermute | solution.py:817
  67.4 0.6 collective-permute-start.9
  68.0 4.6 %collective-permute-done.5.refs_1_ = bf16[16,64,128]{2,1,0:T(8,128)(2,1)S(1)} collective-permute-done((bf16[16,64,128]{2,1,0:T(8,128)(2,1)S(1)}, bf16[16,64,128]{2,1,0:T(8,128)(2,1)S(1)}, u32[]{:S(2)}, u32[]{:S(2)}) %collective-permute-start.5) | collective-permute-done | bytes 262176 | tf_op jit(solution)/shard_map/ppermute | solution.py:873
  72.6 1.5 %collective-permute-done.7.refs_3_ = bf16[576,128]{1,0:T(8,128)(2,1)S(1)} collective-permute-done((bf16[576,128]{1,0:T(8,128)(2,1)S(1)}, bf16[576,128]{1,0:T(8,128)(2,1)S(1)}, u32[]{:S(2)}, u32[]{:S(2)}) %collective-permute-start.7) | collective-permute-done | bytes 147488 | tf_op jit(solution)/shard_map/ppermute | solution.py:817
  74.1 0.0 collective-permute-done.8.refs_4_
  74.1 2.6 %collective-permute-done.9.refs_5_ = bf16[576,128]{1,0:T(8,128)(2,1)S(1)} collective-permute-done((bf16[576,128]{1,0:T(8,128)(2,1)S(1)}, bf16[576,128]{1,0:T(8,128)(2,1)S(1)}, u32[]{:S(2)}, u32[]{:S(2)}) %collective-permute-start.9) | collective-permute-done | bytes 147488 | tf_op jit(solution)/shard_map/ppermute | solution.py:817
  76.7 0.2 cells.1
  76.8 29.0 %all_to_all.20.in_ref = bf16[16,96,128]{2,1,0:T(8,128)(2,1)S(1)} all-to-all(bf16[16,96,128]{2,1,0:T(8,128)(2,1)S(1)} %cells.1), channel_id=1, replica_groups={{0,16,32,48,64,80,96,112,128,144,160,176,192,208,224,240},{8,24,40,56,7..., dimensions={0} | all-to-all | bytes 786432 | tf_op jit(solution)/shard_map/all_to_all | solution.py:876
  105.8 0.1 total.1
  105.9 11.2 %all_to_all.21.in_ref = bf16[8,96,128]{2,1,0:T(8,128)(2,1)S(1)} all-to-all(bf16[8,96,128]{2,1,0:T(8,128)(2,1)S(1)} %total.1), channel_id=1, replica_groups=mesh['dp'=32,'mp'=8] {'mp'}, dimensions={0} | all-to-all | bytes 393216 | tf_op jit(solution)/shard_map/all_to_all | solution.py:877
  117.1 1.4 %finish.1 = (bf16[2,120,256]{2,1,0:T(8,128)(2,1)}, f32[4,120,120]{2,1,0:T(8,128)}, f32[32,512]{1,0:T(8,128)}, f32[16,120]{1,0:T(8,128)}, f32[5,16]{1,0:T(8,128)}) custom-call(s32[1]{0:T(128)} %bitcast.dev_ref, s32[64]{0:T(128)S(1)} %copy-done.5, s32[16]{0:T(128)S(1)} %bitcast.17, bf16[8,96,128]{2,1,0:T(8,128)(2,1)S(1)} %all_to_all.21.in_ref, ...), custom_call_target="tpu_custom_call" | custom-call | tf_op jit(solution)/shard_map/finish/pallas_call | solution.py:799
Async XLA Ops:
  0.6 0.9 copy-start
  1.5 0.7 copy-start.2
  2.3 0.7 copy-start.4
  6.9 21.1 %all-to-all-start = ((bf16[4,2,256,128]{3,2,1,0:T(8,128)(2,1)}), bf16[4,2,256,128]{3,2,1,0:T(8,128)(2,1)S(1)}, u32[]{:S(2)}, u32[]{:S(2)}) async-start(bf16[4,2,256,128]{3,2,1,0:T(8,128)(2,1)} %get-tuple-element.42), calls=%async_computation | async-start | bytes 1048576 | tf_op jit(solution)/shard_map/all_to_all | solution.py:839
  13.9 14.1 %copy-start.5 = (s32[64]{0:T(128)S(1)}, s32[64]{0:T(128)}, u32[]{:S(2)}) copy-start(s32[64]{0:T(128)} %len_ref.7) | copy-start | bytes 772
  13.9 14.1 %copy-start.6 = (s32[16,1]{0,1:T(1,128)S(1)}, s32[16,1]{0,1:T(1,128)}, u32[]{:S(2)}) copy-start(s32[16,1]{0,1:T(1,128)} %param.10) | copy-start | bytes 196
  13.9 14.1 %copy-start.8 = (bf16[2,256,120]{1,2,0:T(8,128)(2,1)S(1)}, bf16[2,256,120]{1,2,0:T(8,128)(2,1)}, u32[]{:S(2)}) copy-start(bf16[2,256,120]{1,2,0:T(8,128)(2,1)} %param.15) | copy-start | bytes 368644
  13.9 14.1 %collective-permute-start.1 = (bf16[2,120,256]{2,1,0:T(8,128)(2,1)}, bf16[2,120,256]{2,1,0:T(8,128)(2,1)S(1)}, u32[]{:S(2)}, u32[]{:S(2)}) collective-permute-start(bf16[2,120,256]{2,1,0:T(8,128)(2,1)} %bitcast.18), channel_id=1, source_target_pairs={{0,128},{8,136},{16,144},{24,152},{32,160},{40,168},{48,176},{56,1... | collective-permute-start | bytes 368648 | tf_op jit(solution)/shard_map/ppermute | solution.py:841
  19.4 8.6 %collective-permute-start = (bf16[2,64,128]{2,1,0:T(8,128)(2,1)S(1)}, bf16[2,64,128]{2,1,0:T(8,128)(2,1)S(1)}, u32[]{:S(2)}, u32[]{:S(2)}) collective-permute-start(bf16[2,64,128]{2,1,0:T(8,128)(2,1)S(1)} %get-tuple-element.43), channel_id=1, source_target_pairs={{3,4},{4,3},{11,12},{12,11},{19,20},{20,19},{27,28},{28,27},{35,36... | collective-permute-start | bytes 98312 | tf_op jit(solution)/shard_map/ppermute | solution.py:844
  32.8 16.4 %all-to-all-start.1 = ((bf16[4,2,320,128]{3,2,1,0:T(8,128)(2,1)}), bf16[4,2,320,128]{3,2,1,0:T(8,128)(2,1)S(1)}, u32[]{:S(2)}, u32[]{:S(2)}) async-start(bf16[4,2,320,128]{3,2,1,0:T(8,128)(2,1)} %get-tuple-element.45), calls=%async_computation.1 | async-start | bytes 1310720 | tf_op jit(solution)/shard_map/all_to_all | solution.py:839
  37.9 11.3 %collective-permute-start.2 = (bf16[120,256]{1,0:T(8,128)(2,1)S(1)}, bf16[120,256]{1,0:T(8,128)(2,1)S(1)}, u32[]{:S(2)}, u32[]{:S(2)}) collective-permute-start(bf16[120,256]{1,0:T(8,128)(2,1)S(1)} %get-tuple-element.46), channel_id=1, source_target_pairs={{0,128},{8,136},{16,144},{24,152},{32,160},{40,168},{48,176},{56,1... | collective-permute-start | bytes 184328 | tf_op jit(solution)/shard_map/ppermute | solution.py:850
  40.7 12.6 %collective-permute-start.3 = (bf16[2,64,128]{2,1,0:T(8,128)(2,1)S(1)}, bf16[2,64,128]{2,1,0:T(8,128)(2,1)S(1)}, u32[]{:S(2)}, u32[]{:S(2)}) collective-permute-start(bf16[2,64,128]{2,1,0:T(8,128)(2,1)S(1)} %get-tuple-element.51), channel_id=1, source_target_pairs={{3,4},{4,3},{11,12},{12,11},{19,20},{20,19},{27,28},{28,27},{35,36... | collective-permute-start | bytes 98312 | tf_op jit(solution)/shard_map/ppermute | solution.py:849
  49.2 4.2 %copy-start.1 = (bf16[512,120]{0,1:T(8,128)(2,1)S(1)}, bf16[512,120]{0,1:T(8,128)(2,1)}, u32[]{:S(2)}) copy-start(bf16[512,120]{0,1:T(8,128)(2,1)} %param.13) | copy-start | bytes 368644
  49.2 4.2 %copy-start.3 = (f32[512,5]{0,1:T(8,128)S(1)}, f32[512,5]{0,1:T(8,128)}, u32[]{:S(2)}) copy-start(f32[512,5]{0,1:T(8,128)} %param.12) | copy-start | bytes 30724
  49.2 4.2 %copy-start.7 = (bf16[2,256,512]{2,1,0:T(8,128)(2,1)S(1)}, bf16[2,256,512]{2,1,0:T(8,128)(2,1)}, u32[]{:S(2)}) copy-start(bf16[2,256,512]{2,1,0:T(8,128)(2,1)} %get-tuple-element.57.m_ref) | copy-start | bytes 1572868
  53.3 7.3 %collective-permute-start.4 = (bf16[2,16,64,128]{3,2,1,0:T(8,128)(2,1)S(1)}, bf16[2,16,64,128]{3,2,1,0:T(8,128)(2,1)S(1)}, u32[]{:S(2)}, u32[]{:S(2)}) collective-permute-start(bf16[2,16,64,128]{3,2,1,0:T(8,128)(2,1)S(1)} %get-tuple-element.60), channel_id=1, source_target_pairs={{0,8},{8,0},{16,24},{24,16},{32,40},{40,32},{48,56},{56,48},{64,72... | collective-permute-start | bytes 1572872 | tf_op jit(solution)/shard_map/ppermute | solution.py:855
  60.6 5.0 %collective-permute-start.6 = (bf16[4,576,128]{2,1,0:T(8,128)(2,1)S(1)}, bf16[4,576,128]{2,1,0:T(8,128)(2,1)S(1)}, u32[]{:S(2)}, u32[]{:S(2)}) collective-permute-start(bf16[4,576,128]{2,1,0:T(8,128)(2,1)S(1)} %get-tuple-element.65), channel_id=1, source_target_pairs={{0,8},{8,0},{16,24},{24,16},{32,40},{40,32},{48,56},{56,48},{64,72... | collective-permute-start | bytes 1769480 | tf_op jit(solution)/shard_map/ppermute | solution.py:870
  64.1 8.5 %collective-permute-start.5 = (bf16[16,64,128]{2,1,0:T(8,128)(2,1)S(1)}, bf16[16,64,128]{2,1,0:T(8,128)(2,1)S(1)}, u32[]{:S(2)}, u32[]{:S(2)}) collective-permute-start(bf16[16,64,128]{2,1,0:T(8,128)(2,1)S(1)} %get-tuple-element.63), channel_id=1, source_target_pairs={{0,4},{1,5},{2,6},{3,7},{4,0},{5,1},{6,2},{7,3},{8,12},{9,13},{10,... | collective-permute-start | bytes 786440 | tf_op jit(solution)/shard_map/ppermute | solution.py:873
  65.8 8.3 %collective-permute-start.7 = (bf16[576,128]{1,0:T(8,128)(2,1)S(1)}, bf16[576,128]{1,0:T(8,128)(2,1)S(1)}, u32[]{:S(2)}, u32[]{:S(2)}) collective-permute-start(bf16[576,128]{1,0:T(8,128)(2,1)S(1)} %get-tuple-element.67), channel_id=1, source_target_pairs={{0,2},{1,3},{2,0},{3,1},{4,6},{5,7},{6,4},{7,5},{8,10},{9,11},{10,... | collective-permute-start | bytes 442376 | tf_op jit(solution)/shard_map/ppermute | solution.py:817
  65.9 8.2 %collective-permute-start.8 = (bf16[576,128]{1,0:T(8,128)(2,1)S(1)}, bf16[576,128]{1,0:T(8,128)(2,1)S(1)}, u32[]{:S(2)}, u32[]{:S(2)}) collective-permute-start(bf16[576,128]{1,0:T(8,128)(2,1)S(1)} %get-tuple-element.68), channel_id=1, source_target_pairs={{0,1},{1,2},{2,3},{3,0},{4,5},{5,6},{6,7},{7,4},{8,9},{9,10},{10,1... | collective-permute-start | bytes 442376 | tf_op jit(solution)/shard_map/ppermute | solution.py:817
  67.4 9.2 %collective-permute-start.9 = (bf16[576,128]{1,0:T(8,128)(2,1)S(1)}, bf16[576,128]{1,0:T(8,128)(2,1)S(1)}, u32[]{:S(2)}, u32[]{:S(2)}) collective-permute-start(bf16[576,128]{1,0:T(8,128)(2,1)S(1)} %get-tuple-element.69), channel_id=1, source_target_pairs={{0,3},{1,0},{2,1},{3,2},{4,7},{5,4},{6,5},{7,6},{8,11},{9,8},{10,9... | collective-permute-start | bytes 442376 | tf_op jit(solution)/shard_map/ppermute | solution.py:817

commit v9 on v7

--- a/solution.py
+++ b/solution.py
@@ -106,29 +106,12 @@
     return pl.BlockSpec(dims, lambda s: (0,) * len(dims), pipeline_mode=pl.Buffered(1))
 
 
-def turn_body(in_ref, ahead_ref, behind_ref, rows, held, sems):
+def turn_body(in_ref, ahead_ref, behind_ref, rows):
     block = pl.program_id(0)
-    blocks = LANES // NEAR
-
-    def fetch(n):
-        count = min(NEAR, GC - n * NEAR)
-        part = pl.ds(n * NEAR, count)
-        return pltpu.make_async_copy(in_ref.at[part], held.at[part], sems.at[n])
-
-    @pl.when(block == 0)
-    def _():
-        for n in range(blocks):
-            fetch(n).start()
-
-    for n in range(blocks):
-
-        @pl.when(block == n)
-        def _():
-            fetch(n).wait()
-
+    blocks = pl.num_programs(0)
     for n in range(NEAR):
         tile = jnp.concatenate(
-            [held[block * NEAR + n].astype(f32), jnp.zeros((LANES - GC, K), f32)], axis=0
+            [in_ref[n].astype(f32), jnp.zeros((LANES - GC, K), f32)], axis=0
         ).T
         if n >= GC % NEAR:
             tile = jnp.where(block == blocks - 1, 0.0, tile)
@@ -152,16 +135,12 @@
             jax.ShapeDtypeStruct((NEAR, LANES, far * LANES), bf16),
             jax.ShapeDtypeStruct((far, LANES, NEAR * LANES), bf16),
         ),
-        in_specs=[HBM],
+        in_specs=[pl.BlockSpec((NEAR, GC, K), lambda b: (b, 0, 0))],
         out_specs=(
             pl.BlockSpec((NEAR, NEAR, far * LANES), lambda b: (0, b, 0)),
             pl.BlockSpec((far, NEAR, NEAR * LANES), lambda b: (0, b, 0)),
         ),
-        scratch_shapes=[
-            pltpu.VMEM((K * NEAR, LANES), f32),
-            pltpu.VMEM((LANES, GC, K), bf16),
-            pltpu.SemaphoreType.DMA((LANES // NEAR,)),
-        ],
+        scratch_shapes=[pltpu.VMEM((K * NEAR, LANES), f32)],
         compiler_params=params(16),
         cost_estimate=cost(0, 12 << 20),
         name="turn",
@@ -251,8 +230,8 @@
             m_ref[0, rows, :] = m.astype(bf16)
             inv_ref[0, rows, :] = jnp.concatenate(
                 [
-                    jnp.broadcast_to(inverse, (CHUNK, LANES)),
-                    jnp.broadcast_to(inverse_two, (CHUNK, LANES)),
+                    jnp.broadcast_to(inverse, (CHUNK, LANES // 2)),
+                    jnp.broadcast_to(inverse_two, (CHUNK, LANES // 2)),
                 ],
                 axis=1,
             )
@@ -280,7 +259,7 @@
             jax.ShapeDtypeStruct((SLOTS, T, C), bf16),
             jax.ShapeDtypeStruct((SLOTS, T, C), bf16),
             jax.ShapeDtypeStruct((SLOTS, T, C), bf16),
-            jax.ShapeDtypeStruct((SLOTS, T, 2 * LANES), f32),
+            jax.ShapeDtypeStruct((SLOTS, T, LANES), f32),
         ),
         in_specs=[SMEM] + [HBM] * 5,
         out_specs=(
@@ -291,7 +270,7 @@
             by_slot(T, C),
             by_slot(T, C),
             by_slot(T, C),
-            by_slot(T, 2 * LANES),
+            by_slot(T, LANES),
         ),
         scratch_shapes=[
             pltpu.VMEM((C // LANES, 2 * T, LANES), f32),
@@ -581,7 +560,7 @@
             scaled = normed_grad * gain_two
             first = jnp.mean(scaled, axis=-1, keepdims=True)
             second = jnp.mean(scaled * m, axis=-1, keepdims=True)
-            inverse_two = inv_ref[0, rows, LANES : LANES + 1]
+            inverse_two = inv_ref[0, rows, LANES // 2 : LANES // 2 + 1]
             pre_grad = inverse_two * (scaled - first - m * second) * slope_ref[
                 0, rows, :
             ].astype(f32)
@@ -667,7 +646,7 @@
             by_slot(T, C),
             by_slot(T, C),
             by_slot(T, C),
-            by_slot(T, 2 * LANES),
+            by_slot(T, LANES),
             once(2 * C, C),
             whole(5, C),
             whole(GC, C),
@@ -889,7 +868,6 @@
         place, features, low, high, ahead, cot, received
     )
     low, high = neighbours(tail, head)
-    other = lax.ppermute(sent, "dp", swap)
     piece, low, high, all_features = lax.optimization_barrier(
         (piece, low, high, all_features)
     )
@@ -908,13 +886,15 @@
         channels,
         proj,
     )
-    send, other, pieces = lax.optimization_barrier((send, other, pieces))
+    send, pieces, sent = lax.optimization_barrier((send, pieces, sent))
     chunks = join(dev, keep, lax.ppermute(send, "dp", core_swap))
     chunks, pieces = lax.optimization_barrier((chunks, pieces))
     rest_parts = [chunks[0]] + [along_x(chunks[step], step) for step in (2, 1, 3)]
     pos_keep, pos_send = taps(scale, place, all_features, pieces)
     stay, leave = halve(dev, pos_keep, lax.ppermute(pos_send, "dp", core_swap))
     pos_parts = (stay, lax.ppermute(leave, "mp", [(i, i ^ X) for i in range(MP)]))
+    other = lax.ppermute(sent, "dp", swap)
+    rest_parts, other = lax.optimization_barrier((rest_parts, other))
     cells = make_cells(pos_parts, rest_parts)
     groups = [list(range(bit, DP, 2)) for bit in range(2)]
     cells = lax.all_to_all(cells, "dp", 0, 0, axis_index_groups=groups, tiled=True)

time: 113 us -> 115 us (1.018)
  Pallas kernels: 18.5 us -> 27.6 us
  starting transfers between devices: 42.3 us -> 36.5 us
  waiting for transfers between devices: 15.2 us -> 13.8 us
    ppermute x9, waiting for transfers between devices: 10.5 us -> 0.32 us  [along_x(): return lax.ppermute(block, 'mp', route)]
    ppermute x1, waiting for transfers between devices: 0.01 us -> 7.81 us  [per_device(): other = lax.ppermute(sent, 'dp', swap)]
    pallas_call x1, Pallas kernels: 2.03 us -> 7.87 us  [backward(): pl.pallas_call(functools.partial(backward_body, scale), grid=(SLOTS,), ou...]
    ppermute x1, starting transfers between devices: 5.17 us -> 0.27 us  [per_device(): chunks = join(dev, keep, lax.ppermute(send, 'dp', core_swap))]
    pallas_call x1, Pallas kernels: 0.73 us -> 4 us  [mix(): pl.pallas_call(mix_body, grid=(SLOTS,), out_shape=(jax.ShapeDtypeStruct((...]
    pallas_call x1, Pallas kernels: 1.67 us -> 4.33 us  [encode(): pl.pallas_call(encode_body, grid=(SLOTS,), out_shape=(jax.ShapeDtypeStruc...]
    pallas_call x1, Pallas kernels: 7.57 us -> 4.93 us  [turn(): pl.pallas_call(turn_body, grid=(LANES // NEAR,), out_shape=(jax.ShapeDtyp...]
    ppermute x2, starting transfers between devices: 8.98 us -> 6.36 us  [neighbours(): lax.ppermute(head, 'mp', backward_route)]
  transfers between devices with their start and end apart: 18 -> 18, of which waited for: 7 -> 5; matrix products, arithmetic and copies ran while one was open for 0% -> 0% of each run, Pallas kernels for 11% -> 19%
where the time goes in v9:
time: 115 us; the launch traced here: 114 us
  starting transfers between devices  36.5 us (32%)
  blocking collectives  30.9 us (27%)
  Pallas kernels  27.6 us (24%)
  waiting for transfers between devices  13.8 us (12%)
  local copies, waits for them, and re-layouts  4.33 us (4%)
    all_to_all x1, blocking collectives, per_device(): lax.all_to_all(cells, 'dp', 0, 0, axis_index_groups=groups, tiled=True)  20.5 us
    ppermute x9, starting transfers between devices, along_x(): return lax.ppermute(block, 'mp', route)  16.7 us
    all_to_all x1, blocking collectives, per_device(): cells = lax.all_to_all(total(cells), 'mp', 0, 0, tiled=True)  10.4 us
    pallas_call x1, Pallas kernels, backward(): pl.pallas_call(functools.partial(backward_body, scale), grid=(SLOTS,), ou...  7.87 us
    ppermute x1, waiting for transfers between devices, per_device(): other = lax.ppermute(sent, 'dp', swap)  7.81 us
    ppermute x1, starting transfers between devices, per_device(): received = lax.ppermute(cot, 'dp', swap)  7.28 us
    ppermute x2, starting transfers between devices, neighbours(): lax.ppermute(head, 'mp', backward_route)  6.36 us
    ppermute x2, starting transfers between devices, neighbours(): lax.ppermute(tail, 'mp', forward)  5.32 us
  transfers between devices with their start and end apart: 18, of which 5 were waited for; matrix products, arithmetic and copies ran while one was open for 0% of the time, Pallas kernels for 19%

profile of v9, /device:TPU:2, one launch (start us, length us, event | category | flops | bytes accessed | tf_op | source)
XLA Modules:
  0.0 114.0 jit_solution(16504800544890429819)
XLA Ops:
  0.6 0.0 copy-start.5
  0.6 7.3 %collective-permute-start.2 = (bf16[2,120,256]{2,1,0:T(8,128)(2,1)}, bf16[2,120,256]{2,1,0:T(8,128)(2,1)S(1)}, u32[]{:S(2)}, u32[]{:S(2)}) collective-permute-start(bf16[2,120,256]{2,1,0:T(8,128)(2,1)} %bitcast.21), channel_id=1, source_target_pairs={{0,128},{8,136},{16,144},{24,152},{32,160},{40,168},{48,176},{56,1... | collective-permute-start | bytes 368648 | tf_op jit(solution)/shard_map/ppermute | solution.py:862
  7.9 0.0 copy-start.2
  7.9 0.9 copy-done.2
  8.8 0.0 copy-start.3
  8.8 0.7 copy-done.3
  9.5 0.0 copy-start.4
  9.5 0.7 copy-done.4
  10.2 0.0 copy-start.6
  10.2 4.3 %encode.1 = (bf16[2,256,128]{2,1,0:T(8,128)(2,1)S(1)}, bf16[2,64,128]{2,1,0:T(8,128)(2,1)S(1)}, bf16[2,64,128]{2,1,0:T(8,128)(2,1)S(1)}, bf16[2,256,1024]{2,1,0:...) custom-call(s32[1]{0:T(128)} %bitcast.dev_ref, ...), custom_call_target="tpu_custom_call" | custom-call | flops 603979776 | bytes 8388608 | tf_op jit(solution)/shard_map/encode/pallas_call | solution.py:251
  14.5 3.4 %collective-permute-start = (bf16[2,64,128]{2,1,0:T(8,128)(2,1)S(1)}, bf16[2,64,128]{2,1,0:T(8,128)(2,1)S(1)}, u32[]{:S(2)}, u32[]{:S(2)}) collective-permute-start(bf16[2,64,128]{2,1,0:T(8,128)(2,1)S(1)} %get-tuple-element.65), channel_id=1, source_target_pairs={{0,1},{1,2},{2,3},{3,4},{4,5},{5,6},{6,7},{8,9},{9,10},{10,11},{11... | collective-permute-start | bytes 98312 | tf_op jit(solution)/shard_map/ppermute | solution.py:835
  17.9 2.4 %collective-permute-start.1 = (bf16[2,64,128]{2,1,0:T(8,128)(2,1)S(1)}, bf16[2,64,128]{2,1,0:T(8,128)(2,1)S(1)}, u32[]{:S(2)}, u32[]{:S(2)}) collective-permute-start(bf16[2,64,128]{2,1,0:T(8,128)(2,1)S(1)} %get-tuple-element.66), channel_id=1, source_target_pairs={{1,0},{2,1},{3,2},{4,3},{5,4},{6,5},{7,6},{9,8},{10,9},{11,10},{12... | collective-permute-start | bytes 98312 | tf_op jit(solution)/shard_map/ppermute | solution.py:835
  20.4 1.6 %collective-permute-start.5 = (bf16[2,256,128]{2,1,0:T(8,128)(2,1)S(1)}, bf16[2,256,128]{2,1,0:T(8,128)(2,1)S(1)}, u32[]{:S(2)}, u32[]{:S(2)}) collective-permute-start(bf16[2,256,128]{2,1,0:T(8,128)(2,1)S(1)} %get-tuple-element.71.feat_ref.refs_0_), channel_id=1, source_target_pairs={{0,1},{1,2},{2,3},{3,0},{4,5},{5,6},{6,7},{7,4},{8,9},{9,10},{10,1... | collective-permute-start | bytes 393224 | tf_op jit(solution)/shard_map/ppermute | solution.py:840
  22.0 0.7 collective-permute-start.6
  22.7 0.0 copy-start
  22.7 2.0 %copy-done = bf16[128,120,120]{0,2,1:T(8,128)(2,1)S(1)} copy-done((bf16[128,120,120]{0,2,1:T(8,128)(2,1)S(1)}, bf16[128,120,120]{0,2,1:T(8,128)(2,1)}, u32[]{:S(2)}) %copy-start) | copy-done | bytes 3686424
  24.7 4.9 %turn.1 = (bf16[16,128,1024]{2,1,0:T(8,128)(2,1)S(1)}, bf16[8,128,2048]{2,1,0:T(8,128)(2,1)S(1)}) custom-call(bf16[120,120,128]{2,1,0:T(8,128)(2,1)S(1)} %bitcast.10), custom_call_target="tpu_custom_call" | custom-call | bytes 12582912 | tf_op jit(solution)/shard_map/turn/pallas_call | solution.py:131
  29.7 0.0 collective-permute-done.low_ref
  29.7 2.6 %collective-permute-start.7 = (bf16[2,256,128]{2,1,0:T(8,128)(2,1)S(1)}, bf16[2,256,128]{2,1,0:T(8,128)(2,1)S(1)}, u32[]{:S(2)}, u32[]{:S(2)}) collective-permute-start(bf16[2,256,128]{2,1,0:T(8,128)(2,1)S(1)} %get-tuple-element.71.feat_ref.refs_0_), channel_id=1, source_target_pairs={{0,3},{1,0},{2,1},{3,2},{4,7},{5,4},{6,5},{7,6},{8,11},{9,8},{10,9... | collective-permute-start | bytes 393224 | tf_op jit(solution)/shard_map/ppermute | solution.py:840
  32.3 0.0 collective-permute-done.1.high_ref
  32.3 0.0 collective-permute-done.2.recv_ref
  32.3 0.0 copy-done.5
  32.3 0.0 copy-done.6
  32.3 0.0 copy-start.1
  32.3 4.0 %mix.1 = (bf16[2,120,256]{2,1,0:T(8,128)(2,1)S(1)}, bf16[120,256]{1,0:T(8,128)(2,1)S(1)}, bf16[2,256,128]{2,1,0:T(8,128)(2,1)S(1)}, bf16[2,64,128]{2,1,0:T(8,128...) custom-call(s32[1]{0:T(128)} %bitcast.dev_ref, s32[64]{0:T(128)S(1)} %copy-done.4, ...), custom_call_target="tpu_custom_call" | custom-call | flops 2550136832 | bytes 7340032 | tf_op jit(solution)/shard_map/mix/pallas_call | solution.py:380
  36.3 1.9 %collective-permute-start.3 = (bf16[2,64,128]{2,1,0:T(8,128)(2,1)S(1)}, bf16[2,64,128]{2,1,0:T(8,128)(2,1)S(1)}, u32[]{:S(2)}, u32[]{:S(2)}) collective-permute-start(bf16[2,64,128]{2,1,0:T(8,128)(2,1)S(1)} %get-tuple-element.69), channel_id=1, source_target_pairs={{0,1},{1,2},{2,3},{3,4},{4,5},{5,6},{6,7},{8,9},{9,10},{10,11},{11... | collective-permute-start | bytes 98312 | tf_op jit(solution)/shard_map/ppermute | solution.py:835
  38.3 3.9 %collective-permute-start.4 = (bf16[2,64,128]{2,1,0:T(8,128)(2,1)S(1)}, bf16[2,64,128]{2,1,0:T(8,128)(2,1)S(1)}, u32[]{:S(2)}, u32[]{:S(2)}) collective-permute-start(bf16[2,64,128]{2,1,0:T(8,128)(2,1)S(1)} %get-tuple-element.70), channel_id=1, source_target_pairs={{1,0},{2,1},{3,2},{4,3},{5,4},{6,5},{7,6},{9,8},{10,9},{11,10},{12... | collective-permute-start | bytes 98312 | tf_op jit(solution)/shard_map/ppermute | solution.py:835
  42.2 0.0 collective-permute-done.5.refs_1_
  42.2 0.0 collective-permute-done.6.refs_2_
  42.2 0.0 collective-permute-done.7.refs_3_
  42.2 0.0 collective-permute-done.3.low_ref
  42.2 1.8 %collective-permute-done.4.high_ref = bf16[2,64,128]{2,1,0:T(8,128)(2,1)S(1)} collective-permute-done((bf16[2,64,128]{2,1,0:T(8,128)(2,1)S(1)}, bf16[2,64,128]{2,1,0:T(8,128)(2,1)S(1)}, u32[]{:S(2)}, u32[]{:S(2)}) %collective-permute-start.4) | collective-permute-done | bytes 32800 | tf_op jit(solution)/shard_map/ppermute | solution.py:835
  44.1 2.0 %collective-permute-start.10 = (bf16[2,320,128]{2,1,0:T(8,128)(2,1)S(1)}, bf16[2,320,128]{2,1,0:T(8,128)(2,1)S(1)}, u32[]{:S(2)}, u32[]{:S(2)}) collective-permute-start(bf16[2,320,128]{2,1,0:T(8,128)(2,1)S(1)} %get-tuple-element.97.refs_4_), channel_id=1, source_target_pairs={{0,3},{1,0},{2,1},{3,2},{4,7},{5,4},{6,5},{7,6},{8,11},{9,8},{10,9... | collective-permute-start | bytes 491528 | tf_op jit(solution)/shard_map/ppermute | solution.py:840
  46.1 1.1 collective-permute-start.8
  47.2 6.5 %collective-permute-start.9 = (bf16[2,320,128]{2,1,0:T(8,128)(2,1)S(1)}, bf16[2,320,128]{2,1,0:T(8,128)(2,1)S(1)}, u32[]{:S(2)}, u32[]{:S(2)}) collective-permute-start(bf16[2,320,128]{2,1,0:T(8,128)(2,1)S(1)} %get-tuple-element.97.refs_4_), channel_id=1, source_target_pairs={{0,2},{1,3},{2,0},{3,1},{4,6},{5,7},{6,4},{7,5},{8,10},{9,11},{10,... | collective-permute-start | bytes 491528 | tf_op jit(solution)/shard_map/ppermute | solution.py:840
  53.6 0.0 copy-done.1
  53.6 7.9 %backward.1 = (bf16[2,512,512]{2,1,0:T(8,128)(2,1)}, bf16[4,576,128]{2,1,0:T(8,128)(2,1)S(1)}, bf16[4,576,128]{2,1,0:T(8,128)(2,1)S(1)}) custom-call(s32[1]{0:T(128)} %bitcast.dev_ref, s32[64]{0:T(128)S(1)} %copy-done.4, s32[16]{0:T(128)S(1)} %bitcast.16, bf16[2,256,128]{2,1,0:T(8,128)(2,1)S(1)} %get-tuple-element.75.slopes_ref, ...), custom_call_target="tpu_custom_call" | custom-call | flops 3758096384 | bytes 14680064 | tf_op jit(solution)/shard_map/backward/pallas_call | solution.py:633
  61.5 0.0 collective-permute-done.10.refs_7_
  61.5 0.0 collective-permute-done.8.refs_5_
  61.5 0.0 collective-permute-done.9.refs_6_
  61.5 0.3 collective-permute-start.11
  61.8 2.0 %collective-permute-done.11.recv_ref = bf16[4,576,128]{2,1,0:T(8,128)(2,1)S(1)} collective-permute-done((bf16[4,576,128]{2,1,0:T(8,128)(2,1)S(1)}, bf16[4,576,128]{2,1,0:T(8,128)(2,1)S(1)}, u32[]{:S(2)}, u32[]{:S(2)}) %collective-permute-start.11) | collective-permute-done | bytes 589856 | tf_op jit(solution)/shard_map/ppermute | solution.py:890
  63.8 0.1 join.1
  63.9 4.6 %taps.1 = (bf16[2,16,64,128]{3,2,1,0:T(8,128)(2,1)S(1)}, bf16[2,16,64,128]{3,2,1,0:T(8,128)(2,1)S(1)}) custom-call(s32[1]{0:T(128)} %bitcast.dev_ref, s32[64]{0:T(128)S(1)} %copy-done.4, s32[16]{0:T(128)S(1)} %bitcast.17, bf16[2,256,128]{2,1,0:T(8,128)(2,1)S(1)} %get-tuple-element.71.feat_ref.refs_0_, ...), custom_call_target="tpu_custom_call" | custom-call | flops 2550136832 | bytes 4194304 | tf_op jit(solution)/shard_map/taps/pallas_call | solution.py:473
  68.5 0.2 collective-permute-start.12
  68.8 1.8 %collective-permute-done.12.recv_ref = bf16[2,16,64,128]{3,2,1,0:T(8,128)(2,1)S(1)} collective-permute-done((bf16[2,16,64,128]{3,2,1,0:T(8,128)(2,1)S(1)}, bf16[2,16,64,128]{3,2,1,0:T(8,128)(2,1)S(1)}, u32[]{:S(2)}, u32[]{:S(2)}) %collective-permute-start.12) | collective-permute-done | bytes 524320 | tf_op jit(solution)/shard_map/ppermute | solution.py:894
  70.5 0.1 halve.1
  70.7 0.1 collective-permute-start.13
  70.8 0.1 collective-permute-start.14
  70.9 0.8 collective-permute-start.15
  71.7 1.3 %collective-permute-start.16 = (bf16[576,128]{1,0:T(8,128)(2,1)S(1)}, bf16[576,128]{1,0:T(8,128)(2,1)S(1)}, u32[]{:S(2)}, u32[]{:S(2)}) collective-permute-start(bf16[576,128]{1,0:T(8,128)(2,1)S(1)} %get-tuple-element.108), channel_id=1, source_target_pairs={{0,3},{1,0},{2,1},{3,2},{4,7},{5,4},{6,5},{7,6},{8,11},{9,8},{10,9... | collective-permute-start | bytes 442376 | tf_op jit(solution)/shard_map/ppermute | solution.py:840
  73.0 0.3 collective-permute-start.17
  73.3 7.8 %collective-permute-done.17.other_ref = bf16[120,256]{1,0:T(8,128)(2,1)S(1)} collective-permute-done((bf16[120,256]{1,0:T(8,128)(2,1)S(1)}, bf16[120,256]{1,0:T(8,128)(2,1)S(1)}, u32[]{:S(2)}, u32[]{:S(2)}) %collective-permute-start.17) | collective-permute-done | bytes 61472 | tf_op jit(solution)/shard_map/ppermute | solution.py:896
  81.1 0.0 collective-permute-done.14.refs_3_
  81.1 0.0 collective-permute-done.15.refs_4_
  81.1 0.3 collective-permute-done.16.refs_5_
  81.4 0.0 collective-permute-done.13.refs_1_
  81.4 0.2 cells.1
  81.6 20.5 %all_to_all.10.in_ref = bf16[16,96,128]{2,1,0:T(8,128)(2,1)S(1)} all-to-all(bf16[16,96,128]{2,1,0:T(8,128)(2,1)S(1)} %cells.1), channel_id=1, replica_groups={{0,16,32,48,64,80,96,112,128,144,160,176,192,208,224,240},{8,24,40,56,7..., dimensions={0} | all-to-all | bytes 786432 | tf_op jit(solution)/shard_map/all_to_all | solution.py:900
  102.0 0.1 total.1
  102.1 10.4 %all_to_all.11.in_ref = bf16[8,96,128]{2,1,0:T(8,128)(2,1)S(1)} all-to-all(bf16[8,96,128]{2,1,0:T(8,128)(2,1)S(1)} %total.1), channel_id=1, replica_groups=mesh['dp'=32,'mp'=8] {'mp'}, dimensions={0} | all-to-all | bytes 393216 | tf_op jit(solution)/shard_map/all_to_all | solution.py:901
  112.5 1.4 %finish.1 = (bf16[2,120,256]{2,1,0:T(8,128)(2,1)}, f32[4,120,120]{2,1,0:T(8,128)}, f32[32,512]{1,0:T(8,128)}, f32[16,120]{1,0:T(8,128)}, f32[5,16]{1,0:T(8,128)}) custom-call(s32[1]{0:T(128)} %bitcast.dev_ref, s32[64]{0:T(128)S(1)} %copy-done.4, s32[16]{0:T(128)S(1)} %bitcast.18, bf16[8,96,128]{2,1,0:T(8,128)(2,1)S(1)} %all_to_all.11.in_ref, ...), custom_call_target="tpu_custom_call" | custom-call | tf_op jit(solution)/shard_map/finish/pallas_call | solution.py:816
Async XLA Ops:
  0.6 31.7 %copy-start.5 = (s32[16,1]{0,1:T(1,128)S(1)}, s32[16,1]{0,1:T(1,128)}, u32[]{:S(2)}) copy-start(s32[16,1]{0,1:T(1,128)} %param.10) | copy-start | bytes 196
  0.6 31.7 %collective-permute-start.2 = (bf16[2,120,256]{2,1,0:T(8,128)(2,1)}, bf16[2,120,256]{2,1,0:T(8,128)(2,1)S(1)}, u32[]{:S(2)}, u32[]{:S(2)}) collective-permute-start(bf16[2,120,256]{2,1,0:T(8,128)(2,1)} %bitcast.21), channel_id=1, source_target_pairs={{0,128},{8,136},{16,144},{24,152},{32,160},{40,168},{48,176},{56,1... | collective-permute-start | bytes 368648 | tf_op jit(solution)/shard_map/ppermute | solution.py:862
  7.9 0.9 copy-start.2
  8.8 0.7 copy-start.3
  9.5 0.7 copy-start.4
  10.2 22.1 %copy-start.6 = (bf16[2,256,120]{1,2,0:T(8,128)(2,1)S(1)}, bf16[2,256,120]{1,2,0:T(8,128)(2,1)}, u32[]{:S(2)}) copy-start(bf16[2,256,120]{1,2,0:T(8,128)(2,1)} %param.15) | copy-start | bytes 368644
  14.5 15.1 %collective-permute-start = (bf16[2,64,128]{2,1,0:T(8,128)(2,1)S(1)}, bf16[2,64,128]{2,1,0:T(8,128)(2,1)S(1)}, u32[]{:S(2)}, u32[]{:S(2)}) collective-permute-start(bf16[2,64,128]{2,1,0:T(8,128)(2,1)S(1)} %get-tuple-element.65), channel_id=1, source_target_pairs={{0,1},{1,2},{2,3},{3,4},{4,5},{5,6},{6,7},{8,9},{9,10},{10,11},{11... | collective-permute-start | bytes 98312 | tf_op jit(solution)/shard_map/ppermute | solution.py:835
  17.9 14.4 %collective-permute-start.1 = (bf16[2,64,128]{2,1,0:T(8,128)(2,1)S(1)}, bf16[2,64,128]{2,1,0:T(8,128)(2,1)S(1)}, u32[]{:S(2)}, u32[]{:S(2)}) collective-permute-start(bf16[2,64,128]{2,1,0:T(8,128)(2,1)S(1)} %get-tuple-element.66), channel_id=1, source_target_pairs={{1,0},{2,1},{3,2},{4,3},{5,4},{6,5},{7,6},{9,8},{10,9},{11,10},{12... | collective-permute-start | bytes 98312 | tf_op jit(solution)/shard_map/ppermute | solution.py:835
  20.4 21.8 %collective-permute-start.5 = (bf16[2,256,128]{2,1,0:T(8,128)(2,1)S(1)}, bf16[2,256,128]{2,1,0:T(8,128)(2,1)S(1)}, u32[]{:S(2)}, u32[]{:S(2)}) collective-permute-start(bf16[2,256,128]{2,1,0:T(8,128)(2,1)S(1)} %get-tuple-element.71.feat_ref.refs_0_), channel_id=1, source_target_pairs={{0,1},{1,2},{2,3},{3,0},{4,5},{5,6},{6,7},{7,4},{8,9},{9,10},{10,1... | collective-permute-start | bytes 393224 | tf_op jit(solution)/shard_map/ppermute | solution.py:840
  22.0 20.2 %collective-permute-start.6 = (bf16[2,256,128]{2,1,0:T(8,128)(2,1)S(1)}, bf16[2,256,128]{2,1,0:T(8,128)(2,1)S(1)}, u32[]{:S(2)}, u32[]{:S(2)}) collective-permute-start(bf16[2,256,128]{2,1,0:T(8,128)(2,1)S(1)} %get-tuple-element.71.feat_ref.refs_0_), channel_id=1, source_target_pairs={{0,2},{1,3},{2,0},{3,1},{4,6},{5,7},{6,4},{7,5},{8,10},{9,11},{10,... | collective-permute-start | bytes 393224 | tf_op jit(solution)/shard_map/ppermute | solution.py:840
  22.7 2.0 %copy-start = (bf16[128,120,120]{0,2,1:T(8,128)(2,1)S(1)}, bf16[128,120,120]{0,2,1:T(8,128)(2,1)}, u32[]{:S(2)}) copy-start(bf16[128,120,120]{0,2,1:T(8,128)(2,1)} %param.14) | copy-start | bytes 11059204
  29.7 12.5 %collective-permute-start.7 = (bf16[2,256,128]{2,1,0:T(8,128)(2,1)S(1)}, bf16[2,256,128]{2,1,0:T(8,128)(2,1)S(1)}, u32[]{:S(2)}, u32[]{:S(2)}) collective-permute-start(bf16[2,256,128]{2,1,0:T(8,128)(2,1)S(1)} %get-tuple-element.71.feat_ref.refs_0_), channel_id=1, source_target_pairs={{0,3},{1,0},{2,1},{3,2},{4,7},{5,4},{6,5},{7,6},{8,11},{9,8},{10,9... | collective-permute-start | bytes 393224 | tf_op jit(solution)/shard_map/ppermute | solution.py:840
  32.3 21.3 %copy-start.1 = (bf16[1024,512]{1,0:T(8,128)(2,1)S(1)}, bf16[1024,512]{1,0:T(8,128)(2,1)}, u32[]{:S(2)}) copy-start(bf16[1024,512]{1,0:T(8,128)(2,1)} %conv_ref.1) | copy-start | bytes 3145732
  36.3 5.9 %collective-permute-start.3 = (bf16[2,64,128]{2,1,0:T(8,128)(2,1)S(1)}, bf16[2,64,128]{2,1,0:T(8,128)(2,1)S(1)}, u32[]{:S(2)}, u32[]{:S(2)}) collective-permute-start(bf16[2,64,128]{2,1,0:T(8,128)(2,1)S(1)} %get-tuple-element.69), channel_id=1, source_target_pairs={{0,1},{1,2},{2,3},{3,4},{4,5},{5,6},{6,7},{8,9},{9,10},{10,11},{11... | collective-permute-start | bytes 98312 | tf_op jit(solution)/shard_map/ppermute | solution.py:835
  38.3 5.8 %collective-permute-start.4 = (bf16[2,64,128]{2,1,0:T(8,128)(2,1)S(1)}, bf16[2,64,128]{2,1,0:T(8,128)(2,1)S(1)}, u32[]{:S(2)}, u32[]{:S(2)}) collective-permute-start(bf16[2,64,128]{2,1,0:T(8,128)(2,1)S(1)} %get-tuple-element.70), channel_id=1, source_target_pairs={{1,0},{2,1},{3,2},{4,3},{5,4},{6,5},{7,6},{9,8},{10,9},{11,10},{12... | collective-permute-start | bytes 98312 | tf_op jit(solution)/shard_map/ppermute | solution.py:835
  44.1 17.4 %collective-permute-start.10 = (bf16[2,320,128]{2,1,0:T(8,128)(2,1)S(1)}, bf16[2,320,128]{2,1,0:T(8,128)(2,1)S(1)}, u32[]{:S(2)}, u32[]{:S(2)}) collective-permute-start(bf16[2,320,128]{2,1,0:T(8,128)(2,1)S(1)} %get-tuple-element.97.refs_4_), channel_id=1, source_target_pairs={{0,3},{1,0},{2,1},{3,2},{4,7},{5,4},{6,5},{7,6},{8,11},{9,8},{10,9... | collective-permute-start | bytes 491528 | tf_op jit(solution)/shard_map/ppermute | solution.py:840
  46.1 15.4 %collective-permute-start.8 = (bf16[2,320,128]{2,1,0:T(8,128)(2,1)S(1)}, bf16[2,320,128]{2,1,0:T(8,128)(2,1)S(1)}, u32[]{:S(2)}, u32[]{:S(2)}) collective-permute-start(bf16[2,320,128]{2,1,0:T(8,128)(2,1)S(1)} %get-tuple-element.97.refs_4_), channel_id=1, source_target_pairs={{0,1},{1,2},{2,3},{3,0},{4,5},{5,6},{6,7},{7,4},{8,9},{9,10},{10,1... | collective-permute-start | bytes 491528 | tf_op jit(solution)/shard_map/ppermute | solution.py:840
  47.2 14.3 %collective-permute-start.9 = (bf16[2,320,128]{2,1,0:T(8,128)(2,1)S(1)}, bf16[2,320,128]{2,1,0:T(8,128)(2,1)S(1)}, u32[]{:S(2)}, u32[]{:S(2)}) collective-permute-start(bf16[2,320,128]{2,1,0:T(8,128)(2,1)S(1)} %get-tuple-element.97.refs_4_), channel_id=1, source_target_pairs={{0,2},{1,3},{2,0},{3,1},{4,6},{5,7},{6,4},{7,5},{8,10},{9,11},{10,... | collective-permute-start | bytes 491528 | tf_op jit(solution)/shard_map/ppermute | solution.py:840
  61.5 2.3 %collective-permute-start.11 = (bf16[4,576,128]{2,1,0:T(8,128)(2,1)S(1)}, bf16[4,576,128]{2,1,0:T(8,128)(2,1)S(1)}, u32[]{:S(2)}, u32[]{:S(2)}) collective-permute-start(bf16[4,576,128]{2,1,0:T(8,128)(2,1)S(1)} %get-tuple-element.88), channel_id=1, source_target_pairs={{0,8},{8,0},{16,24},{24,16},{32,40},{40,32},{48,56},{56,48},{64,72... | collective-permute-start | bytes 1769480 | tf_op jit(solution)/shard_map/ppermute | solution.py:890
  68.5 2.0 %collective-permute-start.12 = (bf16[2,16,64,128]{3,2,1,0:T(8,128)(2,1)S(1)}, bf16[2,16,64,128]{3,2,1,0:T(8,128)(2,1)S(1)}, u32[]{:S(2)}, u32[]{:S(2)}) collective-permute-start(bf16[2,16,64,128]{3,2,1,0:T(8,128)(2,1)S(1)} %get-tuple-element.102), channel_id=1, source_target_pairs={{0,8},{8,0},{16,24},{24,16},{32,40},{40,32},{48,56},{56,48},{64,72... | collective-permute-start | bytes 1572872 | tf_op jit(solution)/shard_map/ppermute | solution.py:894
  70.7 10.7 %collective-permute-start.13 = (bf16[16,64,128]{2,1,0:T(8,128)(2,1)S(1)}, bf16[16,64,128]{2,1,0:T(8,128)(2,1)S(1)}, u32[]{:S(2)}, u32[]{:S(2)}) collective-permute-start(bf16[16,64,128]{2,1,0:T(8,128)(2,1)S(1)} %get-tuple-element.104), channel_id=1, source_target_pairs={{0,4},{1,5},{2,6},{3,7},{4,0},{5,1},{6,2},{7,3},{8,12},{9,13},{10,... | collective-permute-start | bytes 786440 | tf_op jit(solution)/shard_map/ppermute | solution.py:895
  70.8 10.3 %collective-permute-start.14 = (bf16[576,128]{1,0:T(8,128)(2,1)S(1)}, bf16[576,128]{1,0:T(8,128)(2,1)S(1)}, u32[]{:S(2)}, u32[]{:S(2)}) collective-permute-start(bf16[576,128]{1,0:T(8,128)(2,1)S(1)} %get-tuple-element.106), channel_id=1, source_target_pairs={{0,2},{1,3},{2,0},{3,1},{4,6},{5,7},{6,4},{7,5},{8,10},{9,11},{10,... | collective-permute-start | bytes 442376 | tf_op jit(solution)/shard_map/ppermute | solution.py:840
  70.9 10.2 %collective-permute-start.15 = (bf16[576,128]{1,0:T(8,128)(2,1)S(1)}, bf16[576,128]{1,0:T(8,128)(2,1)S(1)}, u32[]{:S(2)}, u32[]{:S(2)}) collective-permute-start(bf16[576,128]{1,0:T(8,128)(2,1)S(1)} %get-tuple-element.107), channel_id=1, source_target_pairs={{0,1},{1,2},{2,3},{3,0},{4,5},{5,6},{6,7},{7,4},{8,9},{9,10},{10,1... | collective-permute-start | bytes 442376 | tf_op jit(solution)/shard_map/ppermute | solution.py:840
  71.7 9.7 %collective-permute-start.16 = (bf16[576,128]{1,0:T(8,128)(2,1)S(1)}, bf16[576,128]{1,0:T(8,128)(2,1)S(1)}, u32[]{:S(2)}, u32[]{:S(2)}) collective-permute-start(bf16[576,128]{1,0:T(8,128)(2,1)S(1)} %get-tuple-element.108), channel_id=1, source_target_pairs={{0,3},{1,0},{2,1},{3,2},{4,7},{5,4},{6,5},{7,6},{8,11},{9,8},{10,9... | collective-permute-start | bytes 442376 | tf_op jit(solution)/shard_map/ppermute | solution.py:840
  73.0 8.1 %collective-permute-start.17 = (bf16[120,256]{1,0:T(8,128)(2,1)S(1)}, bf16[120,256]{1,0:T(8,128)(2,1)S(1)}, u32[]{:S(2)}, u32[]{:S(2)}) collective-permute-start(bf16[120,256]{1,0:T(8,128)(2,1)S(1)} %get-tuple-element.109), channel_id=1, source_target_pairs={{0,128},{8,136},{16,144},{24,152},{32,160},{40,168},{48,176},{56,1... | collective-permute-start | bytes 184328 | tf_op jit(solution)/shard_map/ppermute | solution.py:896

commit v10 on v9

--- a/solution.py
+++ b/solution.py
@@ -868,9 +868,7 @@
         place, features, low, high, ahead, cot, received
     )
     low, high = neighbours(tail, head)
-    piece, low, high, all_features = lax.optimization_barrier(
-        (piece, low, high, all_features)
-    )
+    piece, all_features = lax.optimization_barrier((piece, all_features))
     pieces = around_x(piece)
     audio_grad, keep, send = backward(
         scale,
@@ -894,10 +892,10 @@
     stay, leave = halve(dev, pos_keep, lax.ppermute(pos_send, "dp", core_swap))
     pos_parts = (stay, lax.ppermute(leave, "mp", [(i, i ^ X) for i in range(MP)]))
     other = lax.ppermute(sent, "dp", swap)
-    rest_parts, other = lax.optimization_barrier((rest_parts, other))
     cells = make_cells(pos_parts, rest_parts)
     groups = [list(range(bit, DP, 2)) for bit in range(2)]
     cells = lax.all_to_all(cells, "dp", 0, 0, axis_index_groups=groups, tiled=True)
+    cells, other = lax.optimization_barrier((cells, other))
     cells = lax.all_to_all(total(cells), "mp", 0, 0, tiled=True)
     hidden, grad_pos, grad_conv, grad_proj, grad_channels = finish(place, cells, states, other)
     return (

time: 115 us -> 112 us (0.974)
  blocking collectives: 30.9 us -> 10.4 us
  starting transfers between devices: 36.5 us -> 46.2 us
  waiting for transfers between devices: 13.8 us -> 20.6 us
    all_to_all x1 -> x0, blocking collectives: 20.5 us -> none  [per_device(): lax.all_to_all(cells, 'dp', 0, 0, axis_index_groups=groups, tiled=True)]
    all_to_all x0 -> x1, starting transfers between devices: none -> 5.75 us  [per_device(): lax.all_to_all(cells, 'dp', 0, 0, axis_index_groups=groups, tiled=True)]
    ppermute x9, waiting for transfers between devices: 0.32 us -> 5.96 us  [along_x(): return lax.ppermute(block, 'mp', route)]
    ppermute x1, starting transfers between devices: 0.32 us -> 5.84 us  [per_device(): other = lax.ppermute(sent, 'dp', swap)]
    ppermute x1, waiting for transfers between devices: 7.81 us -> 10.8 us  [per_device(): other = lax.ppermute(sent, 'dp', swap)]
    ppermute x2, waiting for transfers between devices: 1.84 us -> 0.01 us  [neighbours(): lax.ppermute(head, 'mp', backward_route)]
    ppermute x9, starting transfers between devices: 16.7 us -> 15.1 us  [along_x(): return lax.ppermute(block, 'mp', route)]
    unnamed x14 -> x16, local copies, waits for them, and re-layouts: 4.33 us -> 4.34 us
  transfers between devices with their start and end apart: 18 -> 19, of which waited for: 5 -> 6; matrix products, arithmetic and copies ran while one was open for 0% -> 0% of each run, Pallas kernels for 19% -> 19%
where the time goes in v10:
time: 112 us; the launch traced here: 111 us
  starting transfers between devices  46.2 us (41%)
  Pallas kernels  28.4 us (25%)
  waiting for transfers between devices  20.6 us (18%)
  blocking collectives  10.4 us (9%)
  local copies, waits for them, and re-layouts  4.34 us (4%)
    ppermute x9, starting transfers between devices, along_x(): return lax.ppermute(block, 'mp', route)  15.1 us
    ppermute x1, waiting for transfers between devices, per_device(): other = lax.ppermute(sent, 'dp', swap)  10.8 us
    all_to_all x1, blocking collectives, per_device(): cells = lax.all_to_all(total(cells), 'mp', 0, 0, tiled=True)  10.4 us
    pallas_call x1, Pallas kernels, backward(): pl.pallas_call(functools.partial(backward_body, scale), grid=(SLOTS,), ou...  7.9 us
    ppermute x1, starting transfers between devices, per_device(): received = lax.ppermute(cot, 'dp', swap)  7.28 us
    ppermute x2, starting transfers between devices, neighbours(): lax.ppermute(head, 'mp', backward_route)  6.36 us
    ppermute x9, waiting for transfers between devices, along_x(): return lax.ppermute(block, 'mp', route)  5.96 us
    ppermute x1, starting transfers between devices, per_device(): other = lax.ppermute(sent, 'dp', swap)  5.84 us
  transfers between devices with their start and end apart: 19, of which 6 were waited for; matrix products, arithmetic and copies ran while one was open for 0% of the time, Pallas kernels for 19%

profile of v10, /device:TPU:2, one launch (start us, length us, event | category | flops | bytes accessed | tf_op | source)
XLA Modules:
  0.0 110.8 jit_solution(18084009266830725602)
XLA Ops:
  0.6 0.0 copy-start.6
  0.6 7.3 %collective-permute-start.2 = (bf16[2,120,256]{2,1,0:T(8,128)(2,1)}, bf16[2,120,256]{2,1,0:T(8,128)(2,1)S(1)}, u32[]{:S(2)}, u32[]{:S(2)}) collective-permute-start(bf16[2,120,256]{2,1,0:T(8,128)(2,1)} %bitcast.21), channel_id=1, source_target_pairs={{0,128},{8,136},{16,144},{24,152},{32,160},{40,168},{48,176},{56,1... | collective-permute-start | bytes 368648 | tf_op jit(solution)/shard_map/ppermute | solution.py:862
  7.9 0.0 copy-start.2
  7.9 0.9 copy-done.2
  8.8 0.0 copy-start.3
  8.8 0.7 copy-done.3
  9.5 0.0 copy-start.4
  9.5 0.7 copy-done.4
  10.2 0.0 copy-start.7
  10.2 4.3 %encode.1 = (bf16[2,256,128]{2,1,0:T(8,128)(2,1)S(1)}, bf16[2,64,128]{2,1,0:T(8,128)(2,1)S(1)}, bf16[2,64,128]{2,1,0:T(8,128)(2,1)S(1)}, bf16[2,256,1024]{2,1,0:...) custom-call(s32[1]{0:T(128)} %bitcast.dev_ref, ...), custom_call_target="tpu_custom_call" | custom-call | flops 603979776 | bytes 8388608 | tf_op jit(solution)/shard_map/encode/pallas_call | solution.py:251
  14.5 3.4 %collective-permute-start = (bf16[2,64,128]{2,1,0:T(8,128)(2,1)S(1)}, bf16[2,64,128]{2,1,0:T(8,128)(2,1)S(1)}, u32[]{:S(2)}, u32[]{:S(2)}) collective-permute-start(bf16[2,64,128]{2,1,0:T(8,128)(2,1)S(1)} %get-tuple-element.60), channel_id=1, source_target_pairs={{0,1},{1,2},{2,3},{3,4},{4,5},{5,6},{6,7},{8,9},{9,10},{10,11},{11... | collective-permute-start | bytes 98312 | tf_op jit(solution)/shard_map/ppermute | solution.py:835
  17.9 2.4 %collective-permute-start.1 = (bf16[2,64,128]{2,1,0:T(8,128)(2,1)S(1)}, bf16[2,64,128]{2,1,0:T(8,128)(2,1)S(1)}, u32[]{:S(2)}, u32[]{:S(2)}) collective-permute-start(bf16[2,64,128]{2,1,0:T(8,128)(2,1)S(1)} %get-tuple-element.61), channel_id=1, source_target_pairs={{1,0},{2,1},{3,2},{4,3},{5,4},{6,5},{7,6},{9,8},{10,9},{11,10},{12... | collective-permute-start | bytes 98312 | tf_op jit(solution)/shard_map/ppermute | solution.py:835
  20.4 1.6 %collective-permute-start.3 = (bf16[2,256,128]{2,1,0:T(8,128)(2,1)S(1)}, bf16[2,256,128]{2,1,0:T(8,128)(2,1)S(1)}, u32[]{:S(2)}, u32[]{:S(2)}) collective-permute-start(bf16[2,256,128]{2,1,0:T(8,128)(2,1)S(1)} %get-tuple-element.64.feat_ref.refs_0_), channel_id=1, source_target_pairs={{0,1},{1,2},{2,3},{3,0},{4,5},{5,6},{6,7},{7,4},{8,9},{9,10},{10,1... | collective-permute-start | bytes 393224 | tf_op jit(solution)/shard_map/ppermute | solution.py:840
  22.0 0.7 collective-permute-start.4
  22.7 2.0 %copy-done = bf16[128,120,120]{0,2,1:T(8,128)(2,1)S(1)} copy-done((bf16[128,120,120]{0,2,1:T(8,128)(2,1)S(1)}, bf16[128,120,120]{0,2,1:T(8,128)(2,1)}, u32[]{:S(2)}) %copy-start) | copy-done | bytes 3686424
  24.7 4.9 %turn.1 = (bf16[16,128,1024]{2,1,0:T(8,128)(2,1)S(1)}, bf16[8,128,2048]{2,1,0:T(8,128)(2,1)S(1)}) custom-call(bf16[120,120,128]{2,1,0:T(8,128)(2,1)S(1)} %bitcast.10), custom_call_target="tpu_custom_call" | custom-call | bytes 12582912 | tf_op jit(solution)/shard_map/turn/pallas_call | solution.py:131
  29.7 0.0 collective-permute-done.low_ref
  29.7 2.6 %collective-permute-start.5 = (bf16[2,256,128]{2,1,0:T(8,128)(2,1)S(1)}, bf16[2,256,128]{2,1,0:T(8,128)(2,1)S(1)}, u32[]{:S(2)}, u32[]{:S(2)}) collective-permute-start(bf16[2,256,128]{2,1,0:T(8,128)(2,1)S(1)} %get-tuple-element.64.feat_ref.refs_0_), channel_id=1, source_target_pairs={{0,3},{1,0},{2,1},{3,2},{4,7},{5,4},{6,5},{7,6},{8,11},{9,8},{10,9... | collective-permute-start | bytes 393224 | tf_op jit(solution)/shard_map/ppermute | solution.py:840
  32.3 0.0 collective-permute-done.1.high_ref
  32.3 0.0 collective-permute-done.2.recv_ref
  32.3 0.0 copy-done.6
  32.3 0.0 copy-done.7
  32.3 0.0 copy-start.1
  32.3 4.0 %mix.1 = (bf16[2,120,256]{2,1,0:T(8,128)(2,1)S(1)}, bf16[120,256]{1,0:T(8,128)(2,1)S(1)}, bf16[2,256,128]{2,1,0:T(8,128)(2,1)S(1)}, bf16[2,64,128]{2,1,0:T(8,128...) custom-call(s32[1]{0:T(128)} %bitcast.dev_ref, s32[64]{0:T(128)S(1)} %copy-done.4, ...), custom_call_target="tpu_custom_call" | custom-call | flops 2550136832 | bytes 7340032 | tf_op jit(solution)/shard_map/mix/pallas_call | solution.py:380
  36.3 1.9 %collective-permute-start.6 = (bf16[2,64,128]{2,1,0:T(8,128)(2,1)S(1)}, bf16[2,64,128]{2,1,0:T(8,128)(2,1)S(1)}, u32[]{:S(2)}, u32[]{:S(2)}) collective-permute-start(bf16[2,64,128]{2,1,0:T(8,128)(2,1)S(1)} %get-tuple-element.69), channel_id=1, source_target_pairs={{0,1},{1,2},{2,3},{3,4},{4,5},{5,6},{6,7},{8,9},{9,10},{10,11},{11... | collective-permute-start | bytes 98312 | tf_op jit(solution)/shard_map/ppermute | solution.py:835
  38.3 3.9 %collective-permute-start.7 = (bf16[2,64,128]{2,1,0:T(8,128)(2,1)S(1)}, bf16[2,64,128]{2,1,0:T(8,128)(2,1)S(1)}, u32[]{:S(2)}, u32[]{:S(2)}) collective-permute-start(bf16[2,64,128]{2,1,0:T(8,128)(2,1)S(1)} %get-tuple-element.70), channel_id=1, source_target_pairs={{1,0},{2,1},{3,2},{4,3},{5,4},{6,5},{7,6},{9,8},{10,9},{11,10},{12... | collective-permute-start | bytes 98312 | tf_op jit(solution)/shard_map/ppermute | solution.py:835
  42.2 0.0 collective-permute-done.3.refs_1_
  42.2 0.0 collective-permute-done.4.refs_2_
  42.2 0.0 collective-permute-done.5.refs_3_
  42.2 0.1 collective-permute-start.10
  42.3 2.0 %collective-permute-start.8 = (bf16[2,320,128]{2,1,0:T(8,128)(2,1)S(1)}, bf16[2,320,128]{2,1,0:T(8,128)(2,1)S(1)}, u32[]{:S(2)}, u32[]{:S(2)}) collective-permute-start(bf16[2,320,128]{2,1,0:T(8,128)(2,1)S(1)} %get-tuple-element.90.refs_4_), channel_id=1, source_target_pairs={{0,1},{1,2},{2,3},{3,0},{4,5},{5,6},{6,7},{7,4},{8,9},{9,10},{10,1... | collective-permute-start | bytes 491528 | tf_op jit(solution)/shard_map/ppermute | solution.py:840
  44.3 3.4 %collective-permute-start.9 = (bf16[2,320,128]{2,1,0:T(8,128)(2,1)S(1)}, bf16[2,320,128]{2,1,0:T(8,128)(2,1)S(1)}, u32[]{:S(2)}, u32[]{:S(2)}) collective-permute-start(bf16[2,320,128]{2,1,0:T(8,128)(2,1)S(1)} %get-tuple-element.90.refs_4_), channel_id=1, source_target_pairs={{0,2},{1,3},{2,0},{3,1},{4,6},{5,7},{6,4},{7,5},{8,10},{9,11},{10,... | collective-permute-start | bytes 491528 | tf_op jit(solution)/shard_map/ppermute | solution.py:840
  47.7 0.0 collective-permute-done.6.low_ref
  47.7 0.0 collective-permute-done.7.high_ref
  47.7 0.0 copy-done.1
  47.8 7.9 %backward.1 = (bf16[2,512,512]{2,1,0:T(8,128)(2,1)}, bf16[4,576,128]{2,1,0:T(8,128)(2,1)S(1)}, bf16[4,576,128]{2,1,0:T(8,128)(2,1)S(1)}) custom-call(s32[1]{0:T(128)} %bitcast.dev_ref, s32[64]{0:T(128)S(1)} %copy-done.4, s32[16]{0:T(128)S(1)} %bitcast.16, bf16[2,256,128]{2,1,0:T(8,128)(2,1)S(1)} %get-tuple-element.68.slopes_ref, ...), custom_call_target="tpu_custom_call" | custom-call | flops 3758096384 | bytes 14680064 | tf_op jit(solution)/shard_map/backward/pallas_call | solution.py:633
  55.7 0.0 collective-permute-done.10.refs_7_
  55.7 0.0 collective-permute-done.8.refs_5_
  55.7 0.0 collective-permute-done.9.refs_6_
  55.7 0.3 collective-permute-start.11
  55.9 2.0 %collective-permute-done.11.recv_ref = bf16[4,576,128]{2,1,0:T(8,128)(2,1)S(1)} collective-permute-done((bf16[4,576,128]{2,1,0:T(8,128)(2,1)S(1)}, bf16[4,576,128]{2,1,0:T(8,128)(2,1)S(1)}, u32[]{:S(2)}, u32[]{:S(2)}) %collective-permute-start.11) | collective-permute-done | bytes 589856 | tf_op jit(solution)/shard_map/ppermute | solution.py:888
  57.9 0.1 join.1
  58.1 4.6 %taps.1 = (bf16[2,16,64,128]{3,2,1,0:T(8,128)(2,1)S(1)}, bf16[2,16,64,128]{3,2,1,0:T(8,128)(2,1)S(1)}) custom-call(s32[1]{0:T(128)} %bitcast.dev_ref, s32[64]{0:T(128)S(1)} %copy-done.4, s32[16]{0:T(128)S(1)} %bitcast.17, bf16[2,256,128]{2,1,0:T(8,128)(2,1)S(1)} %get-tuple-element.64.feat_ref.refs_0_, ...), custom_call_target="tpu_custom_call" | custom-call | flops 2550136832 | bytes 4194304 | tf_op jit(solution)/shard_map/taps/pallas_call | solution.py:473
  62.7 0.0 copy-start.5
  62.7 0.2 collective-permute-start.12
  62.9 1.8 %collective-permute-done.12.recv_ref = bf16[2,16,64,128]{3,2,1,0:T(8,128)(2,1)S(1)} collective-permute-done((bf16[2,16,64,128]{3,2,1,0:T(8,128)(2,1)S(1)}, bf16[2,16,64,128]{3,2,1,0:T(8,128)(2,1)S(1)}, u32[]{:S(2)}, u32[]{:S(2)}) %collective-permute-start.12) | collective-permute-done | bytes 524320 | tf_op jit(solution)/shard_map/ppermute | solution.py:892
  64.7 0.1 halve.1
  64.8 0.1 collective-permute-start.13
  64.9 2.7 %collective-permute-start.14 = (bf16[576,128]{1,0:T(8,128)(2,1)S(1)}, bf16[576,128]{1,0:T(8,128)(2,1)S(1)}, u32[]{:S(2)}, u32[]{:S(2)}) collective-permute-start(bf16[576,128]{1,0:T(8,128)(2,1)S(1)} %get-tuple-element.99), channel_id=1, source_target_pairs={{0,2},{1,3},{2,0},{3,1},{4,6},{5,7},{6,4},{7,5},{8,10},{9,11},{10,... | collective-permute-start | bytes 442376 | tf_op jit(solution)/shard_map/ppermute | solution.py:840
  67.6 0.2 collective-permute-start.15
  67.8 1.8 %collective-permute-start.16 = (bf16[576,128]{1,0:T(8,128)(2,1)S(1)}, bf16[576,128]{1,0:T(8,128)(2,1)S(1)}, u32[]{:S(2)}, u32[]{:S(2)}) collective-permute-start(bf16[576,128]{1,0:T(8,128)(2,1)S(1)} %get-tuple-element.101), channel_id=1, source_target_pairs={{0,3},{1,0},{2,1},{3,2},{4,7},{5,4},{6,5},{7,6},{8,11},{9,8},{10,9... | collective-permute-start | bytes 442376 | tf_op jit(solution)/shard_map/ppermute | solution.py:840
  69.6 3.6 %collective-permute-done.14.refs_3_ = bf16[576,128]{1,0:T(8,128)(2,1)S(1)} collective-permute-done((bf16[576,128]{1,0:T(8,128)(2,1)S(1)}, bf16[576,128]{1,0:T(8,128)(2,1)S(1)}, u32[]{:S(2)}, u32[]{:S(2)}) %collective-permute-start.14) | collective-permute-done | bytes 147488 | tf_op jit(solution)/shard_map/ppermute | solution.py:840
  73.2 0.5 collective-permute-done.15.refs_4_
  73.7 1.9 %collective-permute-done.16.refs_5_ = bf16[576,128]{1,0:T(8,128)(2,1)S(1)} collective-permute-done((bf16[576,128]{1,0:T(8,128)(2,1)S(1)}, bf16[576,128]{1,0:T(8,128)(2,1)S(1)}, u32[]{:S(2)}, u32[]{:S(2)}) %collective-permute-start.16) | collective-permute-done | bytes 147488 | tf_op jit(solution)/shard_map/ppermute | solution.py:840
  75.6 0.0 collective-permute-done.13.refs_1_
  75.6 0.9 cells.1
  76.5 5.7 %all-to-all-start = ((bf16[16,96,128]{2,1,0:T(8,128)(2,1)}), bf16[16,96,128]{2,1,0:T(8,128)(2,1)S(1)}, u32[]{:S(2)}, u32[]{:S(2)}) async-start(bf16[16,96,128]{2,1,0:T(8,128)(2,1)} %cells.1), calls=%async_computation | async-start | bytes 786432 | tf_op jit(solution)/shard_map/all_to_all | solution.py:897
  82.3 5.8 %collective-permute-start.17 = (bf16[120,256]{1,0:T(8,128)(2,1)S(1)}, bf16[120,256]{1,0:T(8,128)(2,1)S(1)}, u32[]{:S(2)}, u32[]{:S(2)}) collective-permute-start(bf16[120,256]{1,0:T(8,128)(2,1)S(1)} %get-tuple-element.102), channel_id=1, source_target_pairs={{0,128},{8,136},{16,144},{24,152},{32,160},{40,168},{48,176},{56,1... | collective-permute-start | bytes 184328 | tf_op jit(solution)/shard_map/ppermute | solution.py:894
  88.1 10.8 %collective-permute-done.17.other_ref = bf16[120,256]{1,0:T(8,128)(2,1)S(1)} collective-permute-done((bf16[120,256]{1,0:T(8,128)(2,1)S(1)}, bf16[120,256]{1,0:T(8,128)(2,1)S(1)}, u32[]{:S(2)}, u32[]{:S(2)}) %collective-permute-start.17) | collective-permute-done | bytes 61472 | tf_op jit(solution)/shard_map/ppermute | solution.py:894
  98.9 0.0 all-to-all-done.in_ref
  98.9 0.1 total.1
  99.0 10.4 %all_to_all.10.in_ref = bf16[8,96,128]{2,1,0:T(8,128)(2,1)S(1)} all-to-all(bf16[8,96,128]{2,1,0:T(8,128)(2,1)S(1)} %total.1), channel_id=1, replica_groups=mesh['dp'=32,'mp'=8] {'mp'}, dimensions={0} | all-to-all | bytes 393216 | tf_op jit(solution)/shard_map/all_to_all | solution.py:899
  109.4 0.0 copy-done.5
  109.4 1.4 %finish.1 = (bf16[2,120,256]{2,1,0:T(8,128)(2,1)}, f32[4,120,120]{2,1,0:T(8,128)}, f32[32,512]{1,0:T(8,128)}, f32[16,120]{1,0:T(8,128)}, f32[5,16]{1,0:T(8,128)}) custom-call(s32[1]{0:T(128)} %bitcast.dev_ref, s32[64]{0:T(128)S(1)} %copy-done.5, s32[16]{0:T(128)S(1)} %bitcast.18, bf16[8,96,128]{2,1,0:T(8,128)(2,1)S(1)} %all_to_all.10.in_ref, ...), custom_call_target="tpu_custom_call" | custom-call | tf_op jit(solution)/shard_map/finish/pallas_call | solution.py:816
  (1 shorter events, 0.0 us)
Async XLA Ops:
  0.6 31.7 %copy-start.6 = (s32[16,1]{0,1:T(1,128)S(1)}, s32[16,1]{0,1:T(1,128)}, u32[]{:S(2)}) copy-start(s32[16,1]{0,1:T(1,128)} %param.10) | copy-start | bytes 196
  0.6 31.7 %collective-permute-start.2 = (bf16[2,120,256]{2,1,0:T(8,128)(2,1)}, bf16[2,120,256]{2,1,0:T(8,128)(2,1)S(1)}, u32[]{:S(2)}, u32[]{:S(2)}) collective-permute-start(bf16[2,120,256]{2,1,0:T(8,128)(2,1)} %bitcast.21), channel_id=1, source_target_pairs={{0,128},{8,136},{16,144},{24,152},{32,160},{40,168},{48,176},{56,1... | collective-permute-start | bytes 368648 | tf_op jit(solution)/shard_map/ppermute | solution.py:862
  7.9 0.9 copy-start.2
  8.8 0.7 copy-start.3
  9.5 0.7 copy-start.4
  10.2 22.1 %copy-start.7 = (bf16[2,256,120]{1,2,0:T(8,128)(2,1)S(1)}, bf16[2,256,120]{1,2,0:T(8,128)(2,1)}, u32[]{:S(2)}) copy-start(bf16[2,256,120]{1,2,0:T(8,128)(2,1)} %param.15) | copy-start | bytes 368644
  14.5 15.1 %collective-permute-start = (bf16[2,64,128]{2,1,0:T(8,128)(2,1)S(1)}, bf16[2,64,128]{2,1,0:T(8,128)(2,1)S(1)}, u32[]{:S(2)}, u32[]{:S(2)}) collective-permute-start(bf16[2,64,128]{2,1,0:T(8,128)(2,1)S(1)} %get-tuple-element.60), channel_id=1, source_target_pairs={{0,1},{1,2},{2,3},{3,4},{4,5},{5,6},{6,7},{8,9},{9,10},{10,11},{11... | collective-permute-start | bytes 98312 | tf_op jit(solution)/shard_map/ppermute | solution.py:835
  17.9 14.4 %collective-permute-start.1 = (bf16[2,64,128]{2,1,0:T(8,128)(2,1)S(1)}, bf16[2,64,128]{2,1,0:T(8,128)(2,1)S(1)}, u32[]{:S(2)}, u32[]{:S(2)}) collective-permute-start(bf16[2,64,128]{2,1,0:T(8,128)(2,1)S(1)} %get-tuple-element.61), channel_id=1, source_target_pairs={{1,0},{2,1},{3,2},{4,3},{5,4},{6,5},{7,6},{9,8},{10,9},{11,10},{12... | collective-permute-start | bytes 98312 | tf_op jit(solution)/shard_map/ppermute | solution.py:835
  20.4 21.8 %collective-permute-start.3 = (bf16[2,256,128]{2,1,0:T(8,128)(2,1)S(1)}, bf16[2,256,128]{2,1,0:T(8,128)(2,1)S(1)}, u32[]{:S(2)}, u32[]{:S(2)}) collective-permute-start(bf16[2,256,128]{2,1,0:T(8,128)(2,1)S(1)} %get-tuple-element.64.feat_ref.refs_0_), channel_id=1, source_target_pairs={{0,1},{1,2},{2,3},{3,0},{4,5},{5,6},{6,7},{7,4},{8,9},{9,10},{10,1... | collective-permute-start | bytes 393224 | tf_op jit(solution)/shard_map/ppermute | solution.py:840
  22.0 20.2 %collective-permute-start.4 = (bf16[2,256,128]{2,1,0:T(8,128)(2,1)S(1)}, bf16[2,256,128]{2,1,0:T(8,128)(2,1)S(1)}, u32[]{:S(2)}, u32[]{:S(2)}) collective-permute-start(bf16[2,256,128]{2,1,0:T(8,128)(2,1)S(1)} %get-tuple-element.64.feat_ref.refs_0_), channel_id=1, source_target_pairs={{0,2},{1,3},{2,0},{3,1},{4,6},{5,7},{6,4},{7,5},{8,10},{9,11},{10,... | collective-permute-start | bytes 393224 | tf_op jit(solution)/shard_map/ppermute | solution.py:840
  22.7 2.0 %copy-start = (bf16[128,120,120]{0,2,1:T(8,128)(2,1)S(1)}, bf16[128,120,120]{0,2,1:T(8,128)(2,1)}, u32[]{:S(2)}) copy-start(bf16[128,120,120]{0,2,1:T(8,128)(2,1)} %param.14) | copy-start | bytes 11059204
  29.7 12.5 %collective-permute-start.5 = (bf16[2,256,128]{2,1,0:T(8,128)(2,1)S(1)}, bf16[2,256,128]{2,1,0:T(8,128)(2,1)S(1)}, u32[]{:S(2)}, u32[]{:S(2)}) collective-permute-start(bf16[2,256,128]{2,1,0:T(8,128)(2,1)S(1)} %get-tuple-element.64.feat_ref.refs_0_), channel_id=1, source_target_pairs={{0,3},{1,0},{2,1},{3,2},{4,7},{5,4},{6,5},{7,6},{8,11},{9,8},{10,9... | collective-permute-start | bytes 393224 | tf_op jit(solution)/shard_map/ppermute | solution.py:840
  32.3 15.4 %copy-start.1 = (bf16[1024,512]{1,0:T(8,128)(2,1)S(1)}, bf16[1024,512]{1,0:T(8,128)(2,1)}, u32[]{:S(2)}) copy-start(bf16[1024,512]{1,0:T(8,128)(2,1)} %conv_ref.1) | copy-start | bytes 3145732
  36.3 11.4 %collective-permute-start.6 = (bf16[2,64,128]{2,1,0:T(8,128)(2,1)S(1)}, bf16[2,64,128]{2,1,0:T(8,128)(2,1)S(1)}, u32[]{:S(2)}, u32[]{:S(2)}) collective-permute-start(bf16[2,64,128]{2,1,0:T(8,128)(2,1)S(1)} %get-tuple-element.69), channel_id=1, source_target_pairs={{0,1},{1,2},{2,3},{3,4},{4,5},{5,6},{6,7},{8,9},{9,10},{10,11},{11... | collective-permute-start | bytes 98312 | tf_op jit(solution)/shard_map/ppermute | solution.py:835
  38.3 9.5 %collective-permute-start.7 = (bf16[2,64,128]{2,1,0:T(8,128)(2,1)S(1)}, bf16[2,64,128]{2,1,0:T(8,128)(2,1)S(1)}, u32[]{:S(2)}, u32[]{:S(2)}) collective-permute-start(bf16[2,64,128]{2,1,0:T(8,128)(2,1)S(1)} %get-tuple-element.70), channel_id=1, source_target_pairs={{1,0},{2,1},{3,2},{4,3},{5,4},{6,5},{7,6},{9,8},{10,9},{11,10},{12... | collective-permute-start | bytes 98312 | tf_op jit(solution)/shard_map/ppermute | solution.py:835
  42.2 13.4 %collective-permute-start.10 = (bf16[2,320,128]{2,1,0:T(8,128)(2,1)S(1)}, bf16[2,320,128]{2,1,0:T(8,128)(2,1)S(1)}, u32[]{:S(2)}, u32[]{:S(2)}) collective-permute-start(bf16[2,320,128]{2,1,0:T(8,128)(2,1)S(1)} %get-tuple-element.90.refs_4_), channel_id=1, source_target_pairs={{0,3},{1,0},{2,1},{3,2},{4,7},{5,4},{6,5},{7,6},{8,11},{9,8},{10,9... | collective-permute-start | bytes 491528 | tf_op jit(solution)/shard_map/ppermute | solution.py:840
  42.3 13.3 %collective-permute-start.8 = (bf16[2,320,128]{2,1,0:T(8,128)(2,1)S(1)}, bf16[2,320,128]{2,1,0:T(8,128)(2,1)S(1)}, u32[]{:S(2)}, u32[]{:S(2)}) collective-permute-start(bf16[2,320,128]{2,1,0:T(8,128)(2,1)S(1)} %get-tuple-element.90.refs_4_), channel_id=1, source_target_pairs={{0,1},{1,2},{2,3},{3,0},{4,5},{5,6},{6,7},{7,4},{8,9},{9,10},{10,1... | collective-permute-start | bytes 491528 | tf_op jit(solution)/shard_map/ppermute | solution.py:840
  44.3 11.3 %collective-permute-start.9 = (bf16[2,320,128]{2,1,0:T(8,128)(2,1)S(1)}, bf16[2,320,128]{2,1,0:T(8,128)(2,1)S(1)}, u32[]{:S(2)}, u32[]{:S(2)}) collective-permute-start(bf16[2,320,128]{2,1,0:T(8,128)(2,1)S(1)} %get-tuple-element.90.refs_4_), channel_id=1, source_target_pairs={{0,2},{1,3},{2,0},{3,1},{4,6},{5,7},{6,4},{7,5},{8,10},{9,11},{10,... | collective-permute-start | bytes 491528 | tf_op jit(solution)/shard_map/ppermute | solution.py:840
  55.7 2.3 %collective-permute-start.11 = (bf16[4,576,128]{2,1,0:T(8,128)(2,1)S(1)}, bf16[4,576,128]{2,1,0:T(8,128)(2,1)S(1)}, u32[]{:S(2)}, u32[]{:S(2)}) collective-permute-start(bf16[4,576,128]{2,1,0:T(8,128)(2,1)S(1)} %get-tuple-element.81), channel_id=1, source_target_pairs={{0,8},{8,0},{16,24},{24,16},{32,40},{40,32},{48,56},{56,48},{64,72... | collective-permute-start | bytes 1769480 | tf_op jit(solution)/shard_map/ppermute | solution.py:888
  62.7 46.7 %copy-start.5 = (s32[64]{0:T(128)S(1)}, s32[64]{0:T(128)}, u32[]{:S(2)}) copy-start(s32[64]{0:T(128)} %len_ref.7) | copy-start | bytes 772
  62.7 2.0 %collective-permute-start.12 = (bf16[2,16,64,128]{3,2,1,0:T(8,128)(2,1)S(1)}, bf16[2,16,64,128]{3,2,1,0:T(8,128)(2,1)S(1)}, u32[]{:S(2)}, u32[]{:S(2)}) collective-permute-start(bf16[2,16,64,128]{3,2,1,0:T(8,128)(2,1)S(1)} %get-tuple-element.95), channel_id=1, source_target_pairs={{0,8},{8,0},{16,24},{24,16},{32,40},{40,32},{48,56},{56,48},{64,72... | collective-permute-start | bytes 1572872 | tf_op jit(solution)/shard_map/ppermute | solution.py:892
  64.8 10.7 %collective-permute-start.13 = (bf16[16,64,128]{2,1,0:T(8,128)(2,1)S(1)}, bf16[16,64,128]{2,1,0:T(8,128)(2,1)S(1)}, u32[]{:S(2)}, u32[]{:S(2)}) collective-permute-start(bf16[16,64,128]{2,1,0:T(8,128)(2,1)S(1)} %get-tuple-element.97), channel_id=1, source_target_pairs={{0,4},{1,5},{2,6},{3,7},{4,0},{5,1},{6,2},{7,3},{8,12},{9,13},{10,... | collective-permute-start | bytes 786440 | tf_op jit(solution)/shard_map/ppermute | solution.py:893
  64.9 8.3 %collective-permute-start.14 = (bf16[576,128]{1,0:T(8,128)(2,1)S(1)}, bf16[576,128]{1,0:T(8,128)(2,1)S(1)}, u32[]{:S(2)}, u32[]{:S(2)}) collective-permute-start(bf16[576,128]{1,0:T(8,128)(2,1)S(1)} %get-tuple-element.99), channel_id=1, source_target_pairs={{0,2},{1,3},{2,0},{3,1},{4,6},{5,7},{6,4},{7,5},{8,10},{9,11},{10,... | collective-permute-start | bytes 442376 | tf_op jit(solution)/shard_map/ppermute | solution.py:840
  67.6 6.1 %collective-permute-start.15 = (bf16[576,128]{1,0:T(8,128)(2,1)S(1)}, bf16[576,128]{1,0:T(8,128)(2,1)S(1)}, u32[]{:S(2)}, u32[]{:S(2)}) collective-permute-start(bf16[576,128]{1,0:T(8,128)(2,1)S(1)} %get-tuple-element.100), channel_id=1, source_target_pairs={{0,1},{1,2},{2,3},{3,0},{4,5},{5,6},{6,7},{7,4},{8,9},{9,10},{10,1... | collective-permute-start | bytes 442376 | tf_op jit(solution)/shard_map/ppermute | solution.py:840
  67.8 7.8 %collective-permute-start.16 = (bf16[576,128]{1,0:T(8,128)(2,1)S(1)}, bf16[576,128]{1,0:T(8,128)(2,1)S(1)}, u32[]{:S(2)}, u32[]{:S(2)}) collective-permute-start(bf16[576,128]{1,0:T(8,128)(2,1)S(1)} %get-tuple-element.101), channel_id=1, source_target_pairs={{0,3},{1,0},{2,1},{3,2},{4,7},{5,4},{6,5},{7,6},{8,11},{9,8},{10,9... | collective-permute-start | bytes 442376 | tf_op jit(solution)/shard_map/ppermute | solution.py:840
  76.5 22.4 %all-to-all-start = ((bf16[16,96,128]{2,1,0:T(8,128)(2,1)}), bf16[16,96,128]{2,1,0:T(8,128)(2,1)S(1)}, u32[]{:S(2)}, u32[]{:S(2)}) async-start(bf16[16,96,128]{2,1,0:T(8,128)(2,1)} %cells.1), calls=%async_computation | async-start | bytes 786432 | tf_op jit(solution)/shard_map/all_to_all | solution.py:897
  82.3 16.7 %collective-permute-start.17 = (bf16[120,256]{1,0:T(8,128)(2,1)S(1)}, bf16[120,256]{1,0:T(8,128)(2,1)S(1)}, u32[]{:S(2)}, u32[]{:S(2)}) collective-permute-start(bf16[120,256]{1,0:T(8,128)(2,1)S(1)} %get-tuple-element.102), channel_id=1, source_target_pairs={{0,128},{8,136},{16,144},{24,152},{32,160},{40,168},{48,176},{56,1... | collective-permute-start | bytes 184328 | tf_op jit(solution)/shard_map/ppermute | solution.py:894

commit v11 on v10

--- a/solution.py
+++ b/solution.py
@@ -884,18 +884,17 @@
         channels,
         proj,
     )
-    send, pieces, sent = lax.optimization_barrier((send, pieces, sent))
+    other = lax.ppermute(sent, "dp", swap)
+    send, pieces, other = lax.optimization_barrier((send, pieces, other))
     chunks = join(dev, keep, lax.ppermute(send, "dp", core_swap))
     chunks, pieces = lax.optimization_barrier((chunks, pieces))
     rest_parts = [chunks[0]] + [along_x(chunks[step], step) for step in (2, 1, 3)]
     pos_keep, pos_send = taps(scale, place, all_features, pieces)
     stay, leave = halve(dev, pos_keep, lax.ppermute(pos_send, "dp", core_swap))
     pos_parts = (stay, lax.ppermute(leave, "mp", [(i, i ^ X) for i in range(MP)]))
-    other = lax.ppermute(sent, "dp", swap)
     cells = make_cells(pos_parts, rest_parts)
     groups = [list(range(bit, DP, 2)) for bit in range(2)]
     cells = lax.all_to_all(cells, "dp", 0, 0, axis_index_groups=groups, tiled=True)
-    cells, other = lax.optimization_barrier((cells, other))
     cells = lax.all_to_all(total(cells), "mp", 0, 0, tiled=True)
     hidden, grad_pos, grad_conv, grad_proj, grad_channels = finish(place, cells, states, other)
     return (

time: 112 us -> 112 us (level)
  blocking collectives: 10.4 us -> 41.5 us
  starting transfers between devices: 46.2 us -> 32.3 us
  waiting for transfers between devices: 20.6 us -> 10.9 us
  Pallas kernels: 28.4 us -> 21.7 us
    all_to_all x0 -> x1, blocking collectives: none -> 32.7 us  [per_device(): lax.all_to_all(cells, 'dp', 0, 0, axis_index_groups=groups, tiled=True)]
    ppermute x1, waiting for transfers between devices: 10.8 us -> 0.01 us  [per_device(): other = lax.ppermute(sent, 'dp', swap)]
    all_to_all x1 -> x0, starting transfers between devices: 5.75 us -> none  [per_device(): lax.all_to_all(cells, 'dp', 0, 0, axis_index_groups=groups, tiled=True)]
    ppermute x1, starting transfers between devices: 5.84 us -> 1.4 us  [per_device(): other = lax.ppermute(sent, 'dp', swap)]
    ppermute x9, starting transfers between devices: 15.1 us -> 11.2 us  [along_x(): return lax.ppermute(block, 'mp', route)]
    pallas_call x1, Pallas kernels: 7.9 us -> 4.98 us  [backward(): pl.pallas_call(functools.partial(backward_body, scale), grid=(SLOTS,), ou...]
    ppermute x2, starting transfers between devices: 6.36 us -> 8.07 us  [neighbours(): lax.ppermute(head, 'mp', backward_route)]
    pallas_call x1, Pallas kernels: 4 us -> 2.36 us  [mix(): pl.pallas_call(mix_body, grid=(SLOTS,), out_shape=(jax.ShapeDtypeStruct((...]
  transfers between devices with their start and end apart: 19 -> 18, of which waited for: 6 -> 6; matrix products, arithmetic and copies ran while one was open for 0% -> 0% of each run, Pallas kernels for 19% -> 14%
where the time goes in v11:
time: 112 us
  blocking collectives  41.5 us (37%)
  starting transfers between devices  32.3 us (29%)
  Pallas kernels  21.7 us (19%)
  waiting for transfers between devices  10.9 us (10%)
  local copies, waits for them, and re-layouts  4.33 us (4%)
    all_to_all x1, blocking collectives, per_device(): lax.all_to_all(cells, 'dp', 0, 0, axis_index_groups=groups, tiled=True)  32.7 us
    ppermute x9, starting transfers between devices, along_x(): return lax.ppermute(block, 'mp', route)  11.2 us
    all_to_all x1, blocking collectives, per_device(): cells = lax.all_to_all(total(cells), 'mp', 0, 0, tiled=True)  8.86 us
    ppermute x2, starting transfers between devices, neighbours(): lax.ppermute(head, 'mp', backward_route)  8.07 us
    ppermute x1, starting transfers between devices, per_device(): received = lax.ppermute(cot, 'dp', swap)  7.28 us
    ppermute x9, waiting for transfers between devices, along_x(): return lax.ppermute(block, 'mp', route)  7.07 us
    pallas_call x1, Pallas kernels, backward(): pl.pallas_call(functools.partial(backward_body, scale), grid=(SLOTS,), ou...  4.98 us
    pallas_call x1, Pallas kernels, turn(): pl.pallas_call(turn_body, grid=(LANES // NEAR,), out_shape=(jax.ShapeDtyp...  4.93 us
  transfers between devices with their start and end apart: 18, of which 6 were waited for; matrix products, arithmetic and copies ran while one was open for 0% of the time, Pallas kernels for 14%

profile of v11, /device:TPU:2, one launch (start us, length us, event | category | flops | bytes accessed | tf_op | source)
XLA Modules:
  0.0 111.5 jit_solution(3034224979237131344)
XLA Ops:
  0.6 0.0 copy-start.5
  0.6 7.3 %collective-permute-start.2 = (bf16[2,120,256]{2,1,0:T(8,128)(2,1)}, bf16[2,120,256]{2,1,0:T(8,128)(2,1)S(1)}, u32[]{:S(2)}, u32[]{:S(2)}) collective-permute-start(bf16[2,120,256]{2,1,0:T(8,128)(2,1)} %bitcast.21), channel_id=1, source_target_pairs={{0,128},{8,136},{16,144},{24,152},{32,160},{40,168},{48,176},{56,1... | collective-permute-start | bytes 368648 | tf_op jit(solution)/shard_map/ppermute | solution.py:862
  7.9 0.0 copy-start.2
  7.9 0.9 copy-done.2
  8.8 0.0 copy-start.3
  8.8 0.7 copy-done.3
  9.5 0.0 copy-start.4
  9.5 0.7 copy-done.4
  10.2 0.0 copy-start.6
  10.2 2.9 %encode.1 = (bf16[2,256,128]{2,1,0:T(8,128)(2,1)S(1)}, bf16[2,64,128]{2,1,0:T(8,128)(2,1)S(1)}, bf16[2,64,128]{2,1,0:T(8,128)(2,1)S(1)}, bf16[2,256,1024]{2,1,0:...) custom-call(s32[1]{0:T(128)} %bitcast.dev_ref, ...), custom_call_target="tpu_custom_call" | custom-call | flops 603979776 | bytes 8388608 | tf_op jit(solution)/shard_map/encode/pallas_call | solution.py:251
  13.2 2.1 %collective-permute-start = (bf16[2,64,128]{2,1,0:T(8,128)(2,1)S(1)}, bf16[2,64,128]{2,1,0:T(8,128)(2,1)S(1)}, u32[]{:S(2)}, u32[]{:S(2)}) collective-permute-start(bf16[2,64,128]{2,1,0:T(8,128)(2,1)S(1)} %get-tuple-element.58), channel_id=1, source_target_pairs={{0,1},{1,2},{2,3},{3,4},{4,5},{5,6},{6,7},{8,9},{9,10},{10,11},{11... | collective-permute-start | bytes 98312 | tf_op jit(solution)/shard_map/ppermute | solution.py:835
  15.3 3.7 %collective-permute-start.1 = (bf16[2,64,128]{2,1,0:T(8,128)(2,1)S(1)}, bf16[2,64,128]{2,1,0:T(8,128)(2,1)S(1)}, u32[]{:S(2)}, u32[]{:S(2)}) collective-permute-start(bf16[2,64,128]{2,1,0:T(8,128)(2,1)S(1)} %get-tuple-element.59), channel_id=1, source_target_pairs={{1,0},{2,1},{3,2},{4,3},{5,4},{6,5},{7,6},{9,8},{10,9},{11,10},{12... | collective-permute-start | bytes 98312 | tf_op jit(solution)/shard_map/ppermute | solution.py:835
  19.0 0.3 collective-permute-start.3
  19.3 1.2 %collective-permute-start.4 = (bf16[2,256,128]{2,1,0:T(8,128)(2,1)S(1)}, bf16[2,256,128]{2,1,0:T(8,128)(2,1)S(1)}, u32[]{:S(2)}, u32[]{:S(2)}) collective-permute-start(bf16[2,256,128]{2,1,0:T(8,128)(2,1)S(1)} %get-tuple-element.62.feat_ref.refs_0_), channel_id=1, source_target_pairs={{0,2},{1,3},{2,0},{3,1},{4,6},{5,7},{6,4},{7,5},{8,10},{9,11},{10,... | collective-permute-start | bytes 393224 | tf_op jit(solution)/shard_map/ppermute | solution.py:840
  20.5 0.0 copy-start
  20.5 2.0 %copy-done = bf16[128,120,120]{0,2,1:T(8,128)(2,1)S(1)} copy-done((bf16[128,120,120]{0,2,1:T(8,128)(2,1)S(1)}, bf16[128,120,120]{0,2,1:T(8,128)(2,1)}, u32[]{:S(2)}) %copy-start) | copy-done | bytes 3686424
  22.6 4.9 %turn.1 = (bf16[16,128,1024]{2,1,0:T(8,128)(2,1)S(1)}, bf16[8,128,2048]{2,1,0:T(8,128)(2,1)S(1)}) custom-call(bf16[120,120,128]{2,1,0:T(8,128)(2,1)S(1)} %bitcast.10), custom_call_target="tpu_custom_call" | custom-call | bytes 12582912 | tf_op jit(solution)/shard_map/turn/pallas_call | solution.py:131
  27.5 0.0 collective-permute-done.low_ref
  27.5 2.1 %collective-permute-start.5 = (bf16[2,256,128]{2,1,0:T(8,128)(2,1)S(1)}, bf16[2,256,128]{2,1,0:T(8,128)(2,1)S(1)}, u32[]{:S(2)}, u32[]{:S(2)}) collective-permute-start(bf16[2,256,128]{2,1,0:T(8,128)(2,1)S(1)} %get-tuple-element.62.feat_ref.refs_0_), channel_id=1, source_target_pairs={{0,3},{1,0},{2,1},{3,2},{4,7},{5,4},{6,5},{7,6},{8,11},{9,8},{10,9... | collective-permute-start | bytes 393224 | tf_op jit(solution)/shard_map/ppermute | solution.py:840
  29.6 0.0 collective-permute-done.1.high_ref
  29.6 0.0 collective-permute-done.2.recv_ref
  29.6 0.0 copy-done.5
  29.6 0.0 copy-done.6
  29.7 0.0 copy-start.1
  29.7 2.4 %mix.1 = (bf16[2,120,256]{2,1,0:T(8,128)(2,1)S(1)}, bf16[120,256]{1,0:T(8,128)(2,1)S(1)}, bf16[2,256,128]{2,1,0:T(8,128)(2,1)S(1)}, bf16[2,64,128]{2,1,0:T(8,128...) custom-call(s32[1]{0:T(128)} %bitcast.dev_ref, s32[64]{0:T(128)S(1)} %copy-done.4, ...), custom_call_target="tpu_custom_call" | custom-call | flops 2550136832 | bytes 7340032 | tf_op jit(solution)/shard_map/mix/pallas_call | solution.py:380
  32.0 1.9 %collective-permute-start.6 = (bf16[2,64,128]{2,1,0:T(8,128)(2,1)S(1)}, bf16[2,64,128]{2,1,0:T(8,128)(2,1)S(1)}, u32[]{:S(2)}, u32[]{:S(2)}) collective-permute-start(bf16[2,64,128]{2,1,0:T(8,128)(2,1)S(1)} %get-tuple-element.67), channel_id=1, source_target_pairs={{0,1},{1,2},{2,3},{3,4},{4,5},{5,6},{6,7},{8,9},{9,10},{10,11},{11... | collective-permute-start | bytes 98312 | tf_op jit(solution)/shard_map/ppermute | solution.py:835
  34.0 4.3 %collective-permute-start.7 = (bf16[2,64,128]{2,1,0:T(8,128)(2,1)S(1)}, bf16[2,64,128]{2,1,0:T(8,128)(2,1)S(1)}, u32[]{:S(2)}, u32[]{:S(2)}) collective-permute-start(bf16[2,64,128]{2,1,0:T(8,128)(2,1)S(1)} %get-tuple-element.68), channel_id=1, source_target_pairs={{1,0},{2,1},{3,2},{4,3},{5,4},{6,5},{7,6},{9,8},{10,9},{11,10},{12... | collective-permute-start | bytes 98312 | tf_op jit(solution)/shard_map/ppermute | solution.py:835
  38.3 0.0 collective-permute-done.3.refs_1_
  38.3 1.4 %collective-permute-start.11 = (bf16[120,256]{1,0:T(8,128)(2,1)S(1)}, bf16[120,256]{1,0:T(8,128)(2,1)S(1)}, u32[]{:S(2)}, u32[]{:S(2)}) collective-permute-start(bf16[120,256]{1,0:T(8,128)(2,1)S(1)} %get-tuple-element.78), channel_id=1, source_target_pairs={{0,128},{8,136},{16,144},{24,152},{32,160},{40,168},{48,176},{56,1... | collective-permute-start | bytes 184328 | tf_op jit(solution)/shard_map/ppermute | solution.py:887
  39.7 0.0 collective-permute-done.4.refs_2_
  39.7 0.0 collective-permute-done.5.refs_3_
  39.7 0.0 collective-permute-start.10
  39.7 2.0 %collective-permute-start.8 = (bf16[2,320,128]{2,1,0:T(8,128)(2,1)S(1)}, bf16[2,320,128]{2,1,0:T(8,128)(2,1)S(1)}, u32[]{:S(2)}, u32[]{:S(2)}) collective-permute-start(bf16[2,320,128]{2,1,0:T(8,128)(2,1)S(1)} %get-tuple-element.88.refs_4_), channel_id=1, source_target_pairs={{0,1},{1,2},{2,3},{3,0},{4,5},{5,6},{6,7},{7,4},{8,9},{9,10},{10,1... | collective-permute-start | bytes 491528 | tf_op jit(solution)/shard_map/ppermute | solution.py:840
  41.8 0.0 collective-permute-done.6.low_ref
  41.8 0.7 collective-permute-start.9
  42.5 0.0 collective-permute-done.7.high_ref
  42.5 0.0 copy-done.1
  42.5 5.0 %backward.1 = (bf16[2,512,512]{2,1,0:T(8,128)(2,1)}, bf16[4,576,128]{2,1,0:T(8,128)(2,1)S(1)}, bf16[4,576,128]{2,1,0:T(8,128)(2,1)S(1)}) custom-call(s32[1]{0:T(128)} %bitcast.dev_ref, s32[64]{0:T(128)S(1)} %copy-done.4, s32[16]{0:T(128)S(1)} %bitcast.16, bf16[2,256,128]{2,1,0:T(8,128)(2,1)S(1)} %get-tuple-element.66.slopes_ref, ...), custom_call_target="tpu_custom_call" | custom-call | flops 3758096384 | bytes 14680064 | tf_op jit(solution)/shard_map/backward/pallas_call | solution.py:633
  47.5 0.0 collective-permute-done.11.other_ref
  47.5 0.0 collective-permute-done.10.refs_7_
  47.5 0.0 collective-permute-done.8.refs_5_
  47.5 1.1 %collective-permute-done.9.refs_6_ = bf16[2,320,128]{2,1,0:T(8,128)(2,1)S(1)} collective-permute-done((bf16[2,320,128]{2,1,0:T(8,128)(2,1)S(1)}, bf16[2,320,128]{2,1,0:T(8,128)(2,1)S(1)}, u32[]{:S(2)}, u32[]{:S(2)}) %collective-permute-start.9) | collective-permute-done | bytes 163872 | tf_op jit(solution)/shard_map/ppermute | solution.py:840
  48.6 0.0 collective-permute-start.12
  48.6 2.0 %collective-permute-done.12.recv_ref = bf16[4,576,128]{2,1,0:T(8,128)(2,1)S(1)} collective-permute-done((bf16[4,576,128]{2,1,0:T(8,128)(2,1)S(1)}, bf16[4,576,128]{2,1,0:T(8,128)(2,1)S(1)}, u32[]{:S(2)}, u32[]{:S(2)}) %collective-permute-start.12) | collective-permute-done | bytes 589856 | tf_op jit(solution)/shard_map/ppermute | solution.py:889
  50.6 0.1 join.1
  50.7 4.6 %taps.1 = (bf16[2,16,64,128]{3,2,1,0:T(8,128)(2,1)S(1)}, bf16[2,16,64,128]{3,2,1,0:T(8,128)(2,1)S(1)}) custom-call(s32[1]{0:T(128)} %bitcast.dev_ref, s32[64]{0:T(128)S(1)} %copy-done.4, s32[16]{0:T(128)S(1)} %bitcast.17, bf16[2,256,128]{2,1,0:T(8,128)(2,1)S(1)} %get-tuple-element.62.feat_ref.refs_0_, ...), custom_call_target="tpu_custom_call" | custom-call | flops 2550136832 | bytes 4194304 | tf_op jit(solution)/shard_map/taps/pallas_call | solution.py:473
  55.4 0.2 collective-permute-start.13
  55.6 1.8 %collective-permute-done.13.recv_ref = bf16[2,16,64,128]{3,2,1,0:T(8,128)(2,1)S(1)} collective-permute-done((bf16[2,16,64,128]{3,2,1,0:T(8,128)(2,1)S(1)}, bf16[2,16,64,128]{3,2,1,0:T(8,128)(2,1)S(1)}, u32[]{:S(2)}, u32[]{:S(2)}) %collective-permute-start.13) | collective-permute-done | bytes 524320 | tf_op jit(solution)/shard_map/ppermute | solution.py:893
  57.4 0.1 halve.1
  57.5 0.1 collective-permute-start.14
  57.6 0.8 collective-permute-start.15
  58.4 4.0 %collective-permute-start.16 = (bf16[576,128]{1,0:T(8,128)(2,1)S(1)}, bf16[576,128]{1,0:T(8,128)(2,1)S(1)}, u32[]{:S(2)}, u32[]{:S(2)}) collective-permute-start(bf16[576,128]{1,0:T(8,128)(2,1)S(1)} %get-tuple-element.98), channel_id=1, source_target_pairs={{0,1},{1,2},{2,3},{3,0},{4,5},{5,6},{6,7},{7,4},{8,9},{9,10},{10,1... | collective-permute-start | bytes 442376 | tf_op jit(solution)/shard_map/ppermute | solution.py:840
  62.4 0.0 collective-permute-start.17
  62.4 3.4 %collective-permute-done.15.refs_3_ = bf16[576,128]{1,0:T(8,128)(2,1)S(1)} collective-permute-done((bf16[576,128]{1,0:T(8,128)(2,1)S(1)}, bf16[576,128]{1,0:T(8,128)(2,1)S(1)}, u32[]{:S(2)}, u32[]{:S(2)}) %collective-permute-start.15) | collective-permute-done | bytes 147488 | tf_op jit(solution)/shard_map/ppermute | solution.py:840
  65.8 2.5 %collective-permute-done.16.refs_4_ = bf16[576,128]{1,0:T(8,128)(2,1)S(1)} collective-permute-done((bf16[576,128]{1,0:T(8,128)(2,1)S(1)}, bf16[576,128]{1,0:T(8,128)(2,1)S(1)}, u32[]{:S(2)}, u32[]{:S(2)}) %collective-permute-start.16) | collective-permute-done | bytes 147488 | tf_op jit(solution)/shard_map/ppermute | solution.py:840
  68.2 0.1 collective-permute-done.17.refs_5_
  68.3 0.0 collective-permute-done.14.refs_1_
  68.3 0.2 cells.1
  68.5 32.7 %all_to_all.10.in_ref = bf16[16,96,128]{2,1,0:T(8,128)(2,1)S(1)} all-to-all(bf16[16,96,128]{2,1,0:T(8,128)(2,1)S(1)} %cells.1), channel_id=1, replica_groups={{0,16,32,48,64,80,96,112,128,144,160,176,192,208,224,240},{8,24,40,56,7..., dimensions={0} | all-to-all | bytes 786432 | tf_op jit(solution)/shard_map/all_to_all | solution.py:897
  101.2 0.1 total.1
  101.3 8.9 %all_to_all.11.in_ref = bf16[8,96,128]{2,1,0:T(8,128)(2,1)S(1)} all-to-all(bf16[8,96,128]{2,1,0:T(8,128)(2,1)S(1)} %total.1), channel_id=1, replica_groups=mesh['dp'=32,'mp'=8] {'mp'}, dimensions={0} | all-to-all | bytes 393216 | tf_op jit(solution)/shard_map/all_to_all | solution.py:898
  110.1 1.4 %finish.1 = (bf16[2,120,256]{2,1,0:T(8,128)(2,1)}, f32[4,120,120]{2,1,0:T(8,128)}, f32[32,512]{1,0:T(8,128)}, f32[16,120]{1,0:T(8,128)}, f32[5,16]{1,0:T(8,128)}) custom-call(s32[1]{0:T(128)} %bitcast.dev_ref, s32[64]{0:T(128)S(1)} %copy-done.4, s32[16]{0:T(128)S(1)} %bitcast.18, bf16[8,96,128]{2,1,0:T(8,128)(2,1)S(1)} %all_to_all.11.in_ref, ...), custom_call_target="tpu_custom_call" | custom-call | tf_op jit(solution)/shard_map/finish/pallas_call | solution.py:816
Async XLA Ops:
  0.6 29.0 %copy-start.5 = (s32[16,1]{0,1:T(1,128)S(1)}, s32[16,1]{0,1:T(1,128)}, u32[]{:S(2)}) copy-start(s32[16,1]{0,1:T(1,128)} %param.10) | copy-start | bytes 196
  0.6 29.0 %collective-permute-start.2 = (bf16[2,120,256]{2,1,0:T(8,128)(2,1)}, bf16[2,120,256]{2,1,0:T(8,128)(2,1)S(1)}, u32[]{:S(2)}, u32[]{:S(2)}) collective-permute-start(bf16[2,120,256]{2,1,0:T(8,128)(2,1)} %bitcast.21), channel_id=1, source_target_pairs={{0,128},{8,136},{16,144},{24,152},{32,160},{40,168},{48,176},{56,1... | collective-permute-start | bytes 368648 | tf_op jit(solution)/shard_map/ppermute | solution.py:862
  7.9 0.9 copy-start.2
  8.8 0.7 copy-start.3
  9.5 0.7 copy-start.4
  10.2 19.4 %copy-start.6 = (bf16[2,256,120]{1,2,0:T(8,128)(2,1)S(1)}, bf16[2,256,120]{1,2,0:T(8,128)(2,1)}, u32[]{:S(2)}) copy-start(bf16[2,256,120]{1,2,0:T(8,128)(2,1)} %param.15) | copy-start | bytes 368644
  13.2 14.4 %collective-permute-start = (bf16[2,64,128]{2,1,0:T(8,128)(2,1)S(1)}, bf16[2,64,128]{2,1,0:T(8,128)(2,1)S(1)}, u32[]{:S(2)}, u32[]{:S(2)}) collective-permute-start(bf16[2,64,128]{2,1,0:T(8,128)(2,1)S(1)} %get-tuple-element.58), channel_id=1, source_target_pairs={{0,1},{1,2},{2,3},{3,4},{4,5},{5,6},{6,7},{8,9},{9,10},{10,11},{11... | collective-permute-start | bytes 98312 | tf_op jit(solution)/shard_map/ppermute | solution.py:835
  15.3 14.4 %collective-permute-start.1 = (bf16[2,64,128]{2,1,0:T(8,128)(2,1)S(1)}, bf16[2,64,128]{2,1,0:T(8,128)(2,1)S(1)}, u32[]{:S(2)}, u32[]{:S(2)}) collective-permute-start(bf16[2,64,128]{2,1,0:T(8,128)(2,1)S(1)} %get-tuple-element.59), channel_id=1, source_target_pairs={{1,0},{2,1},{3,2},{4,3},{5,4},{6,5},{7,6},{9,8},{10,9},{11,10},{12... | collective-permute-start | bytes 98312 | tf_op jit(solution)/shard_map/ppermute | solution.py:835
  19.0 19.3 %collective-permute-start.3 = (bf16[2,256,128]{2,1,0:T(8,128)(2,1)S(1)}, bf16[2,256,128]{2,1,0:T(8,128)(2,1)S(1)}, u32[]{:S(2)}, u32[]{:S(2)}) collective-permute-start(bf16[2,256,128]{2,1,0:T(8,128)(2,1)S(1)} %get-tuple-element.62.feat_ref.refs_0_), channel_id=1, source_target_pairs={{0,1},{1,2},{2,3},{3,0},{4,5},{5,6},{6,7},{7,4},{8,9},{9,10},{10,1... | collective-permute-start | bytes 393224 | tf_op jit(solution)/shard_map/ppermute | solution.py:840
  19.3 20.4 %collective-permute-start.4 = (bf16[2,256,128]{2,1,0:T(8,128)(2,1)S(1)}, bf16[2,256,128]{2,1,0:T(8,128)(2,1)S(1)}, u32[]{:S(2)}, u32[]{:S(2)}) collective-permute-start(bf16[2,256,128]{2,1,0:T(8,128)(2,1)S(1)} %get-tuple-element.62.feat_ref.refs_0_), channel_id=1, source_target_pairs={{0,2},{1,3},{2,0},{3,1},{4,6},{5,7},{6,4},{7,5},{8,10},{9,11},{10,... | collective-permute-start | bytes 393224 | tf_op jit(solution)/shard_map/ppermute | solution.py:840
  20.5 2.0 %copy-start = (bf16[128,120,120]{0,2,1:T(8,128)(2,1)S(1)}, bf16[128,120,120]{0,2,1:T(8,128)(2,1)}, u32[]{:S(2)}) copy-start(bf16[128,120,120]{0,2,1:T(8,128)(2,1)} %param.14) | copy-start | bytes 11059204
  27.5 12.2 %collective-permute-start.5 = (bf16[2,256,128]{2,1,0:T(8,128)(2,1)S(1)}, bf16[2,256,128]{2,1,0:T(8,128)(2,1)S(1)}, u32[]{:S(2)}, u32[]{:S(2)}) collective-permute-start(bf16[2,256,128]{2,1,0:T(8,128)(2,1)S(1)} %get-tuple-element.62.feat_ref.refs_0_), channel_id=1, source_target_pairs={{0,3},{1,0},{2,1},{3,2},{4,7},{5,4},{6,5},{7,6},{8,11},{9,8},{10,9... | collective-permute-start | bytes 393224 | tf_op jit(solution)/shard_map/ppermute | solution.py:840
  29.7 12.8 %copy-start.1 = (bf16[1024,512]{1,0:T(8,128)(2,1)S(1)}, bf16[1024,512]{1,0:T(8,128)(2,1)}, u32[]{:S(2)}) copy-start(bf16[1024,512]{1,0:T(8,128)(2,1)} %conv_ref.1) | copy-start | bytes 3145732
  32.0 9.7 %collective-permute-start.6 = (bf16[2,64,128]{2,1,0:T(8,128)(2,1)S(1)}, bf16[2,64,128]{2,1,0:T(8,128)(2,1)S(1)}, u32[]{:S(2)}, u32[]{:S(2)}) collective-permute-start(bf16[2,64,128]{2,1,0:T(8,128)(2,1)S(1)} %get-tuple-element.67), channel_id=1, source_target_pairs={{0,1},{1,2},{2,3},{3,4},{4,5},{5,6},{6,7},{8,9},{9,10},{10,11},{11... | collective-permute-start | bytes 98312 | tf_op jit(solution)/shard_map/ppermute | solution.py:835
  34.0 8.5 %collective-permute-start.7 = (bf16[2,64,128]{2,1,0:T(8,128)(2,1)S(1)}, bf16[2,64,128]{2,1,0:T(8,128)(2,1)S(1)}, u32[]{:S(2)}, u32[]{:S(2)}) collective-permute-start(bf16[2,64,128]{2,1,0:T(8,128)(2,1)S(1)} %get-tuple-element.68), channel_id=1, source_target_pairs={{1,0},{2,1},{3,2},{4,3},{5,4},{6,5},{7,6},{9,8},{10,9},{11,10},{12... | collective-permute-start | bytes 98312 | tf_op jit(solution)/shard_map/ppermute | solution.py:835
  38.3 9.1 %collective-permute-start.11 = (bf16[120,256]{1,0:T(8,128)(2,1)S(1)}, bf16[120,256]{1,0:T(8,128)(2,1)S(1)}, u32[]{:S(2)}, u32[]{:S(2)}) collective-permute-start(bf16[120,256]{1,0:T(8,128)(2,1)S(1)} %get-tuple-element.78), channel_id=1, source_target_pairs={{0,128},{8,136},{16,144},{24,152},{32,160},{40,168},{48,176},{56,1... | collective-permute-start | bytes 184328 | tf_op jit(solution)/shard_map/ppermute | solution.py:887
  39.7 7.7 %collective-permute-start.10 = (bf16[2,320,128]{2,1,0:T(8,128)(2,1)S(1)}, bf16[2,320,128]{2,1,0:T(8,128)(2,1)S(1)}, u32[]{:S(2)}, u32[]{:S(2)}) collective-permute-start(bf16[2,320,128]{2,1,0:T(8,128)(2,1)S(1)} %get-tuple-element.88.refs_4_), channel_id=1, source_target_pairs={{0,3},{1,0},{2,1},{3,2},{4,7},{5,4},{6,5},{7,6},{8,11},{9,8},{10,9... | collective-permute-start | bytes 491528 | tf_op jit(solution)/shard_map/ppermute | solution.py:840
  39.7 7.7 %collective-permute-start.8 = (bf16[2,320,128]{2,1,0:T(8,128)(2,1)S(1)}, bf16[2,320,128]{2,1,0:T(8,128)(2,1)S(1)}, u32[]{:S(2)}, u32[]{:S(2)}) collective-permute-start(bf16[2,320,128]{2,1,0:T(8,128)(2,1)S(1)} %get-tuple-element.88.refs_4_), channel_id=1, source_target_pairs={{0,1},{1,2},{2,3},{3,0},{4,5},{5,6},{6,7},{7,4},{8,9},{9,10},{10,1... | collective-permute-start | bytes 491528 | tf_op jit(solution)/shard_map/ppermute | solution.py:840
  41.8 6.8 %collective-permute-start.9 = (bf16[2,320,128]{2,1,0:T(8,128)(2,1)S(1)}, bf16[2,320,128]{2,1,0:T(8,128)(2,1)S(1)}, u32[]{:S(2)}, u32[]{:S(2)}) collective-permute-start(bf16[2,320,128]{2,1,0:T(8,128)(2,1)S(1)} %get-tuple-element.88.refs_4_), channel_id=1, source_target_pairs={{0,2},{1,3},{2,0},{3,1},{4,6},{5,7},{6,4},{7,5},{8,10},{9,11},{10,... | collective-permute-start | bytes 491528 | tf_op jit(solution)/shard_map/ppermute | solution.py:840
  48.6 2.0 %collective-permute-start.12 = (bf16[4,576,128]{2,1,0:T(8,128)(2,1)S(1)}, bf16[4,576,128]{2,1,0:T(8,128)(2,1)S(1)}, u32[]{:S(2)}, u32[]{:S(2)}) collective-permute-start(bf16[4,576,128]{2,1,0:T(8,128)(2,1)S(1)} %get-tuple-element.79), channel_id=1, source_target_pairs={{0,8},{8,0},{16,24},{24,16},{32,40},{40,32},{48,56},{56,48},{64,72... | collective-permute-start | bytes 1769480 | tf_op jit(solution)/shard_map/ppermute | solution.py:889
  55.4 2.0 %collective-permute-start.13 = (bf16[2,16,64,128]{3,2,1,0:T(8,128)(2,1)S(1)}, bf16[2,16,64,128]{3,2,1,0:T(8,128)(2,1)S(1)}, u32[]{:S(2)}, u32[]{:S(2)}) collective-permute-start(bf16[2,16,64,128]{3,2,1,0:T(8,128)(2,1)S(1)} %get-tuple-element.93), channel_id=1, source_target_pairs={{0,8},{8,0},{16,24},{24,16},{32,40},{40,32},{48,56},{56,48},{64,72... | collective-permute-start | bytes 1572872 | tf_op jit(solution)/shard_map/ppermute | solution.py:893
  57.5 10.9 %collective-permute-start.14 = (bf16[16,64,128]{2,1,0:T(8,128)(2,1)S(1)}, bf16[16,64,128]{2,1,0:T(8,128)(2,1)S(1)}, u32[]{:S(2)}, u32[]{:S(2)}) collective-permute-start(bf16[16,64,128]{2,1,0:T(8,128)(2,1)S(1)} %get-tuple-element.95), channel_id=1, source_target_pairs={{0,4},{1,5},{2,6},{3,7},{4,0},{5,1},{6,2},{7,3},{8,12},{9,13},{10,... | collective-permute-start | bytes 786440 | tf_op jit(solution)/shard_map/ppermute | solution.py:894
  57.6 8.2 %collective-permute-start.15 = (bf16[576,128]{1,0:T(8,128)(2,1)S(1)}, bf16[576,128]{1,0:T(8,128)(2,1)S(1)}, u32[]{:S(2)}, u32[]{:S(2)}) collective-permute-start(bf16[576,128]{1,0:T(8,128)(2,1)S(1)} %get-tuple-element.97), channel_id=1, source_target_pairs={{0,2},{1,3},{2,0},{3,1},{4,6},{5,7},{6,4},{7,5},{8,10},{9,11},{10,... | collective-permute-start | bytes 442376 | tf_op jit(solution)/shard_map/ppermute | solution.py:840
  58.4 9.9 %collective-permute-start.16 = (bf16[576,128]{1,0:T(8,128)(2,1)S(1)}, bf16[576,128]{1,0:T(8,128)(2,1)S(1)}, u32[]{:S(2)}, u32[]{:S(2)}) collective-permute-start(bf16[576,128]{1,0:T(8,128)(2,1)S(1)} %get-tuple-element.98), channel_id=1, source_target_pairs={{0,1},{1,2},{2,3},{3,0},{4,5},{5,6},{6,7},{7,4},{8,9},{9,10},{10,1... | collective-permute-start | bytes 442376 | tf_op jit(solution)/shard_map/ppermute | solution.py:840
  62.4 5.9 %collective-permute-start.17 = (bf16[576,128]{1,0:T(8,128)(2,1)S(1)}, bf16[576,128]{1,0:T(8,128)(2,1)S(1)}, u32[]{:S(2)}, u32[]{:S(2)}) collective-permute-start(bf16[576,128]{1,0:T(8,128)(2,1)S(1)} %get-tuple-element.99), channel_id=1, source_target_pairs={{0,3},{1,0},{2,1},{3,2},{4,7},{5,4},{6,5},{7,6},{8,11},{9,8},{10,9... | collective-permute-start | bytes 442376 | tf_op jit(solution)/shard_map/ppermute | solution.py:840

commit v12 on v11

--- a/solution.py
+++ b/solution.py
@@ -418,7 +418,7 @@
 
 def taps_body(scale, dev_ref, len_ref, mov_ref, *refs):
     feat_refs, piece_refs, (keep_ref, send_ref) = refs[:X], refs[X : 2 * X], refs[2 * X : 2 * X + 2]
-    ext, windows, turned, sums = refs[2 * X + 2 :]
+    ext, windows, turned, sums, later = refs[2 * X + 2 :]
     place = Place(dev_ref, len_ref, mov_ref)
     slot = pl.program_id(0)
     spread = X * T
@@ -434,7 +434,9 @@
             x = lax.rem(place.x + (X - step), X)
             at = pl.multiple_of(x * T, T)
             ext[pl.ds(REACH + at, T), :] = feat_ref[0].astype(f32)
-            turned[:, pl.ds(at, T)] = piece_ref[0, :T, :].astype(f32).T.astype(bf16)
+            slopes = piece_ref[0, :T, :].astype(f32)
+            turned[:LANES, pl.ds(at, T)] = slopes.T.astype(bf16)
+            later[pl.ds(NEAR + at, T), :] = slopes
 
             @pl.when(x == 0)
             def _():
@@ -448,8 +450,15 @@
             windows[:, j * LANES : (j + 1) * LANES] = ext[
                 pl.ds(place.x + 4 * j, rows), :
             ].astype(bf16)
-        for q in range(K // NEAR):
-            sums[q] += nn(turned[...], windows[q * NEAR : q * NEAR + spread, :])
+        turned[:LANES, spread:] = jnp.zeros((LANES, LANES), bf16)
+        later[:NEAR, :] = jnp.zeros((NEAR, LANES), f32)
+        later[NEAR + spread :, :] = jnp.zeros((LANES - NEAR, LANES), f32)
+        turned[LANES:, :] = later[...].T.astype(bf16)
+        depth = spread + NEAR
+        for q in range(0, K // NEAR, 2):
+            pair = nn(turned[:, :depth], windows[q * NEAR : q * NEAR + depth, :])
+            sums[q] += pair[:LANES, :]
+            sums[q + 1] += pair[LANES:, :]
 
     @pl.when(slot == SLOTS - 1)
     def _():
@@ -479,8 +488,9 @@
         scratch_shapes=[
             pltpu.VMEM((spread + 2 * REACH, LANES), f32),
             pltpu.VMEM((spread + NEAR * (K // NEAR - 1), 4 * LANES), bf16),
-            pltpu.VMEM((LANES, spread), bf16),
+            pltpu.VMEM((2 * LANES, spread + LANES), bf16),
             pltpu.VMEM((K // NEAR, LANES, 4 * LANES), f32),
+            pltpu.VMEM((spread + LANES, LANES), f32),
         ],
         compiler_params=params(16),
         cost_estimate=cost(2 * SLOTS * SPAN * K * LANES * LANES, 4 << 20),

time: 112 us -> 109 us (0.973)
  blocking collectives: 41.5 us -> 32.2 us
  starting transfers between devices: 32.3 us -> 39.7 us
  Pallas kernels: 21.7 us -> 16.4 us
  waiting for transfers between devices: 10.9 us -> 14.8 us
    all_to_all x1, blocking collectives: 32.7 us -> 21.6 us  [per_device(): lax.all_to_all(cells, 'dp', 0, 0, axis_index_groups=groups, tiled=True)]
    ppermute x1, starting transfers between devices: 0.01 us -> 4.7 us  [per_device(): chunks = join(dev, keep, lax.ppermute(send, 'dp', core_swap))]
    pallas_call x1, Pallas kernels: 4.98 us -> 2.07 us  [backward(): pl.pallas_call(functools.partial(backward_body, scale), grid=(SLOTS,), ou...]
    ppermute x1, waiting for transfers between devices: 0.01 us -> 2.6 us  [per_device(): other = lax.ppermute(sent, 'dp', swap)]
    ppermute x9, waiting for transfers between devices: 7.07 us -> 8.99 us  [along_x(): return lax.ppermute(block, 'mp', route)]
    all_to_all x1, blocking collectives: 8.86 us -> 10.5 us  [per_device(): cells = lax.all_to_all(total(cells), 'mp', 0, 0, tiled=True)]
    pallas_call x1, Pallas kernels: 2.36 us -> 0.73 us  [mix(): pl.pallas_call(mix_body, grid=(SLOTS,), out_shape=(jax.ShapeDtypeStruct((...]
    ppermute x1, starting transfers between devices: 0.09 us -> 1.64 us  [per_device(): lax.ppermute(leave, 'mp', [(i, i ^ X) for i in range(MP)])]
  transfers between devices with their start and end apart: 18 -> 18, of which waited for: 6 -> 7; matrix products, arithmetic and copies ran while one was open for 0% -> 0% of each run, Pallas kernels for 14% -> 9%
where the time goes in v12:
time: 109 us; the launch traced here: 108 us
  starting transfers between devices  39.7 us (36%)
  blocking collectives  32.2 us (30%)
  Pallas kernels  16.4 us (15%)
  waiting for transfers between devices  14.8 us (14%)
  local copies, waits for them, and re-layouts  4.33 us (4%)
    all_to_all x1, blocking collectives, per_device(): lax.all_to_all(cells, 'dp', 0, 0, axis_index_groups=groups, tiled=True)  21.6 us
    ppermute x9, starting transfers between devices, along_x(): return lax.ppermute(block, 'mp', route)  11.2 us
    all_to_all x1, blocking collectives, per_device(): cells = lax.all_to_all(total(cells), 'mp', 0, 0, tiled=True)  10.5 us
    ppermute x9, waiting for transfers between devices, along_x(): return lax.ppermute(block, 'mp', route)  8.99 us
    ppermute x2, starting transfers between devices, neighbours(): lax.ppermute(head, 'mp', backward_route)  8.99 us
    ppermute x1, starting transfers between devices, per_device(): received = lax.ppermute(cot, 'dp', swap)  7.28 us
    ppermute x2, starting transfers between devices, neighbours(): lax.ppermute(tail, 'mp', forward)  5.32 us
    pallas_call x1, Pallas kernels, taps(): pl.pallas_call(functools.partial(taps_body, scale), grid=(SLOTS,), out_sh...  5.11 us
  transfers between devices with their start and end apart: 18, of which 7 were waited for; matrix products, arithmetic and copies ran while one was open for 0% of the time, Pallas kernels for 9%

profile of v12, /device:TPU:2, one launch (start us, length us, event | category | flops | bytes accessed | tf_op | source)
XLA Modules:
  0.0 108.2 jit_solution(4620333933856381519)
XLA Ops:
  0.6 0.0 copy-start.5
  0.6 7.3 %collective-permute-start.2 = (bf16[2,120,256]{2,1,0:T(8,128)(2,1)}, bf16[2,120,256]{2,1,0:T(8,128)(2,1)S(1)}, u32[]{:S(2)}, u32[]{:S(2)}) collective-permute-start(bf16[2,120,256]{2,1,0:T(8,128)(2,1)} %bitcast.21), channel_id=1, source_target_pairs={{0,128},{8,136},{16,144},{24,152},{32,160},{40,168},{48,176},{56,1... | collective-permute-start | bytes 368648 | tf_op jit(solution)/shard_map/ppermute | solution.py:872
  7.9 0.0 copy-start.2
  7.9 0.9 copy-done.2
  8.8 0.0 copy-start.3
  8.8 0.7 copy-done.3
  9.5 0.0 copy-start.4
  9.5 0.7 copy-done.4
  10.2 0.0 copy-start.6
  10.2 1.7 %encode.1 = (bf16[2,256,128]{2,1,0:T(8,128)(2,1)S(1)}, bf16[2,64,128]{2,1,0:T(8,128)(2,1)S(1)}, bf16[2,64,128]{2,1,0:T(8,128)(2,1)S(1)}, bf16[2,256,1024]{2,1,0:...) custom-call(s32[1]{0:T(128)} %bitcast.dev_ref, ...), custom_call_target="tpu_custom_call" | custom-call | flops 603979776 | bytes 8388608 | tf_op jit(solution)/shard_map/encode/pallas_call | solution.py:251
  11.9 3.4 %collective-permute-start = (bf16[2,64,128]{2,1,0:T(8,128)(2,1)S(1)}, bf16[2,64,128]{2,1,0:T(8,128)(2,1)S(1)}, u32[]{:S(2)}, u32[]{:S(2)}) collective-permute-start(bf16[2,64,128]{2,1,0:T(8,128)(2,1)S(1)} %get-tuple-element.58), channel_id=1, source_target_pairs={{0,1},{1,2},{2,3},{3,4},{4,5},{5,6},{6,7},{8,9},{9,10},{10,11},{11... | collective-permute-start | bytes 98312 | tf_op jit(solution)/shard_map/ppermute | solution.py:845
  15.3 3.0 %collective-permute-start.1 = (bf16[2,64,128]{2,1,0:T(8,128)(2,1)S(1)}, bf16[2,64,128]{2,1,0:T(8,128)(2,1)S(1)}, u32[]{:S(2)}, u32[]{:S(2)}) collective-permute-start(bf16[2,64,128]{2,1,0:T(8,128)(2,1)S(1)} %get-tuple-element.59), channel_id=1, source_target_pairs={{1,0},{2,1},{3,2},{4,3},{5,4},{6,5},{7,6},{9,8},{10,9},{11,10},{12... | collective-permute-start | bytes 98312 | tf_op jit(solution)/shard_map/ppermute | solution.py:845
  18.3 1.0 collective-permute-start.3
  19.3 0.7 collective-permute-start.4
  20.0 0.0 copy-start
  20.0 2.0 %copy-done = bf16[128,120,120]{0,2,1:T(8,128)(2,1)S(1)} copy-done((bf16[128,120,120]{0,2,1:T(8,128)(2,1)S(1)}, bf16[128,120,120]{0,2,1:T(8,128)(2,1)}, u32[]{:S(2)}) %copy-start) | copy-done | bytes 3686424
  22.1 4.9 %turn.1 = (bf16[16,128,1024]{2,1,0:T(8,128)(2,1)S(1)}, bf16[8,128,2048]{2,1,0:T(8,128)(2,1)S(1)}) custom-call(bf16[120,120,128]{2,1,0:T(8,128)(2,1)S(1)} %bitcast.10), custom_call_target="tpu_custom_call" | custom-call | bytes 12582912 | tf_op jit(solution)/shard_map/turn/pallas_call | solution.py:131
  27.0 0.0 collective-permute-done.low_ref
  27.0 2.6 %collective-permute-start.5 = (bf16[2,256,128]{2,1,0:T(8,128)(2,1)S(1)}, bf16[2,256,128]{2,1,0:T(8,128)(2,1)S(1)}, u32[]{:S(2)}, u32[]{:S(2)}) collective-permute-start(bf16[2,256,128]{2,1,0:T(8,128)(2,1)S(1)} %get-tuple-element.62.feat_ref.refs_0_), channel_id=1, source_target_pairs={{0,3},{1,0},{2,1},{3,2},{4,7},{5,4},{6,5},{7,6},{8,11},{9,8},{10,9... | collective-permute-start | bytes 393224 | tf_op jit(solution)/shard_map/ppermute | solution.py:850
  29.6 0.0 collective-permute-done.1.high_ref
  29.6 0.0 collective-permute-done.2.recv_ref
  29.6 0.0 copy-done.5
  29.6 0.0 copy-done.6
  29.7 0.0 copy-start.1
  29.7 0.7 mix.1
  30.4 1.9 %collective-permute-start.6 = (bf16[2,64,128]{2,1,0:T(8,128)(2,1)S(1)}, bf16[2,64,128]{2,1,0:T(8,128)(2,1)S(1)}, u32[]{:S(2)}, u32[]{:S(2)}) collective-permute-start(bf16[2,64,128]{2,1,0:T(8,128)(2,1)S(1)} %get-tuple-element.67), channel_id=1, source_target_pairs={{0,1},{1,2},{2,3},{3,4},{4,5},{5,6},{6,7},{8,9},{9,10},{10,11},{11... | collective-permute-start | bytes 98312 | tf_op jit(solution)/shard_map/ppermute | solution.py:845
  32.3 6.0 %collective-permute-start.7 = (bf16[2,64,128]{2,1,0:T(8,128)(2,1)S(1)}, bf16[2,64,128]{2,1,0:T(8,128)(2,1)S(1)}, u32[]{:S(2)}, u32[]{:S(2)}) collective-permute-start(bf16[2,64,128]{2,1,0:T(8,128)(2,1)S(1)} %get-tuple-element.68), channel_id=1, source_target_pairs={{1,0},{2,1},{3,2},{4,3},{5,4},{6,5},{7,6},{9,8},{10,9},{11,10},{12... | collective-permute-start | bytes 98312 | tf_op jit(solution)/shard_map/ppermute | solution.py:845
  38.3 0.0 collective-permute-done.3.refs_1_
  38.3 0.1 collective-permute-start.11
  38.4 0.0 collective-permute-done.4.refs_2_
  38.4 0.0 collective-permute-done.5.refs_3_
  38.5 0.1 collective-permute-start.10
  38.5 2.0 %collective-permute-start.8 = (bf16[2,320,128]{2,1,0:T(8,128)(2,1)S(1)}, bf16[2,320,128]{2,1,0:T(8,128)(2,1)S(1)}, u32[]{:S(2)}, u32[]{:S(2)}) collective-permute-start(bf16[2,320,128]{2,1,0:T(8,128)(2,1)S(1)} %get-tuple-element.88.refs_4_), channel_id=1, source_target_pairs={{0,1},{1,2},{2,3},{3,0},{4,5},{5,6},{6,7},{7,4},{8,9},{9,10},{10,1... | collective-permute-start | bytes 491528 | tf_op jit(solution)/shard_map/ppermute | solution.py:850
  40.6 0.0 collective-permute-done.6.low_ref
  40.6 1.6 %collective-permute-start.9 = (bf16[2,320,128]{2,1,0:T(8,128)(2,1)S(1)}, bf16[2,320,128]{2,1,0:T(8,128)(2,1)S(1)}, u32[]{:S(2)}, u32[]{:S(2)}) collective-permute-start(bf16[2,320,128]{2,1,0:T(8,128)(2,1)S(1)} %get-tuple-element.88.refs_4_), channel_id=1, source_target_pairs={{0,2},{1,3},{2,0},{3,1},{4,6},{5,7},{6,4},{7,5},{8,10},{9,11},{10,... | collective-permute-start | bytes 491528 | tf_op jit(solution)/shard_map/ppermute | solution.py:850
  42.2 0.0 collective-permute-done.7.high_ref
  42.2 0.0 copy-done.1
  42.2 2.1 %backward.1 = (bf16[2,512,512]{2,1,0:T(8,128)(2,1)}, bf16[4,576,128]{2,1,0:T(8,128)(2,1)S(1)}, bf16[4,576,128]{2,1,0:T(8,128)(2,1)S(1)}) custom-call(s32[1]{0:T(128)} %bitcast.dev_ref, s32[64]{0:T(128)S(1)} %copy-done.4, s32[16]{0:T(128)S(1)} %bitcast.16, bf16[2,256,128]{2,1,0:T(8,128)(2,1)S(1)} %get-tuple-element.66.slopes_ref, ...), custom_call_target="tpu_custom_call" | custom-call | flops 3758096384 | bytes 14680064 | tf_op jit(solution)/shard_map/backward/pallas_call | solution.py:643
  44.3 2.6 %collective-permute-done.11.other_ref = bf16[120,256]{1,0:T(8,128)(2,1)S(1)} collective-permute-done((bf16[120,256]{1,0:T(8,128)(2,1)S(1)}, bf16[120,256]{1,0:T(8,128)(2,1)S(1)}, u32[]{:S(2)}, u32[]{:S(2)}) %collective-permute-start.11) | collective-permute-done | bytes 61472 | tf_op jit(solution)/shard_map/ppermute | solution.py:897
  46.9 0.0 collective-permute-done.10.refs_7_
  46.9 0.0 collective-permute-done.8.refs_5_
  46.9 1.6 %collective-permute-done.9.refs_6_ = bf16[2,320,128]{2,1,0:T(8,128)(2,1)S(1)} collective-permute-done((bf16[2,320,128]{2,1,0:T(8,128)(2,1)S(1)}, bf16[2,320,128]{2,1,0:T(8,128)(2,1)S(1)}, u32[]{:S(2)}, u32[]{:S(2)}) %collective-permute-start.9) | collective-permute-done | bytes 163872 | tf_op jit(solution)/shard_map/ppermute | solution.py:850
  48.5 4.7 %collective-permute-start.12 = (bf16[4,576,128]{2,1,0:T(8,128)(2,1)S(1)}, bf16[4,576,128]{2,1,0:T(8,128)(2,1)S(1)}, u32[]{:S(2)}, u32[]{:S(2)}) collective-permute-start(bf16[4,576,128]{2,1,0:T(8,128)(2,1)S(1)} %get-tuple-element.79), channel_id=1, source_target_pairs={{0,8},{8,0},{16,24},{24,16},{32,40},{40,32},{48,56},{56,48},{64,72... | collective-permute-start | bytes 1769480 | tf_op jit(solution)/shard_map/ppermute | solution.py:899
  53.2 1.6 %collective-permute-done.12.recv_ref = bf16[4,576,128]{2,1,0:T(8,128)(2,1)S(1)} collective-permute-done((bf16[4,576,128]{2,1,0:T(8,128)(2,1)S(1)}, bf16[4,576,128]{2,1,0:T(8,128)(2,1)S(1)}, u32[]{:S(2)}, u32[]{:S(2)}) %collective-permute-start.12) | collective-permute-done | bytes 589856 | tf_op jit(solution)/shard_map/ppermute | solution.py:899
  54.8 0.1 join.1
  55.0 5.1 %taps.1 = (bf16[2,16,64,128]{3,2,1,0:T(8,128)(2,1)S(1)}, bf16[2,16,64,128]{3,2,1,0:T(8,128)(2,1)S(1)}) custom-call(s32[1]{0:T(128)} %bitcast.dev_ref, s32[64]{0:T(128)S(1)} %copy-done.4, s32[16]{0:T(128)S(1)} %bitcast.17, bf16[2,256,128]{2,1,0:T(8,128)(2,1)S(1)} %get-tuple-element.62.feat_ref.refs_0_, ...), custom_call_target="tpu_custom_call" | custom-call | flops 2550136832 | bytes 4194304 | tf_op jit(solution)/shard_map/taps/pallas_call | solution.py:482
  60.1 0.5 collective-permute-start.13
  60.5 1.5 %collective-permute-done.13.recv_ref = bf16[2,16,64,128]{3,2,1,0:T(8,128)(2,1)S(1)} collective-permute-done((bf16[2,16,64,128]{3,2,1,0:T(8,128)(2,1)S(1)}, bf16[2,16,64,128]{3,2,1,0:T(8,128)(2,1)S(1)}, u32[]{:S(2)}, u32[]{:S(2)}) %collective-permute-start.13) | collective-permute-done | bytes 524320 | tf_op jit(solution)/shard_map/ppermute | solution.py:903
  62.1 0.1 halve.1
  62.2 1.6 %collective-permute-start.14 = (bf16[16,64,128]{2,1,0:T(8,128)(2,1)S(1)}, bf16[16,64,128]{2,1,0:T(8,128)(2,1)S(1)}, u32[]{:S(2)}, u32[]{:S(2)}) collective-permute-start(bf16[16,64,128]{2,1,0:T(8,128)(2,1)S(1)} %get-tuple-element.95), channel_id=1, source_target_pairs={{0,4},{1,5},{2,6},{3,7},{4,0},{5,1},{6,2},{7,3},{8,12},{9,13},{10,... | collective-permute-start | bytes 786440 | tf_op jit(solution)/shard_map/ppermute | solution.py:904
  63.8 1.0 collective-permute-start.15
  64.9 0.5 collective-permute-start.16
  65.4 1.6 %collective-permute-start.17 = (bf16[576,128]{1,0:T(8,128)(2,1)S(1)}, bf16[576,128]{1,0:T(8,128)(2,1)S(1)}, u32[]{:S(2)}, u32[]{:S(2)}) collective-permute-start(bf16[576,128]{1,0:T(8,128)(2,1)S(1)} %get-tuple-element.99), channel_id=1, source_target_pairs={{0,3},{1,0},{2,1},{3,2},{4,7},{5,4},{6,5},{7,6},{8,11},{9,8},{10,9... | collective-permute-start | bytes 442376 | tf_op jit(solution)/shard_map/ppermute | solution.py:850
  67.0 5.1 %collective-permute-done.15.refs_3_ = bf16[576,128]{1,0:T(8,128)(2,1)S(1)} collective-permute-done((bf16[576,128]{1,0:T(8,128)(2,1)S(1)}, bf16[576,128]{1,0:T(8,128)(2,1)S(1)}, u32[]{:S(2)}, u32[]{:S(2)}) %collective-permute-start.15) | collective-permute-done | bytes 147488 | tf_op jit(solution)/shard_map/ppermute | solution.py:850
  72.1 1.9 %collective-permute-done.16.refs_4_ = bf16[576,128]{1,0:T(8,128)(2,1)S(1)} collective-permute-done((bf16[576,128]{1,0:T(8,128)(2,1)S(1)}, bf16[576,128]{1,0:T(8,128)(2,1)S(1)}, u32[]{:S(2)}, u32[]{:S(2)}) %collective-permute-start.16) | collective-permute-done | bytes 147488 | tf_op jit(solution)/shard_map/ppermute | solution.py:850
  74.0 0.4 collective-permute-done.17.refs_5_
  74.3 0.0 collective-permute-done.14.refs_1_
  74.3 0.2 cells.1
  74.5 21.6 %all_to_all.10.in_ref = bf16[16,96,128]{2,1,0:T(8,128)(2,1)S(1)} all-to-all(bf16[16,96,128]{2,1,0:T(8,128)(2,1)S(1)} %cells.1), channel_id=1, replica_groups={{0,16,32,48,64,80,96,112,128,144,160,176,192,208,224,240},{8,24,40,56,7..., dimensions={0} | all-to-all | bytes 786432 | tf_op jit(solution)/shard_map/all_to_all | solution.py:907
  96.2 0.1 total.1
  96.2 10.5 %all_to_all.11.in_ref = bf16[8,96,128]{2,1,0:T(8,128)(2,1)S(1)} all-to-all(bf16[8,96,128]{2,1,0:T(8,128)(2,1)S(1)} %total.1), channel_id=1, replica_groups=mesh['dp'=32,'mp'=8] {'mp'}, dimensions={0} | all-to-all | bytes 393216 | tf_op jit(solution)/shard_map/all_to_all | solution.py:908
  106.8 1.4 %finish.1 = (bf16[2,120,256]{2,1,0:T(8,128)(2,1)}, f32[4,120,120]{2,1,0:T(8,128)}, f32[32,512]{1,0:T(8,128)}, f32[16,120]{1,0:T(8,128)}, f32[5,16]{1,0:T(8,128)}) custom-call(s32[1]{0:T(128)} %bitcast.dev_ref, s32[64]{0:T(128)S(1)} %copy-done.4, s32[16]{0:T(128)S(1)} %bitcast.18, bf16[8,96,128]{2,1,0:T(8,128)(2,1)S(1)} %all_to_all.11.in_ref, ...), custom_call_target="tpu_custom_call" | custom-call | tf_op jit(solution)/shard_map/finish/pallas_call | solution.py:826
Async XLA Ops:
  0.6 29.0 %copy-start.5 = (s32[16,1]{0,1:T(1,128)S(1)}, s32[16,1]{0,1:T(1,128)}, u32[]{:S(2)}) copy-start(s32[16,1]{0,1:T(1,128)} %param.10) | copy-start | bytes 196
  0.6 29.0 %collective-permute-start.2 = (bf16[2,120,256]{2,1,0:T(8,128)(2,1)}, bf16[2,120,256]{2,1,0:T(8,128)(2,1)S(1)}, u32[]{:S(2)}, u32[]{:S(2)}) collective-permute-start(bf16[2,120,256]{2,1,0:T(8,128)(2,1)} %bitcast.21), channel_id=1, source_target_pairs={{0,128},{8,136},{16,144},{24,152},{32,160},{40,168},{48,176},{56,1... | collective-permute-start | bytes 368648 | tf_op jit(solution)/shard_map/ppermute | solution.py:872
  7.9 0.9 copy-start.2
  8.8 0.7 copy-start.3
  9.5 0.7 copy-start.4
  10.2 19.4 %copy-start.6 = (bf16[2,256,120]{1,2,0:T(8,128)(2,1)S(1)}, bf16[2,256,120]{1,2,0:T(8,128)(2,1)}, u32[]{:S(2)}) copy-start(bf16[2,256,120]{1,2,0:T(8,128)(2,1)} %param.15) | copy-start | bytes 368644
  11.9 15.1 %collective-permute-start = (bf16[2,64,128]{2,1,0:T(8,128)(2,1)S(1)}, bf16[2,64,128]{2,1,0:T(8,128)(2,1)S(1)}, u32[]{:S(2)}, u32[]{:S(2)}) collective-permute-start(bf16[2,64,128]{2,1,0:T(8,128)(2,1)S(1)} %get-tuple-element.58), channel_id=1, source_target_pairs={{0,1},{1,2},{2,3},{3,4},{4,5},{5,6},{6,7},{8,9},{9,10},{10,11},{11... | collective-permute-start | bytes 98312 | tf_op jit(solution)/shard_map/ppermute | solution.py:845
  15.3 14.4 %collective-permute-start.1 = (bf16[2,64,128]{2,1,0:T(8,128)(2,1)S(1)}, bf16[2,64,128]{2,1,0:T(8,128)(2,1)S(1)}, u32[]{:S(2)}, u32[]{:S(2)}) collective-permute-start(bf16[2,64,128]{2,1,0:T(8,128)(2,1)S(1)} %get-tuple-element.59), channel_id=1, source_target_pairs={{1,0},{2,1},{3,2},{4,3},{5,4},{6,5},{7,6},{9,8},{10,9},{11,10},{12... | collective-permute-start | bytes 98312 | tf_op jit(solution)/shard_map/ppermute | solution.py:845
  18.3 20.0 %collective-permute-start.3 = (bf16[2,256,128]{2,1,0:T(8,128)(2,1)S(1)}, bf16[2,256,128]{2,1,0:T(8,128)(2,1)S(1)}, u32[]{:S(2)}, u32[]{:S(2)}) collective-permute-start(bf16[2,256,128]{2,1,0:T(8,128)(2,1)S(1)} %get-tuple-element.62.feat_ref.refs_0_), channel_id=1, source_target_pairs={{0,1},{1,2},{2,3},{3,0},{4,5},{5,6},{6,7},{7,4},{8,9},{9,10},{10,1... | collective-permute-start | bytes 393224 | tf_op jit(solution)/shard_map/ppermute | solution.py:850
  19.3 19.1 %collective-permute-start.4 = (bf16[2,256,128]{2,1,0:T(8,128)(2,1)S(1)}, bf16[2,256,128]{2,1,0:T(8,128)(2,1)S(1)}, u32[]{:S(2)}, u32[]{:S(2)}) collective-permute-start(bf16[2,256,128]{2,1,0:T(8,128)(2,1)S(1)} %get-tuple-element.62.feat_ref.refs_0_), channel_id=1, source_target_pairs={{0,2},{1,3},{2,0},{3,1},{4,6},{5,7},{6,4},{7,5},{8,10},{9,11},{10,... | collective-permute-start | bytes 393224 | tf_op jit(solution)/shard_map/ppermute | solution.py:850
  20.0 2.0 %copy-start = (bf16[128,120,120]{0,2,1:T(8,128)(2,1)S(1)}, bf16[128,120,120]{0,2,1:T(8,128)(2,1)}, u32[]{:S(2)}) copy-start(bf16[128,120,120]{0,2,1:T(8,128)(2,1)} %param.14) | copy-start | bytes 11059204
  27.0 11.4 %collective-permute-start.5 = (bf16[2,256,128]{2,1,0:T(8,128)(2,1)S(1)}, bf16[2,256,128]{2,1,0:T(8,128)(2,1)S(1)}, u32[]{:S(2)}, u32[]{:S(2)}) collective-permute-start(bf16[2,256,128]{2,1,0:T(8,128)(2,1)S(1)} %get-tuple-element.62.feat_ref.refs_0_), channel_id=1, source_target_pairs={{0,3},{1,0},{2,1},{3,2},{4,7},{5,4},{6,5},{7,6},{8,11},{9,8},{10,9... | collective-permute-start | bytes 393224 | tf_op jit(solution)/shard_map/ppermute | solution.py:850
  29.7 12.6 %copy-start.1 = (bf16[1024,512]{1,0:T(8,128)(2,1)S(1)}, bf16[1024,512]{1,0:T(8,128)(2,1)}, u32[]{:S(2)}) copy-start(bf16[1024,512]{1,0:T(8,128)(2,1)} %conv_ref.1) | copy-start | bytes 3145732
  30.4 10.2 %collective-permute-start.6 = (bf16[2,64,128]{2,1,0:T(8,128)(2,1)S(1)}, bf16[2,64,128]{2,1,0:T(8,128)(2,1)S(1)}, u32[]{:S(2)}, u32[]{:S(2)}) collective-permute-start(bf16[2,64,128]{2,1,0:T(8,128)(2,1)S(1)} %get-tuple-element.67), channel_id=1, source_target_pairs={{0,1},{1,2},{2,3},{3,4},{4,5},{5,6},{6,7},{8,9},{9,10},{10,11},{11... | collective-permute-start | bytes 98312 | tf_op jit(solution)/shard_map/ppermute | solution.py:845
  32.3 9.9 %collective-permute-start.7 = (bf16[2,64,128]{2,1,0:T(8,128)(2,1)S(1)}, bf16[2,64,128]{2,1,0:T(8,128)(2,1)S(1)}, u32[]{:S(2)}, u32[]{:S(2)}) collective-permute-start(bf16[2,64,128]{2,1,0:T(8,128)(2,1)S(1)} %get-tuple-element.68), channel_id=1, source_target_pairs={{1,0},{2,1},{3,2},{4,3},{5,4},{6,5},{7,6},{9,8},{10,9},{11,10},{12... | collective-permute-start | bytes 98312 | tf_op jit(solution)/shard_map/ppermute | solution.py:845
  38.3 8.6 %collective-permute-start.11 = (bf16[120,256]{1,0:T(8,128)(2,1)S(1)}, bf16[120,256]{1,0:T(8,128)(2,1)S(1)}, u32[]{:S(2)}, u32[]{:S(2)}) collective-permute-start(bf16[120,256]{1,0:T(8,128)(2,1)S(1)} %get-tuple-element.78), channel_id=1, source_target_pairs={{0,128},{8,136},{16,144},{24,152},{32,160},{40,168},{48,176},{56,1... | collective-permute-start | bytes 184328 | tf_op jit(solution)/shard_map/ppermute | solution.py:897
  38.5 8.4 %collective-permute-start.10 = (bf16[2,320,128]{2,1,0:T(8,128)(2,1)S(1)}, bf16[2,320,128]{2,1,0:T(8,128)(2,1)S(1)}, u32[]{:S(2)}, u32[]{:S(2)}) collective-permute-start(bf16[2,320,128]{2,1,0:T(8,128)(2,1)S(1)} %get-tuple-element.88.refs_4_), channel_id=1, source_target_pairs={{0,3},{1,0},{2,1},{3,2},{4,7},{5,4},{6,5},{7,6},{8,11},{9,8},{10,9... | collective-permute-start | bytes 491528 | tf_op jit(solution)/shard_map/ppermute | solution.py:850
  38.5 8.3 %collective-permute-start.8 = (bf16[2,320,128]{2,1,0:T(8,128)(2,1)S(1)}, bf16[2,320,128]{2,1,0:T(8,128)(2,1)S(1)}, u32[]{:S(2)}, u32[]{:S(2)}) collective-permute-start(bf16[2,320,128]{2,1,0:T(8,128)(2,1)S(1)} %get-tuple-element.88.refs_4_), channel_id=1, source_target_pairs={{0,1},{1,2},{2,3},{3,0},{4,5},{5,6},{6,7},{7,4},{8,9},{9,10},{10,1... | collective-permute-start | bytes 491528 | tf_op jit(solution)/shard_map/ppermute | solution.py:850
  40.6 7.9 %collective-permute-start.9 = (bf16[2,320,128]{2,1,0:T(8,128)(2,1)S(1)}, bf16[2,320,128]{2,1,0:T(8,128)(2,1)S(1)}, u32[]{:S(2)}, u32[]{:S(2)}) collective-permute-start(bf16[2,320,128]{2,1,0:T(8,128)(2,1)S(1)} %get-tuple-element.88.refs_4_), channel_id=1, source_target_pairs={{0,2},{1,3},{2,0},{3,1},{4,6},{5,7},{6,4},{7,5},{8,10},{9,11},{10,... | collective-permute-start | bytes 491528 | tf_op jit(solution)/shard_map/ppermute | solution.py:850
  48.5 6.3 %collective-permute-start.12 = (bf16[4,576,128]{2,1,0:T(8,128)(2,1)S(1)}, bf16[4,576,128]{2,1,0:T(8,128)(2,1)S(1)}, u32[]{:S(2)}, u32[]{:S(2)}) collective-permute-start(bf16[4,576,128]{2,1,0:T(8,128)(2,1)S(1)} %get-tuple-element.79), channel_id=1, source_target_pairs={{0,8},{8,0},{16,24},{24,16},{32,40},{40,32},{48,56},{56,48},{64,72... | collective-permute-start | bytes 1769480 | tf_op jit(solution)/shard_map/ppermute | solution.py:899
  60.1 2.0 %collective-permute-start.13 = (bf16[2,16,64,128]{3,2,1,0:T(8,128)(2,1)S(1)}, bf16[2,16,64,128]{3,2,1,0:T(8,128)(2,1)S(1)}, u32[]{:S(2)}, u32[]{:S(2)}) collective-permute-start(bf16[2,16,64,128]{3,2,1,0:T(8,128)(2,1)S(1)} %get-tuple-element.93), channel_id=1, source_target_pairs={{0,8},{8,0},{16,24},{24,16},{32,40},{40,32},{48,56},{56,48},{64,72... | collective-permute-start | bytes 1572872 | tf_op jit(solution)/shard_map/ppermute | solution.py:903
  62.2 12.1 %collective-permute-start.14 = (bf16[16,64,128]{2,1,0:T(8,128)(2,1)S(1)}, bf16[16,64,128]{2,1,0:T(8,128)(2,1)S(1)}, u32[]{:S(2)}, u32[]{:S(2)}) collective-permute-start(bf16[16,64,128]{2,1,0:T(8,128)(2,1)S(1)} %get-tuple-element.95), channel_id=1, source_target_pairs={{0,4},{1,5},{2,6},{3,7},{4,0},{5,1},{6,2},{7,3},{8,12},{9,13},{10,... | collective-permute-start | bytes 786440 | tf_op jit(solution)/shard_map/ppermute | solution.py:904
  63.8 8.3 %collective-permute-start.15 = (bf16[576,128]{1,0:T(8,128)(2,1)S(1)}, bf16[576,128]{1,0:T(8,128)(2,1)S(1)}, u32[]{:S(2)}, u32[]{:S(2)}) collective-permute-start(bf16[576,128]{1,0:T(8,128)(2,1)S(1)} %get-tuple-element.97), channel_id=1, source_target_pairs={{0,2},{1,3},{2,0},{3,1},{4,6},{5,7},{6,4},{7,5},{8,10},{9,11},{10,... | collective-permute-start | bytes 442376 | tf_op jit(solution)/shard_map/ppermute | solution.py:850
  64.9 9.1 %collective-permute-start.16 = (bf16[576,128]{1,0:T(8,128)(2,1)S(1)}, bf16[576,128]{1,0:T(8,128)(2,1)S(1)}, u32[]{:S(2)}, u32[]{:S(2)}) collective-permute-start(bf16[576,128]{1,0:T(8,128)(2,1)S(1)} %get-tuple-element.98), channel_id=1, source_target_pairs={{0,1},{1,2},{2,3},{3,0},{4,5},{5,6},{6,7},{7,4},{8,9},{9,10},{10,1... | collective-permute-start | bytes 442376 | tf_op jit(solution)/shard_map/ppermute | solution.py:850
  65.4 9.0 %collective-permute-start.17 = (bf16[576,128]{1,0:T(8,128)(2,1)S(1)}, bf16[576,128]{1,0:T(8,128)(2,1)S(1)}, u32[]{:S(2)}, u32[]{:S(2)}) collective-permute-start(bf16[576,128]{1,0:T(8,128)(2,1)S(1)} %get-tuple-element.99), channel_id=1, source_target_pairs={{0,3},{1,0},{2,1},{3,2},{4,7},{5,4},{6,5},{7,6},{8,11},{9,8},{10,9... | collective-permute-start | bytes 442376 | tf_op jit(solution)/shard_map/ppermute | solution.py:850
